TPU v7x, 32 devices: a whole 2x2x4 slice. The times are simulated.
32 devices in a mesh: batch: 4 (over z), row: 2 (over x), col: 4 (over y, core).
Axes of the slice: x: 2, y: 2, z: 4, core: 2. Of those that a mesh axis runs over, the one named last changes fastest.
Arguments:
- latents: bfloat16 [8, 4, 64, 64], P('batch', None, 'row', 'col'), may hold values from -6 to 6
- conditioning: bfloat16 [8, 1152], P('batch'), may hold values from -6 to 6
- kept_index: int32 [8, 1024], P('batch'), may hold values from 0 to 1023, each once within a row
- kept_count: int32 [8], P('batch'), may hold values from 256 to 768
- patch_weight: bfloat16 [16, 1152], P(None, 'batch'), may hold values from -1.5 to 1.5
- patch_bias: bfloat16 [1152], P('batch'), may hold values from -3 to 3
- adaptive_weight: bfloat16 [2, 1152, 6912], P(None, 'batch'), may hold values from -0.1875 to 0.1875
- adaptive_bias: bfloat16 [2, 6912], P(None, 'batch'), may hold values from -1.75 to 1.75
- project_weight: bfloat16 [2, 1152, 3456], P(None, 'batch'), may hold values from -0.1875 to 0.1875
- project_bias: bfloat16 [2, 2304], P(None, 'batch'), may hold values from -1.75 to 1.75
- attend_weight: bfloat16 [2, 1152, 1152], P(None, 'batch'), may hold values from -0.75 to 0.75
- attend_bias: bfloat16 [2, 1152], P(None, 'batch'), may hold values from -1.75 to 1.75
- expand_weight: bfloat16 [2, 1152, 4608], P(None, 'batch'), may hold values from -0.1875 to 0.1875
- expand_bias: bfloat16 [2, 4608], P(None, 'batch'), may hold values from -1.75 to 1.75
- shrink_weight: bfloat16 [2, 4608, 1152], P(None, None, 'batch'), may hold values from -0.125 to 0.125
- shrink_bias: bfloat16 [2, 1152], P(None, 'batch'), may hold values from -1.75 to 1.75
- final_adaptive: bfloat16 [1152, 2304], P('batch'), may hold values from -0.1875 to 0.1875
- final_offset: bfloat16 [2304], P('batch'), may hold values from -1.75 to 1.75
- final_weight: bfloat16 [1152, 32], P('batch'), may hold values from -0.1875 to 0.1875
- final_bias: bfloat16 [32], replicated, may hold values from -3 to 3
- cotangent: bfloat16 [8, 8, 64, 64], P('batch', None, 'row', 'col'), may hold values from -6 to 6
Outputs:
- prediction: float32 [8, 8, 64, 64], P('batch', None, 'row', 'col')
- latent_grad: float32 [8, 4, 64, 64], P('batch', None, 'row', 'col')
- conditioning_grad: float32 [8, 1152], P('batch')
- patch_weight_grad: float32 [16, 1152], P(None, 'batch')
- patch_bias_grad: float32 [1152], P('batch')
- adaptive_weight_grad: float32 [2, 1152, 6912], P(None, 'batch')
- adaptive_bias_grad: float32 [2, 6912], P(None, 'batch')
- project_weight_grad: float32 [2, 1152, 3456], P(None, 'batch')
- project_bias_grad: float32 [2, 2304], P(None, 'batch')
- attend_weight_grad: float32 [2, 1152, 1152], P(None, 'batch')
- attend_bias_grad: float32 [2, 1152], P(None, 'batch')
- expand_weight_grad: float32 [2, 1152, 4608], P(None, 'batch')
- expand_bias_grad: float32 [2, 4608], P(None, 'batch')
- shrink_weight_grad: float32 [2, 4608, 1152], P(None, None, 'batch')
- shrink_bias_grad: float32 [2, 1152], P(None, 'batch')
- final_adaptive_grad: float32 [1152, 2304], P('batch')
- final_offset_grad: float32 [2304], P('batch')
- final_weight_grad: float32 [1152, 32], P('batch')
- final_bias_grad: float32 [32], replicated
Inputs may be any that keep to these rules, and one draw needn't show every extreme that they name: Each row lists all 1024 tokens of its image once; the tokens that the routed block keeps are kept_index[i, j] for j < kept_count[i]. Token t lies at grid row t // 32 and column t % 32.
All inputs are finite; a program needn't handle non-finite values.
Results may differ from a plain program's by a relative error of at most 0.018.
Values may be sent and summed in bfloat16 or wider, within the bound.
A program may use at most 384 MiB of HBM per device.

v0:
```python
from functools import partial

import jax
import jax.numpy as jnp
from jax import lax
from jax.sharding import PartitionSpec as P

HEADS = 16
PATCH = 2


norm_epsilon = 1e-06
masked_score = -1e30


def sincos_part(coords, count):
    omega = 1.0 / 10000.0 ** (jnp.arange(count, dtype=jnp.float32) / count)
    angles = coords[:, None] * omega[None, :]
    return jnp.concatenate([jnp.sin(angles), jnp.cos(angles)], axis=1)


def modulate(resid, shift_part, scale_part):
    centered = resid - jnp.mean(resid, axis=-1, keepdims=True)
    variance = jnp.mean(centered * centered, axis=-1, keepdims=True)
    return centered * lax.rsqrt(variance + norm_epsilon) * (1.0 + scale_part) + shift_part


def to_tokens(planes, patch_side):
    images, channels, height, breadth = planes.shape
    shaped = planes.reshape(
        images, channels, height // patch_side, patch_side, breadth // patch_side, patch_side
    )
    return shaped.transpose(0, 2, 4, 3, 5, 1).reshape(
        images, height // patch_side * (breadth // patch_side), patch_side * patch_side * channels
    )


def to_planes(token_rows, patch_side, channels, rows_tile, cols_tile):
    images = token_rows.shape[0]
    shaped = token_rows.reshape(images, rows_tile, cols_tile, patch_side, patch_side, channels)
    return shaped.transpose(0, 5, 1, 3, 2, 4).reshape(
        images, channels, rows_tile * patch_side, cols_tile * patch_side
    )


def dense(left, right):
    return jnp.einsum("...k,kn->...n", left, right, preferred_element_type=jnp.float32)


def dense_back(grad_rows, right):
    return jnp.einsum("...n,kn->...k", grad_rows, right, preferred_element_type=jnp.float32)


def weight_grad(left, grad_rows):
    return jnp.einsum("isk,isn->kn", left, grad_rows, preferred_element_type=jnp.float32)


def split_heads(token_rows, heads):
    images, length, model_width = token_rows.shape
    return token_rows.reshape(images, length, heads, model_width // heads)


def attention_scores(query_heads, key_heads, key_mask):
    factor = query_heads.shape[-1] ** (-0.5)
    scores = (
        jnp.einsum("iqhe,ikhe->ihqk", query_heads, key_heads, preferred_element_type=jnp.float32)
        * factor
    )
    if key_mask is None:
        return scores
    return jnp.where(key_mask[:, None, None, :], scores, masked_score)


def attend_forward(queries, keys_all, values_all, key_mask, heads):
    scores = attention_scores(split_heads(queries, heads), split_heads(keys_all, heads), key_mask)
    row_peak = jnp.max(scores, axis=-1, keepdims=True)
    log_total = row_peak + jnp.log(jnp.sum(jnp.exp(scores - row_peak), axis=-1, keepdims=True))
    weights_low = jnp.exp(scores - log_total).astype(jnp.bfloat16)
    mixed = jnp.einsum(
        "ihqk,ikhe->iqhe",
        weights_low,
        split_heads(values_all, heads),
        preferred_element_type=jnp.float32,
    )
    return (mixed.reshape(queries.shape).astype(jnp.bfloat16), log_total)


def attend_backward(queries, keys_all, values_all, key_mask, log_total, grad_mixed, heads):
    query_heads = split_heads(queries, heads)
    key_heads = split_heads(keys_all, heads)
    value_heads = split_heads(values_all, heads)
    factor = query_heads.shape[-1] ** (-0.5)
    weights_full = jnp.exp(attention_scores(query_heads, key_heads, key_mask) - log_total)
    grad_heads = split_heads(grad_mixed, heads)
    grad_weights = jnp.einsum(
        "iqhe,ikhe->ihqk", grad_heads, value_heads, preferred_element_type=jnp.float32
    )
    row_dot = jnp.sum(weights_full * grad_weights, axis=-1, keepdims=True)
    grad_scores = (weights_full * (grad_weights - row_dot)).astype(jnp.bfloat16)
    grad_queries = (
        jnp.einsum("ihqk,ikhe->iqhe", grad_scores, key_heads, preferred_element_type=jnp.float32)
        * factor
    )
    key_terms = (
        jnp.einsum("ihqk,iqhe->ikhe", grad_scores, query_heads, preferred_element_type=jnp.float32)
        * factor
    )
    value_terms = jnp.einsum(
        "ihqk,iqhe->ikhe",
        weights_full.astype(jnp.bfloat16),
        grad_heads,
        preferred_element_type=jnp.float32,
    )
    return (
        grad_queries.reshape(queries.shape).astype(jnp.bfloat16),
        key_terms.reshape(keys_all.shape),
        value_terms.reshape(values_all.shape),
    )


def layer_forward(resid, silu_cond, layer_weights, kept_rows, key_mask, heads):
    (
        adaptive_full,
        adaptive_offset,
        project_full,
        project_offset,
        attend_full,
        attend_offset,
        expand_full,
        expand_offset,
        shrink_full,
        shrink_offset,
    ) = layer_weights
    model_width = resid.shape[-1]
    modulation = dense(silu_cond, adaptive_full) + adaptive_offset.astype(jnp.float32)
    pieces = [
        modulation[:, None, slot_number * model_width : (slot_number + 1) * model_width]
        for slot_number in range(6)
    ]
    normed = modulate(resid, pieces[0], pieces[1]).astype(jnp.bfloat16)
    projected = dense(normed, project_full)
    bias_values = project_offset.astype(jnp.float32)
    queries = (projected[..., :model_width] + bias_values[:model_width]).astype(jnp.bfloat16)
    keys_local = projected[..., model_width : 2 * model_width].astype(jnp.bfloat16)
    values_local = (projected[..., 2 * model_width :] + bias_values[model_width:]).astype(
        jnp.bfloat16
    )
    keys_all, values_all = (
        lax.all_gather(keys_local, ("row", "col"), axis=1, tiled=True),
        lax.all_gather(values_local, ("row", "col"), axis=1, tiled=True),
    )
    mixed, log_total = attend_forward(queries, keys_all, values_all, key_mask, heads)
    attended = dense(mixed, attend_full) + attend_offset.astype(jnp.float32)
    resid_mid = resid + kept_rows * pieces[2] * attended
    normed_mid = modulate(resid_mid, pieces[3], pieces[4]).astype(jnp.bfloat16)
    hidden = dense(normed_mid, expand_full) + expand_offset.astype(jnp.float32)
    active = jax.nn.gelu(hidden, approximate=True).astype(jnp.bfloat16)
    expanded = dense(active, shrink_full) + shrink_offset.astype(jnp.float32)
    resid_out = resid_mid + kept_rows * pieces[5] * expanded
    return (
        resid_out,
        (
            resid,
            pieces,
            normed,
            queries,
            keys_all,
            values_all,
            mixed,
            log_total,
            attended,
            resid_mid,
            normed_mid,
            hidden,
            active,
            expanded,
        ),
    )


def layer_backward(grad_out, layer_weights, kept_rows, key_mask, saved, heads):
    (
        adaptive_full,
        adaptive_offset,
        project_full,
        project_offset,
        attend_full,
        attend_offset,
        expand_full,
        expand_offset,
        shrink_full,
        shrink_offset,
    ) = layer_weights
    (
        resid,
        pieces,
        normed,
        queries,
        keys_all,
        values_all,
        mixed,
        log_total,
        attended,
        resid_mid,
        normed_mid,
        hidden,
        active,
        expanded,
    ) = saved
    gated_out = kept_rows * grad_out
    grad_gate_mlp = jnp.sum(gated_out * expanded, axis=1)
    grad_expanded = (gated_out * pieces[5]).astype(jnp.bfloat16)
    shrink_term = weight_grad(active, grad_expanded)
    shrink_bias_term = jnp.sum(grad_expanded.astype(jnp.float32), axis=(0, 1))
    gelu_pull = jax.vjp(partial(jax.nn.gelu, approximate=True), hidden)[1]
    grad_hidden = gelu_pull(dense_back(grad_expanded, shrink_full))[0].astype(jnp.bfloat16)
    expand_term = weight_grad(normed_mid, grad_hidden)
    expand_bias_term = jnp.sum(grad_hidden.astype(jnp.float32), axis=(0, 1))
    mid_pull = jax.vjp(modulate, resid_mid, pieces[3], pieces[4])[1]
    grad_mid, grad_shift_mlp, grad_scale_mlp = mid_pull(dense_back(grad_hidden, expand_full))
    grad_mid = grad_mid + grad_out
    gated_mid = kept_rows * grad_mid
    grad_gate_attn = jnp.sum(gated_mid * attended, axis=1)
    grad_attended = (gated_mid * pieces[2]).astype(jnp.bfloat16)
    attend_term = weight_grad(mixed, grad_attended)
    attend_bias_term = jnp.sum(grad_attended.astype(jnp.float32), axis=(0, 1))
    grad_mixed = dense_back(grad_attended, attend_full).astype(jnp.bfloat16)
    grad_queries, key_terms, value_terms = attend_backward(
        queries, keys_all, values_all, key_mask, log_total, grad_mixed, heads
    )
    grad_keys, grad_values = (
        lax.psum_scatter(
            key_terms.astype(jnp.bfloat16), ("row", "col"), scatter_dimension=1, tiled=True
        ).astype(jnp.float32),
        lax.psum_scatter(
            value_terms.astype(jnp.bfloat16), ("row", "col"), scatter_dimension=1, tiled=True
        ).astype(jnp.float32),
    )
    grad_values_low = grad_values.astype(jnp.bfloat16)
    grad_projected = jnp.concatenate(
        [grad_queries, grad_keys.astype(jnp.bfloat16), grad_values_low], axis=-1
    )
    project_term = weight_grad(normed, grad_projected)
    project_bias_term = jnp.concatenate(
        [
            jnp.sum(grad_queries.astype(jnp.float32), axis=(0, 1)),
            jnp.sum(grad_values_low.astype(jnp.float32), axis=(0, 1)),
        ]
    )
    first_pull = jax.vjp(modulate, resid, pieces[0], pieces[1])[1]
    grad_in, grad_shift_attn, grad_scale_attn = first_pull(dense_back(grad_projected, project_full))
    grad_in = grad_in + grad_mid
    mod_term = jnp.concatenate(
        [
            grad_shift_attn[:, 0],
            grad_scale_attn[:, 0],
            grad_gate_attn,
            grad_shift_mlp[:, 0],
            grad_scale_mlp[:, 0],
            grad_gate_mlp,
        ],
        axis=-1,
    )
    return (
        grad_in,
        mod_term,
        (
            project_term,
            project_bias_term,
            attend_term,
            attend_bias_term,
            expand_term,
            expand_bias_term,
            shrink_term,
            shrink_bias_term,
        ),
    )


def reduce_block(weight_terms):
    (
        project_term,
        project_bias_term,
        attend_term,
        attend_bias_term,
        expand_term,
        expand_bias_term,
        shrink_term,
        shrink_bias_term,
    ) = weight_terms
    (
        project_part,
        project_bias_part,
        attend_part,
        attend_bias_part,
        expand_part,
        expand_bias_part,
        shrink_part,
        shrink_bias_part,
    ) = (
        lax.psum_scatter(
            project_term.astype(jnp.bfloat16), "batch", scatter_dimension=0, tiled=True
        ).astype(jnp.float32),
        lax.psum_scatter(
            project_bias_term.astype(jnp.bfloat16), "batch", scatter_dimension=0, tiled=True
        ).astype(jnp.float32),
        lax.psum_scatter(
            attend_term.astype(jnp.bfloat16), "batch", scatter_dimension=0, tiled=True
        ).astype(jnp.float32),
        lax.psum_scatter(
            attend_bias_term.astype(jnp.bfloat16), "batch", scatter_dimension=0, tiled=True
        ).astype(jnp.float32),
        lax.psum_scatter(
            expand_term.astype(jnp.bfloat16), "batch", scatter_dimension=0, tiled=True
        ).astype(jnp.float32),
        lax.psum_scatter(
            expand_bias_term.astype(jnp.bfloat16), "batch", scatter_dimension=0, tiled=True
        ).astype(jnp.float32),
        lax.psum_scatter(
            shrink_term.astype(jnp.bfloat16), "batch", scatter_dimension=1, tiled=True
        ).astype(jnp.float32),
        lax.psum_scatter(
            shrink_bias_term.astype(jnp.bfloat16), "batch", scatter_dimension=0, tiled=True
        ).astype(jnp.float32),
    )
    summed = (
        lax.psum(project_part.astype(jnp.bfloat16), ("row", "col")).astype(jnp.float32),
        lax.psum(project_bias_part.astype(jnp.bfloat16), ("row", "col")).astype(jnp.float32),
        lax.psum(attend_part.astype(jnp.bfloat16), ("row", "col")).astype(jnp.float32),
        lax.psum(attend_bias_part.astype(jnp.bfloat16), ("row", "col")).astype(jnp.float32),
        lax.psum(expand_part.astype(jnp.bfloat16), ("row", "col")).astype(jnp.float32),
        lax.psum(expand_bias_part.astype(jnp.bfloat16), ("row", "col")).astype(jnp.float32),
        lax.psum(shrink_part.astype(jnp.bfloat16), ("row", "col")).astype(jnp.float32),
        lax.psum(shrink_bias_part.astype(jnp.bfloat16), ("row", "col")).astype(jnp.float32),
    )
    return summed


def body(
    latents,
    conditioning,
    kept_index,
    kept_count,
    patch_weight,
    patch_bias,
    adaptive_weight,
    adaptive_bias,
    project_weight,
    project_bias,
    attend_weight,
    attend_bias,
    expand_weight,
    expand_bias,
    shrink_weight,
    shrink_bias,
    final_adaptive,
    final_offset,
    final_weight,
    final_bias,
    cotangent,
):
    row_count = lax.axis_size("row")
    col_count = lax.axis_size("col")
    row_place = lax.axis_index("row")
    col_place = lax.axis_index("col")
    images = latents.shape[0]
    rows_tile = latents.shape[2] // PATCH
    cols_tile = latents.shape[3] // PATCH
    tile_tokens = rows_tile * cols_tile
    sequence = tile_tokens * row_count * col_count
    model_width = conditioning.shape[1]
    depth_count = adaptive_weight.shape[0]
    token_ids = jnp.arange(sequence, dtype=jnp.int32)
    listed = jnp.logical_and(
        kept_index[:, :, None] == token_ids[None, None, :],
        (token_ids[None, :] < kept_count[:, None])[:, :, None],
    )
    kept_grid = jnp.any(listed, axis=1).reshape(images, row_count, rows_tile, col_count, cols_tile)
    key_order = kept_grid.transpose(0, 1, 3, 2, 4).reshape(
        images, row_count * col_count, tile_tokens
    )
    kept_here = lax.dynamic_index_in_dim(
        key_order, row_place * col_count + col_place, axis=1, keepdims=False
    )
    routed_keys = key_order.reshape(images, sequence)
    routed_rows = kept_here.astype(jnp.float32)[:, :, None]
    every_row = jnp.ones((images, tile_tokens, 1), jnp.float32)
    half_width = model_width // 2
    row_table = sincos_part(
        (row_place * rows_tile + jnp.arange(rows_tile, dtype=jnp.int32)).astype(jnp.float32),
        model_width // 4,
    )
    col_table = sincos_part(
        (col_place * cols_tile + jnp.arange(cols_tile, dtype=jnp.int32)).astype(jnp.float32),
        model_width // 4,
    )
    position = jnp.concatenate(
        [
            jnp.broadcast_to(row_table[:, None, :], (rows_tile, cols_tile, half_width)),
            jnp.broadcast_to(col_table[None, :, :], (rows_tile, cols_tile, half_width)),
        ],
        axis=2,
    ).reshape(tile_tokens, model_width)
    patch_full, patch_bias_full, final_adaptive_full, final_offset_full, final_weight_full = (
        lax.all_gather(patch_weight, "batch", axis=1, tiled=True),
        lax.all_gather(patch_bias, "batch", axis=0, tiled=True),
        lax.all_gather(final_adaptive, "batch", axis=0, tiled=True),
        lax.all_gather(final_offset, "batch", axis=0, tiled=True),
        lax.all_gather(final_weight, "batch", axis=0, tiled=True),
    )
    patches = to_tokens(latents, PATCH)
    resid = dense(patches, patch_full) + patch_bias_full.astype(jnp.float32) + position
    cond_values = conditioning.astype(jnp.float32)
    silu_cond = jax.nn.silu(cond_values).astype(jnp.bfloat16)
    records = []
    for block_number in range(depth_count):
        layer_weights = (
            lax.all_gather(adaptive_weight[block_number], "batch", axis=0, tiled=True),
            lax.all_gather(adaptive_bias[block_number], "batch", axis=0, tiled=True),
            lax.all_gather(project_weight[block_number], "batch", axis=0, tiled=True),
            lax.all_gather(project_bias[block_number], "batch", axis=0, tiled=True),
            lax.all_gather(attend_weight[block_number], "batch", axis=0, tiled=True),
            lax.all_gather(attend_bias[block_number], "batch", axis=0, tiled=True),
            lax.all_gather(expand_weight[block_number], "batch", axis=0, tiled=True),
            lax.all_gather(expand_bias[block_number], "batch", axis=0, tiled=True),
            lax.all_gather(shrink_weight[block_number], "batch", axis=1, tiled=True),
            lax.all_gather(shrink_bias[block_number], "batch", axis=0, tiled=True),
        )
        kept_rows = every_row if block_number == 0 else routed_rows
        key_mask = None if block_number == 0 else routed_keys
        resid, saved = layer_forward(resid, silu_cond, layer_weights, kept_rows, key_mask, HEADS)
        records.append((layer_weights, kept_rows, key_mask, saved))
    final_mod = dense(silu_cond, final_adaptive_full) + final_offset_full.astype(jnp.float32)
    final_shift = final_mod[:, None, :model_width]
    final_scale = final_mod[:, None, model_width:]
    final_normed = modulate(resid, final_shift, final_scale).astype(jnp.bfloat16)
    outputs = dense(final_normed, final_weight_full) + final_bias.astype(jnp.float32)
    prediction = to_planes(outputs, PATCH, cotangent.shape[1], rows_tile, cols_tile)
    grad_outputs = to_tokens(cotangent, PATCH)
    final_bias_grad = lax.psum(
        jnp.sum(grad_outputs.astype(jnp.float32), axis=(0, 1)), ("batch", "row", "col")
    )
    final_weight_term = weight_grad(final_normed, grad_outputs)
    final_pull = jax.vjp(modulate, resid, final_shift, final_scale)[1]
    grad_resid, grad_final_shift, grad_final_scale = final_pull(
        dense_back(grad_outputs, final_weight_full)
    )
    final_mod_term = jnp.concatenate([grad_final_shift[:, 0], grad_final_scale[:, 0]], axis=-1)
    block_sums = [None] * depth_count
    mod_terms = [None] * depth_count
    for block_number in reversed(range(depth_count)):
        layer_weights, kept_rows, key_mask, saved = records[block_number]
        grad_resid, mod_terms[block_number], weight_terms = layer_backward(
            grad_resid, layer_weights, kept_rows, key_mask, saved, HEADS
        )
        block_sums[block_number] = reduce_block(weight_terms)
    block_mods, final_mod_total = (
        lax.psum(jnp.stack(mod_terms).astype(jnp.bfloat16), ("row", "col")).astype(jnp.float32),
        lax.psum(final_mod_term.astype(jnp.bfloat16), ("row", "col")).astype(jnp.float32),
    )
    block_mods_low = block_mods.astype(jnp.bfloat16)
    final_mod_low = final_mod_total.astype(jnp.bfloat16)
    grad_silu = dense_back(final_mod_low, final_adaptive_full)
    for block_number in range(depth_count):
        grad_silu = grad_silu + dense_back(
            block_mods_low[block_number], records[block_number][0][0]
        )
    conditioning_grad = jax.vjp(jax.nn.silu, cond_values)[1](grad_silu)[0]
    adaptive_terms = jnp.stack(
        [
            jnp.einsum(
                "ik,in->kn",
                silu_cond,
                block_mods_low[block_number],
                preferred_element_type=jnp.float32,
            )
            for block_number in range(depth_count)
        ]
    )
    adaptive_bias_terms = jnp.sum(block_mods_low.astype(jnp.float32), axis=1)
    final_adaptive_term = jnp.einsum(
        "ik,in->kn", silu_cond, final_mod_low, preferred_element_type=jnp.float32
    )
    final_offset_term = jnp.sum(final_mod_low.astype(jnp.float32), axis=0)
    adaptive_weight_grad, adaptive_bias_grad, final_adaptive_grad, final_offset_grad = (
        lax.psum_scatter(
            adaptive_terms.astype(jnp.bfloat16), "batch", scatter_dimension=1, tiled=True
        ).astype(jnp.float32),
        lax.psum_scatter(
            adaptive_bias_terms.astype(jnp.bfloat16), "batch", scatter_dimension=1, tiled=True
        ).astype(jnp.float32),
        lax.psum_scatter(
            final_adaptive_term.astype(jnp.bfloat16), "batch", scatter_dimension=0, tiled=True
        ).astype(jnp.float32),
        lax.psum_scatter(
            final_offset_term.astype(jnp.bfloat16), "batch", scatter_dimension=0, tiled=True
        ).astype(jnp.float32),
    )
    patch_bias_term = jnp.sum(grad_resid, axis=(0, 1))
    grad_embed = grad_resid.astype(jnp.bfloat16)
    patch_term = weight_grad(patches, grad_embed)
    latent_grad = to_planes(
        dense_back(grad_embed, patch_full), PATCH, latents.shape[1], rows_tile, cols_tile
    )
    patch_part, patch_bias_part, final_weight_part = (
        lax.psum_scatter(
            patch_term.astype(jnp.bfloat16), "batch", scatter_dimension=1, tiled=True
        ).astype(jnp.float32),
        lax.psum_scatter(
            patch_bias_term.astype(jnp.bfloat16), "batch", scatter_dimension=0, tiled=True
        ).astype(jnp.float32),
        lax.psum_scatter(
            final_weight_term.astype(jnp.bfloat16), "batch", scatter_dimension=0, tiled=True
        ).astype(jnp.float32),
    )
    outer_done = lax.psum((patch_part, patch_bias_part, final_weight_part), ("row", "col"))
    patch_weight_grad, patch_bias_grad, final_weight_grad = outer_done
    project_weight_grad = jnp.stack(
        [block_sums[block_number][0] for block_number in range(depth_count)]
    )
    project_bias_grad = jnp.stack(
        [block_sums[block_number][1] for block_number in range(depth_count)]
    )
    attend_weight_grad = jnp.stack(
        [block_sums[block_number][2] for block_number in range(depth_count)]
    )
    attend_bias_grad = jnp.stack(
        [block_sums[block_number][3] for block_number in range(depth_count)]
    )
    expand_weight_grad = jnp.stack(
        [block_sums[block_number][4] for block_number in range(depth_count)]
    )
    expand_bias_grad = jnp.stack(
        [block_sums[block_number][5] for block_number in range(depth_count)]
    )
    shrink_weight_grad = jnp.stack(
        [block_sums[block_number][6] for block_number in range(depth_count)]
    )
    shrink_bias_grad = jnp.stack(
        [block_sums[block_number][7] for block_number in range(depth_count)]
    )
    return (
        prediction,
        latent_grad,
        conditioning_grad,
        patch_weight_grad,
        patch_bias_grad,
        adaptive_weight_grad,
        adaptive_bias_grad,
        project_weight_grad,
        project_bias_grad,
        attend_weight_grad,
        attend_bias_grad,
        expand_weight_grad,
        expand_bias_grad,
        shrink_weight_grad,
        shrink_bias_grad,
        final_adaptive_grad,
        final_offset_grad,
        final_weight_grad,
        final_bias_grad,
    )


def solution(mesh):
    placed = (
        P("batch", None, "row", "col"),
        P("batch", None),
        P("batch", None),
        P("batch"),
        P(None, "batch"),
        P("batch"),
        P(None, "batch", None),
        P(None, "batch"),
        P(None, "batch", None),
        P(None, "batch"),
        P(None, "batch", None),
        P(None, "batch"),
        P(None, "batch", None),
        P(None, "batch"),
        P(None, None, "batch"),
        P(None, "batch"),
        P("batch", None),
        P("batch"),
        P("batch", None),
        P(),
        P("batch", None, "row", "col"),
    )
    return jax.shard_map(
        body,
        mesh=mesh,
        in_specs=placed,
        out_specs=(
            P("batch", None, "row", "col"),
            P("batch", None, "row", "col"),
            P("batch", None),
            P(None, "batch"),
            P("batch"),
            P(None, "batch", None),
            P(None, "batch"),
            P(None, "batch", None),
            P(None, "batch"),
            P(None, "batch", None),
            P(None, "batch"),
            P(None, "batch", None),
            P(None, "batch"),
            P(None, None, "batch"),
            P(None, "batch"),
            P("batch", None),
            P("batch"),
            P("batch", None),
            P(),
        ),
        check_vma=False,
    )
```

profile of v0, /device:TPU:0, one launch (start us, length us, event | category | flops | bytes accessed | tf_op | source)
XLA Modules:
  0.0 4467.8 jit_solution(13084970294225279948)
XLA Ops:
  23.5 36.0 all-reduce.25
  59.5 25.1 all-gather.20
  87.7 203.8 %all-gather.48.cloned.1.call-done = bf16[1,1152,6912]{2,1,0:T(8,128)(2,1)} async-done(((bf16[1,288,6912]{2,1,0:T(8,128)(2,1)}), bf16[1,1152,6912]{2,1,0:T(8,128)(2,1)}) %all-gather.48.cloned.1.call-update) | async-done | bytes 15925264 | tf_op jit(solution)/shard_map/all_gather | solution.py:418
  299.9 135.1 %all-gather.50.cloned.1.call-done = bf16[1,1152,3456]{2,1,0:T(8,128)(2,1)} async-done(((bf16[1,288,3456]{2,1,0:T(8,128)(2,1)}), bf16[1,1152,3456]{2,1,0:T(8,128)(2,1)}) %all-gather.50.cloned.1.call-update) | async-done | bytes 7962640 | tf_op jit(solution)/shard_map/all_gather | solution.py:420
  479.5 229.0 %all-gather.58.cloned.1.call-done = bf16[1,1152,6912]{2,1,0:T(8,128)(2,1)} async-done(((bf16[1,288,6912]{2,1,0:T(8,128)(2,1)}), bf16[1,1152,6912]{2,1,0:T(8,128)(2,1)}) %all-gather.58.cloned.1.call-update) | async-done | bytes 15925264 | tf_op jit(solution)/shard_map/all_gather | solution.py:418
  717.2 30.8 all-gather.38.cloned.1.call-done
  754.6 34.1 all-gather.40.cloned.1.call-done
  816.0 29.4 all-gather.52.cloned.1.call-done
  849.7 182.8 %all-gather.54.cloned.1.call-done = bf16[1,1152,4608]{2,1,0:T(8,128)(2,1)} async-done(((bf16[1,288,4608]{2,1,0:T(8,128)(2,1)}), bf16[1,1152,4608]{2,1,0:T(8,128)(2,1)}) %all-gather.54.cloned.1.call-update) | async-done | bytes 10616848 | tf_op jit(solution)/shard_map/all_gather | solution.py:424
  1042.0 176.9 %all-gather.56.cloned.1.call-done = bf16[1,4608,1152]{1,2,0:T(8,128)(2,1)} async-done(((bf16[1,4608,288]{1,2,0:T(8,128)(2,1)}), bf16[1,4608,1152]{1,2,0:T(8,128)(2,1)}) %all-gather.56.cloned.1.call-update) | async-done | bytes 10616848 | tf_op jit(solution)/shard_map/all_gather | solution.py:426
  1229.2 132.7 %all-gather.60.cloned.1.call-done = bf16[1,1152,3456]{2,1,0:T(8,128)(2,1)} async-done(((bf16[1,288,3456]{2,1,0:T(8,128)(2,1)}), bf16[1,1152,3456]{2,1,0:T(8,128)(2,1)}) %all-gather.60.cloned.1.call-update) | async-done | bytes 7962640 | tf_op jit(solution)/shard_map/all_gather | solution.py:420
  1409.5 53.0 %all-gather.46.cloned.1.call-done = bf16[1152,2304]{1,0:T(8,128)(2,1)} async-done(((bf16[288,2304]{1,0:T(8,128)(2,1)}), bf16[1152,2304]{1,0:T(8,128)(2,1)}) %all-gather.46.cloned.1.call-update) | async-done | bytes 5308432 | tf_op jit(solution)/shard_map/all_gather | solution.py:407
  1467.8 34.1 all-gather.42.cloned.1.call-done
  1508.7 33.9 all-gather.44.cloned.1.call-done
  1569.7 29.9 all-gather.62.cloned.1.call-done
  1604.5 181.4 %all-gather.64.cloned.1.call-done = bf16[1,1152,4608]{2,1,0:T(8,128)(2,1)} async-done(((bf16[1,288,4608]{2,1,0:T(8,128)(2,1)}), bf16[1,1152,4608]{2,1,0:T(8,128)(2,1)}) %all-gather.64.cloned.1.call-update) | async-done | bytes 10616848 | tf_op jit(solution)/shard_map/all_gather | solution.py:424
  1795.3 176.9 %all-gather.66.cloned.1.call-done = bf16[1,4608,1152]{1,2,0:T(8,128)(2,1)} async-done(((bf16[1,4608,288]{1,2,0:T(8,128)(2,1)}), bf16[1,4608,1152]{1,2,0:T(8,128)(2,1)}) %all-gather.66.cloned.1.call-update) | async-done | bytes 10616848 | tf_op jit(solution)/shard_map/all_gather | solution.py:426
  2078.0 57.6 %reduce-scatter.24.cloned.1.call-done = bf16[2,128,1152]{2,1,0:T(8,128)(2,1)} async-done(((bf16[2,1024,1152]{2,1,0:T(8,128)(2,1)}), bf16[2,128,1152]{2,1,0:T(8,128)(2,1)}) %reduce-scatter.24.cloned.1.call-update) | async-done | bytes 589840 | tf_op jit(solution)/shard_map/reduce_scatter | solution.py:232
  2251.3 39.9 reduce-scatter.28.cloned.1.call-done
  2416.7 34.2 reduce-scatter.40.cloned.1.call-done
  2450.9 55.3 %reduce-scatter.38.cloned.1.call-done = bf16[288,1152]{1,0:T(8,128)(2,1)} async-done(((bf16[1152,1152]{1,0:T(8,128)(2,1)}), bf16[288,1152]{1,0:T(8,128)(2,1)}) %reduce-scatter.38.cloned.1.call-update) | async-done | bytes 663568 | tf_op jit(solution)/shard_map/reduce_scatter | solution.py:307
  2506.3 182.9 %reduce-scatter.48.cloned.1.call-done = bf16[4608,288]{0,1:T(8,128)(2,1)} async-done(((bf16[4608,1152]{0,1:T(8,128)(2,1)}), bf16[4608,288]{0,1:T(8,128)(2,1)}) %reduce-scatter.48.cloned.1.call-update) | async-done | bytes 2654224 | tf_op jit(solution)/shard_map/reduce_scatter | solution.py:319
  2689.2 184.0 %reduce-scatter.44.cloned.1.call-done = bf16[288,4608]{1,0:T(8,128)(2,1)} async-done(((bf16[1152,4608]{1,0:T(8,128)(2,1)}), bf16[288,4608]{1,0:T(8,128)(2,1)}) %reduce-scatter.44.cloned.1.call-update) | async-done | bytes 2654224 | tf_op jit(solution)/shard_map/reduce_scatter | solution.py:313
  2873.1 142.2 %reduce-scatter.36.cloned.1.call-done = bf16[288,3456]{1,0:T(8,128)(2,1)} async-done(((bf16[1152,3456]{1,0:T(8,128)(2,1)}), bf16[288,3456]{1,0:T(8,128)(2,1)}) %reduce-scatter.36.cloned.1.call-update) | async-done | bytes 1990672 | tf_op jit(solution)/shard_map/reduce_scatter | solution.py:301
  3015.3 183.0 %reduce-scatter.46.cloned.1.call-done = bf16[4608,288]{0,1:T(8,128)(2,1)} async-done(((bf16[4608,1152]{0,1:T(8,128)(2,1)}), bf16[4608,288]{0,1:T(8,128)(2,1)}) %reduce-scatter.46.cloned.1.call-update) | async-done | bytes 2654224 | tf_op jit(solution)/shard_map/reduce_scatter | solution.py:319
  3198.3 184.1 %reduce-scatter.42.cloned.1.call-done = bf16[288,4608]{1,0:T(8,128)(2,1)} async-done(((bf16[1152,4608]{1,0:T(8,128)(2,1)}), bf16[288,4608]{1,0:T(8,128)(2,1)}) %reduce-scatter.42.cloned.1.call-update) | async-done | bytes 2654224 | tf_op jit(solution)/shard_map/reduce_scatter | solution.py:313
  3382.4 141.5 %reduce-scatter.34.cloned.1.call-done = bf16[288,3456]{1,0:T(8,128)(2,1)} async-done(((bf16[1152,3456]{1,0:T(8,128)(2,1)}), bf16[288,3456]{1,0:T(8,128)(2,1)}) %reduce-scatter.34.cloned.1.call-update) | async-done | bytes 1990672 | tf_op jit(solution)/shard_map/reduce_scatter | solution.py:301
  3540.7 21.7 pad_maximum_fusion
  3563.8 43.5 psum.175
  3656.4 25.0 all-reduce.20
  3707.1 214.4 %all-reduce.31.cloned.1.call-done = (bf16[1,288,3456]{2,1,0:T(8,128)(2,1)}, bf16[1,288,3456]{2,1,0:T(8,128)(2,1)}, bf16[1,288,1152]{2,1,0:T(8,128)(2,1)}, bf16[1...) async-done(((bf16[1,288,3456]{2,1,0:T(8,128)(2,1)}, ...) | async-done | bytes 15925264 | tf_op jit(solution)/shard_map/psum | solution.py:327
  3940.4 509.8 %reduce-scatter.32.cloned.1.call-done = bf16[2,288,6912]{2,1,0:T(8,128)(2,1)} async-done(((bf16[2,1152,6912]{2,1,0:T(8,128)(2,1)}), bf16[2,288,6912]{2,1,0:T(8,128)(2,1)}) %reduce-scatter.32.cloned.1.call-update) | async-done | bytes 7962640 | tf_op jit(solution)/shard_map/reduce_scatter | solution.py:486
  (655 shorter events, 703.2 us)
Async XLA Ops:
  7.2 284.4 %all-gather.48.cloned.1.call-start = ((), (), s32[]{:S(2)}) async-start(), calls=%async_computation.36 | async-start | bytes 19906560 | tf_op jit(solution)/shard_map/all_gather | solution.py:418
  12.9 422.1 %all-gather.50.cloned.1.call-start = ((), (), s32[]{:S(2)}) async-start(), calls=%async_computation.37 | async-start | bytes 9953280 | tf_op jit(solution)/shard_map/all_gather | solution.py:420
  17.4 691.1 %all-gather.58.cloned.1.call-start = ((), (), s32[]{:S(2)}) async-start(), calls=%async_computation.41 | async-start | bytes 19906560 | tf_op jit(solution)/shard_map/all_gather | solution.py:418
  18.2 729.8 %all-gather.38.cloned.1.call-start = ((), (), s32[]{:S(2)}) async-start(), calls=%async_computation.17 | async-start | bytes 5308416 | tf_op jit(solution)/shard_map/all_gather | solution.py:150
  443.8 344.9 %all-gather.40.cloned.1.call-start = ((), (), s32[]{:S(2)}) async-start(), calls=%async_computation.18 | async-start | bytes 5308416 | tf_op jit(solution)/shard_map/all_gather | solution.py:149
  446.2 399.2 %all-gather.52.cloned.1.call-start = ((), (), s32[]{:S(2)}) async-start(), calls=%async_computation.38 | async-start | bytes 3317760 | tf_op jit(solution)/shard_map/all_gather | solution.py:422
  449.0 583.4 %all-gather.54.cloned.1.call-start = ((), (), s32[]{:S(2)}) async-start(), calls=%async_computation.39 | async-start | bytes 13271040 | tf_op jit(solution)/shard_map/all_gather | solution.py:424
  454.9 764.0 %all-gather.56.cloned.1.call-start = ((), (), s32[]{:S(2)}) async-start(), calls=%async_computation.40 | async-start | bytes 13271040 | tf_op jit(solution)/shard_map/all_gather | solution.py:426
  460.5 901.5 %all-gather.60.cloned.1.call-start = ((), (), s32[]{:S(2)}) async-start(), calls=%async_computation.42 | async-start | bytes 9953280 | tf_op jit(solution)/shard_map/all_gather | solution.py:420
  461.2 1001.3 %all-gather.46.cloned.1.call-start = ((), (), s32[]{:S(2)}) async-start(), calls=%async_computation.21 | async-start | bytes 6635520 | tf_op jit(solution)/shard_map/all_gather | solution.py:407
  461.8 1040.2 %all-gather.42.cloned.1.call-start = ((), (), s32[]{:S(2)}) async-start(), calls=%async_computation.19 | async-start | bytes 5308416 | tf_op jit(solution)/shard_map/all_gather | solution.py:150
  1371.0 171.7 %all-gather.44.cloned.1.call-start = ((), (), s32[]{:S(2)}) async-start(), calls=%async_computation.20 | async-start | bytes 5308416 | tf_op jit(solution)/shard_map/all_gather | solution.py:149
  1373.4 226.2 %all-gather.62.cloned.1.call-start = ((), (), s32[]{:S(2)}) async-start(), calls=%async_computation.43 | async-start | bytes 3317760 | tf_op jit(solution)/shard_map/all_gather | solution.py:422
  1374.1 411.8 %all-gather.64.cloned.1.call-start = ((), (), s32[]{:S(2)}) async-start(), calls=%async_computation.44 | async-start | bytes 13271040 | tf_op jit(solution)/shard_map/all_gather | solution.py:424
  1374.7 597.5 %all-gather.66.cloned.1.call-start = ((), (), s32[]{:S(2)}) async-start(), calls=%async_computation.45 | async-start | bytes 13271040 | tf_op jit(solution)/shard_map/all_gather | solution.py:426
  1375.3 702.7 %reduce-scatter.26.cloned.1.call-start = ((), (), s32[]{:S(2)}) async-start(), calls=%async_computation.23 | async-start | bytes 5308416 | tf_op jit(solution)/shard_map/reduce_scatter | solution.py:235
  2066.0 185.3 %reduce-scatter.30.cloned.1.call-start = ((), (), s32[]{:S(2)}) async-start(), calls=%async_computation.25 | async-start | bytes 5308416 | tf_op jit(solution)/shard_map/reduce_scatter | solution.py:235
  2179.4 111.8 %reduce-scatter.28.cloned.1.call-start = ((), (), s32[]{:S(2)}) async-start(), calls=%async_computation.24 | async-start | bytes 5308416 | tf_op jit(solution)/shard_map/reduce_scatter | solution.py:232
  2218.1 191.8 %all-reduce.29.cloned.1.call-start = ((), (), s32[]{:S(2)}) async-start(), calls=%async_computation.49 | async-start | bytes 169984 | tf_op jit(solution)/shard_map/psum | solution.py:458
  2347.4 158.9 %reduce-scatter.38.cloned.1.call-start = ((), (), s32[]{:S(2)}) async-start(), calls=%async_computation.29 | async-start | bytes 3317760 | tf_op jit(solution)/shard_map/reduce_scatter | solution.py:307
  2351.1 338.0 %reduce-scatter.48.cloned.1.call-start = ((), (), s32[]{:S(2)}) async-start(), calls=%async_computation.34 | async-start | bytes 13271040 | tf_op jit(solution)/shard_map/reduce_scatter | solution.py:319
  2360.9 512.2 %reduce-scatter.44.cloned.1.call-start = ((), (), s32[]{:S(2)}) async-start(), calls=%async_computation.32 | async-start | bytes 13271040 | tf_op jit(solution)/shard_map/reduce_scatter | solution.py:313
  2370.9 644.5 %reduce-scatter.36.cloned.1.call-start = ((), (), s32[]{:S(2)}) async-start(), calls=%async_computation.28 | async-start | bytes 9953280 | tf_op jit(solution)/shard_map/reduce_scatter | solution.py:301
  2378.8 819.5 %reduce-scatter.46.cloned.1.call-start = ((), (), s32[]{:S(2)}) async-start(), calls=%async_computation.33 | async-start | bytes 13271040 | tf_op jit(solution)/shard_map/reduce_scatter | solution.py:319
  2389.3 993.1 %reduce-scatter.42.cloned.1.call-start = ((), (), s32[]{:S(2)}) async-start(), calls=%async_computation.31 | async-start | bytes 13271040 | tf_op jit(solution)/shard_map/reduce_scatter | solution.py:313
  2399.0 1124.9 %reduce-scatter.34.cloned.1.call-start = ((), (), s32[]{:S(2)}) async-start(), calls=%async_computation.27 | async-start | bytes 9953280 | tf_op jit(solution)/shard_map/reduce_scatter | solution.py:301
  2406.1 1203.2 %reduce-scatter.56.cloned.1.call-start = ((), (), s32[]{:S(2)}) async-start(), calls=%async_computation.48 | async-start | bytes 368640
  2408.6 1246.8 %reduce-scatter.52.cloned.1.call-start = ((), (), s32[]{:S(2)}) async-start(), calls=%async_computation.46 | async-start | bytes 368640
  2409.8 1271.6 %reduce-scatter.54.cloned.1.call-start = ((), (), s32[]{:S(2)}) async-start(), calls=%async_computation.47 | async-start | bytes 2211840
  2412.7 1291.4 %reduce-scatter.50.cloned.1.call-start = ((), (), s32[]{:S(2)}) async-start(), calls=%async_computation.35 | async-start | bytes 6635520 | tf_op jit(solution)/shard_map/reduce_scatter | solution.py:492
  2416.7 1504.8 %all-reduce.31.cloned.1.call-start = ((), (), s32[]{:S(2)}) async-start(), calls=%async_computation.50 | async-start | bytes 31850496 | tf_op jit(solution)/shard_map/psum | solution.py:327
  3523.9 926.3 %reduce-scatter.32.cloned.1.call-start = ((), (), s32[]{:S(2)}) async-start(), calls=%async_computation.26 | async-start | bytes 39813120 | tf_op jit(solution)/shard_map/reduce_scatter | solution.py:486
  (162 other events, 8617.1 us)
Sparse Core Ops, SparseCore 0:
  13.0 278.4 all-gather.47
  293.7 141.2 all-gather.49
  437.1 271.3 all-gather.57
  710.9 37.0 all-gather.37
  749.7 38.9 all-gather.39
  790.1 55.3 all-gather.51
  847.6 184.8 all-gather.53
  1034.6 184.2 all-gather.55
  1221.1 140.8 all-gather.59
  1363.4 99.1 all-gather.45
  1464.4 37.4 all-gather.41
  1503.7 38.9 all-gather.43
  1544.2 55.3 all-gather.61
  1601.0 184.8 all-gather.63
  1787.9 184.2 all-gather.65
  2025.9 52.0 reduce-scatter.25
  2081.7 53.8 reduce-scatter.23
  2179.5 53.8 reduce-scatter.29
  2237.2 53.9 reduce-scatter.27
  2343.8 50.3 all-reduce.28
  2397.1 53.7 reduce-scatter.39
  2453.9 52.3 reduce-scatter.37
  2509.3 179.8 reduce-scatter.47
  2691.9 181.1 reduce-scatter.43
  2876.2 139.1 reduce-scatter.35
  3017.6 180.6 reduce-scatter.45
  3201.2 181.1 reduce-scatter.41
  3384.7 139.1 reduce-scatter.33
  3569.6 37.6 reduce-scatter.53
  3609.6 94.3 reduce-scatter.49
  3709.7 211.7 all-reduce.30
  3923.9 526.2 reduce-scatter.31
  (2 shorter events, 38.5 us)
where the time goes:
time: 4480 us; the launch traced here: 4470 us
  waiting for transfers between devices  3620 us (81%)
  matrix products  327 us (7%)
  blocking collectives  212 us (5%)
  local copies, waits for them, and re-layouts  152 us (3%)
  other arithmetic  134 us (3%)
    reduce_scatter x1, waiting for transfers between devices, body(): lax.psum_scatter(adaptive_terms.astype(jnp.bfloat16), 'batch', scatter_di...  510 us
    all_gather x2, waiting for transfers between devices, body(): lax.all_gather(adaptive_weight[block_number], 'batch', axis=0, tiled=True)  433 us
    reduce_scatter x2, waiting for transfers between devices, reduce_block(): lax.psum_scatter(expand_term.astype(jnp.bfloat16), 'batch', scatter_dimen...  368 us
    reduce_scatter x2, waiting for transfers between devices, reduce_block(): lax.psum_scatter(shrink_term.astype(jnp.bfloat16), 'batch', scatter_dimen...  366 us
    all_gather x2, waiting for transfers between devices, body(): lax.all_gather(expand_weight[block_number], 'batch', axis=0, tiled=True)  364 us
    all_gather x2, waiting for transfers between devices, body(): lax.all_gather(shrink_weight[block_number], 'batch', axis=1, tiled=True)  354 us
    reduce_scatter x2, waiting for transfers between devices, reduce_block(): lax.psum_scatter(project_term.astype(jnp.bfloat16), 'batch', scatter_dime...  284 us
    all_gather x2, waiting for transfers between devices, body(): lax.all_gather(project_weight[block_number], 'batch', axis=0, tiled=True)  268 us
  transfers between devices with their start and end apart: 34, of which 29 were waited for; matrix products, arithmetic and copies ran while one was open for 10% of the time, Pallas kernels for 0%

commit v1 on v0

v1 whole, which is shorter than its diff:
```python
import jax
import jax.numpy as jnp
from jax import lax
from jax.sharding import PartitionSpec as P

HEADS = 16
PATCH = 2
LANES = 128
PLANE = ("row", "col")

norm_epsilon = 1e-06
masked_score = -1e30
f32 = jnp.float32
bf16 = jnp.bfloat16


def to_tokens(planes, patch_side):
    images, channels, height, breadth = planes.shape
    shaped = planes.reshape(
        images, channels, height // patch_side, patch_side, breadth // patch_side, patch_side
    )
    return shaped.transpose(0, 2, 4, 3, 5, 1).reshape(
        images, height // patch_side * (breadth // patch_side), patch_side * patch_side * channels
    )


def to_planes(token_rows, patch_side, channels, rows_tile, cols_tile):
    images = token_rows.shape[0]
    shaped = token_rows.reshape(images, rows_tile, cols_tile, patch_side, patch_side, channels)
    return shaped.transpose(0, 5, 1, 3, 2, 4).reshape(
        images, channels, rows_tile * patch_side, cols_tile * patch_side
    )


def dot(left, right, dims, precision=None):
    return lax.dot_general(left, right, (dims, ((), ())), precision=precision, preferred_element_type=f32)


def norm_parts(resid):
    centered = resid - jnp.mean(resid, axis=-1, keepdims=True)
    rstd = lax.rsqrt(jnp.mean(centered * centered, axis=-1, keepdims=True) + norm_epsilon)
    return centered * rstd, rstd


def modulate(resid, shift_part, scale_part):
    return norm_parts(resid)[0] * (1.0 + scale_part) + shift_part


def modulate_back(resid, scale_part, grad):
    unit, rstd = norm_parts(resid)
    inner = grad * (1.0 + scale_part)
    grad_in = rstd * (
        inner
        - jnp.mean(inner, axis=-1, keepdims=True)
        - unit * jnp.mean(inner * unit, axis=-1, keepdims=True)
    )
    return grad_in, jnp.sum(grad, axis=1), jnp.sum(grad * unit, axis=1)


def gather_tokens(local):
    full = lax.all_gather(local, PLANE, axis=1)
    return full.reshape(local.shape[0], -1, local.shape[-1])


def scatter_tokens(partial, length):
    low = partial.astype(bf16)
    return lax.psum_scatter(low, PLANE, scatter_dimension=1, tiled=True).astype(f32)


def attention_forward(normed, weights, key_mask):
    project, project_bias, attend = weights
    full = gather_tokens(normed)
    images, length, _ = full.shape
    width = project.shape[1] // 3
    heads = width // LANES
    projected = (jnp.einsum("isd,dn->isn", full, project, preferred_element_type=f32) + project_bias).astype(bf16)
    queries, keys, values = (
        projected[..., part * width : (part + 1) * width].reshape(images, length, heads, LANES)
        for part in range(3)
    )
    factor = HEAD_SIZE ** (-0.5)
    scores = jnp.einsum("ishe,iuhe->ihsu", queries, keys, preferred_element_type=f32) * factor
    if key_mask is not None:
        scores = jnp.where(key_mask[:, None, None, :], scores, masked_score)
    peak = jnp.max(scores, axis=-1, keepdims=True)
    log_total = peak + jnp.log(jnp.sum(jnp.exp(scores - peak), axis=-1, keepdims=True))
    probs = jnp.exp(scores - log_total).astype(bf16)
    mixed = jnp.einsum("ihsu,iuhe->ishe", probs, values, preferred_element_type=f32)
    mixed = mixed.astype(bf16).reshape(images, length, width)
    partial = jnp.einsum("isn,nd->isd", mixed, attend, preferred_element_type=f32)
    attended = scatter_tokens(partial, normed.shape[1])
    return attended, (full, queries, keys, values, mixed, log_total)


def attention_backward(grad_attended, weights, key_mask, saved):
    project, _, attend = weights
    normed, queries, keys, values, mixed, log_total = saved
    images, length, heads, _ = queries.shape
    full = gather_tokens(grad_attended)
    grad_attend = jnp.einsum("isn,isd->nd", mixed, full, preferred_element_type=f32)
    grad_attend_bias = jnp.sum(full.astype(f32), axis=(0, 1))
    grad_mixed = jnp.einsum("isd,nd->isn", full, attend, preferred_element_type=f32).astype(bf16)
    grad_heads = grad_mixed.reshape(queries.shape)
    factor = HEAD_SIZE ** (-0.5)
    scores = jnp.einsum("ishe,iuhe->ihsu", queries, keys, preferred_element_type=f32) * factor
    if key_mask is not None:
        scores = jnp.where(key_mask[:, None, None, :], scores, masked_score)
    probs = jnp.exp(scores - log_total)
    dprobs = jnp.einsum("ishe,iuhe->ihsu", grad_heads, values, preferred_element_type=f32)
    row_dot = jnp.sum(probs * dprobs, axis=-1, keepdims=True)
    grad_scores = (probs * (dprobs - row_dot)).astype(bf16)
    grad_queries = jnp.einsum("ihsu,iuhe->ishe", grad_scores, keys, preferred_element_type=f32) * factor
    grad_keys = jnp.einsum("ihsu,ishe->iuhe", grad_scores, queries, preferred_element_type=f32) * factor
    grad_values = jnp.einsum("ihsu,ishe->iuhe", probs.astype(bf16), grad_heads, preferred_element_type=f32)
    grad_projected = jnp.concatenate(
        [part.astype(bf16).reshape(images, length, -1) for part in (grad_queries, grad_keys, grad_values)], axis=-1
    )
    grad_project = jnp.einsum("isd,isn->dn", normed, grad_projected, preferred_element_type=f32)
    grad_project_bias = jnp.sum(grad_projected.astype(f32), axis=(0, 1))
    partial = jnp.einsum("isn,dn->isd", grad_projected, project, preferred_element_type=f32)
    grad_normed = scatter_tokens(partial, grad_attended.shape[1])
    return grad_normed, grad_project, grad_project_bias, grad_attend, grad_attend_bias


def mlp_forward(normed, weights):
    expand, expand_bias, shrink = weights
    full = gather_tokens(normed)
    hidden = jnp.einsum("isd,dn->isn", full, expand, preferred_element_type=f32) + expand_bias
    active = jax.nn.gelu(hidden, approximate=True).astype(bf16)
    partial = jnp.einsum("isn,nd->isd", active, shrink, preferred_element_type=f32)
    return scatter_tokens(partial, normed.shape[1]), (full, hidden)


def mlp_backward(grad_expanded, weights, saved):
    expand, _, shrink = weights
    normed, hidden = saved
    full = gather_tokens(grad_expanded)
    active, pull = jax.vjp(lambda h: jax.nn.gelu(h, approximate=True), hidden)
    grad_shrink = jnp.einsum("isn,isd->nd", active.astype(bf16), full, preferred_element_type=f32)
    grad_shrink_bias = jnp.sum(full.astype(f32), axis=(0, 1))
    grad_active = jnp.einsum("isd,nd->isn", full, shrink, preferred_element_type=f32)
    grad_hidden = pull(grad_active)[0].astype(bf16)
    grad_expand = jnp.einsum("isd,isn->dn", normed, grad_hidden, preferred_element_type=f32)
    grad_expand_bias = jnp.sum(grad_hidden.astype(f32), axis=(0, 1))
    partial = jnp.einsum("isn,dn->isd", grad_hidden, expand, preferred_element_type=f32)
    grad_normed = scatter_tokens(partial, grad_expanded.shape[1])
    return grad_normed, grad_expand, grad_expand_bias, grad_shrink, grad_shrink_bias


HEAD_SIZE = 72


def pad_heads(array, axis):
    shape = array.shape
    heads = shape[axis] // HEAD_SIZE
    split = array.reshape(shape[:axis] + (heads, HEAD_SIZE) + shape[axis + 1 :])
    widths = [(0, 0)] * split.ndim
    widths[axis + 1] = (0, LANES - HEAD_SIZE)
    return jnp.pad(split, widths).reshape(shape[:axis] + (heads * LANES,) + shape[axis + 1 :])


def unpad_heads(array, axis):
    shape = array.shape
    heads = shape[axis] // LANES
    split = array.reshape(shape[:axis] + (heads, LANES) + shape[axis + 1 :])
    kept = lax.slice_in_dim(split, 0, HEAD_SIZE, axis=axis + 1)
    return kept.reshape(shape[:axis] + (heads * HEAD_SIZE,) + shape[axis + 1 :])


def gather_small(arrays, dims):
    flat = jnp.concatenate([array.reshape(-1) for array in arrays])
    every = lax.all_gather(flat, "batch", axis=0)
    out = []
    start = 0
    for array, dim in zip(arrays, dims):
        piece = every[:, start : start + array.size].reshape((-1,) + array.shape)
        start += array.size
        piece = jnp.moveaxis(piece, 0, dim)
        shape = list(array.shape)
        shape[dim] = -1
        out.append(piece.reshape(shape))
    return out


def body(
    latents,
    conditioning,
    kept_index,
    kept_count,
    patch_weight,
    patch_bias,
    adaptive_weight,
    adaptive_bias,
    project_weight,
    project_bias,
    attend_weight,
    attend_bias,
    expand_weight,
    expand_bias,
    shrink_weight,
    shrink_bias,
    final_adaptive,
    final_offset,
    final_weight,
    final_bias,
    cotangent,
):
    rows, cols, ranks = lax.axis_size("row"), lax.axis_size("col"), lax.axis_size("batch")
    team = rows * cols
    place = lax.axis_index("row") * cols + lax.axis_index("col")
    rank = lax.axis_index("batch")
    images, channels_in = latents.shape[:2]
    channels_out = cotangent.shape[1]
    rows_tile, cols_tile = latents.shape[2] // PATCH, latents.shape[3] // PATCH
    tile_tokens = rows_tile * cols_tile
    sequence = tile_tokens * team
    width = conditioning.shape[1]
    depth = adaptive_weight.shape[0]
    shard = adaptive_weight.shape[1]
    kept_local = tile_tokens * 3 // 4
    highest = lax.Precision.HIGHEST

    head_cols = width // team
    hidden_cols = expand_weight.shape[2] // team

    def slice_of(array, axis, count):
        return lax.dynamic_slice_in_dim(array, place * count, count, axis=axis)

    blocks = []
    for b in range(depth):
        project_own = lax.dynamic_index_in_dim(
            project_weight[b].reshape(shard, 3, team, head_cols), place, axis=2, keepdims=False
        )
        project_full = lax.all_gather(project_own, "batch", axis=0, tiled=True)
        gap = jnp.zeros((head_cols, width), bf16)
        padded = jnp.concatenate([gap, attend_weight[b], gap], axis=0)
        start = jnp.clip(place * head_cols - rank * shard + head_cols, 0, shard + head_cols)
        attend_full = lax.psum(lax.dynamic_slice_in_dim(padded, start, head_cols, axis=0), "batch")
        expand_full = lax.all_gather(slice_of(expand_weight[b], 1, hidden_cols), "batch", axis=0, tiled=True)
        shrink_full = lax.all_gather(slice_of(shrink_weight[b], 0, hidden_cols), "batch", axis=1, tiled=True)
        blocks.append(
            (
                pad_heads(project_full, 2).reshape(width, -1),
                pad_heads(attend_full, 0),
                expand_full,
                shrink_full,
            )
        )

    (
        patch_full,
        patch_bias_full,
        adaptive_offset,
        project_offset,
        attend_offset,
        expand_offset,
        shrink_offset,
        final_offset_full,
        final_full,
        cond_all,
    ) = gather_small(
        [
            patch_weight,
            patch_bias,
            adaptive_bias,
            project_bias,
            attend_bias,
            expand_bias,
            shrink_bias,
            final_offset,
            final_weight,
            conditioning,
        ],
        [1, 0, 1, 1, 1, 1, 1, 0, 0, 0],
    )

    patch_tiles = to_tokens(latents, PATCH)
    grad_tiles = to_tokens(cotangent, PATCH)
    patch_in, patch_out = patch_tiles.shape[2], grad_tiles.shape[2]
    tiles = lax.all_gather(jnp.concatenate([patch_tiles, grad_tiles], axis=2), PLANE, axis=1)
    whole = tiles.reshape(images, rows, cols, rows_tile, cols_tile, -1).transpose(0, 1, 3, 2, 4, 5)
    whole = whole.reshape(images, sequence, patch_in + patch_out)
    grid_cols = cols * cols_tile
    own_ids = lax.dynamic_index_in_dim(
        kept_index.reshape(images, tile_tokens, team), place, axis=2, keepdims=False
    )
    pick = (own_ids[:, :, None] == jnp.arange(sequence, dtype=jnp.int32)).astype(bf16)
    own = jnp.einsum("ikt,itc->ikc", pick, whole, preferred_element_type=f32).astype(bf16)
    patches, grad_outputs = own[..., :patch_in], own[..., patch_in:]
    order = jnp.arange(kept_local, dtype=jnp.int32)[:, None] * team + jnp.arange(team, dtype=jnp.int32)
    kept_grid = order[None] < kept_count[:, None, None]
    key_mask = kept_grid.transpose(0, 2, 1).reshape(images, team * kept_local)
    kept_rows = lax.dynamic_index_in_dim(kept_grid, place, axis=2, keepdims=False).astype(f32)[:, :, None]

    count = width // 4
    omega = 1.0 / 10000.0 ** (jnp.arange(count, dtype=f32) / count)
    angles = jnp.arange(max(rows * rows_tile, grid_cols), dtype=f32)[:, None] * omega[None, :]
    along = jnp.concatenate([jnp.sin(angles), jnp.cos(angles)], axis=1)
    places = jnp.arange(along.shape[0], dtype=jnp.int32)

    def position_of(coords):
        chosen = (coords[..., None] == places).astype(f32)
        return jnp.einsum("ikt,tc->ikc", chosen, along, precision=highest)

    position = jnp.concatenate(
        [position_of(own_ids // grid_cols), position_of(own_ids % grid_cols)], axis=-1
    )
    resid = (
        jnp.einsum("ikc,cd->ikd", patches, patch_full, preferred_element_type=f32)
        + patch_bias_full.astype(f32)
        + position
    )

    silu_all = jax.nn.silu(cond_all.astype(f32)).astype(bf16)
    silu_rows = lax.dynamic_slice_in_dim(silu_all, rank * shard, shard, axis=1)
    mod_cols, final_cols = adaptive_weight.shape[2] // team, final_adaptive.shape[1] // team
    parts = [
        dot(silu_rows, slice_of(adaptive_weight[b], 1, mod_cols), ((1,), (0,))) for b in range(depth)
    ] + [dot(silu_rows, slice_of(final_adaptive, 1, final_cols), ((1,), (0,)))]
    mods = lax.psum_scatter(jnp.concatenate(parts, axis=1), "batch", scatter_dimension=0, tiled=True)
    mods = lax.all_gather(mods, PLANE, axis=1)
    pieces = []
    for b in range(depth):
        block_mod = mods[:, :, b * mod_cols : (b + 1) * mod_cols].reshape(images, -1)
        block_mod = (block_mod + adaptive_offset[b].astype(f32)).reshape(images, 6, 1, width)
        pieces.append([block_mod[:, s] for s in range(6)])
    final_mod = mods[:, :, depth * mod_cols :].reshape(images, -1) + final_offset_full.astype(f32)
    final_mod = final_mod.reshape(images, 2, 1, width)
    final_shift, final_scale = final_mod[:, 0], final_mod[:, 1]

    records = []
    for b in range(depth):
        project, attend, expand, shrink = blocks[b]
        shift1, scale1, gate1, shift2, scale2, gate2 = pieces[b]
        bias = project_offset[b].astype(f32).reshape(2, team, head_cols)
        bias = lax.dynamic_index_in_dim(bias, place, axis=1, keepdims=False)
        bias = pad_heads(jnp.stack([bias[0], jnp.zeros_like(bias[0]), bias[1]]), 1).reshape(-1)
        attention_weights = (project, bias, attend)
        mlp_weights = (expand, slice_of(expand_offset[b].astype(f32), 0, hidden_cols), shrink)
        routed = b > 0
        mask = key_mask if routed else None
        base = resid[:, :kept_local] if routed else resid
        gate_rows = kept_rows if routed else 1.0
        normed = modulate(base, shift1, scale1).astype(bf16)
        attended, attention_saved = attention_forward(normed, attention_weights, mask)
        attended = attended + attend_offset[b].astype(f32)
        mid = base + gate_rows * gate1 * attended
        normed_mid = modulate(mid, shift2, scale2).astype(bf16)
        expanded, mlp_saved = mlp_forward(normed_mid, mlp_weights)
        expanded = expanded + shrink_offset[b].astype(f32)
        after = mid + gate_rows * gate2 * expanded
        records.append((base, mid, attended, expanded, attention_weights, mlp_weights, mask, gate_rows, attention_saved, mlp_saved))
        resid = jnp.concatenate([after, resid[:, kept_local:]], axis=1) if routed else after

    final_normed = modulate(resid, final_shift, final_scale).astype(bf16)
    outputs = jnp.einsum("ikd,dc->ikc", final_normed, final_full, preferred_element_type=f32) + final_bias.astype(f32)
    final_bias_term = jnp.sum(grad_outputs.astype(f32), axis=(0, 1))
    final_weight_term = jnp.einsum("ikd,ikc->dc", final_normed, grad_outputs, preferred_element_type=f32)
    grad_final = jnp.einsum("ikc,dc->ikd", grad_outputs, final_full, preferred_element_type=f32)
    grad_resid, grad_final_shift, grad_final_scale = modulate_back(resid, final_scale, grad_final)
    final_mod_term = jnp.stack([grad_final_shift, grad_final_scale], axis=1)

    mod_terms = [None] * depth
    block_grads = [None] * depth
    for b in reversed(range(depth)):
        base, mid, attended, expanded, attention_weights, mlp_weights, mask, gate_rows, attention_saved, mlp_saved = records[b]
        shift1, scale1, gate1, shift2, scale2, gate2 = pieces[b]
        routed = b > 0
        grad_after = grad_resid[:, :kept_local] if routed else grad_resid
        gated = gate_rows * grad_after
        grad_gate2 = jnp.sum(gated * expanded, axis=1)
        grad_expanded = (gated * gate2).astype(bf16)
        grad_normed_mid, grad_expand, grad_expand_bias, grad_shrink, grad_shrink_bias = mlp_backward(
            grad_expanded, mlp_weights, mlp_saved
        )
        grad_mid, grad_shift2, grad_scale2 = modulate_back(mid, scale2, grad_normed_mid)
        grad_mid = grad_mid + grad_after
        gated = gate_rows * grad_mid
        grad_gate1 = jnp.sum(gated * attended, axis=1)
        grad_attended = (gated * gate1).astype(bf16)
        grad_normed, grad_project, grad_project_bias, grad_attend, grad_attend_bias = attention_backward(
            grad_attended, attention_weights, mask, attention_saved
        )
        grad_base, grad_shift1, grad_scale1 = modulate_back(base, scale1, grad_normed)
        grad_base = grad_base + grad_mid
        grad_resid = jnp.concatenate([grad_base, grad_resid[:, kept_local:]], axis=1) if routed else grad_base
        mod_terms[b] = jnp.stack(
            [grad_shift1, grad_scale1, grad_gate1, grad_shift2, grad_scale2, grad_gate2], axis=1
        )
        grad_project = unpad_heads(grad_project.reshape(width, 3, -1), 2).astype(bf16)
        grad_project = lax.psum_scatter(grad_project, "batch", scatter_dimension=0, tiled=True)
        grad_project = lax.all_gather(grad_project, PLANE, axis=2).reshape(shard, -1)
        grad_attend = lax.psum(unpad_heads(grad_attend, 0).astype(bf16), "batch")
        grad_attend = lax.all_gather(grad_attend, PLANE, axis=0, tiled=True)
        grad_attend = lax.dynamic_slice_in_dim(grad_attend, rank * shard, shard, axis=0)
        grad_expand = lax.psum_scatter(grad_expand.astype(bf16), "batch", scatter_dimension=0, tiled=True)
        grad_expand = lax.all_gather(grad_expand, PLANE, axis=1, tiled=True)
        grad_shrink = lax.psum_scatter(grad_shrink.astype(bf16), "batch", scatter_dimension=1, tiled=True)
        grad_shrink = lax.all_gather(grad_shrink, PLANE, axis=0, tiled=True)
        grad_bias = unpad_heads(grad_project_bias.reshape(3, -1), 1)
        grad_bias = jnp.stack([grad_bias[0], grad_bias[2]])
        block_grads[b] = (
            grad_project.astype(f32),
            grad_attend.astype(f32),
            grad_expand.astype(f32),
            grad_shrink.astype(f32),
            grad_bias,
            grad_attend_bias,
            grad_expand_bias,
            grad_shrink_bias,
        )

    mod_all = jnp.concatenate([jnp.stack(mod_terms, axis=1).reshape(images, -1), final_mod_term.reshape(images, -1)], axis=1)
    mod_low = lax.psum(mod_all, PLANE).astype(bf16)
    mod_every = lax.all_gather(mod_low, "batch", axis=0, tiled=True)
    mod_width = adaptive_weight.shape[2]
    block_mods = [mod_every[:, b * mod_width : (b + 1) * mod_width] for b in range(depth)]
    final_mods = mod_every[:, depth * mod_width :]
    adaptive_weight_grad = jnp.stack([dot(silu_rows, m, ((0,), (0,))) for m in block_mods])
    final_adaptive_grad = dot(silu_rows, final_mods, ((0,), (0,)))
    mod_sum = jnp.sum(mod_every.astype(f32), axis=0)
    offset_cols, final_offset_cols = adaptive_bias.shape[1], final_offset.shape[0]
    adaptive_bias_grad = lax.dynamic_slice_in_dim(
        mod_sum[: depth * mod_width].reshape(depth, mod_width), rank * offset_cols, offset_cols, axis=1
    )
    final_offset_grad = lax.dynamic_slice_in_dim(
        mod_sum[depth * mod_width :], rank * final_offset_cols, final_offset_cols
    )
    grad_silu = dot(final_mods, final_adaptive, ((1,), (1,)))
    for b in range(depth):
        grad_silu = grad_silu + dot(block_mods[b], adaptive_weight[b], ((1,), (1,)))
    grad_silu = lax.all_to_all(grad_silu.reshape(ranks, images, shard), "batch", 0, 0)
    grad_silu = grad_silu.transpose(1, 0, 2).reshape(images, width)
    conditioning_grad = jax.vjp(jax.nn.silu, conditioning.astype(f32))[1](grad_silu)[0]

    patch_bias_term = jnp.sum(grad_resid, axis=(0, 1))
    grad_embed = grad_resid.astype(bf16)
    patch_term = jnp.einsum("ikc,ikd->cd", patches, grad_embed, preferred_element_type=f32)
    grad_patches = jnp.einsum("ikd,cd->ikc", grad_embed, patch_full, preferred_element_type=f32)
    ordered = lax.all_gather(jnp.concatenate([outputs, grad_patches], axis=2), PLANE, axis=2)
    ordered = ordered.reshape(images, sequence, patch_out + patch_in)
    tile_rows = lax.axis_index("row") * rows_tile + jnp.arange(rows_tile, dtype=jnp.int32)
    tile_cols = lax.axis_index("col") * cols_tile + jnp.arange(cols_tile, dtype=jnp.int32)
    tile_ids = (tile_rows[:, None] * grid_cols + tile_cols).reshape(-1)
    back = (kept_index[:, None, :] == tile_ids[None, :, None]).astype(f32)
    tile_out = jnp.einsum("itj,ijc->itc", back, ordered, precision=highest)
    prediction = to_planes(tile_out[..., :patch_out], PATCH, channels_out, rows_tile, cols_tile)
    latent_grad = to_planes(tile_out[..., patch_out:], PATCH, channels_in, rows_tile, cols_tile)

    def scattered(full, axis, parted):
        return lax.psum_scatter(full, "batch", scatter_dimension=axis, tiled=True) if parted else full

    token_sums = lax.psum(
        (patch_term, patch_bias_term, final_weight_term, final_bias_term), ("batch", "row", "col")
    )
    patch_weight_grad = lax.dynamic_slice_in_dim(token_sums[0], rank * shard, shard, axis=1)
    patch_bias_grad = lax.dynamic_slice_in_dim(token_sums[1], rank * shard, shard)
    final_weight_grad = lax.dynamic_slice_in_dim(token_sums[2], rank * shard, shard, axis=0)
    final_bias_grad = token_sums[3]
    stacked = [jnp.stack([block_grads[b][n] for b in range(depth)]) for n in range(8)]
    bias_sums = lax.psum((stacked[4], stacked[5], stacked[6], stacked[7]), "batch")
    project_sum = lax.all_gather(bias_sums[0], PLANE, axis=2).reshape(depth, -1)
    expand_sum = lax.all_gather(bias_sums[2], PLANE, axis=1, tiled=True)

    def rank_part(full):
        part = full.shape[1] // ranks
        return lax.dynamic_slice_in_dim(full, rank * part, part, axis=1)

    return (
        prediction,
        latent_grad,
        conditioning_grad,
        patch_weight_grad,
        patch_bias_grad,
        adaptive_weight_grad,
        adaptive_bias_grad,
        stacked[0],
        rank_part(project_sum),
        stacked[1],
        rank_part(bias_sums[1]),
        stacked[2],
        rank_part(expand_sum),
        stacked[3],
        rank_part(bias_sums[3]),
        final_adaptive_grad,
        final_offset_grad,
        final_weight_grad,
        final_bias_grad,
    )


def solution(mesh):
    tokens = P("batch", None, "row", "col")
    placed = (
        tokens,
        P("batch", None),
        P("batch", None),
        P("batch"),
        P(None, "batch"),
        P("batch"),
        P(None, "batch", None),
        P(None, "batch"),
        P(None, "batch", None),
        P(None, "batch"),
        P(None, "batch", None),
        P(None, "batch"),
        P(None, "batch", None),
        P(None, "batch"),
        P(None, None, "batch"),
        P(None, "batch"),
        P("batch", None),
        P("batch"),
        P("batch", None),
        P(),
        tokens,
    )
    return jax.shard_map(
        body,
        mesh=mesh,
        in_specs=placed,
        out_specs=(tokens, tokens, P("batch", None)) + placed[4:16] + (placed[16], P("batch"), P("batch", None), P()),
        check_vma=False,
    )
```

time: 4480 us -> 1930 us (0.43)
  waiting for transfers between devices: 3620 us -> 1070 us
  matrix products: 327 us -> 252 us
  local copies, waits for them, and re-layouts: 152 us -> 209 us
    reduce_scatter x14 -> x12, waiting for transfers between devices: 1740 us -> 416 us  [the longest x8 378 us: scatter_tokens(): lax.psum_scatter(low, PLANE, scatter_dimension=1, tiled=True).astype(f32)]
    all_gather x15 -> x20, waiting for transfers between devices: 1660 us -> 430 us  [the longest x8 180 us: gather_tokens(): full = lax.all_gather(local, PLANE, axis=1)]
    unnamed x37, waiting for transfers between devices: 4.03 us -> 225 us
    psum x2 -> x1, waiting for transfers between devices: 214 us -> 0.01 us  [body(): lax.psum((patch_term, patch_bias_term, final_weight_term, final_bias_term...]
    all_gather x4 -> x8, blocking collectives: 67.8 us -> 145 us  [the longest x2 84.7 us: body(): project_full = lax.all_gather(project_own, 'batch', axis=0, tiled=True)]
    dot_general x51 -> x55, matrix products: 327 us -> 252 us  [the longest x2 19.6 us: mlp_backward(): jnp.einsum('isd,nd->isn', full, shrink, preferred_element_type=f32)]
    unnamed x3 -> x1, blocking collectives: 75.5 us -> 17.8 us
  transfers between devices with their start and end apart: 34 -> 36, of which waited for: 29 -> 27; matrix products, arithmetic and copies ran while one was open for 10% -> 19% of each run, Pallas kernels for 0% -> 0%
where the time goes in v1:
time: 1930 us; the launch traced here: 1920 us
  waiting for transfers between devices  1070 us (55%)
  matrix products  252 us (13%)
  blocking collectives  247 us (13%)
  local copies, waits for them, and re-layouts  209 us (11%)
  other arithmetic  116 us (6%)
  between operations  19.3 us (1%)
    reduce_scatter x8, waiting for transfers between devices, scatter_tokens(): lax.psum_scatter(low, PLANE, scatter_dimension=1, tiled=True).astype(f32)  378 us
    unnamed x37, waiting for transfers between devices  225 us
    all_gather x8, waiting for transfers between devices, gather_tokens(): full = lax.all_gather(local, PLANE, axis=1)  180 us
    all_gather x2, blocking collectives, body(): project_full = lax.all_gather(project_own, 'batch', axis=0, tiled=True)  84.7 us
    all_gather x2, waiting for transfers between devices, body(): lax.all_gather(slice_of(shrink_weight[b], 0, hidden_cols), 'batch', axis=...  60.1 us
    all_gather x2, waiting for transfers between devices, body(): lax.all_gather(slice_of(expand_weight[b], 1, hidden_cols), 'batch', axis=...  60 us
    all_gather x2, waiting for transfers between devices, body(): grad_attend = lax.all_gather(grad_attend, PLANE, axis=0, tiled=True)  59.8 us
    all_gather x2, waiting for transfers between devices, body(): grad_shrink = lax.all_gather(grad_shrink, PLANE, axis=0, tiled=True)  46.6 us
  transfers between devices with their start and end apart: 36, of which 27 were waited for; matrix products, arithmetic and copies ran while one was open for 19% of the time, Pallas kernels for 0%

profile of v1, /device:TPU:0, one launch (start us, length us, event | category | flops | bytes accessed | tf_op | source)
XLA Modules:
  0.0 1922.2 jit_solution(11874671031560288191)
XLA Ops:
  43.5 27.4 %all-reduce.23.cloned.1.call-done = (bf16[100224]{0:T(1024)(128)(2,1)}, bf16[2,72,1152]{2,1,0:T(8,128)(2,1)}, bf16[2,72,1152]{2,1,0:T(8,128)(2,1)}) async-done(((bf16[100224]{0:T(1024)(128)(2,1)}, bf16[2,72,1152]{2,1,0:T(8,128)(2,1)}, bf16[2,72,1152]{2,1,0:T(8,128)(2,1)}), (bf16[100224]{0:T(1024)(128)(2,1)}, bf16[2,72,1152]{2,1,0:T(8,128)(2,1)}, ...) | async-done | bytes 864016
  78.7 17.8 all-reduce.7
  118.9 42.4 %all-gather.4 = bf16[1152,3,1,144]{3,1,2,0:T(4,128)(2,1)} all-gather(bf16[288,3,1,144]{3,1,2,0:T(4,128)(2,1)S(1)} %copy.235), channel_id=6, replica_groups=mesh['batch'=4,'row'=2,'col'=4] {'batch'}, dimensions={0}, use_global_device_ids=true | all-gather | bytes 1244160 | tf_op jit(solution)/shard_map/all_gather | solution.py:234
  215.4 44.6 %reduce-scatter.13.cloned.1.call-done = bf16[2,128,1152]{2,1,0:T(8,128)(2,1)} async-done(((bf16[2,1024,1152]{2,1,0:T(8,128)(2,1)}), bf16[2,128,1152]{2,1,0:T(8,128)(2,1)}) %reduce-scatter.13.cloned.1.call-update) | async-done | bytes 589840 | tf_op jit(solution)/shard_map/reduce_scatter | solution.py:67
  269.2 27.8 %all-gather.57.cloned.1.call-done = bf16[1,1152,576]{2,1,0:T(8,128)(2,1)} async-done(((bf16[1,288,576]{2,1,0:T(8,128)(2,1)}), bf16[1,1152,576]{2,1,0:T(8,128)(2,1)}) %all-gather.57.cloned.1.call-update) | async-done | bytes 1327120 | tf_op jit(solution)/shard_map/all_gather | solution.py:239
  297.0 40.3 %all-gather.55.cloned.1.call-done = bf16[2,1024,1152]{2,1,0:T(8,128)(2,1)} async-done(((bf16[2,128,1152]{2,1,0:T(8,128)(2,1)}), bf16[2,1024,1152]{2,1,0:T(8,128)(2,1)}) %all-gather.55.cloned.1.call-update) | async-done | bytes 4718608 | tf_op jit(solution)/shard_map/all_gather | solution.py:61
  345.6 29.3 %all-gather.59.cloned.1.call-done = bf16[1,576,1152]{1,2,0:T(8,128)(2,1)} async-done(((bf16[1,576,288]{1,2,0:T(8,128)(2,1)}), bf16[1,576,1152]{1,2,0:T(8,128)(2,1)}) %all-gather.59.cloned.1.call-update) | async-done | bytes 1327120 | tf_op jit(solution)/shard_map/all_gather | solution.py:240
  387.3 50.6 %reduce-scatter.15.cloned.1.call-done = bf16[2,128,1152]{2,1,0:T(8,128)(2,1)} async-done(((bf16[2,1024,1152]{2,1,0:T(8,128)(2,1)}), bf16[2,128,1152]{2,1,0:T(8,128)(2,1)}) %reduce-scatter.15.cloned.1.call-update) | async-done | bytes 589840 | tf_op jit(solution)/shard_map/reduce_scatter | solution.py:67
  446.9 42.3 %all-gather.9 = bf16[1152,3,1,144]{3,1,2,0:T(4,128)(2,1)} all-gather(bf16[288,3,1,144]{3,1,2,0:T(4,128)(2,1)S(1)} %copy.244), channel_id=11, replica_groups=mesh['batch'=4,'row'=2,'col'=4] {'batch'}, dimensions={0}, use_global_device_ids=true | all-gather | bytes 1244160 | tf_op jit(solution)/shard_map/all_gather | solution.py:234
  515.6 46.5 %reduce-scatter.17.cloned.1.call-done = bf16[2,96,1152]{2,1,0:T(8,128)(2,1)} async-done(((bf16[2,768,1152]{2,1,0:T(8,128)(2,1)}), bf16[2,96,1152]{2,1,0:T(8,128)(2,1)}) %reduce-scatter.17.cloned.1.call-update) | async-done | bytes 442384 | tf_op jit(solution)/shard_map/reduce_scatter | solution.py:67
  567.5 32.2 %all-gather.65.cloned.1.call-done = bf16[1,1152,576]{2,1,0:T(8,128)(2,1)} async-done(((bf16[1,288,576]{2,1,0:T(8,128)(2,1)}), bf16[1,1152,576]{2,1,0:T(8,128)(2,1)}) %all-gather.65.cloned.1.call-update) | async-done | bytes 1327120 | tf_op jit(solution)/shard_map/all_gather | solution.py:239
  599.7 35.4 %all-gather.63.cloned.1.call-done = bf16[2,768,1152]{2,1,0:T(8,128)(2,1)} async-done(((bf16[2,96,1152]{2,1,0:T(8,128)(2,1)}), bf16[2,768,1152]{2,1,0:T(8,128)(2,1)}) %all-gather.63.cloned.1.call-update) | async-done | bytes 3538960 | tf_op jit(solution)/shard_map/all_gather | solution.py:61
  641.8 30.8 %all-gather.67.cloned.1.call-done = bf16[1,576,1152]{1,2,0:T(8,128)(2,1)} async-done(((bf16[1,576,288]{1,2,0:T(8,128)(2,1)}), bf16[1,576,1152]{1,2,0:T(8,128)(2,1)}) %all-gather.67.cloned.1.call-update) | async-done | bytes 1327120 | tf_op jit(solution)/shard_map/all_gather | solution.py:240
  687.3 40.4 %reduce-scatter.19.cloned.1.call-done = bf16[2,96,1152]{2,1,0:T(8,128)(2,1)} async-done(((bf16[2,768,1152]{2,1,0:T(8,128)(2,1)}), bf16[2,96,1152]{2,1,0:T(8,128)(2,1)}) %reduce-scatter.19.cloned.1.call-update) | async-done | bytes 442384 | tf_op jit(solution)/shard_map/reduce_scatter | solution.py:67
  735.6 33.6 %all-gather.69.cloned.1.call-done = bf16[2,768,1152]{2,1,0:T(8,128)(2,1)} async-done(((bf16[2,96,1152]{2,1,0:T(8,128)(2,1)}), bf16[2,768,1152]{2,1,0:T(8,128)(2,1)}) %all-gather.69.cloned.1.call-update) | async-done | bytes 3538960 | tf_op jit(solution)/shard_map/all_gather | solution.py:61
  784.3 48.2 %reduce-scatter.21.cloned.1.call-done = bf16[2,96,1152]{2,1,0:T(8,128)(2,1)} async-done(((bf16[2,768,1152]{2,1,0:T(8,128)(2,1)}), bf16[2,96,1152]{2,1,0:T(8,128)(2,1)}) %reduce-scatter.21.cloned.1.call-update) | async-done | bytes 442384 | tf_op jit(solution)/shard_map/reduce_scatter | solution.py:67
  842.3 32.1 %all-gather.71.cloned.1.call-done = bf16[2,768,1152]{2,1,0:T(8,128)(2,1)} async-done(((bf16[2,96,1152]{2,1,0:T(8,128)(2,1)}), bf16[2,768,1152]{2,1,0:T(8,128)(2,1)}) %all-gather.71.cloned.1.call-update) | async-done | bytes 3538960 | tf_op jit(solution)/shard_map/all_gather | solution.py:61
  911.2 46.2 %reduce-scatter.23.cloned.1.call-done = bf16[2,96,1152]{2,1,0:T(8,128)(2,1)} async-done(((bf16[2,768,1152]{2,1,0:T(8,128)(2,1)}), bf16[2,96,1152]{2,1,0:T(8,128)(2,1)}) %reduce-scatter.23.cloned.1.call-update) | async-done | bytes 442384 | tf_op jit(solution)/shard_map/reduce_scatter | solution.py:67
  962.8 39.0 %all-gather.47.cloned.1.call-done = bf16[2,8,128,1152]{3,2,0,1:T(8,128)(2,1)} async-done(((bf16[2,1,128,1152]{3,2,0,1:T(8,128)(2,1)}), bf16[2,8,128,1152]{3,2,0,1:T(8,128)(2,1)}) %all-gather.47.cloned.1.call-update) | async-done | bytes 4718608 | tf_op jit(solution)/shard_map/all_gather | solution.py:61
  1022.6 54.0 %reduce-scatter.25.cloned.1.call-done = bf16[2,128,1152]{2,1,0:T(8,128)(2,1)} async-done(((bf16[2,1024,1152]{2,1,0:T(8,128)(2,1)}), bf16[2,128,1152]{2,1,0:T(8,128)(2,1)}) %reduce-scatter.25.cloned.1.call-update) | async-done | bytes 589840 | tf_op jit(solution)/shard_map/reduce_scatter | solution.py:67
  1229.9 34.8 %reduce-scatter.33.cloned.1.call-done = bf16[576,288]{0,1:T(8,128)(2,1)} async-done(((bf16[576,1152]{0,1:T(8,128)(2,1)}), bf16[576,288]{0,1:T(8,128)(2,1)}) %reduce-scatter.33.cloned.1.call-update) | async-done | bytes 331792 | tf_op jit(solution)/shard_map/reduce_scatter | solution.py:398
  1265.4 196.4 %all-reduce.21.cloned.1.call-done = (bf16[1152,3,144]{2,1,0:T(4,128)(2,1)}, bf16[1152,3,144]{2,1,0:T(4,128)(2,1)}, bf16[144,1152]{1,0:T(8,128)(2,1)}, bf16[144,1152]{1,0:T(8,128)(2,1)}) async-done(((bf16[1152,3,144]{2,1,0:T(4,128)(2,1)}, bf16[1152,3,144]{2,1,0:T(4,128)(2,1)}, bf16[144,1152]{1,0:T(8,128)(2,1)}, bf16[144,1152]{1,0:T(8,128)(2,1)}), (bf16[1152,3,144]{2,1,0:T(4,128)(2,1)}, ...) | async-done | bytes 2654224
  1504.1 23.2 %all-gather.85.cloned.1.call-done = bf16[8,576,288]{1,2,0:T(8,128)(2,1)} async-done(((bf16[1,576,288]{1,2,0:T(8,128)(2,1)}), bf16[8,576,288]{1,2,0:T(8,128)(2,1)}) %all-gather.85.cloned.1.call-update) | async-done | bytes 2654224 | tf_op jit(solution)/shard_map/all_gather | solution.py:399
  1537.4 47.8 %reduce-scatter.27.cloned.1.call-done = bf16[2,128,1152]{2,1,0:T(8,128)(2,1)} async-done(((bf16[2,1024,1152]{2,1,0:T(8,128)(2,1)}), bf16[2,128,1152]{2,1,0:T(8,128)(2,1)}) %reduce-scatter.27.cloned.1.call-update) | async-done | bytes 589840 | tf_op jit(solution)/shard_map/reduce_scatter | solution.py:67
  1604.0 14.7 all-gather.79.cloned.1.call-done
  1628.8 23.4 %all-gather.83.cloned.1.call-done = bf16[8,576,288]{1,2,0:T(8,128)(2,1)} async-done(((bf16[1,576,288]{1,2,0:T(8,128)(2,1)}), bf16[8,576,288]{1,2,0:T(8,128)(2,1)}) %all-gather.83.cloned.1.call-update) | async-done | bytes 2654224 | tf_op jit(solution)/shard_map/all_gather | solution.py:399
  1677.5 19.1 all-reduce.12
  1729.8 24.9 %psum.93 = bf16[2,16128]{1,0:T(2,128)(2,1)S(1)} all-reduce(f32[2,16128]{1,0:T(2,128)S(1)} %pad_maximum_fusion.6), channel_id=1, replica_groups=mesh['batch'=4,'row'=2,'col'=4] {'row','col'}, use_global_device_ids=true, to_apply=%region_51.52 | all-reduce | flops 32256 | bytes 193536 | tf_op jit(solution)/shard_map/psum | solution.py:414
  1754.7 14.2 all-gather.20
  1802.9 40.0 %all-reduce.10 = (f32[1152]{0:T(1024)S(1)}, f32[32]{0:T(128)}) all-reduce(f32[1152]{0:T(1024)S(1)} %copy-done.114, f32[32]{0:T(128)S(1)} %copy-done.149), channel_id=1, replica_groups=mesh['batch'=4,'row'=2,'col'=4] {'batch','row','col'}, use_global_device_ids=true, to_apply=%region_54.55 | all-reduce | flops 1184 | bytes 9472 | tf_op jit(solution)/shard_map/psum | solution.py:453
  1851.4 28.7 %all-gather.51.cloned.1.call-done = bf16[1152,1152]{1,0:T(8,128)(2,1)} async-done(((bf16[144,1152]{1,0:T(8,128)(2,1)}), bf16[1152,1152]{1,0:T(8,128)(2,1)}) %all-gather.51.cloned.1.call-update) | async-done | bytes 2654224 | tf_op jit(solution)/shard_map/all_gather | solution.py:394
  1881.2 31.2 %all-gather.49.cloned.1.call-done = bf16[1152,1152]{1,0:T(8,128)(2,1)} async-done(((bf16[144,1152]{1,0:T(8,128)(2,1)}), bf16[1152,1152]{1,0:T(8,128)(2,1)}) %all-gather.49.cloned.1.call-update) | async-done | bytes 2654224 | tf_op jit(solution)/shard_map/all_gather | solution.py:394
  (792 shorter events, 643.8 us)
Async XLA Ops:
  20.9 148.2 %all-gather.53.cloned.1.call-start = ((), (), s32[]{:S(2)}) async-start(), calls=%async_computation.28 | async-start | bytes 5308416 | tf_op jit(solution)/shard_map/all_gather | solution.py:61
  108.8 151.2 %reduce-scatter.13.cloned.1.call-start = ((), (), s32[]{:S(2)}) async-start(), calls=%async_computation.13 | async-start | bytes 5308416 | tf_op jit(solution)/shard_map/reduce_scatter | solution.py:67
  207.6 89.4 %all-gather.57.cloned.1.call-start = ((), (), s32[]{:S(2)}) async-start(), calls=%async_computation.30 | async-start | bytes 1843200 | tf_op jit(solution)/shard_map/all_gather | solution.py:239
  213.0 124.3 %all-gather.55.cloned.1.call-start = ((), (), s32[]{:S(2)}) async-start(), calls=%async_computation.29 | async-start | bytes 5308416 | tf_op jit(solution)/shard_map/all_gather | solution.py:61
  263.5 111.4 %all-gather.59.cloned.1.call-start = ((), (), s32[]{:S(2)}) async-start(), calls=%async_computation.31 | async-start | bytes 1843200 | tf_op jit(solution)/shard_map/all_gather | solution.py:240
  268.9 168.9 %reduce-scatter.15.cloned.1.call-start = ((), (), s32[]{:S(2)}) async-start(), calls=%async_computation.14 | async-start | bytes 5308416 | tf_op jit(solution)/shard_map/reduce_scatter | solution.py:67
  384.9 109.8 %all-gather.61.cloned.1.call-start = ((), (), s32[]{:S(2)}) async-start(), calls=%async_computation.32 | async-start | bytes 3981312 | tf_op jit(solution)/shard_map/all_gather | solution.py:61
  441.2 121.0 %reduce-scatter.17.cloned.1.call-start = ((), (), s32[]{:S(2)}) async-start(), calls=%async_computation.15 | async-start | bytes 3981312 | tf_op jit(solution)/shard_map/reduce_scatter | solution.py:67
  515.3 119.7 %all-gather.63.cloned.1.call-start = ((), (), s32[]{:S(2)}) async-start(), calls=%async_computation.33 | async-start | bytes 3981312 | tf_op jit(solution)/shard_map/all_gather | solution.py:61
  565.1 107.4 %all-gather.67.cloned.1.call-start = ((), (), s32[]{:S(2)}) async-start(), calls=%async_computation.35 | async-start | bytes 1843200 | tf_op jit(solution)/shard_map/all_gather | solution.py:240
  567.1 160.6 %reduce-scatter.19.cloned.1.call-start = ((), (), s32[]{:S(2)}) async-start(), calls=%async_computation.16 | async-start | bytes 3981312 | tf_op jit(solution)/shard_map/reduce_scatter | solution.py:67
  735.1 97.4 %reduce-scatter.21.cloned.1.call-start = ((), (), s32[]{:S(2)}) async-start(), calls=%async_computation.17 | async-start | bytes 3981312 | tf_op jit(solution)/shard_map/reduce_scatter | solution.py:67
  784.3 90.1 %all-gather.71.cloned.1.call-start = ((), (), s32[]{:S(2)}) async-start(), calls=%async_computation.37 | async-start | bytes 3981312 | tf_op jit(solution)/shard_map/all_gather | solution.py:61
  840.2 117.1 %reduce-scatter.23.cloned.1.call-start = ((), (), s32[]{:S(2)}) async-start(), calls=%async_computation.18 | async-start | bytes 3981312 | tf_op jit(solution)/shard_map/reduce_scatter | solution.py:67
  909.1 92.6 %all-gather.47.cloned.1.call-start = ((), (), s32[]{:S(2)}) async-start(), calls=%async_computation.19 | async-start | bytes 5308416 | tf_op jit(solution)/shard_map/all_gather | solution.py:61
  962.7 113.9 %reduce-scatter.25.cloned.1.call-start = ((), (), s32[]{:S(2)}) async-start(), calls=%async_computation.20 | async-start | bytes 5308416 | tf_op jit(solution)/shard_map/reduce_scatter | solution.py:67
  1022.6 116.2 %all-gather.73.cloned.1.call-start = ((), (), s32[]{:S(2)}) async-start(), calls=%async_computation.38 | async-start | bytes 5308416 | tf_op jit(solution)/shard_map/all_gather | solution.py:61
  1083.9 133.7 %reduce-scatter.31.cloned.1.call-start = ((), (), s32[]{:S(2)}) async-start(), calls=%async_computation.25 | async-start | bytes 1843200 | tf_op jit(solution)/shard_map/reduce_scatter | solution.py:396
  1090.6 127.5 %reduce-scatter.35.cloned.1.call-start = ((), (), s32[]{:S(2)}) async-start(), calls=%async_computation.27 | async-start | bytes 1843200 | tf_op jit(solution)/shard_map/reduce_scatter | solution.py:398
  1098.9 131.0 %reduce-scatter.29.cloned.1.call-start = ((), (), s32[]{:S(2)}) async-start(), calls=%async_computation.24 | async-start | bytes 1843200 | tf_op jit(solution)/shard_map/reduce_scatter | solution.py:396
  1107.1 157.6 %reduce-scatter.33.cloned.1.call-start = ((), (), s32[]{:S(2)}) async-start(), calls=%async_computation.26 | async-start | bytes 1843200 | tf_op jit(solution)/shard_map/reduce_scatter | solution.py:398
  1138.5 323.3 %all-reduce.21.cloned.1.call-start = ((), (), s32[]{:S(2)}) async-start(), calls=%async_computation.46 | async-start | bytes 10764288
  1217.4 276.6 %all-gather.81.cloned.1.call-start = ((), (), s32[]{:S(2)}) async-start(), calls=%async_computation.42 | async-start | bytes 3317760 | tf_op jit(solution)/shard_map/all_gather | solution.py:397
  1218.0 309.2 %all-gather.85.cloned.1.call-start = ((), (), s32[]{:S(2)}) async-start(), calls=%async_computation.44 | async-start | bytes 3317760 | tf_op jit(solution)/shard_map/all_gather | solution.py:399
  1218.6 366.6 %reduce-scatter.27.cloned.1.call-start = ((), (), s32[]{:S(2)}) async-start(), calls=%async_computation.21 | async-start | bytes 5308416 | tf_op jit(solution)/shard_map/reduce_scatter | solution.py:67
  1227.0 391.8 %all-gather.79.cloned.1.call-start = ((), (), s32[]{:S(2)}) async-start(), calls=%async_computation.41 | async-start | bytes 3317760 | tf_op jit(solution)/shard_map/all_gather | solution.py:397
  1229.9 422.3 %all-gather.83.cloned.1.call-start = ((), (), s32[]{:S(2)}) async-start(), calls=%async_computation.43 | async-start | bytes 3317760 | tf_op jit(solution)/shard_map/all_gather | solution.py:399
  1264.7 451.9 %all-gather.77.cloned.1.call-start = ((), (), s32[]{:S(2)}) async-start(), calls=%async_computation.40 | async-start | bytes 2985984 | tf_op jit(solution)/shard_map/all_gather | solution.py:392
  1466.0 253.8 %all-gather.75.cloned.1.call-start = ((), (), s32[]{:S(2)}) async-start(), calls=%async_computation.39 | async-start | bytes 2985984 | tf_op jit(solution)/shard_map/all_gather | solution.py:392
  1470.2 378.2 %all-reduce.19.cloned.1.call-start = ((), (), s32[]{:S(2)}) async-start(), calls=%async_computation.45 | async-start | bytes 442368 | tf_op jit(solution)/shard_map/psum | solution.py:453
  1592.5 287.5 %all-gather.51.cloned.1.call-start = ((), (), s32[]{:S(2)}) async-start(), calls=%async_computation.23 | async-start | bytes 2985984 | tf_op jit(solution)/shard_map/all_gather | solution.py:394
  1595.4 317.0 %all-gather.49.cloned.1.call-start = ((), (), s32[]{:S(2)}) async-start(), calls=%async_computation.22 | async-start | bytes 2985984 | tf_op jit(solution)/shard_map/all_gather | solution.py:394
  (170 other events, 3986.8 us)
Sparse Core Ops, SparseCore 0:
  21.0 49.8 all-reduce.22
  108.9 36.3 all-gather.52
  207.7 52.2 reduce-scatter.12
  261.5 35.4 all-gather.56
  299.5 37.7 all-gather.54
  339.4 35.4 all-gather.58
  385.0 52.7 reduce-scatter.14
  441.3 33.9 all-gather.60
  513.4 48.7 reduce-scatter.16
  564.2 35.4 all-gather.64
  602.2 32.8 all-gather.62
  637.0 35.4 all-gather.66
  680.7 46.9 reduce-scatter.18
  735.2 33.9 all-gather.68
  784.4 48.0 reduce-scatter.20
  840.4 33.9 all-gather.70
  909.2 48.1 reduce-scatter.22
  962.8 38.8 all-gather.46
  1022.7 53.8 reduce-scatter.24
  1084.0 38.8 all-gather.72
  1125.3 33.7 reduce-scatter.30
  1161.5 32.6 reduce-scatter.34
  1197.2 32.6 reduce-scatter.28
  1232.0 32.6 reduce-scatter.32
  1268.1 193.6 all-reduce.20
  1495.7 31.4 all-gather.84
  1531.3 53.8 reduce-scatter.26
  1587.2 31.4 all-gather.78
  1620.6 31.4 all-gather.82
  1686.6 30.4 all-gather.74
  1723.5 123.2 all-reduce.18
  1848.8 31.1 all-gather.50
  (3 shorter events, 90.8 us)

commit v2 on v1

--- a/solution.py
+++ b/solution.py
@@ -1,6 +1,8 @@
 import jax
 import jax.numpy as jnp
 from jax import lax
+from jax.experimental import pallas as pl
+from jax.experimental.pallas import tpu as pltpu
 from jax.sharding import PartitionSpec as P
 
 HEADS = 16
@@ -57,94 +59,673 @@
     return grad_in, jnp.sum(grad, axis=1), jnp.sum(grad * unit, axis=1)
 
 
-def gather_tokens(local):
-    full = lax.all_gather(local, PLANE, axis=1)
-    return full.reshape(local.shape[0], -1, local.shape[-1])
-
-
-def scatter_tokens(partial, length):
-    low = partial.astype(bf16)
-    return lax.psum_scatter(low, PLANE, scatter_dimension=1, tiled=True).astype(f32)
-
-
-def attention_forward(normed, weights, key_mask):
-    project, project_bias, attend = weights
-    full = gather_tokens(normed)
-    images, length, _ = full.shape
-    width = project.shape[1] // 3
-    heads = width // LANES
-    projected = (jnp.einsum("isd,dn->isn", full, project, preferred_element_type=f32) + project_bias).astype(bf16)
-    queries, keys, values = (
-        projected[..., part * width : (part + 1) * width].reshape(images, length, heads, LANES)
-        for part in range(3)
-    )
-    factor = HEAD_SIZE ** (-0.5)
-    scores = jnp.einsum("ishe,iuhe->ihsu", queries, keys, preferred_element_type=f32) * factor
-    if key_mask is not None:
-        scores = jnp.where(key_mask[:, None, None, :], scores, masked_score)
-    peak = jnp.max(scores, axis=-1, keepdims=True)
-    log_total = peak + jnp.log(jnp.sum(jnp.exp(scores - peak), axis=-1, keepdims=True))
-    probs = jnp.exp(scores - log_total).astype(bf16)
-    mixed = jnp.einsum("ihsu,iuhe->ishe", probs, values, preferred_element_type=f32)
-    mixed = mixed.astype(bf16).reshape(images, length, width)
-    partial = jnp.einsum("isn,nd->isd", mixed, attend, preferred_element_type=f32)
-    attended = scatter_tokens(partial, normed.shape[1])
-    return attended, (full, queries, keys, values, mixed, log_total)
-
-
-def attention_backward(grad_attended, weights, key_mask, saved):
-    project, _, attend = weights
-    normed, queries, keys, values, mixed, log_total = saved
-    images, length, heads, _ = queries.shape
-    full = gather_tokens(grad_attended)
-    grad_attend = jnp.einsum("isn,isd->nd", mixed, full, preferred_element_type=f32)
-    grad_attend_bias = jnp.sum(full.astype(f32), axis=(0, 1))
-    grad_mixed = jnp.einsum("isd,nd->isn", full, attend, preferred_element_type=f32).astype(bf16)
-    grad_heads = grad_mixed.reshape(queries.shape)
-    factor = HEAD_SIZE ** (-0.5)
-    scores = jnp.einsum("ishe,iuhe->ihsu", queries, keys, preferred_element_type=f32) * factor
-    if key_mask is not None:
-        scores = jnp.where(key_mask[:, None, None, :], scores, masked_score)
-    probs = jnp.exp(scores - log_total)
-    dprobs = jnp.einsum("ishe,iuhe->ihsu", grad_heads, values, preferred_element_type=f32)
-    row_dot = jnp.sum(probs * dprobs, axis=-1, keepdims=True)
-    grad_scores = (probs * (dprobs - row_dot)).astype(bf16)
-    grad_queries = jnp.einsum("ihsu,iuhe->ishe", grad_scores, keys, preferred_element_type=f32) * factor
-    grad_keys = jnp.einsum("ihsu,ishe->iuhe", grad_scores, queries, preferred_element_type=f32) * factor
-    grad_values = jnp.einsum("ihsu,ishe->iuhe", probs.astype(bf16), grad_heads, preferred_element_type=f32)
-    grad_projected = jnp.concatenate(
-        [part.astype(bf16).reshape(images, length, -1) for part in (grad_queries, grad_keys, grad_values)], axis=-1
-    )
-    grad_project = jnp.einsum("isd,isn->dn", normed, grad_projected, preferred_element_type=f32)
-    grad_project_bias = jnp.sum(grad_projected.astype(f32), axis=(0, 1))
-    partial = jnp.einsum("isn,dn->isd", grad_projected, project, preferred_element_type=f32)
-    grad_normed = scatter_tokens(partial, grad_attended.shape[1])
-    return grad_normed, grad_project, grad_project_bias, grad_attend, grad_attend_bias
-
-
-def mlp_forward(normed, weights):
+def sides():
+    row, col = lax.axis_index("row"), lax.axis_index("col")
+    core = lax.rem(col, 2)
+    across = col // 2
+    chip = row * 2 + across
+    chips = {
+        "own": chip,
+        "x": (1 - row) * 2 + across,
+        "y": row * 2 + 1 - across,
+        "far": (1 - row) * 2 + 1 - across,
+    }
+    address = {
+        "x": {"row": 1 - row},
+        "y": {"col": lax.rem(col + 2, 4)},
+        "core": {"col": col + 1 - 2 * core},
+    }
+    return core, chips, address
+
+
+def greet(address):
+    barrier = pltpu.get_barrier_semaphore()
+    for who in address.values():
+        pl.semaphore_signal(barrier, inc=1, device_id=who, device_id_type=pl.DeviceIdType.MESH)
+    pl.semaphore_wait(barrier, len(address))
+
+
+class Copies:
+    def __init__(self, send, recv, address):
+        self.send, self.recv, self.address = send, recv, address
+        self.started = {}
+
+    def go(self, slot, source, target, who):
+        copy = pltpu.make_async_remote_copy(
+            src_ref=source,
+            dst_ref=target,
+            send_sem=self.send.at[slot],
+            recv_sem=self.recv.at[slot],
+            device_id=self.address[who],
+            device_id_type=pl.DeviceIdType.MESH,
+        )
+        copy.start()
+        self.started[slot] = copy
+
+    def arrived(self, *slots):
+        for slot in slots:
+            self.started[slot].wait_recv()
+
+    def drain(self):
+        for copy in self.started.values():
+            copy.wait_send()
+
+
+class Gather(Copies):
+    def __init__(self, full, send, recv, place):
+        core, chips, address = place
+        super().__init__(send, recv, address)
+        self.full, self.half = full, full.shape[1] // 2
+        self.at = {name: core * 4 + chip for name, chip in chips.items()}
+
+    def whole(self, name):
+        return self.full.at[self.at[name]]
+
+    def part(self, name, second):
+        return self.full.at[self.at[name], pl.ds(self.half * second, self.half)]
+
+    def first(self):
+        own = self.whole("own")
+        self.go(0, own, own, "x")
+        self.go(1, own, own, "y")
+        self.go(2, own, own, "core")
+
+    def second(self):
+        self.arrived(0)
+        self.go(3, self.part("x", 0), self.part("x", 0), "y")
+        self.arrived(1)
+        self.go(4, self.part("y", 1), self.part("y", 1), "x")
+        self.go(5, self.whole("x"), self.whole("x"), "core")
+        self.go(6, self.whole("y"), self.whole("y"), "core")
+
+    def finish(self):
+        self.arrived(3, 4)
+        self.go(7, self.whole("far"), self.whole("far"), "core")
+        self.arrived(2, 5, 6, 7)
+
+
+class Scatter(Copies):
+    def __init__(self, core_out, core_in, total, hop_out, hop_in, send, recv, place):
+        _, self.chips, address = place
+        super().__init__(send, recv, address)
+        self.core_out, self.core_in, self.total = core_out, core_in, total
+        self.hop_out, self.hop_in = hop_out, hop_in
+        self.half = total.shape[1] // 2
+
+    def cross(self):
+        self.go(0, self.core_out, self.core_in, "core")
+
+    def hop(self, slot, value, who):
+        self.hop_out[slot] = value.astype(bf16)
+        self.go(1 + slot, self.hop_out.at[slot], self.hop_in.at[slot], who)
+
+    def first(self):
+        self.arrived(0)
+        half = self.half
+
+        def summed(name):
+            chip = self.chips[name]
+            return self.total[chip] + self.core_in[chip].astype(f32)
+
+        far = summed("far")
+        self.hop(0, far[:half], "x")
+        self.hop(2, far[half:], "y")
+        x_sum = summed("x")
+        self.hop(1, x_sum[:half], "x")
+        self.total[self.chips["x"], half:] = x_sum[half:]
+        y_sum = summed("y")
+        self.hop(3, y_sum[half:], "y")
+        self.total[self.chips["y"], :half] = y_sum[:half]
+
+    def second(self):
+        half = self.half
+        self.arrived(1)
+        self.hop(4, self.total[self.chips["y"], :half] + self.hop_in[0].astype(f32), "y")
+        self.arrived(3)
+        self.hop(5, self.total[self.chips["x"], half:] + self.hop_in[2].astype(f32), "x")
+
+    def finish(self):
+        self.arrived(2, 4, 5, 6)
+        half, own = self.half, self.chips["own"]
+        base = self.total[own] + self.core_in[own].astype(f32)
+        low = base[:half] + self.hop_in[1].astype(f32) + self.hop_in[4].astype(f32)
+        high = base[half:] + self.hop_in[3].astype(f32) + self.hop_in[5].astype(f32)
+        return jnp.concatenate([low, high], axis=0)
+
+
+def comm_scratch(images, length, width):
+    half = length // 2
+    return [
+        pltpu.VMEM((images, 4, length, width), bf16),
+        pltpu.VMEM((images, 4, length, width), bf16),
+        pltpu.VMEM((images, 4, length, width), f32),
+        pltpu.VMEM((images, 6, half, width), bf16),
+        pltpu.VMEM((images, 6, half, width), bf16),
+        pltpu.SemaphoreType.DMA((images, 8)),
+        pltpu.SemaphoreType.DMA((images, 8)),
+        pltpu.SemaphoreType.DMA((images, 7)),
+        pltpu.SemaphoreType.DMA((images, 7)),
+    ]
+
+
+def exchanges(full, comm, place):
+    core_out, core_in, total, hop_out, hop_in, gs, gr, ss, sr = comm
+    images = full.shape[0]
+    gathers = [Gather(full.at[i], gs.at[i], gr.at[i], place) for i in range(images)]
+    scatters = [
+        Scatter(
+            core_out.at[i], core_in.at[i], total.at[i], hop_out.at[i], hop_in.at[i], ss.at[i], sr.at[i], place
+        )
+        for i in range(images)
+    ]
+    return gathers, scatters
+
+
+def flat(value):
+    return value.reshape(value.shape[0] * value.shape[1], value.shape[2])
+
+
+def halves(core):
+    return ((1 - core) * 4, True), (core * 4, False)
+
+
+def keep_partial(partial, scatter, sibling):
+    shape = scatter.total.shape
+    if sibling:
+        scatter.core_out[...] = partial.astype(bf16).reshape(shape)
+        scatter.cross()
+    else:
+        scatter.total[...] = partial.reshape(shape)
+
+
+def column_sum(value):
+    return jnp.sum(value, axis=0, keepdims=True)
+
+
+def row_sums(value):
+    ones = jnp.ones((8, value.shape[0]), bf16)
+    return dot(ones, value, ((1,), (0,)))
+
+
+GELU_ROOT = 0.7978845608028654
+GELU_CUBE = 0.044715
+NN, NT, TN = ((1,), (0,)), ((1,), (1,)), ((0,), (0,))
+
+
+def gelu(hidden):
+    inner = GELU_ROOT * (hidden + GELU_CUBE * (hidden * hidden * hidden))
+    return 0.5 * hidden * (1.0 + jnp.tanh(inner))
+
+
+def gelu_with_slope(hidden):
+    square = hidden * hidden
+    bend = jnp.tanh(GELU_ROOT * hidden * (1.0 + GELU_CUBE * square))
+    rise = 0.5 * (1.0 + bend)
+    slope = rise + 0.5 * hidden * (1.0 - bend * bend) * (GELU_ROOT + 3.0 * GELU_ROOT * GELU_CUBE * square)
+    return hidden * rise, slope
+
+
+def modulate_back_rows(resid, scale_part, grad):
+    unit, rstd = norm_parts(resid)
+    inner = grad * (1.0 + scale_part)
+    grad_in = rstd * (
+        inner
+        - jnp.mean(inner, axis=-1, keepdims=True)
+        - unit * jnp.mean(inner * unit, axis=-1, keepdims=True)
+    )
+    return grad_in, column_sum(grad), column_sum(grad * unit)
+
+
+def call(kernel, name, ident, outs, scratch, flops, *args):
+    vmem = pl.BlockSpec(memory_space=pltpu.VMEM)
+    moved = sum(a.size * a.dtype.itemsize for a in args) + sum(o.size * o.dtype.itemsize for o in outs)
+    return pl.pallas_call(
+        kernel,
+        name=name,
+        out_shape=outs,
+        in_specs=[vmem] * len(args),
+        out_specs=[vmem] * len(outs),
+        scratch_shapes=scratch,
+        compiler_params=pltpu.CompilerParams(
+            collective_id=ident, has_side_effects=True, vmem_limit_bytes=60 * 2**20
+        ),
+        cost_estimate=pl.CostEstimate(flops=flops, bytes_accessed=moved, transcendentals=0),
+    )(*args)
+
+
+def shaped(shape, kind):
+    return jax.ShapeDtypeStruct(shape, kind)
+
+
+def mlp_forward_kernel(
+    mid, gate_rows, vecs, expand, expand_bias, shrink, full, hidden, expanded, after, *comm
+):
+    place = sides()
+    core, chips, address = place
+    images = full.shape[0]
+    gathers, scatters = exchanges(full, comm, place)
+    greet(address)
+    own = core * 4 + chips["own"]
+
+    def begin(i):
+        full[i, own] = modulate(mid[i], vecs[i, 0:1], vecs[i, 1:2]).astype(bf16)
+        gathers[i].first()
+
+    def compute(i, between):
+        for step, (start, sibling) in enumerate(halves(core)):
+            value = dot(flat(full[i, pl.ds(start, 4)]), expand[...], NN) + expand_bias[...]
+            hidden[i, pl.ds(start, 4)] = value.reshape(4, -1, value.shape[1])
+            partial = dot(gelu(value).astype(bf16), shrink[...], NN)
+            keep_partial(partial, scatters[i], sibling)
+            between[step]()
+
+    def end(i):
+        value = scatters[i].finish() + vecs[i, 3:4]
+        expanded[i] = value
+        after[i] = mid[i] + gate_rows[i] * vecs[i, 2:3] * value
+
+    begin(0)
+    gathers[0].second()
+    begin(1)
+    gathers[0].finish()
+    compute(0, (gathers[1].second, scatters[0].first))
+    gathers[1].finish()
+    compute(1, (scatters[0].second, scatters[1].first))
+    end(0)
+    scatters[1].second()
+    end(1)
+    for part in gathers + scatters:
+        part.drain()
+
+
+def mlp_forward(mid, gate_rows, vecs, weights, ident):
     expand, expand_bias, shrink = weights
-    full = gather_tokens(normed)
-    hidden = jnp.einsum("isd,dn->isn", full, expand, preferred_element_type=f32) + expand_bias
-    active = jax.nn.gelu(hidden, approximate=True).astype(bf16)
-    partial = jnp.einsum("isn,nd->isd", active, shrink, preferred_element_type=f32)
-    return scatter_tokens(partial, normed.shape[1]), (full, hidden)
-
-
-def mlp_backward(grad_expanded, weights, saved):
+    images, length, width = mid.shape
+    inner = expand.shape[1]
+    return call(
+        mlp_forward_kernel,
+        "mlp_forward",
+        ident,
+        [
+            shaped((images, 8, length, width), bf16),
+            shaped((images, 8, length, inner), f32),
+            shaped((images, length, width), f32),
+            shaped((images, length, width), f32),
+        ],
+        comm_scratch(images, length, width),
+        4 * images * 8 * length * width * inner * 6,
+        mid,
+        gate_rows,
+        vecs,
+        expand,
+        expand_bias.reshape(1, -1),
+        shrink,
+    )
+
+
+def mlp_backward_kernel(
+    grad_after, mid, expanded, gate_rows, vecs, expand, shrink, normed, hidden,
+    grad_mid, sums, grad_expand, grad_shrink, grad_bias,
+    full, grad_hidden, active, sum_expand, sum_shrink, *comm
+):
+    place = sides()
+    core, chips, address = place
+    gathers, scatters = exchanges(full, comm, place)
+    greet(address)
+    own = core * 4 + chips["own"]
+
+    def begin(i):
+        gated = gate_rows[i] * grad_after[i]
+        low = (gated * vecs[i, 1:2]).astype(bf16)
+        full[i, own] = low
+        gathers[i].first()
+        sums[i, 2:3] = column_sum(gated * expanded[i])
+        sums[i, 3:4] = column_sum(low.astype(f32))
+
+    def compute(i, between):
+        for step, (start, sibling) in enumerate(halves(core)):
+            pull = dot(flat(full[i, pl.ds(start, 4)]), shrink[...], NT)
+            value, slope = gelu_with_slope(flat(hidden[i, pl.ds(start, 4)]))
+            active[i, pl.ds(start, 4)] = value.astype(bf16).reshape(4, -1, value.shape[1])
+            low = (pull * slope).astype(bf16)
+            grad_hidden[i, pl.ds(start, 4)] = low.reshape(4, -1, value.shape[1])
+            keep_partial(dot(low, expand[...], NT), scatters[i], sibling)
+            between[step]()
+
+    def weigh_shrink(i):
+        term = dot(flat(active[i]), flat(full[i]), TN)
+        if i == 0:
+            sum_shrink[...] = term
+        else:
+            grad_shrink[...] = (sum_shrink[...] + term).astype(bf16)
+
+    def weigh_expand(i):
+        low = flat(grad_hidden[i])
+        term = dot(flat(normed[i]), low, TN)
+        if i == 0:
+            sum_expand[...] = term
+            grad_bias[...] = row_sums(low)
+        else:
+            grad_expand[...] = (sum_expand[...] + term).astype(bf16)
+            grad_bias[...] += row_sums(low)
+
+    def end(i):
+        grad, shift_sum, scale_sum = modulate_back_rows(mid[i], vecs[i, 0:1], scatters[i].finish())
+        grad_mid[i] = grad + grad_after[i]
+        sums[i, 0:1] = shift_sum
+        sums[i, 1:2] = scale_sum
+
+    begin(0)
+    gathers[0].second()
+    begin(1)
+    gathers[0].finish()
+    compute(0, (gathers[1].second, scatters[0].first))
+    gathers[1].finish()
+    compute(1, (scatters[0].second, scatters[1].first))
+    weigh_shrink(0)
+    end(0)
+    scatters[1].second()
+    weigh_expand(0)
+    weigh_shrink(1)
+    weigh_expand(1)
+    end(1)
+    for part in gathers + scatters:
+        part.drain()
+
+
+def mlp_backward(grad_after, mid, expanded, gate_rows, vecs, weights, saved, ident):
     expand, _, shrink = weights
     normed, hidden = saved
-    full = gather_tokens(grad_expanded)
-    active, pull = jax.vjp(lambda h: jax.nn.gelu(h, approximate=True), hidden)
-    grad_shrink = jnp.einsum("isn,isd->nd", active.astype(bf16), full, preferred_element_type=f32)
-    grad_shrink_bias = jnp.sum(full.astype(f32), axis=(0, 1))
-    grad_active = jnp.einsum("isd,nd->isn", full, shrink, preferred_element_type=f32)
-    grad_hidden = pull(grad_active)[0].astype(bf16)
-    grad_expand = jnp.einsum("isd,isn->dn", normed, grad_hidden, preferred_element_type=f32)
-    grad_expand_bias = jnp.sum(grad_hidden.astype(f32), axis=(0, 1))
-    partial = jnp.einsum("isn,dn->isd", grad_hidden, expand, preferred_element_type=f32)
-    grad_normed = scatter_tokens(partial, grad_expanded.shape[1])
-    return grad_normed, grad_expand, grad_expand_bias, grad_shrink, grad_shrink_bias
+    images, length, width = mid.shape
+    inner = expand.shape[1]
+    return call(
+        mlp_backward_kernel,
+        "mlp_backward",
+        ident,
+        [
+            shaped((images, length, width), f32),
+            shaped((images, 8, width), f32),
+            shaped((width, inner), bf16),
+            shaped((inner, width), bf16),
+            shaped((8, inner), f32),
+        ],
+        [
+            pltpu.VMEM((images, 8, length, width), bf16),
+            pltpu.VMEM((images, 8, length, inner), bf16),
+            pltpu.VMEM((images, 8, length, inner), bf16),
+            pltpu.VMEM((width, inner), f32),
+            pltpu.VMEM((inner, width), f32),
+        ]
+        + comm_scratch(images, length, width),
+        8 * images * 8 * length * width * inner * 6,
+        grad_after,
+        mid,
+        expanded,
+        gate_rows,
+        vecs,
+        expand,
+        shrink,
+        normed,
+        hidden,
+    )
+
+
+LOG2E = 1.4426950408889634
+
+
+def attention_forward_kernel(
+    base, gate_rows, vecs, project, project_bias, attend, key_bias,
+    full, packed, mixed, log_total, attended, mid, *comm
+):
+    place = sides()
+    core, chips, address = place
+    images, _, length, _ = full.shape
+    gathers, scatters = exchanges(full, comm, place)
+    greet(address)
+    own = core * 4 + chips["own"]
+    span = attend.shape[0]
+    heads = span // LANES
+    tile = 2 * length
+    factor = HEAD_SIZE ** (-0.5) * LOG2E
+
+    def begin(i):
+        full[i, own] = modulate(base[i], vecs[i, 0:1], vecs[i, 1:2]).astype(bf16)
+        gathers[i].first()
+
+    def rows_of(start, count):
+        return pl.ds(pl.multiple_of(start * length, length), count * length)
+
+    def compute(i, between):
+        for start, _ in halves(core):
+            value = dot(flat(full[i, pl.ds(start, 4)]), project[...], NN) + project_bias[...]
+            packed[i, rows_of(start, 4)] = value.astype(bf16)
+        between[0]()
+        for step, (start, sibling) in enumerate(halves(core)):
+
+            def one(t, carry, start=start):
+                rows = pl.ds(pl.multiple_of((start + 2 * t) * length, tile), tile)
+                for h in range(heads):
+                    q, k, v = (
+                        pl.ds(part * span + h * LANES, LANES) for part in range(3)
+                    )
+                    scores = dot(packed[i, rows, q], packed[i, :, k], NT) * factor + key_bias[i]
+                    peak = jnp.max(scores, axis=1, keepdims=True)
+                    probs = jnp.exp2(scores - peak)
+                    total = jnp.sum(probs, axis=1, keepdims=True)
+                    out = dot(probs.astype(bf16), packed[i, :, v], NN) / total
+                    mixed[i, rows, pl.ds(h * LANES, LANES)] = out.astype(bf16)
+                    level = jnp.broadcast_to(peak + jnp.log2(total), (tile, LANES))
+                    log_total[i, h, pl.ds(start // 2 + t, 1)] = level.T[0:1]
+                return carry
+
+            lax.fori_loop(0, 2, one, 0)
+            partial = dot(mixed[i, rows_of(start, 4)], attend[...], NN)
+            keep_partial(partial, scatters[i], sibling)
+            between[1 + step]()
+
+    def end(i):
+        value = scatters[i].finish() + vecs[i, 3:4]
+        attended[i] = value
+        mid[i] = base[i] + gate_rows[i] * vecs[i, 2:3] * value
+
+    def nothing():
+        pass
+
+    begin(0)
+    gathers[0].second()
+    begin(1)
+    gathers[0].finish()
+    compute(0, (gathers[1].second, nothing, scatters[0].first))
+    gathers[1].finish()
+    compute(1, (scatters[0].second, nothing, scatters[1].first))
+    end(0)
+    scatters[1].second()
+    end(1)
+    for part in gathers + scatters:
+        part.drain()
+
+
+def attention_forward(base, gate_rows, vecs, weights, key_bias, ident):
+    project, project_bias, attend = weights
+    images, length, width = base.shape
+    span = attend.shape[0]
+    return call(
+        attention_forward_kernel,
+        "attention_forward",
+        ident,
+        [
+            shaped((images, 8, length, width), bf16),
+            shaped((images, 8 * length, 3 * span), bf16),
+            shaped((images, 8 * length, span), bf16),
+            shaped((images, span // LANES, 4, 2 * length), f32),
+            shaped((images, length, width), f32),
+            shaped((images, length, width), f32),
+        ],
+        comm_scratch(images, length, width),
+        8 * images * 8 * length * width * span * 6,
+        base,
+        gate_rows,
+        vecs,
+        project,
+        project_bias.reshape(1, -1),
+        attend,
+        key_bias,
+    )
+
+
+def attention_backward_kernel(
+    grad_mid, base, attended, gate_rows, vecs, project, attend, key_bias, normed, packed, mixed, log_total,
+    grad_base, sums, grad_project, grad_attend, grad_bias,
+    full, grad_mixed, grad_packed, grad_keys, grad_values, sum_project, sum_attend, *comm
+):
+    place = sides()
+    core, chips, address = place
+    images, _, length, _ = full.shape
+    gathers, scatters = exchanges(full, comm, place)
+    greet(address)
+    own = core * 4 + chips["own"]
+    span = attend.shape[0]
+    heads = span // LANES
+    tile = 2 * length
+    factor = HEAD_SIZE ** (-0.5)
+
+    def begin(i):
+        gated = gate_rows[i] * grad_mid[i]
+        low = (gated * vecs[i, 1:2]).astype(bf16)
+        full[i, own] = low
+        gathers[i].first()
+        sums[i, 2:3] = column_sum(gated * attended[i])
+        sums[i, 3:4] = column_sum(low.astype(f32))
+
+    def rows_of(start, count):
+        return pl.ds(pl.multiple_of(start * length, length), count * length)
+
+    def compute(i, between):
+        grad_mixed[...] = dot(flat(full[i]), attend[...], NT).astype(bf16)
+        between[0]()
+        for h in range(heads):
+            lane = pl.ds(h * LANES, LANES)
+            q, k, v = (pl.ds(part * span + h * LANES, LANES) for part in range(3))
+            keys_turned = packed[i, :, k].T
+
+            def one(t, carry):
+                rows = pl.ds(pl.multiple_of(t * tile, tile), tile)
+                queries, pulls = packed[i, rows, q], grad_mixed[rows, lane]
+                scores = dot(packed[i, :, k], queries, NT) * (factor * LOG2E) + key_bias[i]
+                probs = jnp.exp2(scores - log_total[i, h, pl.ds(t, 1)])
+                dprobs = dot(packed[i, :, v], pulls, NT)
+                row_dot = column_sum(probs * dprobs)
+                grad_scores = (probs * (dprobs - row_dot)).astype(bf16)
+                value_term = dot(probs.astype(bf16), pulls, NN)
+                key_term = dot(grad_scores, queries, NN)
+
+                @pl.when(t == 0)
+                def _():
+                    grad_values[...] = value_term
+                    grad_keys[...] = key_term
+
+                @pl.when(t > 0)
+                def _():
+                    grad_values[...] += value_term
+                    grad_keys[...] += key_term
+
+                query_term = dot(keys_turned, grad_scores, NN) * factor
+                grad_packed[i, rows, q] = query_term.T.astype(bf16)
+                return carry
+
+            lax.fori_loop(0, 4, one, 0)
+            grad_packed[i, :, k] = (grad_keys[...] * factor).astype(bf16)
+            grad_packed[i, :, v] = grad_values[...].astype(bf16)
+            between[1 + h]()
+        for step, (start, sibling) in enumerate(halves(core)):
+            keep_partial(dot(grad_packed[i, rows_of(start, 4)], project[...], NT), scatters[i], sibling)
+
+    def weigh_attend(i):
+        term = dot(mixed[i], flat(full[i]), TN)
+        if i == 0:
+            sum_attend[...] = term
+        else:
+            grad_attend[...] = (sum_attend[...] + term).astype(bf16)
+
+    def weigh_project(i):
+        low = grad_packed[i]
+        term = dot(flat(normed[i]), low, TN)
+        if i == 0:
+            sum_project[...] = term
+            grad_bias[...] = row_sums(low)
+        else:
+            grad_project[...] = (sum_project[...] + term).astype(bf16)
+            grad_bias[...] += row_sums(low)
+
+    def end(i):
+        grad, shift_sum, scale_sum = modulate_back_rows(base[i], vecs[i, 0:1], scatters[i].finish())
+        grad_base[i] = grad + grad_mid[i]
+        sums[i, 0:1] = shift_sum
+        sums[i, 1:2] = scale_sum
+
+    def nothing():
+        pass
+
+    begin(0)
+    gathers[0].second()
+    begin(1)
+    gathers[0].finish()
+    compute(0, (gathers[1].second, nothing, gathers[1].finish))
+    scatters[0].first()
+    compute(1, (scatters[0].second, nothing, nothing))
+    weigh_attend(0)
+    scatters[1].first()
+    weigh_project(0)
+    end(0)
+    scatters[1].second()
+    weigh_attend(1)
+    weigh_project(1)
+    end(1)
+    for part in gathers + scatters:
+        part.drain()
+
+
+def attention_backward(grad_mid, base, attended, gate_rows, vecs, weights, key_bias, saved, ident):
+    project, _, attend = weights
+    normed, packed, mixed, log_total = saved
+    images, length, width = base.shape
+    span = attend.shape[0]
+    tokens = 8 * length
+    return call(
+        attention_backward_kernel,
+        "attention_backward",
+        ident,
+        [
+            shaped((images, length, width), f32),
+            shaped((images, 8, width), f32),
+            shaped((width, 3 * span), bf16),
+            shaped((span, width), bf16),
+            shaped((8, 3 * span), f32),
+        ],
+        [
+            pltpu.VMEM((images, 8, length, width), bf16),
+            pltpu.VMEM((tokens, span), bf16),
+            pltpu.VMEM((images, tokens, 3 * span), bf16),
+            pltpu.VMEM((tokens, LANES), f32),
+            pltpu.VMEM((tokens, LANES), f32),
+            pltpu.VMEM((width, 3 * span), f32),
+            pltpu.VMEM((span, width), f32),
+        ]
+        + comm_scratch(images, length, width),
+        16 * images * 8 * length * width * span * 6,
+        grad_mid,
+        base,
+        attended,
+        gate_rows,
+        vecs,
+        project,
+        attend,
+        key_bias,
+        normed,
+        packed,
+        mixed,
+        log_total,
+    )
 
 
 HEAD_SIZE = 72
@@ -289,7 +870,8 @@
     patches, grad_outputs = own[..., :patch_in], own[..., patch_in:]
     order = jnp.arange(kept_local, dtype=jnp.int32)[:, None] * team + jnp.arange(team, dtype=jnp.int32)
     kept_grid = order[None] < kept_count[:, None, None]
-    key_mask = kept_grid.transpose(0, 2, 1).reshape(images, team * kept_local)
+    chunk_order = kept_grid.reshape(images, kept_local, team // 2, 2).transpose(0, 3, 2, 1)
+    key_bias = jnp.where(chunk_order.reshape(images, team * kept_local), 0.0, masked_score).astype(f32)
     kept_rows = lax.dynamic_index_in_dim(kept_grid, place, axis=2, keepdims=False).astype(f32)[:, :, None]
 
     count = width // 4
@@ -338,18 +920,28 @@
         attention_weights = (project, bias, attend)
         mlp_weights = (expand, slice_of(expand_offset[b].astype(f32), 0, hidden_cols), shrink)
         routed = b > 0
-        mask = key_mask if routed else None
         base = resid[:, :kept_local] if routed else resid
-        gate_rows = kept_rows if routed else 1.0
-        normed = modulate(base, shift1, scale1).astype(bf16)
-        attended, attention_saved = attention_forward(normed, attention_weights, mask)
-        attended = attended + attend_offset[b].astype(f32)
-        mid = base + gate_rows * gate1 * attended
-        normed_mid = modulate(mid, shift2, scale2).astype(bf16)
-        expanded, mlp_saved = mlp_forward(normed_mid, mlp_weights)
-        expanded = expanded + shrink_offset[b].astype(f32)
-        after = mid + gate_rows * gate2 * expanded
-        records.append((base, mid, attended, expanded, attention_weights, mlp_weights, mask, gate_rows, attention_saved, mlp_saved))
+        gate_rows = kept_rows if routed else jnp.ones((images, tile_tokens, 1), f32)
+        keys = key_bias if routed else jnp.zeros((images, sequence), f32)
+
+        def rows_with(parts, bias_row):
+            row = jnp.broadcast_to(bias_row.astype(f32), (images, 1, width))
+            return jnp.concatenate(parts + [row], axis=1)
+
+        *attention_saved, attended, mid = attention_forward(
+            base,
+            gate_rows,
+            rows_with([shift1, scale1, gate1], attend_offset[b]),
+            attention_weights,
+            keys[:, None, :],
+            4 * b,
+        )
+        *mlp_saved, expanded, after = mlp_forward(
+            mid, gate_rows, rows_with([shift2, scale2, gate2], shrink_offset[b]), mlp_weights, 4 * b + 1
+        )
+        records.append(
+            (base, mid, attended, expanded, attention_weights, mlp_weights, keys, gate_rows, attention_saved, mlp_saved)
+        )
         resid = jnp.concatenate([after, resid[:, kept_local:]], axis=1) if routed else after
 
     final_normed = modulate(resid, final_shift, final_scale).astype(bf16)
@@ -363,30 +955,36 @@
     mod_terms = [None] * depth
     block_grads = [None] * depth
     for b in reversed(range(depth)):
-        base, mid, attended, expanded, attention_weights, mlp_weights, mask, gate_rows, attention_saved, mlp_saved = records[b]
+        base, mid, attended, expanded, attention_weights, mlp_weights, keys, gate_rows, attention_saved, mlp_saved = records[b]
         shift1, scale1, gate1, shift2, scale2, gate2 = pieces[b]
         routed = b > 0
         grad_after = grad_resid[:, :kept_local] if routed else grad_resid
-        gated = gate_rows * grad_after
-        grad_gate2 = jnp.sum(gated * expanded, axis=1)
-        grad_expanded = (gated * gate2).astype(bf16)
-        grad_normed_mid, grad_expand, grad_expand_bias, grad_shrink, grad_shrink_bias = mlp_backward(
-            grad_expanded, mlp_weights, mlp_saved
+        grad_mid, mlp_sums, grad_expand, grad_shrink, grad_expand_bias = mlp_backward(
+            grad_after,
+            mid,
+            expanded,
+            gate_rows,
+            jnp.concatenate([scale2, gate2], axis=1),
+            mlp_weights,
+            mlp_saved,
+            4 * b + 2,
         )
-        grad_mid, grad_shift2, grad_scale2 = modulate_back(mid, scale2, grad_normed_mid)
-        grad_mid = grad_mid + grad_after
-        gated = gate_rows * grad_mid
-        grad_gate1 = jnp.sum(gated * attended, axis=1)
-        grad_attended = (gated * gate1).astype(bf16)
-        grad_normed, grad_project, grad_project_bias, grad_attend, grad_attend_bias = attention_backward(
-            grad_attended, attention_weights, mask, attention_saved
+        grad_base, attention_sums, grad_project, grad_attend, grad_project_bias = attention_backward(
+            grad_mid,
+            base,
+            attended,
+            gate_rows,
+            jnp.concatenate([scale1, gate1], axis=1),
+            attention_weights,
+            keys[:, :, None],
+            attention_saved,
+            4 * b + 3,
         )
-        grad_base, grad_shift1, grad_scale1 = modulate_back(base, scale1, grad_normed)
-        grad_base = grad_base + grad_mid
+        grad_expand_bias, grad_project_bias = grad_expand_bias[0], grad_project_bias[0]
+        grad_attend_bias = jnp.sum(attention_sums[:, 3], axis=0)
+        grad_shrink_bias = jnp.sum(mlp_sums[:, 3], axis=0)
         grad_resid = jnp.concatenate([grad_base, grad_resid[:, kept_local:]], axis=1) if routed else grad_base
-        mod_terms[b] = jnp.stack(
-            [grad_shift1, grad_scale1, grad_gate1, grad_shift2, grad_scale2, grad_gate2], axis=1
-        )
+        mod_terms[b] = jnp.concatenate([attention_sums[:, :3], mlp_sums[:, :3]], axis=1)
         grad_project = unpad_heads(grad_project.reshape(width, 3, -1), 2).astype(bf16)
         grad_project = lax.psum_scatter(grad_project, "batch", scatter_dimension=0, tiled=True)
         grad_project = lax.all_gather(grad_project, PLANE, axis=2).reshape(shard, -1)
@@ -458,9 +1056,10 @@
     final_weight_grad = lax.dynamic_slice_in_dim(token_sums[2], rank * shard, shard, axis=0)
     final_bias_grad = token_sums[3]
     stacked = [jnp.stack([block_grads[b][n] for b in range(depth)]) for n in range(8)]
-    bias_sums = lax.psum((stacked[4], stacked[5], stacked[6], stacked[7]), "batch")
-    project_sum = lax.all_gather(bias_sums[0], PLANE, axis=2).reshape(depth, -1)
-    expand_sum = lax.all_gather(bias_sums[2], PLANE, axis=1, tiled=True)
+    project_sum, expand_sum = lax.psum((stacked[4], stacked[6]), "batch")
+    attend_sum, shrink_sum = lax.psum((stacked[5], stacked[7]), ("batch", "row", "col"))
+    project_sum = lax.all_gather(project_sum, PLANE, axis=2).reshape(depth, -1)
+    expand_sum = lax.all_gather(expand_sum, PLANE, axis=1, tiled=True)
 
     def rank_part(full):
         part = full.shape[1] // ranks
@@ -477,11 +1076,11 @@
         stacked[0],
         rank_part(project_sum),
         stacked[1],
-        rank_part(bias_sums[1]),
+        rank_part(attend_sum),
         stacked[2],
         rank_part(expand_sum),
         stacked[3],
-        rank_part(bias_sums[3]),
+        rank_part(shrink_sum),
         final_adaptive_grad,
         final_offset_grad,
         final_weight_grad,

time: 1930 us -> 1430 us (0.74)
  waiting for transfers between devices: 1070 us -> 371 us
  Pallas kernels: 0 us -> 433 us
  matrix products: 252 us -> 35 us
  other arithmetic: 116 us -> 56.8 us
  blocking collectives: 247 us -> 302 us
    pallas_call x0 -> x8, Pallas kernels: none -> 433 us  [call(): pl.pallas_call(kernel, name=name, out_shape=outs, in_specs=[vmem] * len(a...]
    reduce_scatter x10 -> x0, waiting for transfers between devices: 413 us -> none  [the longest x8 378 us: scatter_tokens(): lax.psum_scatter(low, PLANE, scatter_dimension=1, tiled=True).astype(f32)]
    dot_general x36 -> x0, matrix products: 225 us -> none  [the longest x2 19.6 us: mlp_backward(): jnp.einsum('isd,nd->isn', full, shrink, preferred_element_type=f32)]
    all_gather x8 -> x0, waiting for transfers between devices: 180 us -> none  [gather_tokens(): full = lax.all_gather(local, PLANE, axis=1)]
    unnamed x37 -> x26, waiting for transfers between devices: 225 us -> 91.6 us
    reduce_scatter x2, waiting for transfers between devices: 2.84 us -> 67.8 us  [body(): lax.psum_scatter(grad_expand.astype(bf16), 'batch', scatter_dimension=0,...]
    all_gather x2, waiting for transfers between devices: 60.1 us -> 0.02 us  [body(): lax.all_gather(slice_of(shrink_weight[b], 0, hidden_cols), 'batch', axis=...]
    all_gather x2, waiting for transfers between devices: 60 us -> 0.04 us  [body(): lax.all_gather(slice_of(expand_weight[b], 1, hidden_cols), 'batch', axis=...]
  transfers between devices with their start and end apart: 36 -> 22, of which waited for: 27 -> 14; matrix products, arithmetic and copies ran while one was open for 19% -> 17% of each run, Pallas kernels for 0% -> 11%
where the time goes in v2:
time: 1430 us; the launch traced here: 1420 us
  Pallas kernels  433 us (30%)
  waiting for transfers between devices  371 us (26%)
  blocking collectives  302 us (21%)
  local copies, waits for them, and re-layouts  200 us (14%)
  other arithmetic  56.8 us (4%)
  matrix products  35 us (2%)
  between operations  17.1 us (1%)
    pallas_call x8, Pallas kernels, call(): pl.pallas_call(kernel, name=name, out_shape=outs, in_specs=[vmem] * len(a...  433 us
    all_gather x2, blocking collectives, body(): project_full = lax.all_gather(project_own, 'batch', axis=0, tiled=True)  140 us
    unnamed x26, waiting for transfers between devices  91.6 us
    reduce_scatter x2, waiting for transfers between devices, body(): lax.psum_scatter(grad_expand.astype(bf16), 'batch', scatter_dimension=0,...  67.8 us
    all_gather x2, waiting for transfers between devices, body(): lax.all_gather(grad_project, PLANE, axis=2).reshape(shard, -1)  58.5 us
    all_gather x2, waiting for transfers between devices, body(): grad_shrink = lax.all_gather(grad_shrink, PLANE, axis=0, tiled=True)  47.4 us
    all_gather x2, waiting for transfers between devices, body(): grad_expand = lax.all_gather(grad_expand, PLANE, axis=1, tiled=True)  47.4 us
    unnamed x133, local copies, waits for them, and re-layouts  44.6 us
  transfers between devices with their start and end apart: 22, of which 14 were waited for; matrix products, arithmetic and copies ran while one was open for 17% of the time, Pallas kernels for 11%

profile of v2, /device:TPU:0, one launch (start us, length us, event | category | flops | bytes accessed | tf_op | source)
XLA Modules:
  0.0 1418.8 jit_solution(3013896225543569929)
XLA Ops:
  41.2 10.8 all-gather
  70.7 71.5 %all-gather.3 = bf16[1152,3,1,144]{3,1,2,0:T(4,128)(2,1)} all-gather(bf16[288,3,1,144]{3,1,2,0:T(4,128)(2,1)} %copy.144), channel_id=5, replica_groups=mesh['batch'=4,'row'=2,'col'=4] {'batch'}, dimensions={0}, use_global_device_ids=true | all-gather | bytes 1244160 | tf_op jit(solution)/shard_map/all_gather | solution.py:815
  158.0 68.3 %all-gather.6 = bf16[1152,3,1,144]{3,1,2,0:T(4,128)(2,1)} all-gather(bf16[288,3,1,144]{3,1,2,0:T(4,128)(2,1)S(1)} %copy.149), channel_id=8, replica_groups=mesh['batch'=4,'row'=2,'col'=4] {'batch'}, dimensions={0}, use_global_device_ids=true | all-gather | bytes 1244160 | tf_op jit(solution)/shard_map/all_gather | solution.py:815
  243.4 21.4 %all-reduce.7 = f32[8,2016]{1,0:T(8,128)S(1)} all-reduce(f32[8,2016]{1,0:T(8,128)S(1)} %concatenate.69), channel_id=14, replica_groups=mesh['batch'=4,'row'=2,'col'=4] {'batch'}, use_global_device_ids=true, to_apply=%region_0.1.clone | all-reduce | flops 16128 | bytes 129024
  264.8 9.1 all-gather.12
  298.2 56.5 %attention_forward.2 = (bf16[2,8,128,1152]{3,2,1,0:T(8,128)(2,1)}, bf16[2,1024,768]{2,1,0:T(8,128)(2,1)}, bf16[2,1024,256]{2,1,0:T(8,128)(2,1)}, f32[2,2,4,256]{...) custom-call(f32[2,128,1152]{2,1,0:T(8,128)} %fusion.4.base, f32[2,128,1]{2,1,0:T(8,128)} %broadcast_in_dim.22.gate_rows, ...), custom_call_target="tpu_custom_call" | custom-call | flops 28991029248 | bytes 14876672 | tf_op jit(solution)/shard_map/attention_forward/pallas_call | solution.py:282
  357.8 50.7 %mlp_forward.2 = (bf16[2,8,128,1152]{3,2,1,0:T(8,128)(2,1)}, f32[2,8,128,576]{3,2,1,0:T(8,128)}, f32[2,128,1152]{2,1,0:T(8,128)}, f32[2,128,1152]{2,1,0:T(8,128)}) custom-call(f32[2,128,1152]{2,1,0:T(8,128)} %get-tuple-element.59.mid, f32[2,128,1]{2,1,0:T(8,128)} %broadcast_in_dim.22.gate_rows, f32[2,4,1152]{2,1,0:T(4,128)} %pad_maximum_fusion.7.vecs, ...), custom_call_target="tpu_custom_call" | custom-call | flops 32614907904 | bytes 15670528 | tf_op jit(solution)/shard_map/mlp_forward/pallas_call | solution.py:282
  414.4 45.2 %attention_forward.3 = (bf16[2,8,96,1152]{3,2,1,0:T(8,128)(2,1)}, bf16[2,768,768]{2,1,0:T(8,128)(2,1)}, bf16[2,768,256]{2,1,0:T(8,128)(2,1)}, f32[2,2,4,192]{3,2...) custom-call(f32[2,96,1152]{2,1,0:T(8,128)} %slice.315.base, f32[2,96,1]{2,1,0:T(8,128)} %compare_convert_fusion.gate_rows, ...), custom_call_target="tpu_custom_call" | custom-call | flops 21743271936 | bytes 11757312 | tf_op jit(solution)/shard_map/attention_forward/pallas_call | solution.py:282
  459.6 41.3 %mlp_forward.3 = (bf16[2,8,96,1152]{3,2,1,0:T(8,128)(2,1)}, f32[2,8,96,576]{3,2,1,0:T(8,128)}, f32[2,96,1152]{2,1,0:T(8,128)}, f32[2,96,1152]{2,1,0:T(8,128)}) custom-call(f32[2,96,1152]{2,1,0:T(8,128)} %get-tuple-element.61.mid, f32[2,96,1]{2,1,0:T(8,128)} %compare_convert_fusion.gate_rows, f32[2,4,1152]{2,1,0:T(4,128)} %pad_maximum_fusion.9.vecs, ...), custom_call_target="tpu_custom_call" | custom-call | flops 24461180928 | bytes 12426240 | tf_op jit(solution)/shard_map/mlp_forward/pallas_call | solution.py:282
  505.4 42.8 %mlp_backward.2 = (f32[2,96,1152]{2,1,0:T(8,128)}, f32[2,8,1152]{2,1,0:T(8,128)}, bf16[1152,576]{1,0:T(8,128)(2,1)}, bf16[576,1152]{1,0:T(8,128)(2,1)}, f32[8,576]{1,0:T(8,128)}) custom-call(f32[2,96,1152]{2,1,0:T(8,128)} %slice.413.grad_after, f32[2,96,1152]{2,1,0:T(8,128)} %get-tuple-element.61.mid, f32[2,96,1152]{2,1,0:T(8,128)} %get-tuple-element.63.expanded, ...), custom_call_target="tpu_custom_call" | custom-call | flops 48922361856 | bytes 16036608 | tf_op jit(solution)/shard_map/mlp_backward/pallas_call | solution.py:282
  548.2 65.0 %attention_backward.2 = (f32[2,96,1152]{2,1,0:T(8,128)}, f32[2,8,1152]{2,1,0:T(8,128)}, bf16[1152,768]{1,0:T(8,128)(2,1)}, bf16[256,1152]{1,0:T(8,128)(2,1)}, f32[8,768]{1,0:T(8,128)}) custom-call(f32[2,96,1152]{2,1,0:T(8,128)} %get-tuple-element.66.grad_mid, f32[2,96,1152]{2,1,0:T(8,128)} %slice.315.base, f32[2,96,1152]{2,1,0:T(8,128)} %get-tuple-element.67.attended, ...), custom_call_target="tpu_custom_call" | custom-call | flops 43486543872 | bytes 15078144 | tf_op jit(solution)/shard_map/attention_backward/pallas_call | solution.py:282
  617.2 52.3 %mlp_backward.3 = (f32[2,128,1152]{2,1,0:T(8,128)}, f32[2,8,1152]{2,1,0:T(8,128)}, bf16[1152,576]{1,0:T(8,128)(2,1)}, bf16[576,1152]{1,0:T(8,128)(2,1)}, f32[8,576]{1,0:T(8,128)}) custom-call(f32[2,128,1152]{2,1,0:T(8,128)} %pad_maximum_fusion.2.grad_after, f32[2,128,1152]{2,1,0:T(8,128)} %get-tuple-element.59.mid, ...), custom_call_target="tpu_custom_call" | custom-call | flops 65229815808 | bytes 19575808 | tf_op jit(solution)/shard_map/mlp_backward/pallas_call | solution.py:282
  670.6 79.2 %attention_backward.3 = (f32[2,128,1152]{2,1,0:T(8,128)}, f32[2,8,1152]{2,1,0:T(8,128)}, bf16[1152,768]{1,0:T(8,128)(2,1)}, bf16[256,1152]{1,0:T(8,128)(2,1)}, f32[8,768]{1,0:T(8,128)}) custom-call(f32[2,128,1152]{2,1,0:T(8,128)} %get-tuple-element.76.grad_mid, f32[2,128,1152]{2,1,0:T(8,128)} %fusion.4.base, f32[2,128,1152]{2,1,0:T(8,128)} %get-tuple-element.77.attended, ...), custom_call_target="tpu_custom_call" | custom-call | flops 57982058496 | bytes 18492416 | tf_op jit(solution)/shard_map/attention_backward/pallas_call | solution.py:282
  773.2 18.9 %all-reduce.19.cloned.1.call-done = (bf16[144,1152]{1,0:T(8,128)(2,1)}, bf16[144,1152]{1,0:T(8,128)(2,1)}) async-done(((bf16[144,1152]{1,0:T(8,128)(2,1)}, bf16[144,1152]{1,0:T(8,128)(2,1)}), (bf16[144,1152]{1,0:T(8,128)(2,1)}, bf16[144,1152]{1,0:T(8,128)(2,1)})) %all-reduce.19.cloned.1.call-update) | async-done | bytes 663568 | tf_op jit(solution)/shard_map/psum | solution.py:991
  792.7 31.4 %reduce-scatter.21.cloned.1.call-done = bf16[288,432]{1,0:T(8,128)(2,1)} async-done(((bf16[1152,432]{1,0:T(8,128)(2,1)}), bf16[288,432]{1,0:T(8,128)(2,1)}) %reduce-scatter.21.cloned.1.call-update) | async-done | bytes 248848
  826.5 28.6 %reduce-scatter.19.cloned.1.call-done = bf16[288,432]{1,0:T(8,128)(2,1)} async-done(((bf16[1152,432]{1,0:T(8,128)(2,1)}), bf16[288,432]{1,0:T(8,128)(2,1)}) %reduce-scatter.19.cloned.1.call-update) | async-done | bytes 248848
  857.0 33.0 %reduce-scatter.17.cloned.1.call-done = bf16[288,576]{1,0:T(8,128)(2,1)} async-done(((bf16[1152,576]{1,0:T(8,128)(2,1)}), bf16[288,576]{1,0:T(8,128)(2,1)}) %reduce-scatter.17.cloned.1.call-update) | async-done | bytes 331792 | tf_op jit(solution)/shard_map/reduce_scatter | solution.py:994
  890.1 34.8 %reduce-scatter.15.cloned.1.call-done = bf16[288,576]{1,0:T(8,128)(2,1)} async-done(((bf16[1152,576]{1,0:T(8,128)(2,1)}), bf16[288,576]{1,0:T(8,128)(2,1)}) %reduce-scatter.15.cloned.1.call-update) | async-done | bytes 331792 | tf_op jit(solution)/shard_map/reduce_scatter | solution.py:994
  931.0 29.6 %reduce-scatter.25.cloned.1.call-done = bf16[288,576]{1,0:T(8,128)(2,1)} async-done(((bf16[1152,576]{1,0:T(8,128)(2,1)}), bf16[288,576]{1,0:T(8,128)(2,1)}) %reduce-scatter.25.cloned.1.call-update) | async-done | bytes 331792
  965.5 26.9 %psum.93 = bf16[2,16128]{1,0:T(2,128)(2,1)} all-reduce(f32[2,16128]{1,0:T(2,128)S(1)} %pad_maximum_fusion.4), channel_id=1, replica_groups=mesh['batch'=4,'row'=2,'col'=4] {'row','col'}, use_global_device_ids=true, to_apply=%region_9.10 | all-reduce | flops 32256 | bytes 193536 | tf_op jit(solution)/shard_map/psum | solution.py:1012
  992.4 14.7 %all-gather.13 = bf16[4,2,16128]{2,1,0:T(2,128)(2,1)} all-gather(bf16[1,2,16128]{2,1,0:T(2,128)(2,1)} %bitcast.254), channel_id=1, replica_groups=mesh['batch'=4,'row'=2,'col'=4] {'batch'}, dimensions={0}, use_global_device_ids=true | all-gather | bytes 322560 | tf_op jit(solution)/shard_map/all_gather | solution.py:1013
  1027.6 40.7 %all-reduce.8 = (f32[1152]{0:T(1024)S(1)}, f32[2,1152]{1,0:T(2,128)}, f32[2,1152]{1,0:T(2,128)}, f32[32]{0:T(128)}) all-reduce(f32[1152]{0:T(1024)S(1)} %reduce_sum.131, f32[2,1152]{1,0:T(2,128)S(1)} %pad_maximum_fusion.15, f32[2,1152]{1,0:T(2,128)S(1)} %pad_maximum_fusion.16, ...), channel_id=1, replica_groups=mesh['batch'=4,'row'=2,'col'=4] {'batch','row','col'}, use_global_device_ids=true, to_apply=%region_12.13 | all-reduce | flops 5792 | bytes 46336 | tf_op jit(solution)/shard_map/psum | solution.py:1051
  1069.0 11.0 all-reduce.10
  1081.9 10.7 all-gather.9
  1129.1 11.4 pad_maximum_fusion
  1159.4 31.0 %all-gather.32.cloned.1.call-done = bf16[1152,1152]{1,0:T(8,128)(2,1)} async-done(((bf16[144,1152]{1,0:T(8,128)(2,1)}), bf16[1152,1152]{1,0:T(8,128)(2,1)}) %all-gather.32.cloned.1.call-update) | async-done | bytes 2654224 | tf_op jit(solution)/shard_map/all_gather | solution.py:992
  1193.2 29.4 %all-gather.46.cloned.1.call-done = bf16[288,3,1152]{0,2,1:T(8,128)(2,1)} async-done(((bf16[288,3,144]{0,2,1:T(8,128)(2,1)}), bf16[288,3,1152]{0,2,1:T(8,128)(2,1)}) %all-gather.46.cloned.1.call-update) | async-done | bytes 1990672 | tf_op jit(solution)/shard_map/all_gather | solution.py:990
  1225.6 29.2 %all-gather.44.cloned.1.call-done = bf16[288,3,1152]{0,2,1:T(8,128)(2,1)} async-done(((bf16[288,3,144]{0,2,1:T(8,128)(2,1)}), bf16[288,3,1152]{0,2,1:T(8,128)(2,1)}) %all-gather.44.cloned.1.call-update) | async-done | bytes 1990672 | tf_op jit(solution)/shard_map/all_gather | solution.py:990
  1264.3 23.9 %all-gather.50.cloned.1.call-done = bf16[8,576,288]{1,2,0:T(8,128)(2,1)} async-done(((bf16[1,576,288]{1,2,0:T(8,128)(2,1)}), bf16[8,576,288]{1,2,0:T(8,128)(2,1)}) %all-gather.50.cloned.1.call-update) | async-done | bytes 2654224 | tf_op jit(solution)/shard_map/all_gather | solution.py:995
  1298.3 23.5 %all-gather.48.cloned.1.call-done = bf16[8,576,288]{1,2,0:T(8,128)(2,1)} async-done(((bf16[1,576,288]{1,2,0:T(8,128)(2,1)}), bf16[8,576,288]{1,2,0:T(8,128)(2,1)}) %all-gather.48.cloned.1.call-update) | async-done | bytes 2654224 | tf_op jit(solution)/shard_map/all_gather | solution.py:995
  1331.8 23.9 %all-gather.54.cloned.1.call-done = bf16[8,576,288]{1,2,0:T(8,128)(2,1)} async-done(((bf16[1,576,288]{1,2,0:T(8,128)(2,1)}), bf16[8,576,288]{1,2,0:T(8,128)(2,1)}) %all-gather.54.cloned.1.call-update) | async-done | bytes 2654224 | tf_op jit(solution)/shard_map/all_gather | solution.py:997
  1365.9 23.4 %all-gather.52.cloned.1.call-done = bf16[8,576,288]{1,2,0:T(8,128)(2,1)} async-done(((bf16[1,576,288]{1,2,0:T(8,128)(2,1)}), bf16[8,576,288]{1,2,0:T(8,128)(2,1)}) %all-gather.52.cloned.1.call-update) | async-done | bytes 2654224 | tf_op jit(solution)/shard_map/all_gather | solution.py:997
  (445 shorter events, 311.7 us)
Async XLA Ops:
  7.2 235.8 %copy-start = (bf16[288,2304]{1,0:T(8,128)(2,1)S(1)}, bf16[288,2304]{1,0:T(8,128)(2,1)}, u32[]{:S(2)}) copy-start(bf16[288,2304]{1,0:T(8,128)(2,1)} %param.37) | copy-start | bytes 3981316
  7.2 230.1 %all-reduce.21.cloned.1.call-start = ((), (), s32[]{:S(2)}) async-start(), calls=%async_computation.27 | async-start | bytes 1728512
  18.8 336.0 %all-gather.38.cloned.1.call-start = ((), (), s32[]{:S(2)}) async-start(), calls=%async_computation.12 | async-start | bytes 1843200 | tf_op jit(solution)/shard_map/all_gather | solution.py:821
  24.2 333.6 %all-gather.36.cloned.1.call-start = ((), (), s32[]{:S(2)}) async-start(), calls=%async_computation.11 | async-start | bytes 1843200 | tf_op jit(solution)/shard_map/all_gather | solution.py:820
  29.6 382.2 %all-gather.42.cloned.1.call-start = ((), (), s32[]{:S(2)}) async-start(), calls=%async_computation.14 | async-start | bytes 1843200 | tf_op jit(solution)/shard_map/all_gather | solution.py:821
  31.6 428.1 %all-gather.40.cloned.1.call-start = ((), (), s32[]{:S(2)}) async-start(), calls=%async_computation.13 | async-start | bytes 1843200 | tf_op jit(solution)/shard_map/all_gather | solution.py:820
  33.6 758.5 %all-reduce.19.cloned.1.call-start = ((), (), s32[]{:S(2)}) async-start(), calls=%async_computation.26 | async-start | bytes 1327104 | tf_op jit(solution)/shard_map/psum | solution.py:991
  289.4 214.4 %copy-start.28 = (f32[2,1152]{1,0:T(2,128)}, f32[2,1152]{1,0:T(2,128)S(1)}, u32[]{:S(2)}) copy-start(f32[2,1152]{1,0:T(2,128)S(1)} %get-tuple-element.222) | copy-start | bytes 27652
  289.6 213.0 %copy-start.20 = (bf16[1152,32]{1,0:T(8,128)(2,1)}, bf16[1152,32]{1,0:T(8,128)(2,1)S(1)}, u32[]{:S(2)}) copy-start(bf16[1152,32]{1,0:T(8,128)(2,1)S(1)} %reshape_reshape.18) | copy-start | bytes 221188
  409.5 94.4 %copy-start.7 = (f32[2,32,1152]{2,1,0:T(8,128)}, f32[2,32,1152]{2,1,0:T(8,128)S(1)}, u32[]{:S(2)}) copy-start(f32[2,32,1152]{2,1,0:T(8,128)S(1)} %slice.334) | copy-start | bytes 884740
  751.5 72.6 %reduce-scatter.21.cloned.1.call-start = ((), (), s32[]{:S(2)}) async-start(), calls=%async_computation.22 | async-start | bytes 1474560
  757.8 97.3 %reduce-scatter.19.cloned.1.call-start = ((), (), s32[]{:S(2)}) async-start(), calls=%async_computation.21 | async-start | bytes 1474560
  764.0 126.0 %reduce-scatter.17.cloned.1.call-start = ((), (), s32[]{:S(2)}) async-start(), calls=%async_computation.10 | async-start | bytes 1843200 | tf_op jit(solution)/shard_map/reduce_scatter | solution.py:994
  764.8 160.1 %reduce-scatter.15.cloned.1.call-start = ((), (), s32[]{:S(2)}) async-start(), calls=%async_computation.9 | async-start | bytes 1843200 | tf_op jit(solution)/shard_map/reduce_scatter | solution.py:994
  765.4 195.2 %reduce-scatter.25.cloned.1.call-start = ((), (), s32[]{:S(2)}) async-start(), calls=%async_computation.24 | async-start | bytes 1843200
  767.1 336.0 %reduce-scatter.23.cloned.1.call-start = ((), (), s32[]{:S(2)}) async-start(), calls=%async_computation.23 | async-start | bytes 1843200
  769.9 377.5 %all-reduce.17.cloned.1.call-start = ((), (), s32[]{:S(2)}) async-start(), calls=%async_computation.25 | async-start | bytes 442368 | tf_op jit(solution)/shard_map/psum | solution.py:1051
  773.1 151.9 %copy-start.52 = (bf16[32]{0:T(256)(128)(2,1)S(1)}, bf16[32]{0:T(256)(128)(2,1)}, u32[]{:S(2)}) copy-start(bf16[32]{0:T(256)(128)(2,1)} %param.40) | copy-start | bytes 196
  773.1 153.7 %copy-start.41 = (f32[2,1152]{1,0:T(2,128)S(1)}, f32[2,1152]{1,0:T(2,128)}, u32[]{:S(2)}) copy-start(f32[2,1152]{1,0:T(2,128)} %get-tuple-element.156) | copy-start | bytes 27652
  773.1 153.7 %copy-start.40 = (f32[2,1152]{1,0:T(2,128)S(1)}, f32[2,1152]{1,0:T(2,128)}, u32[]{:S(2)}) copy-start(f32[2,1152]{1,0:T(2,128)} %get-tuple-element.159) | copy-start | bytes 27652
  773.1 154.4 %copy-start.35 = (f32[2,8,1152]{2,1,0:T(8,128)S(1)}, f32[2,8,1152]{2,1,0:T(8,128)}, u32[]{:S(2)}) copy-start(f32[2,8,1152]{2,1,0:T(8,128)} %get-tuple-element.86) | copy-start | bytes 221188
  773.1 385.1 %all-gather.34.cloned.1.call-start = ((), (), s32[]{:S(2)}) async-start(), calls=%async_computation.8 | async-start | bytes 2985984 | tf_op jit(solution)/shard_map/all_gather | solution.py:992
  792.1 398.3 %all-gather.32.cloned.1.call-start = ((), (), s32[]{:S(2)}) async-start(), calls=%async_computation.7 | async-start | bytes 2985984 | tf_op jit(solution)/shard_map/all_gather | solution.py:992
  792.7 429.9 %all-gather.46.cloned.1.call-start = ((), (), s32[]{:S(2)}) async-start(), calls=%async_computation.16 | async-start | bytes 2985984 | tf_op jit(solution)/shard_map/all_gather | solution.py:990
  826.1 428.7 %all-gather.44.cloned.1.call-start = ((), (), s32[]{:S(2)}) async-start(), calls=%async_computation.15 | async-start | bytes 2985984 | tf_op jit(solution)/shard_map/all_gather | solution.py:990
  857.0 431.2 %all-gather.50.cloned.1.call-start = ((), (), s32[]{:S(2)}) async-start(), calls=%async_computation.18 | async-start | bytes 3317760 | tf_op jit(solution)/shard_map/all_gather | solution.py:995
  890.0 431.7 %all-gather.48.cloned.1.call-start = ((), (), s32[]{:S(2)}) async-start(), calls=%async_computation.17 | async-start | bytes 3317760 | tf_op jit(solution)/shard_map/all_gather | solution.py:995
  924.9 430.9 %all-gather.54.cloned.1.call-start = ((), (), s32[]{:S(2)}) async-start(), calls=%async_computation.20 | async-start | bytes 3317760 | tf_op jit(solution)/shard_map/all_gather | solution.py:997
  1012.3 67.8 %copy-start.39 = (f32[2,128]{1,0:T(2,128)S(1)}, f32[2,128]{1,0:T(2,128)}, u32[]{:S(2)}) copy-start(f32[2,128]{1,0:T(2,128)} %copy-done.37) | copy-start | bytes 3076
  1012.3 67.8 %copy-start.43 = (f32[2,1152]{1,0:T(2,128)S(1)}, f32[2,1152]{1,0:T(2,128)}, u32[]{:S(2)}) copy-start(f32[2,1152]{1,0:T(2,128)} %get-tuple-element.221) | copy-start | bytes 27652
  1016.7 130.0 %all-to-all-start = ((f32[4,2,288]{2,1,0:T(2,128)}), f32[4,2,288]{2,1,0:T(2,128)S(1)}, u32[]{:S(2)}, u32[]{:S(2)}) async-start(f32[4,2,288]{2,1,0:T(2,128)} %reshape.584), calls=%async_computation | async-start | bytes 24576 | tf_op jit(solution)/shard_map/all_to_all | solution.py:1030
  1020.1 369.3 %all-gather.52.cloned.1.call-start = ((), (), s32[]{:S(2)}) async-start(), calls=%async_computation.19 | async-start | bytes 3317760 | tf_op jit(solution)/shard_map/all_gather | solution.py:997
  (45 other events, 639.0 us)
Sparse Core Ops, SparseCore 0:
  18.9 49.8 all-reduce.20
  70.4 59.0 all-gather.37
  131.1 37.5 all-gather.35
  170.1 57.8 all-gather.41
  229.4 36.3 all-gather.39
  751.7 40.3 all-reduce.18
  795.1 29.0 reduce-scatter.20
  827.2 27.8 reduce-scatter.18
  857.5 32.4 reduce-scatter.16
  892.2 32.6 reduce-scatter.14
  927.9 32.6 reduce-scatter.24
  963.3 32.8 reduce-scatter.22
  1002.7 122.3 all-reduce.16
  1127.0 31.1 all-gather.33
  1160.1 30.2 all-gather.31
  1192.3 30.2 all-gather.45
  1224.5 30.2 all-gather.43
  1256.7 31.4 all-gather.49
  1290.3 31.4 all-gather.47
  1324.2 31.4 all-gather.53
  1357.8 31.4 all-gather.51

commit v3 on v2

--- a/solution.py
+++ b/solution.py
@@ -78,11 +78,255 @@
     return core, chips, address
 
 
-def greet(address):
+def greet(addresses):
     barrier = pltpu.get_barrier_semaphore()
-    for who in address.values():
+    for who in addresses:
         pl.semaphore_signal(barrier, inc=1, device_id=who, device_id_type=pl.DeviceIdType.MESH)
-    pl.semaphore_wait(barrier, len(address))
+    pl.semaphore_wait(barrier, len(addresses))
+
+
+def remote(source, target, send, recv, who):
+    return pltpu.make_async_remote_copy(
+        src_ref=source,
+        dst_ref=target,
+        send_sem=send,
+        recv_sem=recv,
+        device_id=who,
+        device_id_type=pl.DeviceIdType.MESH,
+    )
+
+
+def rank_at(offset):
+    ranks = lax.axis_size("batch")
+    return {"batch": lax.rem(lax.axis_index("batch") + offset + ranks, ranks)}
+
+
+def other_ranks():
+    return [rank_at(offset) for offset in range(1, lax.axis_size("batch"))]
+
+
+def plane_peers():
+    row, col = lax.axis_index("row"), lax.axis_index("col")
+    rows, cols = lax.axis_size("row"), lax.axis_size("col")
+    return [
+        {"row": lax.rem(row + n // cols, rows), "col": lax.rem(col + n % cols, cols)}
+        for n in range(1, rows * cols)
+    ]
+
+
+class Line:
+    reach = 1
+
+    def __init__(self, source):
+        ranks = lax.axis_size("batch")
+        self.ins = [source]
+        self.outs = [jax.ShapeDtypeStruct((ranks,) + source.shape, source.dtype)]
+        self.sems = [(2, ranks - 1), (2, ranks - 1), (1,)]
+
+    def bind(self, ins, outs, sems):
+        (self.source,), (self.target,) = ins, outs
+        self.send, self.recv, self.own = sems
+        self.rank, self.ranks = lax.axis_index("batch"), lax.axis_size("batch")
+        self.steps = self.ranks
+        self.late = 0
+
+    def copy(self, way, r):
+        block = self.rank - r if way == 0 else self.rank + r
+        source = self.source if r == 0 else self.target.at[block]
+        return remote(
+            source, self.target.at[block], self.send.at[way, r], self.recv.at[way, r], rank_at(1 - 2 * way)
+        )
+
+    def holds(self, way, r):
+        return self.rank >= r if way == 0 else self.rank + r < self.ranks
+
+    def sends(self, way, r):
+        edge = self.rank + 1 < self.ranks if way == 0 else self.rank > 0
+        return jnp.logical_and(self.holds(way, r), edge)
+
+    def step(self, r):
+        for way in (0, 1):
+            if r > 0:
+                block = self.rank - r if way == 0 else self.rank + r
+
+                @pl.when(self.holds(way, r))
+                def _(way=way, block=block):
+                    place = self.target.at[block]
+                    remote(place, place, self.send.at[way, r - 1], self.recv.at[way, r - 1], rank_at(1)).wait_recv()
+
+            if r < self.ranks - 1:
+
+                @pl.when(self.sends(way, r))
+                def _(way=way):
+                    self.copy(way, r).start()
+
+        if r == 0:
+            self.stay().start()
+
+    def stay(self):
+        return pltpu.make_async_copy(self.source, self.target.at[self.rank], self.own.at[0])
+
+    def finish(self):
+        for way in (0, 1):
+            for r in range(self.ranks - 1):
+
+                @pl.when(self.sends(way, r))
+                def _(way=way, r=r):
+                    self.copy(way, r).wait_send()
+
+        self.stay().wait()
+
+
+class Chain:
+    reach = 1
+
+    def __init__(self, source, shard):
+        pieces, self.rows, _ = source.shape
+        self.shard = shard
+        self.ins = [source]
+        self.outs = [jax.ShapeDtypeStruct(source.shape, source.dtype)]
+        self.sems = [(pieces, 2), (pieces, 2), (pieces,)]
+
+    def bind(self, ins, outs, sems):
+        (self.source,), (self.target,) = ins, outs
+        self.send, self.recv, self.own = sems
+        self.rank, self.ranks = lax.axis_index("batch"), lax.axis_size("batch")
+        self.steps = self.ranks
+        self.late = 0
+        self.owners = owners_of(self.source.shape[0], self.rows, self.shard)
+
+    def copy(self, j, way, first):
+        source = self.source.at[j] if first else self.target.at[j]
+        return remote(
+            source, self.target.at[j], self.send.at[j, way], self.recv.at[j, way], rank_at(1 - 2 * way)
+        )
+
+    def edge(self, way):
+        return self.rank + 1 < self.ranks if way == 0 else self.rank > 0
+
+    def step(self, r):
+        for j, owner in enumerate(self.owners):
+            for way in (0, 1):
+                away = self.rank - owner if way == 0 else owner - self.rank
+                if r > 0:
+
+                    @pl.when(away == r)
+                    def _(j=j, way=way):
+                        self.copy(j, way, False).wait_recv()
+
+                @pl.when(jnp.logical_and(away == r, self.edge(way)))
+                def _(j=j, way=way):
+                    self.copy(j, way, r == 0).start()
+
+            if r == 0:
+
+                @pl.when(self.rank == owner)
+                def _(j=j):
+                    self.stay(j).start()
+
+    def stay(self, j):
+        return pltpu.make_async_copy(self.source.at[j], self.target.at[j], self.own.at[j])
+
+    def finish(self):
+        for j, owner in enumerate(self.owners):
+            for way in (0, 1):
+                away = self.rank - owner if way == 0 else owner - self.rank
+
+                @pl.when(jnp.logical_and(away >= 0, self.edge(way)))
+                def _(j=j, way=way):
+                    self.copy(j, way, False).wait_send()
+
+            @pl.when(self.rank == owner)
+            def _(j=j):
+                self.stay(j).wait()
+
+
+def team_place():
+    return lax.axis_index("row") * lax.axis_size("col") + lax.axis_index("col")
+
+
+def owners_of(pieces, rows, shard):
+    place = team_place()
+    return [(place * pieces + j) * rows // shard for j in range(pieces)]
+
+
+class Fold:
+    reach = 2
+
+    def __init__(self, source):
+        ranks = lax.axis_size("batch")
+        self.ins = [source]
+        self.outs = [jax.ShapeDtypeStruct((ranks - 1,) + source.shape[1:], source.dtype)]
+        self.sems = [(ranks - 1,), (ranks - 1,)]
+
+    def bind(self, ins, outs, sems):
+        (self.source,), (self.inbox,) = ins, outs
+        self.send, self.recv = sems
+        self.steps = 1
+        self.late = 0
+
+    def copies(self):
+        for n in range(lax.axis_size("batch") - 1):
+            who = rank_at(n + 1)
+            yield remote(
+                self.source.at[who["batch"]], self.inbox.at[n], self.send.at[n], self.recv.at[n], who
+            )
+
+    def step(self, r):
+        for copy in self.copies():
+            copy.start()
+
+    def finish(self):
+        for copy in self.copies():
+            copy.wait()
+
+
+class FoldTo:
+    reach = 2
+
+    def __init__(self, source, shard):
+        pieces, self.rows, width = source.shape
+        others = lax.axis_size("batch") - 1
+        self.shard = shard
+        self.ins = [source]
+        self.outs = [jax.ShapeDtypeStruct((pieces, others, self.rows, width), source.dtype)]
+        self.sems = [(pieces, others), (pieces, others)]
+
+    def bind(self, ins, outs, sems):
+        (self.source,), (self.inbox,) = ins, outs
+        self.send, self.recv = sems
+        self.steps = 1
+        self.late = 0
+        self.rank, self.others = lax.axis_index("batch"), lax.axis_size("batch") - 1
+        self.owners = owners_of(self.source.shape[0], self.rows, self.shard)
+
+    def copy(self, j, n):
+        return remote(
+            self.source.at[j], self.inbox.at[j, n], self.send.at[j, n], self.recv.at[j, n], rank_at(n + 1)
+        )
+
+    def leads(self, j, n):
+        return rank_at(n + 1)["batch"] == self.owners[j]
+
+    def step(self, r):
+        for j in range(len(self.owners)):
+            for n in range(self.others):
+
+                @pl.when(self.leads(j, n))
+                def _(j=j, n=n):
+                    self.copy(j, n).start()
+
+    def finish(self):
+        for j, owner in enumerate(self.owners):
+            for n in range(self.others):
+
+                @pl.when(self.rank == owner)
+                def _(j=j, n=n):
+                    self.copy(j, n).wait_recv()
+
+                @pl.when(self.leads(j, n))
+                def _(j=j, n=n):
+                    self.copy(j, n).wait_send()
 
 
 class Copies:
@@ -91,14 +335,7 @@
         self.started = {}
 
     def go(self, slot, source, target, who):
-        copy = pltpu.make_async_remote_copy(
-            src_ref=source,
-            dst_ref=target,
-            send_sem=self.send.at[slot],
-            recv_sem=self.recv.at[slot],
-            device_id=self.address[who],
-            device_id_type=pl.DeviceIdType.MESH,
-        )
+        copy = remote(source, target, self.send.at[slot], self.recv.at[slot], self.address[who])
         copy.start()
         self.started[slot] = copy
 
@@ -116,6 +353,7 @@
         core, chips, address = place
         super().__init__(send, recv, address)
         self.full, self.half = full, full.shape[1] // 2
+        self.source = None
         self.at = {name: core * 4 + chip for name, chip in chips.items()}
 
     def whole(self, name):
@@ -126,9 +364,10 @@
 
     def first(self):
         own = self.whole("own")
-        self.go(0, own, own, "x")
-        self.go(1, own, own, "y")
-        self.go(2, own, own, "core")
+        source = own if self.source is None else self.source
+        self.go(0, source, own, "x")
+        self.go(1, source, own, "y")
+        self.go(2, source, own, "core")
 
     def second(self):
         self.arrived(0)
@@ -142,6 +381,61 @@
         self.arrived(3, 4)
         self.go(7, self.whole("far"), self.whole("far"), "core")
         self.arrived(2, 5, 6, 7)
+
+
+class PlaneGather:
+    reach = 0
+
+    def __init__(self, source, late=0):
+        self.ins = [source]
+        self.outs = [jax.ShapeDtypeStruct((8,) + source.shape, source.dtype)]
+        self.sems = [(8,), (8,), (1,)]
+        self.late = late
+
+    def bind(self, ins, outs, sems):
+        (self.source,), (self.target,) = ins, outs
+        send, recv, self.own = sems
+        self.gather = Gather(self.target, send, recv, sides())
+        self.gather.source = self.source
+        self.steps = 3
+
+    def stay(self):
+        return pltpu.make_async_copy(self.source, self.gather.whole("own"), self.own.at[0])
+
+    def step(self, r):
+        if r == 0:
+            self.gather.first()
+            self.stay().start()
+        elif r == 1:
+            self.gather.second()
+        else:
+            self.gather.finish()
+
+    def finish(self):
+        self.gather.drain()
+        self.stay().wait()
+
+
+class Background:
+    def __init__(self, tasks):
+        self.tasks = tasks
+        self.now = 0
+
+    def partners(self):
+        reach = max([task.reach for task in self.tasks], default=0)
+        return [[], [rank_at(1), rank_at(-1)], other_ranks()][reach]
+
+    def tick(self):
+        for task in self.tasks:
+            if 0 <= self.now - task.late < task.steps:
+                task.step(self.now - task.late)
+        self.now += 1
+
+    def finish(self):
+        for task in self.tasks:
+            for r in range(max(self.now - task.late, 0), task.steps):
+                task.step(r)
+            task.finish()
 
 
 class Scatter(Copies):
@@ -276,35 +570,263 @@
     return grad_in, column_sum(grad), column_sum(grad * unit)
 
 
-def call(kernel, name, ident, outs, scratch, flops, *args):
-    vmem = pl.BlockSpec(memory_space=pltpu.VMEM)
+def call(kernel, name, ident, outs, scratch, flops, args, tasks=()):
+    vmem, anywhere = pl.BlockSpec(memory_space=pltpu.VMEM), pl.BlockSpec(memory_space=pl.ANY)
     moved = sum(a.size * a.dtype.itemsize for a in args) + sum(o.size * o.dtype.itemsize for o in outs)
-    return pl.pallas_call(
-        kernel,
+    task_ins = [array for task in tasks for array in task.ins]
+    task_outs = [shape for task in tasks for shape in task.outs]
+    task_sems = [pltpu.SemaphoreType.DMA(shape) for task in tasks for shape in task.sems]
+
+    def run(*refs):
+        refs = list(refs)
+
+        def take(count):
+            taken = refs[:count]
+            del refs[:count]
+            return taken
+
+        main_ins, bound_ins = take(len(args)), take(len(task_ins))
+        main_outs, bound_outs = take(len(outs)), take(len(task_outs))
+        main_scratch = take(len(scratch))
+        for task in tasks:
+            ins = [bound_ins.pop(0) for _ in task.ins]
+            results = [bound_outs.pop(0) for _ in task.outs]
+            task.bind(ins, results, take(len(task.sems)))
+        kernel(Background(tasks), *main_ins, *main_outs, *main_scratch)
+
+    results = pl.pallas_call(
+        run,
         name=name,
-        out_shape=outs,
-        in_specs=[vmem] * len(args),
-        out_specs=[vmem] * len(outs),
-        scratch_shapes=scratch,
+        out_shape=list(outs) + task_outs,
+        in_specs=[vmem] * len(args) + [anywhere] * len(task_ins),
+        out_specs=[vmem] * len(outs) + [anywhere] * len(task_outs),
+        scratch_shapes=list(scratch) + task_sems,
         compiler_params=pltpu.CompilerParams(
             collective_id=ident, has_side_effects=True, vmem_limit_bytes=60 * 2**20
         ),
         cost_estimate=pl.CostEstimate(flops=flops, bytes_accessed=moved, transcendentals=0),
-    )(*args)
+    )(*args, *task_ins)
+    return results[: len(outs)], results[len(outs) :]
 
 
 def shaped(shape, kind):
     return jax.ShapeDtypeStruct(shape, kind)
 
 
+def prologue_kernel(background, pack, tiles, packs, every_tile, zs, zr, ps, pr):
+    ranks, peers = other_ranks(), plane_peers()
+    greet(ranks + peers)
+    rank, place = lax.axis_index("batch"), team_place()
+    copies = [
+        remote(pack, packs.at[rank], zs.at[n], zr.at[n], who) for n, who in enumerate(ranks)
+    ] + [remote(tiles, every_tile.at[place], ps.at[n], pr.at[n], who) for n, who in enumerate(peers)]
+    for copy in copies:
+        copy.start()
+    packs[rank] = pack[...]
+    every_tile[place] = tiles[...]
+    for copy in copies:
+        copy.wait()
+
+
+def prologue(pack, tiles, ident):
+    ranks = lax.axis_size("batch")
+    dma = pltpu.SemaphoreType.DMA
+    (packs, every_tile), _ = call(
+        prologue_kernel,
+        "prologue",
+        ident,
+        [shaped((ranks,) + pack.shape, pack.dtype), shaped((8,) + tiles.shape, tiles.dtype)],
+        [dma((ranks - 1,)), dma((ranks - 1,)), dma((7,)), dma((7,))],
+        0,
+        (pack, tiles),
+    )
+    return packs, every_tile
+
+
+def conditioning_kernel(background, parts, mods, inbox, zs, zr, ps, pr):
+    ranks, peers = other_ranks(), plane_peers()
+    greet(ranks + peers)
+    rank, place = lax.axis_index("batch"), team_place()
+    first = [
+        remote(parts.at[who["batch"]], inbox.at[n], zs.at[n], zr.at[n], who) for n, who in enumerate(ranks)
+    ]
+    for copy in first:
+        copy.start()
+    background.tick()
+    total = parts[rank]
+    for n, copy in enumerate(first):
+        copy.wait()
+        total = total + inbox[n]
+    mods[place] = total
+    second = [
+        remote(mods.at[place], mods.at[place], ps.at[n], pr.at[n], who) for n, who in enumerate(peers)
+    ]
+    for copy in second:
+        copy.start()
+    background.tick()
+    for copy in second:
+        copy.wait()
+    background.finish()
+
+
+def conditioning_exchange(parts, ident, tasks):
+    ranks = parts.shape[0]
+    dma = pltpu.SemaphoreType.DMA
+    (mods,), gathered = call(
+        conditioning_kernel,
+        "conditioning",
+        ident,
+        [shaped((8,) + parts.shape[1:], f32)],
+        [
+            pltpu.VMEM((ranks - 1,) + parts.shape[1:], f32),
+            dma((ranks - 1,)),
+            dma((ranks - 1,)),
+            dma((7,)),
+            dma((7,)),
+        ],
+        0,
+        (parts,),
+        tasks,
+    )
+    return mods, gathered
+
+
+def epilogue_kernel(
+    background, mods, sums, biases, tokens, all_mods, all_sums, all_biases, all_tokens,
+    mods_in, sums_in, rank_mods, rank_sums, rank_sums_in, rank_biases_in, ps, pr, zs, zr, qs, qr,
+):
+    ranks, peers = other_ranks(), plane_peers()
+    greet(ranks + peers)
+    rank, place = lax.axis_index("batch"), team_place()
+    cols = lax.axis_size("col")
+    first, extra = [], []
+    for n, who in enumerate(peers):
+        there = who["row"] * cols + who["col"]
+        first.append(remote(mods.at[there], mods_in.at[n], ps.at[0, n], pr.at[0, n], who))
+        first.append(remote(sums.at[there], sums_in.at[n], ps.at[1, n], pr.at[1, n], who))
+        extra.append(remote(tokens, all_tokens.at[place], ps.at[2, n], pr.at[2, n], who))
+    second = [
+        remote(biases, rank_biases_in.at[n], zs.at[0, n], zr.at[0, n], who) for n, who in enumerate(ranks)
+    ]
+    for copy in first + second:
+        copy.start()
+    background.tick()
+    for copy in extra:
+        copy.start()
+    all_tokens[place] = tokens[...]
+    for copy in first:
+        copy.wait()
+    mod_total, sum_total = mods[place], sums[place]
+    for n in range(len(peers)):
+        mod_total = mod_total + mods_in[n]
+        sum_total = sum_total + sums_in[n]
+    rank_mods[rank] = mod_total.astype(bf16)
+    rank_sums[...] = sum_total
+    third = []
+    for n, who in enumerate(ranks):
+        third.append(remote(rank_mods.at[rank], rank_mods.at[rank], zs.at[1, n], zr.at[1, n], who))
+        third.append(remote(rank_sums.at[who["batch"]], rank_sums_in.at[n], zs.at[2, n], zr.at[2, n], who))
+    for copy in third:
+        copy.start()
+    background.tick()
+    bias_total = biases[...]
+    for n, copy in enumerate(second):
+        copy.wait()
+        bias_total = bias_total + rank_biases_in[n]
+    for copy in third:
+        copy.wait()
+    sum_own = rank_sums[rank]
+    for n in range(len(ranks)):
+        sum_own = sum_own + rank_sums_in[n]
+    all_mods[place] = rank_mods[...]
+    all_sums[place] = sum_own
+    all_biases[place] = bias_total
+    last = []
+    for n, who in enumerate(peers):
+        for m, target in enumerate((all_mods, all_sums, all_biases)):
+            last.append(remote(target.at[place], target.at[place], qs.at[m, n], qr.at[m, n], who))
+    for copy in last:
+        copy.start()
+    background.tick()
+    for copy in last + extra:
+        copy.wait()
+    background.finish()
+
+
+def epilogue(mods, sums, biases, tokens, ident, tasks):
+    ranks = lax.axis_size("batch")
+    dma = pltpu.SemaphoreType.DMA
+    return call(
+        epilogue_kernel,
+        "epilogue",
+        ident,
+        [
+            shaped((8, ranks) + mods.shape[1:], bf16),
+            shaped((8,) + sums.shape[2:], f32),
+            shaped((8,) + biases.shape, f32),
+            shaped((8,) + tokens.shape, f32),
+        ],
+        [
+            pltpu.VMEM((7,) + mods.shape[1:], f32),
+            pltpu.VMEM((7,) + sums.shape[1:], f32),
+            pltpu.VMEM((ranks,) + mods.shape[1:], bf16),
+            pltpu.VMEM(sums.shape[1:], f32),
+            pltpu.VMEM((ranks - 1,) + sums.shape[2:], f32),
+            pltpu.VMEM((ranks - 1,) + biases.shape, f32),
+            dma((3, 7)),
+            dma((3, 7)),
+            dma((3, ranks - 1)),
+            dma((3, ranks - 1)),
+            dma((3, 7)),
+            dma((3, 7)),
+        ],
+        0,
+        (mods, sums, biases, tokens),
+        tasks,
+    )
+
+
+def closing_kernel(background, parts, every, zs, zr):
+    ranks = other_ranks()
+    address = sides()[2]
+    greet(ranks + list(address.values()))
+    rank = lax.axis_index("batch")
+    copies = [
+        remote(parts.at[who["batch"]], every.at[rank], zs.at[n], zr.at[n], who) for n, who in enumerate(ranks)
+    ]
+    background.tick()
+    for copy in copies:
+        copy.start()
+    every[rank] = parts[rank]
+    for copy in copies:
+        copy.wait()
+    background.finish()
+
+
+def closing(parts, ident, tasks):
+    ranks = parts.shape[0]
+    dma = pltpu.SemaphoreType.DMA
+    (every,), gathered = call(
+        closing_kernel,
+        "closing",
+        ident,
+        [shaped(parts.shape, f32)],
+        [dma((ranks - 1,)), dma((ranks - 1,))],
+        0,
+        (parts,),
+        tasks,
+    )
+    return every, gathered
+
+
 def mlp_forward_kernel(
-    mid, gate_rows, vecs, expand, expand_bias, shrink, full, hidden, expanded, after, *comm
+    background, mid, gate_rows, vecs, expand, expand_bias, shrink, full, hidden, expanded, after, *comm
 ):
     place = sides()
     core, chips, address = place
     images = full.shape[0]
     gathers, scatters = exchanges(full, comm, place)
-    greet(address)
+    greet(list(address.values()) + background.partners())
     own = core * 4 + chips["own"]
 
     def begin(i):
@@ -315,7 +837,7 @@
         for step, (start, sibling) in enumerate(halves(core)):
             value = dot(flat(full[i, pl.ds(start, 4)]), expand[...], NN) + expand_bias[...]
             hidden[i, pl.ds(start, 4)] = value.reshape(4, -1, value.shape[1])
-            partial = dot(gelu(value).astype(bf16), shrink[...], NN)
+            partial = dot(gelu(value).astype(bf16), shrink[...], NT)
             keep_partial(partial, scatters[i], sibling)
             between[step]()
 
@@ -325,20 +847,24 @@
         after[i] = mid[i] + gate_rows[i] * vecs[i, 2:3] * value
 
     begin(0)
+    background.tick()
     gathers[0].second()
     begin(1)
     gathers[0].finish()
     compute(0, (gathers[1].second, scatters[0].first))
+    background.tick()
     gathers[1].finish()
     compute(1, (scatters[0].second, scatters[1].first))
+    background.tick()
     end(0)
     scatters[1].second()
     end(1)
     for part in gathers + scatters:
         part.drain()
-
-
-def mlp_forward(mid, gate_rows, vecs, weights, ident):
+    background.finish()
+
+
+def mlp_forward(mid, gate_rows, vecs, weights, ident, tasks=()):
     expand, expand_bias, shrink = weights
     images, length, width = mid.shape
     inner = expand.shape[1]
@@ -354,24 +880,27 @@
         ],
         comm_scratch(images, length, width),
         4 * images * 8 * length * width * inner * 6,
-        mid,
-        gate_rows,
-        vecs,
-        expand,
-        expand_bias.reshape(1, -1),
-        shrink,
+        (
+            mid,
+            gate_rows,
+            vecs,
+            expand,
+            expand_bias.reshape(1, -1),
+            shrink,
+        ),
+        tasks,
     )
 
 
 def mlp_backward_kernel(
-    grad_after, mid, expanded, gate_rows, vecs, expand, shrink, normed, hidden,
+    background, grad_after, mid, expanded, gate_rows, vecs, expand, shrink, normed, hidden,
     grad_mid, sums, grad_expand, grad_shrink, grad_bias,
     full, grad_hidden, active, sum_expand, sum_shrink, *comm
 ):
     place = sides()
     core, chips, address = place
     gathers, scatters = exchanges(full, comm, place)
-    greet(address)
+    greet(list(address.values()) + background.partners())
     own = core * 4 + chips["own"]
 
     def begin(i):
@@ -384,7 +913,7 @@
 
     def compute(i, between):
         for step, (start, sibling) in enumerate(halves(core)):
-            pull = dot(flat(full[i, pl.ds(start, 4)]), shrink[...], NT)
+            pull = dot(flat(full[i, pl.ds(start, 4)]), shrink[...], NN)
             value, slope = gelu_with_slope(flat(hidden[i, pl.ds(start, 4)]))
             active[i, pl.ds(start, 4)] = value.astype(bf16).reshape(4, -1, value.shape[1])
             low = (pull * slope).astype(bf16)
@@ -393,7 +922,7 @@
             between[step]()
 
     def weigh_shrink(i):
-        term = dot(flat(active[i]), flat(full[i]), TN)
+        term = dot(flat(full[i]), flat(active[i]), TN)
         if i == 0:
             sum_shrink[...] = term
         else:
@@ -416,6 +945,7 @@
         sums[i, 1:2] = scale_sum
 
     begin(0)
+    background.tick()
     gathers[0].second()
     begin(1)
     gathers[0].finish()
@@ -431,9 +961,10 @@
     end(1)
     for part in gathers + scatters:
         part.drain()
-
-
-def mlp_backward(grad_after, mid, expanded, gate_rows, vecs, weights, saved, ident):
+    background.finish()
+
+
+def mlp_backward(grad_after, mid, expanded, gate_rows, vecs, weights, saved, ident, tasks=()):
     expand, _, shrink = weights
     normed, hidden = saved
     images, length, width = mid.shape
@@ -446,7 +977,7 @@
             shaped((images, length, width), f32),
             shaped((images, 8, width), f32),
             shaped((width, inner), bf16),
-            shaped((inner, width), bf16),
+            shaped((width, inner), bf16),
             shaped((8, inner), f32),
         ],
         [
@@ -454,19 +985,22 @@
             pltpu.VMEM((images, 8, length, inner), bf16),
             pltpu.VMEM((images, 8, length, inner), bf16),
             pltpu.VMEM((width, inner), f32),
-            pltpu.VMEM((inner, width), f32),
+            pltpu.VMEM((width, inner), f32),
         ]
         + comm_scratch(images, length, width),
         8 * images * 8 * length * width * inner * 6,
-        grad_after,
-        mid,
-        expanded,
-        gate_rows,
-        vecs,
-        expand,
-        shrink,
-        normed,
-        hidden,
+        (
+            grad_after,
+            mid,
+            expanded,
+            gate_rows,
+            vecs,
+            expand,
+            shrink,
+            normed,
+            hidden,
+        ),
+        tasks,
     )
 
 
@@ -474,14 +1008,14 @@
 
 
 def attention_forward_kernel(
-    base, gate_rows, vecs, project, project_bias, attend, key_bias,
+    background, base, gate_rows, vecs, project, project_bias, attend, key_bias,
     full, packed, mixed, log_total, attended, mid, *comm
 ):
     place = sides()
     core, chips, address = place
     images, _, length, _ = full.shape
     gathers, scatters = exchanges(full, comm, place)
-    greet(address)
+    greet(list(address.values()) + background.partners())
     own = core * 4 + chips["own"]
     span = attend.shape[0]
     heads = span // LANES
@@ -528,24 +1062,23 @@
         attended[i] = value
         mid[i] = base[i] + gate_rows[i] * vecs[i, 2:3] * value
 
-    def nothing():
-        pass
-
     begin(0)
+    background.tick()
     gathers[0].second()
     begin(1)
     gathers[0].finish()
-    compute(0, (gathers[1].second, nothing, scatters[0].first))
+    compute(0, (gathers[1].second, background.tick, scatters[0].first))
     gathers[1].finish()
-    compute(1, (scatters[0].second, nothing, scatters[1].first))
+    compute(1, (scatters[0].second, background.tick, scatters[1].first))
     end(0)
     scatters[1].second()
     end(1)
     for part in gathers + scatters:
         part.drain()
-
-
-def attention_forward(base, gate_rows, vecs, weights, key_bias, ident):
+    background.finish()
+
+
+def attention_forward(base, gate_rows, vecs, weights, key_bias, ident, tasks=()):
     project, project_bias, attend = weights
     images, length, width = base.shape
     span = attend.shape[0]
@@ -563,18 +1096,21 @@
         ],
         comm_scratch(images, length, width),
         8 * images * 8 * length * width * span * 6,
-        base,
-        gate_rows,
-        vecs,
-        project,
-        project_bias.reshape(1, -1),
-        attend,
-        key_bias,
+        (
+            base,
+            gate_rows,
+            vecs,
+            project,
+            project_bias.reshape(1, -1),
+            attend,
+            key_bias,
+        ),
+        tasks,
     )
 
 
 def attention_backward_kernel(
-    grad_mid, base, attended, gate_rows, vecs, project, attend, key_bias, normed, packed, mixed, log_total,
+    background, grad_mid, base, attended, gate_rows, vecs, project, attend, key_bias, normed, packed, mixed, log_total,
     grad_base, sums, grad_project, grad_attend, grad_bias,
     full, grad_mixed, grad_packed, grad_keys, grad_values, sum_project, sum_attend, *comm
 ):
@@ -582,7 +1118,7 @@
     core, chips, address = place
     images, _, length, _ = full.shape
     gathers, scatters = exchanges(full, comm, place)
-    greet(address)
+    greet(list(address.values()) + background.partners())
     own = core * 4 + chips["own"]
     span = attend.shape[0]
     heads = span // LANES
@@ -667,12 +1203,14 @@
         pass
 
     begin(0)
+    background.tick()
     gathers[0].second()
     begin(1)
     gathers[0].finish()
     compute(0, (gathers[1].second, nothing, gathers[1].finish))
+    background.tick()
     scatters[0].first()
-    compute(1, (scatters[0].second, nothing, nothing))
+    compute(1, (scatters[0].second, background.tick, background.tick))
     weigh_attend(0)
     scatters[1].first()
     weigh_project(0)
@@ -683,9 +1221,10 @@
     end(1)
     for part in gathers + scatters:
         part.drain()
-
-
-def attention_backward(grad_mid, base, attended, gate_rows, vecs, weights, key_bias, saved, ident):
+    background.finish()
+
+
+def attention_backward(grad_mid, base, attended, gate_rows, vecs, weights, key_bias, saved, ident, tasks=()):
     project, _, attend = weights
     normed, packed, mixed, log_total = saved
     images, length, width = base.shape
@@ -713,18 +1252,21 @@
         ]
         + comm_scratch(images, length, width),
         16 * images * 8 * length * width * span * 6,
-        grad_mid,
-        base,
-        attended,
-        gate_rows,
-        vecs,
-        project,
-        attend,
-        key_bias,
-        normed,
-        packed,
-        mixed,
-        log_total,
+        (
+            grad_mid,
+            base,
+            attended,
+            gate_rows,
+            vecs,
+            project,
+            attend,
+            key_bias,
+            normed,
+            packed,
+            mixed,
+            log_total,
+        ),
+        tasks,
     )
 
 
@@ -748,9 +1290,13 @@
     return kept.reshape(shape[:axis] + (heads * HEAD_SIZE,) + shape[axis + 1 :])
 
 
-def gather_small(arrays, dims):
+def pack_flat(arrays, multiple):
     flat = jnp.concatenate([array.reshape(-1) for array in arrays])
-    every = lax.all_gather(flat, "batch", axis=0)
+    return jnp.pad(flat, (0, -flat.size % multiple)).reshape(-1, LANES)
+
+
+def unpack_ranks(packs, arrays, dims):
+    every = packs.reshape(packs.shape[0], -1)
     out = []
     start = 0
     for array, dim in zip(arrays, dims):
@@ -807,27 +1353,40 @@
     def slice_of(array, axis, count):
         return lax.dynamic_slice_in_dim(array, place * count, count, axis=axis)
 
-    blocks = []
-    for b in range(depth):
-        project_own = lax.dynamic_index_in_dim(
-            project_weight[b].reshape(shard, 3, team, head_cols), place, axis=2, keepdims=False
-        )
-        project_full = lax.all_gather(project_own, "batch", axis=0, tiled=True)
-        gap = jnp.zeros((head_cols, width), bf16)
-        padded = jnp.concatenate([gap, attend_weight[b], gap], axis=0)
-        start = jnp.clip(place * head_cols - rank * shard + head_cols, 0, shard + head_cols)
-        attend_full = lax.psum(lax.dynamic_slice_in_dim(padded, start, head_cols, axis=0), "batch")
-        expand_full = lax.all_gather(slice_of(expand_weight[b], 1, hidden_cols), "batch", axis=0, tiled=True)
-        shrink_full = lax.all_gather(slice_of(shrink_weight[b], 0, hidden_cols), "batch", axis=1, tiled=True)
-        blocks.append(
-            (
-                pad_heads(project_full, 2).reshape(width, -1),
-                pad_heads(attend_full, 0),
-                expand_full,
-                shrink_full,
+    piece_rows = min(shard, head_cols)
+    pieces_each = head_cols // piece_rows
+    project_own = lax.dynamic_index_in_dim(
+        project_weight.reshape(depth, shard, 3, team, head_cols), place, axis=3, keepdims=False
+    ).reshape(depth, shard, 3 * head_cols)
+    attend_own = jnp.stack(
+        [
+            lax.dynamic_slice_in_dim(
+                attend_weight, (place * head_cols + j * piece_rows) % shard, piece_rows, axis=1
             )
-        )
-
+            for j in range(pieces_each)
+        ],
+        axis=1,
+    )
+    expand_own = slice_of(expand_weight, 2, hidden_cols)
+    shrink_own = slice_of(shrink_weight, 1, hidden_cols).transpose(0, 2, 1)
+
+    smalls = [
+        patch_weight,
+        patch_bias,
+        adaptive_bias,
+        project_bias,
+        attend_bias,
+        expand_bias,
+        shrink_bias,
+        final_offset,
+        final_weight,
+        conditioning,
+    ]
+    patch_tiles = to_tokens(latents, PATCH)
+    grad_tiles = to_tokens(cotangent, PATCH)
+    patch_in, patch_out = patch_tiles.shape[2], grad_tiles.shape[2]
+    tiles = jnp.concatenate([patch_tiles, grad_tiles], axis=2)
+    packs, every_tile = prologue(pack_flat(smalls, 2048), tiles.reshape(-1, LANES), 8)
     (
         patch_full,
         patch_bias_full,
@@ -839,27 +1398,9 @@
         final_offset_full,
         final_full,
         cond_all,
-    ) = gather_small(
-        [
-            patch_weight,
-            patch_bias,
-            adaptive_bias,
-            project_bias,
-            attend_bias,
-            expand_bias,
-            shrink_bias,
-            final_offset,
-            final_weight,
-            conditioning,
-        ],
-        [1, 0, 1, 1, 1, 1, 1, 0, 0, 0],
-    )
-
-    patch_tiles = to_tokens(latents, PATCH)
-    grad_tiles = to_tokens(cotangent, PATCH)
-    patch_in, patch_out = patch_tiles.shape[2], grad_tiles.shape[2]
-    tiles = lax.all_gather(jnp.concatenate([patch_tiles, grad_tiles], axis=2), PLANE, axis=1)
-    whole = tiles.reshape(images, rows, cols, rows_tile, cols_tile, -1).transpose(0, 1, 3, 2, 4, 5)
+    ) = unpack_ranks(packs, smalls, [1, 0, 1, 1, 1, 1, 1, 0, 0, 0])
+
+    whole = every_tile.reshape((rows, cols, images, rows_tile, cols_tile, -1)).transpose(2, 0, 3, 1, 4, 5)
     whole = whole.reshape(images, sequence, patch_in + patch_out)
     grid_cols = cols * cols_tile
     own_ids = lax.dynamic_index_in_dim(
@@ -899,8 +1440,16 @@
     parts = [
         dot(silu_rows, slice_of(adaptive_weight[b], 1, mod_cols), ((1,), (0,))) for b in range(depth)
     ] + [dot(silu_rows, slice_of(final_adaptive, 1, final_cols), ((1,), (0,)))]
-    mods = lax.psum_scatter(jnp.concatenate(parts, axis=1), "batch", scatter_dimension=0, tiled=True)
-    mods = lax.all_gather(mods, PLANE, axis=1)
+    parts = jnp.concatenate(parts, axis=1).reshape(ranks, images, -1)
+    mods, (project_next, attend_next) = conditioning_exchange(
+        parts, 9, [Line(project_own[0]), Chain(attend_own[0], shard)]
+    )
+    mods = mods.transpose(1, 0, 2)
+
+    def attention_matrices(project_parts, attend_parts):
+        project = pad_heads(project_parts.reshape(width, 3, head_cols), 2).reshape(width, -1)
+        return project, pad_heads(attend_parts.reshape(head_cols, width), 0)
+
     pieces = []
     for b in range(depth):
         block_mod = mods[:, :, b * mod_cols : (b + 1) * mod_cols].reshape(images, -1)
@@ -912,13 +1461,12 @@
 
     records = []
     for b in range(depth):
-        project, attend, expand, shrink = blocks[b]
+        project, attend = attention_matrices(project_next, attend_next)
         shift1, scale1, gate1, shift2, scale2, gate2 = pieces[b]
         bias = project_offset[b].astype(f32).reshape(2, team, head_cols)
         bias = lax.dynamic_index_in_dim(bias, place, axis=1, keepdims=False)
         bias = pad_heads(jnp.stack([bias[0], jnp.zeros_like(bias[0]), bias[1]]), 1).reshape(-1)
         attention_weights = (project, bias, attend)
-        mlp_weights = (expand, slice_of(expand_offset[b].astype(f32), 0, hidden_cols), shrink)
         routed = b > 0
         base = resid[:, :kept_local] if routed else resid
         gate_rows = kept_rows if routed else jnp.ones((images, tile_tokens, 1), f32)
@@ -928,17 +1476,34 @@
             row = jnp.broadcast_to(bias_row.astype(f32), (images, 1, width))
             return jnp.concatenate(parts + [row], axis=1)
 
-        *attention_saved, attended, mid = attention_forward(
+        tasks = [Line(expand_own[b])]
+        if not routed:
+            tasks.append(Line(shrink_own[b]))
+        (*attention_saved, attended, mid), gathered = attention_forward(
             base,
             gate_rows,
             rows_with([shift1, scale1, gate1], attend_offset[b]),
             attention_weights,
             keys[:, None, :],
             4 * b,
+            tasks,
         )
-        *mlp_saved, expanded, after = mlp_forward(
-            mid, gate_rows, rows_with([shift2, scale2, gate2], shrink_offset[b]), mlp_weights, 4 * b + 1
+        expand = gathered[0].reshape(width, hidden_cols)
+        shrink = (shrink_next if routed else gathered[1]).reshape(width, hidden_cols)
+        mlp_weights = (expand, slice_of(expand_offset[b].astype(f32), 0, hidden_cols), shrink)
+        tasks = []
+        if b + 1 < depth:
+            tasks = [Line(project_own[b + 1]), Chain(attend_own[b + 1], shard), Line(shrink_own[b + 1])]
+        (*mlp_saved, expanded, after), gathered = mlp_forward(
+            mid,
+            gate_rows,
+            rows_with([shift2, scale2, gate2], shrink_offset[b]),
+            mlp_weights,
+            4 * b + 1,
+            tasks,
         )
+        if tasks:
+            project_next, attend_next, shrink_next = gathered
         records.append(
             (base, mid, attended, expanded, attention_weights, mlp_weights, keys, gate_rows, attention_saved, mlp_saved)
         )
@@ -953,13 +1518,32 @@
     final_mod_term = jnp.stack([grad_final_shift, grad_final_scale], axis=1)
 
     mod_terms = [None] * depth
-    block_grads = [None] * depth
+    bias_terms = [None] * depth
+    token_terms = [None] * depth
+    spread = [[None, None, None] for _ in range(depth)]
+
+    def folded(source, inbox):
+        own = lax.dynamic_index_in_dim(source, rank, axis=0, keepdims=False)
+        return (own.astype(f32) + jnp.sum(inbox.astype(f32), axis=0)).astype(bf16)
+
+    def fold_mlp(terms, inboxes):
+        return jnp.stack([folded(term, inbox) for term, inbox in zip(terms, inboxes)])
+
+    def fold_attention(terms, inboxes):
+        project_part = folded(terms[0], inboxes[0]).reshape(2, shard // 2, -1)
+        attend_part = terms[1].astype(f32) + jnp.sum(inboxes[1].astype(f32), axis=1)
+        return project_part, attend_part.astype(bf16).reshape(2, head_cols // 2, width)
+
+    attention_terms, waiting = None, []
     for b in reversed(range(depth)):
         base, mid, attended, expanded, attention_weights, mlp_weights, keys, gate_rows, attention_saved, mlp_saved = records[b]
         shift1, scale1, gate1, shift2, scale2, gate2 = pieces[b]
         routed = b > 0
         grad_after = grad_resid[:, :kept_local] if routed else grad_resid
-        grad_mid, mlp_sums, grad_expand, grad_shrink, grad_expand_bias = mlp_backward(
+        tasks = []
+        if attention_terms is not None:
+            tasks = [Fold(attention_terms[0]), FoldTo(attention_terms[1], shard)]
+        (grad_mid, mlp_sums, grad_expand, grad_shrink, grad_expand_bias), inboxes = mlp_backward(
             grad_after,
             mid,
             expanded,
@@ -968,8 +1552,13 @@
             mlp_weights,
             mlp_saved,
             4 * b + 2,
+            tasks,
         )
-        grad_base, attention_sums, grad_project, grad_attend, grad_project_bias = attention_backward(
+        if tasks:
+            waiting += [(b + 1, n, part) for n, part in zip((1, 2), fold_attention(attention_terms, inboxes))]
+        mlp_terms = [term.reshape(ranks, shard, hidden_cols) for term in (grad_expand, grad_shrink)]
+        tasks = [Fold(term) for term in mlp_terms] + [PlaneGather(part, late=1) for _, _, part in waiting]
+        (grad_base, attention_sums, grad_project, grad_attend, grad_project_bias), inboxes = attention_backward(
             grad_mid,
             base,
             attended,
@@ -979,63 +1568,74 @@
             keys[:, :, None],
             attention_saved,
             4 * b + 3,
+            tasks,
         )
-        grad_expand_bias, grad_project_bias = grad_expand_bias[0], grad_project_bias[0]
-        grad_attend_bias = jnp.sum(attention_sums[:, 3], axis=0)
-        grad_shrink_bias = jnp.sum(mlp_sums[:, 3], axis=0)
+        for (block, n, _), every in zip(waiting, inboxes[2:]):
+            spread[block][n] = every
+        waiting = [(b, 0, fold_mlp(mlp_terms, inboxes[:2]))]
+        attention_terms = (
+            unpad_heads(grad_project.reshape(width, 3, -1), 2).reshape(ranks, shard, 3 * head_cols),
+            unpad_heads(grad_attend, 0).reshape(pieces_each, piece_rows, width),
+        )
+        grad_bias = unpad_heads(grad_project_bias[0].reshape(3, -1), 1)
+        bias_terms[b] = jnp.concatenate([grad_bias[0], grad_bias[2], grad_expand_bias[0]])
+        token_terms[b] = jnp.sum(jnp.stack([attention_sums[:, 3], mlp_sums[:, 3]]), axis=1)
         grad_resid = jnp.concatenate([grad_base, grad_resid[:, kept_local:]], axis=1) if routed else grad_base
         mod_terms[b] = jnp.concatenate([attention_sums[:, :3], mlp_sums[:, :3]], axis=1)
-        grad_project = unpad_heads(grad_project.reshape(width, 3, -1), 2).astype(bf16)
-        grad_project = lax.psum_scatter(grad_project, "batch", scatter_dimension=0, tiled=True)
-        grad_project = lax.all_gather(grad_project, PLANE, axis=2).reshape(shard, -1)
-        grad_attend = lax.psum(unpad_heads(grad_attend, 0).astype(bf16), "batch")
-        grad_attend = lax.all_gather(grad_attend, PLANE, axis=0, tiled=True)
-        grad_attend = lax.dynamic_slice_in_dim(grad_attend, rank * shard, shard, axis=0)
-        grad_expand = lax.psum_scatter(grad_expand.astype(bf16), "batch", scatter_dimension=0, tiled=True)
-        grad_expand = lax.all_gather(grad_expand, PLANE, axis=1, tiled=True)
-        grad_shrink = lax.psum_scatter(grad_shrink.astype(bf16), "batch", scatter_dimension=1, tiled=True)
-        grad_shrink = lax.all_gather(grad_shrink, PLANE, axis=0, tiled=True)
-        grad_bias = unpad_heads(grad_project_bias.reshape(3, -1), 1)
-        grad_bias = jnp.stack([grad_bias[0], grad_bias[2]])
-        block_grads[b] = (
-            grad_project.astype(f32),
-            grad_attend.astype(f32),
-            grad_expand.astype(f32),
-            grad_shrink.astype(f32),
-            grad_bias,
-            grad_attend_bias,
-            grad_expand_bias,
-            grad_shrink_bias,
-        )
-
-    mod_all = jnp.concatenate([jnp.stack(mod_terms, axis=1).reshape(images, -1), final_mod_term.reshape(images, -1)], axis=1)
-    mod_low = lax.psum(mod_all, PLANE).astype(bf16)
-    mod_every = lax.all_gather(mod_low, "batch", axis=0, tiled=True)
-    mod_width = adaptive_weight.shape[2]
-    block_mods = [mod_every[:, b * mod_width : (b + 1) * mod_width] for b in range(depth)]
-    final_mods = mod_every[:, depth * mod_width :]
-    adaptive_weight_grad = jnp.stack([dot(silu_rows, m, ((0,), (0,))) for m in block_mods])
-    final_adaptive_grad = dot(silu_rows, final_mods, ((0,), (0,)))
-    mod_sum = jnp.sum(mod_every.astype(f32), axis=0)
-    offset_cols, final_offset_cols = adaptive_bias.shape[1], final_offset.shape[0]
-    adaptive_bias_grad = lax.dynamic_slice_in_dim(
-        mod_sum[: depth * mod_width].reshape(depth, mod_width), rank * offset_cols, offset_cols, axis=1
-    )
-    final_offset_grad = lax.dynamic_slice_in_dim(
-        mod_sum[depth * mod_width :], rank * final_offset_cols, final_offset_cols
-    )
-    grad_silu = dot(final_mods, final_adaptive, ((1,), (1,)))
-    for b in range(depth):
-        grad_silu = grad_silu + dot(block_mods[b], adaptive_weight[b], ((1,), (1,)))
-    grad_silu = lax.all_to_all(grad_silu.reshape(ranks, images, shard), "batch", 0, 0)
-    grad_silu = grad_silu.transpose(1, 0, 2).reshape(images, width)
-    conditioning_grad = jax.vjp(jax.nn.silu, conditioning.astype(f32))[1](grad_silu)[0]
 
     patch_bias_term = jnp.sum(grad_resid, axis=(0, 1))
     grad_embed = grad_resid.astype(bf16)
     patch_term = jnp.einsum("ikc,ikd->cd", patches, grad_embed, preferred_element_type=f32)
     grad_patches = jnp.einsum("ikd,cd->ikc", grad_embed, patch_full, preferred_element_type=f32)
-    ordered = lax.all_gather(jnp.concatenate([outputs, grad_patches], axis=2), PLANE, axis=2)
+
+    mod_slices = [
+        term.reshape(images, team, -1) for term in mod_terms + [final_mod_term]
+    ]
+    mod_slices = jnp.concatenate(mod_slices, axis=2).transpose(1, 0, 2)
+    bias_row = jnp.tile(jnp.pad(final_bias_term, (0, shard - patch_out)), ranks)
+    token_rows = jnp.concatenate(
+        [patch_term, patch_bias_term[None], final_weight_term.T] + token_terms + [bias_row[None]], axis=0
+    )
+    row_count = token_rows.shape[0]
+    token_rows = jnp.pad(token_rows, ((0, -row_count % team), (0, 0)))
+    token_rows = token_rows.reshape(team, -1, ranks, shard).transpose(0, 2, 1, 3)
+    biases = pack_flat(bias_terms, 1024)
+    tokens_out = jnp.concatenate([outputs, grad_patches], axis=2).reshape(-1, LANES)
+    tasks = [Fold(attention_terms[0]), FoldTo(attention_terms[1], shard)]
+    tasks += [PlaneGather(part) for _, _, part in waiting]
+    (all_mods, all_sums, all_biases, all_tokens), inboxes = epilogue(
+        mod_slices, token_rows, biases, tokens_out, 10, tasks
+    )
+    for (block, n, _), every in zip(waiting, inboxes[2:]):
+        spread[block][n] = every
+    last_parts = fold_attention(attention_terms, inboxes[:2])
+
+    mod_every = all_mods.reshape(team, ranks * images, -1).transpose(1, 0, 2)
+    mod_width = adaptive_weight.shape[2]
+    block_mods = [
+        mod_every[:, :, b * mod_cols : (b + 1) * mod_cols].reshape(ranks * images, mod_width) for b in range(depth)
+    ]
+    final_mods = mod_every[:, :, depth * mod_cols :].reshape(ranks * images, -1)
+    grad_silu = dot(final_mods, final_adaptive, NT)
+    for b in range(depth):
+        grad_silu = grad_silu + dot(block_mods[b], adaptive_weight[b], NT)
+    grad_silu, last = closing(
+        grad_silu.reshape(ranks, images, shard), 11, [PlaneGather(part) for part in last_parts]
+    )
+    spread[0][1], spread[0][2] = last
+    grad_silu = grad_silu.transpose(1, 0, 2).reshape(images, width)
+    conditioning_grad = jax.vjp(jax.nn.silu, conditioning.astype(f32))[1](grad_silu)[0]
+    adaptive_weight_grad = jnp.stack([dot(silu_rows, m, TN) for m in block_mods])
+    final_adaptive_grad = dot(silu_rows, final_mods, TN)
+
+    def rank_part(full):
+        part = full.shape[-1] // ranks
+        return lax.dynamic_slice_in_dim(full, rank * part, part, axis=full.ndim - 1)
+
+    adaptive_bias_grad = rank_part(jnp.stack([jnp.sum(m.astype(f32), axis=0) for m in block_mods]))
+    final_offset_grad = rank_part(jnp.sum(final_mods.astype(f32), axis=0))
+
+    ordered = all_tokens.reshape(team, images, tile_tokens, -1).transpose(1, 2, 0, 3)
     ordered = ordered.reshape(images, sequence, patch_out + patch_in)
     tile_rows = lax.axis_index("row") * rows_tile + jnp.arange(rows_tile, dtype=jnp.int32)
     tile_cols = lax.axis_index("col") * cols_tile + jnp.arange(cols_tile, dtype=jnp.int32)
@@ -1045,46 +1645,50 @@
     prediction = to_planes(tile_out[..., :patch_out], PATCH, channels_out, rows_tile, cols_tile)
     latent_grad = to_planes(tile_out[..., patch_out:], PATCH, channels_in, rows_tile, cols_tile)
 
-    def scattered(full, axis, parted):
-        return lax.psum_scatter(full, "batch", scatter_dimension=axis, tiled=True) if parted else full
-
-    token_sums = lax.psum(
-        (patch_term, patch_bias_term, final_weight_term, final_bias_term), ("batch", "row", "col")
-    )
-    patch_weight_grad = lax.dynamic_slice_in_dim(token_sums[0], rank * shard, shard, axis=1)
-    patch_bias_grad = lax.dynamic_slice_in_dim(token_sums[1], rank * shard, shard)
-    final_weight_grad = lax.dynamic_slice_in_dim(token_sums[2], rank * shard, shard, axis=0)
-    final_bias_grad = token_sums[3]
-    stacked = [jnp.stack([block_grads[b][n] for b in range(depth)]) for n in range(8)]
-    project_sum, expand_sum = lax.psum((stacked[4], stacked[6]), "batch")
-    attend_sum, shrink_sum = lax.psum((stacked[5], stacked[7]), ("batch", "row", "col"))
-    project_sum = lax.all_gather(project_sum, PLANE, axis=2).reshape(depth, -1)
-    expand_sum = lax.all_gather(expand_sum, PLANE, axis=1, tiled=True)
-
-    def rank_part(full):
-        part = full.shape[1] // ranks
-        return lax.dynamic_slice_in_dim(full, rank * part, part, axis=1)
+    def in_order(every):
+        split = every.reshape((2, team // 2) + every.shape[1:])
+        return jnp.swapaxes(split, 0, 1).reshape(every.shape)
+
+    project_grads, attend_grads, expand_grads, shrink_grads = [], [], [], []
+    for mlp_every, project_every, attend_every in spread:
+        mlp_every = in_order(mlp_every)
+        expand_grads.append(mlp_every[:, 0].transpose(1, 0, 2).reshape(shard, -1).astype(f32))
+        shrink_grads.append(mlp_every[:, 1].transpose(0, 2, 1).reshape(-1, shard).astype(f32))
+        project_every = in_order(project_every).reshape(team, shard, 3, head_cols)
+        project_grads.append(project_every.transpose(1, 2, 0, 3).reshape(shard, -1).astype(f32))
+        attend_every = in_order(attend_every).reshape(width, width)
+        attend_grads.append(lax.dynamic_slice_in_dim(attend_every, rank * shard, shard, axis=0).astype(f32))
+
+    sums = all_sums.reshape(-1, shard)
+    biases = all_biases.reshape(team, -1)[:, : depth * (2 * head_cols + hidden_cols)]
+    biases = biases.reshape(team, depth, -1).transpose(1, 0, 2)
+    project_bias_grad = jnp.concatenate(
+        [biases[:, :, part * head_cols : (part + 1) * head_cols].reshape(depth, width) for part in range(2)], axis=1
+    )
+    expand_bias_grad = biases[:, :, 2 * head_cols :].reshape(depth, -1)
+    first = patch_in + 1 + patch_out
+    block_sums = sums[first : first + 2 * depth].reshape(depth, 2, shard)
 
     return (
         prediction,
         latent_grad,
         conditioning_grad,
-        patch_weight_grad,
-        patch_bias_grad,
+        sums[:patch_in],
+        sums[patch_in],
         adaptive_weight_grad,
         adaptive_bias_grad,
-        stacked[0],
-        rank_part(project_sum),
-        stacked[1],
-        rank_part(attend_sum),
-        stacked[2],
-        rank_part(expand_sum),
-        stacked[3],
-        rank_part(shrink_sum),
+        jnp.stack(project_grads),
+        rank_part(project_bias_grad),
+        jnp.stack(attend_grads),
+        block_sums[:, 0],
+        jnp.stack(expand_grads),
+        rank_part(expand_bias_grad),
+        jnp.stack(shrink_grads),
+        block_sums[:, 1],
         final_adaptive_grad,
         final_offset_grad,
-        final_weight_grad,
-        final_bias_grad,
+        sums[patch_in + 1 : first].T,
+        sums[first + 2 * depth, :patch_out],
     )
 
 

time: 1430 us -> 975 us (0.68)
  waiting for transfers between devices: 371 us -> 0 us
  blocking collectives: 302 us -> 0 us
  Pallas kernels: 433 us -> 642 us
  local copies, waits for them, and re-layouts: 200 us -> 236 us
    pallas_call x8 -> x12, Pallas kernels: 433 us -> 642 us  [call(): pl.pallas_call(run, name=name, out_shape=list(outs) + task_outs, in_specs...]
    all_gather x8 -> x0, blocking collectives: 202 us -> none  [the longest x2 140 us: body(): project_full = lax.all_gather(project_own, 'batch', axis=0, tiled=True)]
    all_gather x12 -> x0, waiting for transfers between devices: 192 us -> none  [the longest x2 58.5 us: body(): lax.all_gather(grad_project, PLANE, axis=2).reshape(shard, -1)]
    unnamed x26 -> x0, waiting for transfers between devices: 91.6 us -> none
    psum x3 -> x0, blocking collectives: 78.6 us -> none  [the longest x1 40.7 us: body(): lax.psum((patch_term, patch_bias_term, final_weight_term, final_bias_term...]
    reduce_scatter x2 -> x0, waiting for transfers between devices: 67.8 us -> none  [body(): lax.psum_scatter(grad_expand.astype(bf16), 'batch', scatter_dimension=0,...]
    convert_element_type x2 -> x14, local copies, waits for them, and re-layouts: 7.24 us -> 63.9 us  [the longest x6 24.4 us: body(): mlp_every[:, 1].transpose(0, 2, 1).reshape(-1, shard).astype(f32)]
    reshape x19 -> x49, local copies, waits for them, and re-layouts: 8.78 us -> 47.6 us  [the longest x6 30.2 us: in_order(): split = every.reshape((2, team // 2) + every.shape[1:])]
  transfers between devices with their start and end apart: 22 -> 0, of which waited for: 14 -> 0; matrix products, arithmetic and copies ran while one was open for 17% -> 0% of each run, Pallas kernels for 11% -> 0%
where the time goes in v3:
time: 975 us; the launch traced here: 963 us
  Pallas kernels  642 us (66%)
  local copies, waits for them, and re-layouts  236 us (24%)
  other arithmetic  58.1 us (6%)
  matrix products  24.5 us (3%)
    pallas_call x12, Pallas kernels, call(): pl.pallas_call(run, name=name, out_shape=list(outs) + task_outs, in_specs...  642 us
    reshape x6, local copies, waits for them, and re-layouts, in_order(): split = every.reshape((2, team // 2) + every.shape[1:])  30.2 us
    convert_element_type x6, local copies, waits for them, and re-layouts, body(): mlp_every[:, 1].transpose(0, 2, 1).reshape(-1, shard).astype(f32)  24.4 us
    unnamed x138, local copies, waits for them, and re-layouts  24.4 us
    convert_element_type x4, local copies, waits for them, and re-layouts, body(): project_every.transpose(1, 2, 0, 3).reshape(shard, -1).astype(f32)  22.9 us

profile of v3, /device:TPU:0, one launch (start us, length us, event | category | flops | bytes accessed | tf_op | source)
XLA Modules:
  0.0 963.0 jit_solution(11290664127385277419)
XLA Ops:
  13.2 13.1 %prologue.1 = (bf16[4,208,128]{2,1,0:T(8,128)(2,1)}, bf16[8,96,128]{2,1,0:T(8,128)(2,1)}) custom-call(bf16[208,128]{1,0:T(8,128)(2,1)} %pad_bitcast_fusion.refs_0_, bf16[96,128]{1,0:T(8,128)(2,1)} %reshape.753.refs_1_), custom_call_target="tpu_custom_call" | custom-call | bytes 487424 | tf_op jit(solution)/shard_map/prologue/pallas_call | solution.py:597
  33.3 5.7 fusion.76
  42.8 6.5 copy.180
  52.5 29.1 %conditioning.1 = (f32[8,2,2016]{2,1,0:T(2,128)}, bf16[4,288,432]{2,1,0:T(8,128)(2,1)}, bf16[1,144,1152]{2,1,0:T(8,128)(2,1)}) custom-call(f32[4,2,2016]{2,1,0:T(2,128)} %reshape.759.refs_0_, bf16[288,432]{1,0:T(8,128)(2,1)} %copy.181.refs_1_, bf16[1,144,1152]{2,1,0:T(8,128)(2,1)} %get-tuple-element.250.refs_2_), custom_call_target="tpu_custom_call" | custom-call | bytes 193536 | tf_op jit(solution)/shard_map/conditioning/pallas_call | solution.py:597
  103.8 69.4 %attention_forward.2 = (bf16[2,8,128,1152]{3,2,1,0:T(8,128)(2,1)}, bf16[2,1024,768]{2,1,0:T(8,128)(2,1)}, bf16[2,1024,256]{2,1,0:T(8,128)(2,1)}, f32[2,2,4,256]{...) custom-call(f32[2,128,1152]{2,1,0:T(8,128)} %fusion.4.refs_0_.refs_1, ...), custom_call_target="tpu_custom_call" | custom-call | flops 28991029248 | bytes 14876672 | tf_op jit(solution)/shard_map/attention_forward/pallas_call | solution.py:597
  174.9 60.2 %mlp_forward.2 = (bf16[2,8,128,1152]{3,2,1,0:T(8,128)(2,1)}, f32[2,8,128,576]{3,2,1,0:T(8,128)}, f32[2,128,1152]{2,1,0:T(8,128)}, f32[2,128,1152]{2,1,0:T(8,128)...) custom-call(f32[2,128,1152]{2,1,0:T(8,128)} %get-tuple-element.94.refs_0_.refs_1_, ...), custom_call_target="tpu_custom_call" | custom-call | flops 32614907904 | bytes 15670528 | tf_op jit(solution)/shard_map/mlp_forward/pallas_call | solution.py:597
  252.0 52.6 %attention_forward.3 = (bf16[2,8,96,1152]{3,2,1,0:T(8,128)(2,1)}, bf16[2,768,768]{2,1,0:T(8,128)(2,1)}, bf16[2,768,256]{2,1,0:T(8,128)(2,1)}, f32[2,2,4,192]{3,2...) custom-call(f32[2,96,1152]{2,1,0:T(8,128)} %slice.353.refs_0_.refs_1_, ...), custom_call_target="tpu_custom_call" | custom-call | flops 21743271936 | bytes 11757312 | tf_op jit(solution)/shard_map/attention_forward/pallas_call | solution.py:597
  305.3 41.3 %mlp_forward.3 = (bf16[2,8,96,1152]{3,2,1,0:T(8,128)(2,1)}, f32[2,8,96,576]{3,2,1,0:T(8,128)}, f32[2,96,1152]{2,1,0:T(8,128)}, f32[2,96,1152]{2,1,0:T(8,128)}) custom-call(f32[2,96,1152]{2,1,0:T(8,128)} %get-tuple-element.100.refs_0_.refs_1_, f32[2,96,1]{2,1,0:T(8,128)} %compare_convert_fusion.refs_1_.refs_3_, f32[2,4,1152]{2,1,0:T(4,128)} %get-tuple-element.298.refs_2_, ...), custom_call_target="tpu_custom_call" | custom-call | flops 24461180928 | bytes 12426240 | tf_op jit(solution)/shard_map/mlp_forward/pallas_call | solution.py:597
  355.5 43.3 %mlp_backward.2 = (f32[2,96,1152]{2,1,0:T(8,128)}, f32[2,8,1152]{2,1,0:T(8,128)}, bf16[1152,576]{1,0:T(8,128)(2,1)}, bf16[1152,576]{1,0:T(8,128)(2,1)}, f32[8,576]{1,0:T(8,128)}) custom-call(f32[2,96,1152]{2,1,0:T(8,128)} %slice.458.refs_0_, f32[2,96,1152]{2,1,0:T(8,128)} %get-tuple-element.100.refs_0_.refs_1_, f32[2,96,1152]{2,1,0:T(8,128)} %get-tuple-element.104.refs_2_, ...), custom_call_target="tpu_custom_call" | custom-call | flops 48922361856 | bytes 16036608 | tf_op jit(solution)/shard_map/mlp_backward/pallas_call | solution.py:597
  399.9 67.0 %attention_backward.2 = (f32[2,96,1152]{2,1,0:T(8,128)}, f32[2,8,1152]{2,1,0:T(8,128)}, bf16[1152,768]{1,0:T(8,128)(2,1)}, bf16[256,1152]{1,0:T(8,128)(2,1)}, f3...) custom-call(f32[2,96,1152]{2,1,0:T(8,128)} %get-tuple-element.107.refs_0_, ...), custom_call_target="tpu_custom_call" | custom-call | flops 43486543872 | bytes 15078144 | tf_op jit(solution)/shard_map/attention_backward/pallas_call | solution.py:597
  480.3 59.1 %mlp_backward.3 = (f32[2,128,1152]{2,1,0:T(8,128)}, f32[2,8,1152]{2,1,0:T(8,128)}, bf16[1152,576]{1,0:T(8,128)(2,1)}, bf16[1152,576]{1,0:T(8,128)(2,1)}, f32[8,5...) custom-call(f32[2,128,1152]{2,1,0:T(8,128)} %pad_maximum_fusion.2.refs_0_, ...), custom_call_target="tpu_custom_call" | custom-call | flops 65229815808 | bytes 19575808 | tf_op jit(solution)/shard_map/mlp_backward/pallas_call | solution.py:597
  549.4 120.0 %attention_backward.3 = (f32[2,128,1152]{2,1,0:T(8,128)}, f32[2,8,1152]{2,1,0:T(8,128)}, bf16[1152,768]{1,0:T(8,128)(2,1)}, bf16[256,1152]{1,0:T(8,128)(2,1)}, f...) custom-call(f32[2,128,1152]{2,1,0:T(8,128)} %get-tuple-element.121.r, ...), custom_call_target="tpu_custom_call" | custom-call | flops 57982058496 | bytes 18492416 | tf_op jit(solution)/shard_map/attention_backward/pallas_call | solution.py:597
  680.6 5.0 concatenate.86
  712.6 52.8 %epilogue.1 = (bf16[8,4,2,2016]{3,2,1,0:T(2,128)(2,1)}, f32[8,7,288]{2,1,0:T(8,128)}, f32[8,16,128]{2,1,0:T(8,128)}, f32[8,96,128]{2,1,0:T(8,128)}, bf16[3,288,4...) custom-call(f32[8,2,2016]{2,1,0:T(2,128)} %bitcast.338, ...), custom_call_target="tpu_custom_call" | custom-call | bytes 1225728 | tf_op jit(solution)/shard_map/epilogue/pallas_call | solution.py:597
  772.3 3.2 fusion
  783.3 33.7 %closing.1 = (f32[4,2,288]{2,1,0:T(2,128)}, bf16[8,2,144,432]{3,2,1,0:T(8,128)(2,1)}, bf16[8,2,72,1152]{3,2,1,0:T(8,128)(2,1)}) custom-call(f32[4,2,288]{2,1,0:T(2,128)} %reshape.799.refs_0_, bf16[2,144,432]{2,1,0:T(8,128)(2,1)} %fusion.14.refs_1_, bf16[2,72,1152]{2,1,0:T(8,128)(2,1)} %add_convert_fusion.1.refs_2_), custom_call_target="tpu_custom_call" | custom-call | bytes 18432 | tf_op jit(solution)/shard_map/closing/pallas_call | solution.py:597
  822.1 6.0 pad_maximum_fusion
  829.2 10.8 %copy.211 = bf16[2,4,2,144,432]{3,2,4,0,1:T(2,128)(2,1)} copy(bf16[2,4,2,144,432]{4,3,2,1,0:T(8,128)(2,1)} %bitcast.309) | data formatting | bytes 3981312 | tf_op jit(solution)/shard_map/reshape | solution.py:1649
  840.0 8.7 convert_element_type.433
  848.7 3.5 copy.212
  852.2 10.8 %copy.209 = bf16[2,4,2,144,432]{3,2,4,0,1:T(2,128)(2,1)} copy(bf16[2,4,2,144,432]{4,3,2,1,0:T(8,128)(2,1)} %bitcast.310) | data formatting | bytes 3981312 | tf_op jit(solution)/shard_map/reshape | solution.py:1649
  863.0 8.5 convert_element_type.429
  874.0 5.2 maximum_convert_fusion
  879.2 9.5 copy.226
  902.9 5.8 convert_element_type.441
  916.7 5.6 convert_element_type.438
  922.3 7.4 maximum_convert_fusion.1
  930.4 4.5 copy.222
  934.9 5.6 convert_element_type.447
  940.5 4.4 copy.221
  944.9 5.6 convert_element_type.444
  950.5 7.4 maximum_convert_fusion.2
  (425 shorter events, 188.6 us)
Async XLA Ops:
  0.7 41.1 %copy-start = (bf16[288,2304]{1,0:T(8,128)(2,1)S(1)}, bf16[288,2304]{1,0:T(8,128)(2,1)}, u32[]{:S(2)}) copy-start(bf16[288,2304]{1,0:T(8,128)(2,1)} %param.37) | copy-start | bytes 3981316
  0.7 10.2 %copy-start.42 = (bf16[2,4,32,16]{2,3,1,0:T(8,128)(2,1)S(1)}, bf16[2,4,32,16]{2,3,1,0:T(8,128)(2,1)}, u32[]{:S(2)}) copy-start(bf16[2,4,32,16]{2,3,1,0:T(8,128)(2,1)} %param.21) | copy-start | bytes 24580
  10.3 17.5 %copy-start.40 = (s32[2,1024]{1,0:T(2,128)S(1)}, s32[2,1024]{1,0:T(2,128)}, u32[]{:S(2)}) copy-start(s32[2,1024]{1,0:T(2,128)} %param.23) | copy-start | bytes 24580
  27.3 5.8 copy-start.14
  27.6 3.7 copy-start.19
  31.4 7.6 copy-start.35
  33.3 8.4 copy-start.21
  235.3 3.4 copy-start.55
  236.3 114.9 %copy-start.6 = (f32[2,32,1152]{2,1,0:T(8,128)}, f32[2,32,1152]{2,1,0:T(8,128)S(1)}, u32[]{:S(2)}) copy-start(f32[2,32,1152]{2,1,0:T(8,128)S(1)} %slice.369) | copy-start | bytes 884740
  236.3 3.5 copy-start.45
  246.4 4.7 copy-start.61
  246.5 4.9 copy-start.56
  346.6 4.6 copy-start.36
  348.0 4.4 copy-start.48
  348.3 4.1 copy-start.57
  353.8 45.1 %copy-start.5 = (f32[2,128,1152]{2,1,0:T(8,128)}, f32[2,128,1152]{2,1,0:T(8,128)S(1)}, u32[]{:S(2)}) copy-start(f32[2,128,1152]{2,1,0:T(8,128)S(1)} %subtract_multiply_fusion) | copy-start | bytes 3538948
  399.9 67.1 %slice-start = ((f32[2,128,1152]{2,1,0:T(8,128)}), f32[2,32,1152]{2,1,0:T(8,128)S(1)}, s32[]{:S(2)}) async-start(f32[2,128,1152]{2,1,0:T(8,128)} %copy-done.5), calls=%async_computation | async-start | bytes 589824 | tf_op jit(solution)/shard_map/slice | solution.py:1583
  549.4 121.1 %copy-start.43 = (f32[2,8,1152]{2,1,0:T(8,128)S(1)}, f32[2,8,1152]{2,1,0:T(8,128)}, u32[]{:S(2)}) copy-start(f32[2,8,1152]{2,1,0:T(8,128)} %get-tuple-element.136) | copy-start | bytes 221188
  549.4 121.2 %copy-start.44 = (f32[2,8,1152]{2,1,0:T(8,128)S(1)}, f32[2,8,1152]{2,1,0:T(8,128)}, u32[]{:S(2)}) copy-start(f32[2,8,1152]{2,1,0:T(8,128)} %get-tuple-element.135) | copy-start | bytes 221188
  549.4 121.4 %copy-start.52 = (f32[2,1152]{1,0:T(2,128)S(1)}, f32[2,1152]{1,0:T(2,128)}, u32[]{:S(2)}) copy-start(f32[2,1152]{1,0:T(2,128)} %get-tuple-element.216) | copy-start | bytes 27652
  549.4 121.4 %copy-start.51 = (f32[2,1152]{1,0:T(2,128)S(1)}, f32[2,1152]{1,0:T(2,128)}, u32[]{:S(2)}) copy-start(f32[2,1152]{1,0:T(2,128)} %get-tuple-element.219) | copy-start | bytes 27652
  675.6 19.5 %copy-start.20 = (bf16[16,1152,1]{1,0,2:T(8,128)(2,1)S(1)}, bf16[16,1152,1]{1,0,2:T(8,128)(2,1)}, u32[]{:S(2)}) copy-start(bf16[16,1152,1]{1,0,2:T(8,128)(2,1)} %copy-done.19) | copy-start | bytes 110596
  685.7 9.7 %copy-start.62 = (bf16[32]{0:T(256)(128)(2,1)S(1)}, bf16[32]{0:T(256)(128)(2,1)}, u32[]{:S(2)}) copy-start(bf16[32]{0:T(256)(128)(2,1)} %param.40) | copy-start | bytes 196
  685.7 9.7 %copy-start.50 = (f32[2,128]{1,0:T(2,128)S(1)}, f32[2,128]{1,0:T(2,128)}, u32[]{:S(2)}) copy-start(f32[2,128]{1,0:T(2,128)} %copy-done.48) | copy-start | bytes 3076
  685.7 9.7 %copy-start.54 = (f32[2,1152]{1,0:T(2,128)S(1)}, f32[2,1152]{1,0:T(2,128)}, u32[]{:S(2)}) copy-start(f32[2,1152]{1,0:T(2,128)} %get-tuple-element.301) | copy-start | bytes 27652
  685.7 9.7 %copy-start.59 = (f32[2,128]{1,0:T(2,128)S(1)}, f32[2,128]{1,0:T(2,128)}, u32[]{:S(2)}) copy-start(f32[2,128]{1,0:T(2,128)} %copy-done.57) | copy-start | bytes 3076
  712.6 54.4 %copy-start.41 = (s32[2,1024]{1,0:T(2,128)S(1)}, s32[2,1024]{1,0:T(2,128)}, u32[]{:S(2)}) copy-start(s32[2,1024]{1,0:T(2,128)} %param.23) | copy-start | bytes 24580
  768.8 3.2 copy-start.24
  782.3 35.5 %copy-start.46 = (bf16[2,1152]{1,0:T(2,128)(2,1)S(1)}, bf16[2,1152]{1,0:T(2,128)(2,1)}, u32[]{:S(2)}) copy-start(bf16[2,1152]{1,0:T(2,128)(2,1)} %param.22) | copy-start | bytes 13828
  782.3 36.1 %copy-start.25 = (f32[8,7,288]{2,1,0:T(8,128)S(1)}, f32[8,7,288]{2,1,0:T(8,128)}, u32[]{:S(2)}) copy-start(f32[8,7,288]{2,1,0:T(8,128)} %get-tuple-element.151) | copy-start | bytes 193540
  782.5 37.2 %copy-start.22 = (bf16[8,288]{1,0:T(8,128)(2,1)S(1)}, bf16[8,288]{1,0:T(8,128)(2,1)}, u32[]{:S(2)}) copy-start(bf16[8,288]{1,0:T(8,128)(2,1)} %copy-done.21) | copy-start | bytes 13828
  879.2 9.5 copy-start.34
  (32 other events, 64.4 us)

commit v4 on v3

--- a/solution.py
+++ b/solution.py
@@ -1,3 +1,5 @@
+from functools import partial
+
 import jax
 import jax.numpy as jnp
 from jax import lax
@@ -284,21 +286,22 @@
 class FoldTo:
     reach = 2
 
-    def __init__(self, source, shard):
-        pieces, self.rows, width = source.shape
+    def __init__(self, shape, shard, late):
+        pieces, self.rows, width = shape
         others = lax.axis_size("batch") - 1
         self.shard = shard
-        self.ins = [source]
-        self.outs = [jax.ShapeDtypeStruct((pieces, others, self.rows, width), source.dtype)]
+        self.ins = []
+        self.outs = [jax.ShapeDtypeStruct((pieces, others, self.rows, width), bf16)]
         self.sems = [(pieces, others), (pieces, others)]
+        self.late, self.pieces = late, pieces
 
     def bind(self, ins, outs, sems):
-        (self.source,), (self.inbox,) = ins, outs
+        (self.inbox,) = outs
+        self.source = None
         self.send, self.recv = sems
         self.steps = 1
-        self.late = 0
         self.rank, self.others = lax.axis_index("batch"), lax.axis_size("batch") - 1
-        self.owners = owners_of(self.source.shape[0], self.rows, self.shard)
+        self.owners = owners_of(self.pieces, self.rows, self.shard)
 
     def copy(self, j, n):
         return remote(
@@ -613,32 +616,40 @@
     return jax.ShapeDtypeStruct(shape, kind)
 
 
-def prologue_kernel(background, pack, tiles, packs, every_tile, zs, zr, ps, pr):
+def prologue_kernel(background, *refs):
+    count = (len(refs) - 6) // 2
+    smalls, tiles = refs[:count], refs[count]
+    packs, every_tile = refs[count + 1 : 2 * count + 1], refs[2 * count + 1]
+    zs, zr, ps, pr = refs[2 * count + 2 :]
     ranks, peers = other_ranks(), plane_peers()
     greet(ranks + peers)
     rank, place = lax.axis_index("batch"), team_place()
     copies = [
-        remote(pack, packs.at[rank], zs.at[n], zr.at[n], who) for n, who in enumerate(ranks)
+        remote(small, pack.at[rank], zs.at[m, n], zr.at[m, n], who)
+        for m, (small, pack) in enumerate(zip(smalls, packs))
+        for n, who in enumerate(ranks)
     ] + [remote(tiles, every_tile.at[place], ps.at[n], pr.at[n], who) for n, who in enumerate(peers)]
     for copy in copies:
         copy.start()
-    packs[rank] = pack[...]
+    for small, pack in zip(smalls, packs):
+        pack[rank] = small[...]
     every_tile[place] = tiles[...]
     for copy in copies:
         copy.wait()
 
 
-def prologue(pack, tiles, ident):
+def prologue(smalls, tiles, ident):
     ranks = lax.axis_size("batch")
     dma = pltpu.SemaphoreType.DMA
-    (packs, every_tile), _ = call(
+    (*packs, every_tile), _ = call(
         prologue_kernel,
         "prologue",
         ident,
-        [shaped((ranks,) + pack.shape, pack.dtype), shaped((8,) + tiles.shape, tiles.dtype)],
-        [dma((ranks - 1,)), dma((ranks - 1,)), dma((7,)), dma((7,))],
+        [shaped((ranks,) + small.shape, small.dtype) for small in smalls]
+        + [shaped((8,) + tiles.shape, tiles.dtype)],
+        [dma((len(smalls), ranks - 1)), dma((len(smalls), ranks - 1)), dma((7,)), dma((7,))],
         0,
-        (pack, tiles),
+        (*smalls, tiles),
     )
     return packs, every_tile
 
@@ -692,13 +703,52 @@
 
 
 def epilogue_kernel(
-    background, mods, sums, biases, tokens, all_mods, all_sums, all_biases, all_tokens,
-    mods_in, sums_in, rank_mods, rank_sums, rank_sums_in, rank_biases_in, ps, pr, zs, zr, qs, qr,
+    depth, background, *refs,
 ):
+    refs = list(refs)
+
+    def take(count):
+        taken = refs[:count]
+        del refs[:count]
+        return taken
+
+    block_sums, (final_sums,) = take(2 * depth), take(1)
+    block_biases = take(2 * depth)
+    patch_term, final_term, edge_rows, tokens = take(4)
+    all_mods, all_sums, all_biases, all_tokens = take(4)
+    mods, sums, biases, mods_in, sums_in, rank_mods, rank_sums, rank_biases_in, ps, pr, zs, zr, qs, qr = refs
     ranks, peers = other_ranks(), plane_peers()
-    greet(ranks + peers)
     rank, place = lax.axis_index("batch"), team_place()
     cols = lax.axis_size("col")
+    images = final_sums.shape[0]
+    each = sums.shape[1]
+
+    mods[...] = jnp.zeros_like(mods)
+    sums[...] = jnp.zeros_like(sums)
+    biases[...] = jnp.zeros_like(biases)
+    for i in range(images):
+        for b in range(depth):
+            for p in range(6):
+                n = 6 * b + p
+                source = block_sums[2 * b + p // 3]
+                mods[n // 2, i * 2 + n % 2] = source[i, p % 3]
+        for p in range(2):
+            n = 6 * depth + p
+            mods[n // 2, i * 2 + n % 2] = final_sums[i, p]
+    rows = [patch_term[n] for n in range(patch_term.shape[0])]
+    rows += [final_term[n] for n in range(final_term.shape[0])]
+    rows += [edge_rows[n] for n in range(edge_rows.shape[0])]
+    for source in block_sums:
+        total = source[0, 3]
+        for i in range(1, images):
+            total = total + source[i, 3]
+        rows.append(total)
+    for n, row in enumerate(rows):
+        sums[n // each, n % each] = row
+    for n, source in enumerate(block_biases):
+        biases[n, : source.shape[1]] = source[0]
+
+    greet(ranks + peers)
     first, extra = [], []
     for n, who in enumerate(peers):
         there = who["row"] * cols + who["col"]
@@ -721,11 +771,11 @@
         mod_total = mod_total + mods_in[n]
         sum_total = sum_total + sums_in[n]
     rank_mods[rank] = mod_total.astype(bf16)
-    rank_sums[...] = sum_total
+    rank_sums[rank] = sum_total
     third = []
     for n, who in enumerate(ranks):
         third.append(remote(rank_mods.at[rank], rank_mods.at[rank], zs.at[1, n], zr.at[1, n], who))
-        third.append(remote(rank_sums.at[who["batch"]], rank_sums_in.at[n], zs.at[2, n], zr.at[2, n], who))
+        third.append(remote(rank_sums.at[rank], rank_sums.at[rank], zs.at[2, n], zr.at[2, n], who))
     for copy in third:
         copy.start()
     background.tick()
@@ -735,9 +785,9 @@
         bias_total = bias_total + rank_biases_in[n]
     for copy in third:
         copy.wait()
-    sum_own = rank_sums[rank]
-    for n in range(len(ranks)):
-        sum_own = sum_own + rank_sums_in[n]
+    sum_own = rank_sums[0]
+    for n in range(1, rank_sums.shape[0]):
+        sum_own = sum_own + rank_sums[n]
     all_mods[place] = rank_mods[...]
     all_sums[place] = sum_own
     all_biases[place] = bias_total
@@ -753,26 +803,35 @@
     background.finish()
 
 
-def epilogue(mods, sums, biases, tokens, ident, tasks):
+def epilogue(block_sums, final_sums, block_biases, patch_term, final_term, edge_rows, tokens, ident, tasks):
     ranks = lax.axis_size("batch")
     dma = pltpu.SemaphoreType.DMA
+    depth = len(block_sums) // 2
+    images, _, width = final_sums.shape
+    count = patch_term.shape[0] + final_term.shape[0] + edge_rows.shape[0] + len(block_sums)
+    each = -(-count // 8)
+    widest = max(source.shape[1] for source in block_biases)
+    mods, sums = (8, 2 * images, width), (8, each, width)
+    biases = (8, widest)
     return call(
-        epilogue_kernel,
+        partial(epilogue_kernel, depth),
         "epilogue",
         ident,
         [
-            shaped((8, ranks) + mods.shape[1:], bf16),
-            shaped((8,) + sums.shape[2:], f32),
-            shaped((8,) + biases.shape, f32),
+            shaped((8, ranks) + mods[1:], bf16),
+            shaped(sums, f32),
+            shaped((8,) + biases, f32),
             shaped((8,) + tokens.shape, f32),
         ],
         [
-            pltpu.VMEM((7,) + mods.shape[1:], f32),
-            pltpu.VMEM((7,) + sums.shape[1:], f32),
-            pltpu.VMEM((ranks,) + mods.shape[1:], bf16),
-            pltpu.VMEM(sums.shape[1:], f32),
-            pltpu.VMEM((ranks - 1,) + sums.shape[2:], f32),
-            pltpu.VMEM((ranks - 1,) + biases.shape, f32),
+            pltpu.VMEM(mods, f32),
+            pltpu.VMEM(sums, f32),
+            pltpu.VMEM(biases, f32),
+            pltpu.VMEM((7,) + mods[1:], f32),
+            pltpu.VMEM((7,) + sums[1:], f32),
+            pltpu.VMEM((ranks,) + mods[1:], bf16),
+            pltpu.VMEM((ranks,) + sums[1:], f32),
+            pltpu.VMEM((ranks - 1,) + biases, f32),
             dma((3, 7)),
             dma((3, 7)),
             dma((3, ranks - 1)),
@@ -781,7 +840,7 @@
             dma((3, 7)),
         ],
         0,
-        (mods, sums, biases, tokens),
+        (*block_sums, final_sums, *block_biases, patch_term, final_term, edge_rows, tokens),
         tasks,
     )
 
@@ -820,17 +879,24 @@
 
 
 def mlp_forward_kernel(
-    background, mid, gate_rows, vecs, expand, expand_bias, shrink, full, hidden, expanded, after, *comm
+    block, background, mid, gate_rows, vecs, expand, expand_bias, shrink, full, hidden, expanded, after, *comm
 ):
     place = sides()
     core, chips, address = place
     images = full.shape[0]
     gathers, scatters = exchanges(full, comm, place)
     greet(list(address.values()) + background.partners())
+
+    def row(i, n):
+        return vecs[i, n : n + 1]
+
+    def gate(i):
+        return gate_rows[i] if block > 0 else 1.0
+
     own = core * 4 + chips["own"]
 
     def begin(i):
-        full[i, own] = modulate(mid[i], vecs[i, 0:1], vecs[i, 1:2]).astype(bf16)
+        full[i, own] = modulate(mid[i], row(i, 6 * block + 3), row(i, 6 * block + 4)).astype(bf16)
         gathers[i].first()
 
     def compute(i, between):
@@ -842,9 +908,9 @@
             between[step]()
 
     def end(i):
-        value = scatters[i].finish() + vecs[i, 3:4]
+        value = scatters[i].finish() + row(i, offset_row(vecs, block, 1))
         expanded[i] = value
-        after[i] = mid[i] + gate_rows[i] * vecs[i, 2:3] * value
+        after[i] = mid[i] + gate(i) * row(i, 6 * block + 5) * value
 
     begin(0)
     background.tick()
@@ -864,12 +930,12 @@
     background.finish()
 
 
-def mlp_forward(mid, gate_rows, vecs, weights, ident, tasks=()):
+def mlp_forward(block, mid, gate_rows, vecs, weights, ident, tasks=()):
     expand, expand_bias, shrink = weights
     images, length, width = mid.shape
     inner = expand.shape[1]
     return call(
-        mlp_forward_kernel,
+        partial(mlp_forward_kernel, block),
         "mlp_forward",
         ident,
         [
@@ -893,7 +959,7 @@
 
 
 def mlp_backward_kernel(
-    background, grad_after, mid, expanded, gate_rows, vecs, expand, shrink, normed, hidden,
+    block, background, grad_after, mid, expanded, gate_rows, vecs, expand, shrink, normed, hidden,
     grad_mid, sums, grad_expand, grad_shrink, grad_bias,
     full, grad_hidden, active, sum_expand, sum_shrink, *comm
 ):
@@ -901,11 +967,19 @@
     core, chips, address = place
     gathers, scatters = exchanges(full, comm, place)
     greet(list(address.values()) + background.partners())
+
+    def row(i, n):
+        return vecs[i, n : n + 1]
+
+    def gate(i):
+        return gate_rows[i] if block > 0 else 1.0
+
     own = core * 4 + chips["own"]
+    length = full.shape[2]
 
     def begin(i):
-        gated = gate_rows[i] * grad_after[i]
-        low = (gated * vecs[i, 1:2]).astype(bf16)
+        gated = gate(i) * grad_after[i, :length]
+        low = (gated * row(i, 6 * block + 5)).astype(bf16)
         full[i, own] = low
         gathers[i].first()
         sums[i, 2:3] = column_sum(gated * expanded[i])
@@ -939,8 +1013,8 @@
             grad_bias[...] += row_sums(low)
 
     def end(i):
-        grad, shift_sum, scale_sum = modulate_back_rows(mid[i], vecs[i, 0:1], scatters[i].finish())
-        grad_mid[i] = grad + grad_after[i]
+        grad, shift_sum, scale_sum = modulate_back_rows(mid[i], row(i, 6 * block + 4), scatters[i].finish())
+        grad_mid[i] = grad + grad_after[i, :length]
         sums[i, 0:1] = shift_sum
         sums[i, 1:2] = scale_sum
 
@@ -964,13 +1038,13 @@
     background.finish()
 
 
-def mlp_backward(grad_after, mid, expanded, gate_rows, vecs, weights, saved, ident, tasks=()):
+def mlp_backward(block, grad_after, mid, expanded, gate_rows, vecs, weights, saved, ident, tasks=()):
     expand, _, shrink = weights
     normed, hidden = saved
     images, length, width = mid.shape
     inner = expand.shape[1]
     return call(
-        mlp_backward_kernel,
+        partial(mlp_backward_kernel, block),
         "mlp_backward",
         ident,
         [
@@ -1007,15 +1081,55 @@
 LOG2E = 1.4426950408889634
 
 
+def offset_row(vecs, block, kind):
+    depth = (vecs.shape[1] - 2) // 8
+    return 6 * depth + 2 + 2 * block + kind
+
+
+def pad_lanes(value):
+    gap = jnp.zeros((value.shape[0], LANES - HEAD_SIZE), value.dtype)
+    parts = []
+    for start in range(0, value.shape[1], HEAD_SIZE):
+        parts += [value[:, start : start + HEAD_SIZE], gap]
+    return jnp.concatenate(parts, axis=1)
+
+
+def pad_rows(value):
+    gap = jnp.zeros((LANES - HEAD_SIZE, value.shape[1]), value.dtype)
+    parts = []
+    for start in range(0, value.shape[0], HEAD_SIZE):
+        parts += [value[start : start + HEAD_SIZE], gap]
+    return jnp.concatenate(parts, axis=0)
+
+
+def cut_lanes(value):
+    return jnp.concatenate(
+        [value[:, start : start + HEAD_SIZE] for start in range(0, value.shape[1], LANES)], axis=1
+    )
+
+
+def cut_rows(value):
+    return jnp.concatenate(
+        [value[start : start + HEAD_SIZE] for start in range(0, value.shape[0], LANES)], axis=0
+    )
+
+
 def attention_forward_kernel(
-    background, base, gate_rows, vecs, project, project_bias, attend, key_bias,
-    full, packed, mixed, log_total, attended, mid, *comm
+    block, background, base, gate_rows, vecs, project_own, project_bias, attend_own, key_bias,
+    full, packed, mixed, log_total, attended, mid, project, attend, *comm
 ):
     place = sides()
     core, chips, address = place
     images, _, length, _ = full.shape
     gathers, scatters = exchanges(full, comm, place)
     greet(list(address.values()) + background.partners())
+
+    def row(i, n):
+        return vecs[i, n : n + 1]
+
+    def gate(i):
+        return gate_rows[i] if block > 0 else 1.0
+
     own = core * 4 + chips["own"]
     span = attend.shape[0]
     heads = span // LANES
@@ -1023,7 +1137,7 @@
     factor = HEAD_SIZE ** (-0.5) * LOG2E
 
     def begin(i):
-        full[i, own] = modulate(base[i], vecs[i, 0:1], vecs[i, 1:2]).astype(bf16)
+        full[i, own] = modulate(base[i, :length], row(i, 6 * block), row(i, 6 * block + 1)).astype(bf16)
         gathers[i].first()
 
     def rows_of(start, count):
@@ -1042,7 +1156,9 @@
                     q, k, v = (
                         pl.ds(part * span + h * LANES, LANES) for part in range(3)
                     )
-                    scores = dot(packed[i, rows, q], packed[i, :, k], NT) * factor + key_bias[i]
+                    scores = dot(packed[i, rows, q], packed[i, :, k], NT) * factor
+                    if block > 0:
+                        scores = scores + key_bias[i]
                     peak = jnp.max(scores, axis=1, keepdims=True)
                     probs = jnp.exp2(scores - peak)
                     total = jnp.sum(probs, axis=1, keepdims=True)
@@ -1058,12 +1174,14 @@
             between[1 + step]()
 
     def end(i):
-        value = scatters[i].finish() + vecs[i, 3:4]
+        value = scatters[i].finish() + row(i, offset_row(vecs, block, 0))
         attended[i] = value
-        mid[i] = base[i] + gate_rows[i] * vecs[i, 2:3] * value
+        mid[i] = base[i, :length] + gate(i) * row(i, 6 * block + 2) * value
 
     begin(0)
     background.tick()
+    project[...] = pad_lanes(project_own[...])
+    attend[...] = pad_rows(attend_own[...])
     gathers[0].second()
     begin(1)
     gathers[0].finish()
@@ -1078,12 +1196,12 @@
     background.finish()
 
 
-def attention_forward(base, gate_rows, vecs, weights, key_bias, ident, tasks=()):
+def attention_forward(block, length, base, gate_rows, vecs, weights, key_bias, ident, tasks=()):
     project, project_bias, attend = weights
-    images, length, width = base.shape
-    span = attend.shape[0]
+    images, _, width = base.shape
+    span = attend.shape[0] // HEAD_SIZE * LANES
     return call(
-        attention_forward_kernel,
+        partial(attention_forward_kernel, block),
         "attention_forward",
         ident,
         [
@@ -1093,6 +1211,8 @@
             shaped((images, span // LANES, 4, 2 * length), f32),
             shaped((images, length, width), f32),
             shaped((images, length, width), f32),
+            shaped((width, 3 * span), bf16),
+            shaped((span, width), bf16),
         ],
         comm_scratch(images, length, width),
         8 * images * 8 * length * width * span * 6,
@@ -1110,7 +1230,7 @@
 
 
 def attention_backward_kernel(
-    background, grad_mid, base, attended, gate_rows, vecs, project, attend, key_bias, normed, packed, mixed, log_total,
+    block, background, grad_mid, base, attended, gate_rows, vecs, project, attend, key_bias, normed, packed, mixed, log_total,
     grad_base, sums, grad_project, grad_attend, grad_bias,
     full, grad_mixed, grad_packed, grad_keys, grad_values, sum_project, sum_attend, *comm
 ):
@@ -1119,6 +1239,13 @@
     images, _, length, _ = full.shape
     gathers, scatters = exchanges(full, comm, place)
     greet(list(address.values()) + background.partners())
+
+    def row(i, n):
+        return vecs[i, n : n + 1]
+
+    def gate(i):
+        return gate_rows[i] if block > 0 else 1.0
+
     own = core * 4 + chips["own"]
     span = attend.shape[0]
     heads = span // LANES
@@ -1126,8 +1253,8 @@
     factor = HEAD_SIZE ** (-0.5)
 
     def begin(i):
-        gated = gate_rows[i] * grad_mid[i]
-        low = (gated * vecs[i, 1:2]).astype(bf16)
+        gated = gate(i) * grad_mid[i]
+        low = (gated * row(i, 6 * block + 2)).astype(bf16)
         full[i, own] = low
         gathers[i].first()
         sums[i, 2:3] = column_sum(gated * attended[i])
@@ -1147,7 +1274,9 @@
             def one(t, carry):
                 rows = pl.ds(pl.multiple_of(t * tile, tile), tile)
                 queries, pulls = packed[i, rows, q], grad_mixed[rows, lane]
-                scores = dot(packed[i, :, k], queries, NT) * (factor * LOG2E) + key_bias[i]
+                scores = dot(packed[i, :, k], queries, NT) * (factor * LOG2E)
+                if block > 0:
+                    scores = scores + key_bias[i]
                 probs = jnp.exp2(scores - log_total[i, h, pl.ds(t, 1)])
                 dprobs = dot(packed[i, :, v], pulls, NT)
                 row_dot = column_sum(probs * dprobs)
@@ -1181,7 +1310,7 @@
         if i == 0:
             sum_attend[...] = term
         else:
-            grad_attend[...] = (sum_attend[...] + term).astype(bf16)
+            grad_attend[...] = cut_rows(sum_attend[...] + term).astype(bf16).reshape(grad_attend.shape)
 
     def weigh_project(i):
         low = grad_packed[i]
@@ -1190,33 +1319,46 @@
             sum_project[...] = term
             grad_bias[...] = row_sums(low)
         else:
-            grad_project[...] = (sum_project[...] + term).astype(bf16)
+            grad_project[...] = cut_lanes(sum_project[...] + term).astype(bf16)
             grad_bias[...] += row_sums(low)
 
     def end(i):
-        grad, shift_sum, scale_sum = modulate_back_rows(base[i], vecs[i, 0:1], scatters[i].finish())
+        grad, shift_sum, scale_sum = modulate_back_rows(base[i, :length], row(i, 6 * block + 1), scatters[i].finish())
         grad_base[i] = grad + grad_mid[i]
         sums[i, 0:1] = shift_sum
         sums[i, 1:2] = scale_sum
 
     def nothing():
         pass
+
+    def begin_extra():
+        gathers[1].second()
+        background.tick()
+
+    def early_attend():
+        weigh_attend(0)
+        weigh_attend(1)
+        for task in background.tasks:
+            if task.source is None:
+                task.source = grad_attend
+        background.tick()
+
+    def middle():
+        scatters[0].second()
+        background.tick()
 
     begin(0)
     background.tick()
     gathers[0].second()
     begin(1)
     gathers[0].finish()
-    compute(0, (gathers[1].second, nothing, gathers[1].finish))
-    background.tick()
+    compute(0, (begin_extra, gathers[1].finish, nothing))
     scatters[0].first()
-    compute(1, (scatters[0].second, background.tick, background.tick))
-    weigh_attend(0)
+    compute(1, (early_attend, middle, background.tick))
     scatters[1].first()
     weigh_project(0)
     end(0)
     scatters[1].second()
-    weigh_attend(1)
     weigh_project(1)
     end(1)
     for part in gathers + scatters:
@@ -1224,21 +1366,23 @@
     background.finish()
 
 
-def attention_backward(grad_mid, base, attended, gate_rows, vecs, weights, key_bias, saved, ident, tasks=()):
-    project, _, attend = weights
+def attention_backward(
+    block, attend_shape, grad_mid, base, attended, gate_rows, vecs, weights, key_bias, saved, ident, tasks=()
+):
+    project, attend = weights
     normed, packed, mixed, log_total = saved
-    images, length, width = base.shape
+    images, length, width = grad_mid.shape
     span = attend.shape[0]
     tokens = 8 * length
     return call(
-        attention_backward_kernel,
+        partial(attention_backward_kernel, block),
         "attention_backward",
         ident,
         [
             shaped((images, length, width), f32),
             shaped((images, 8, width), f32),
-            shaped((width, 3 * span), bf16),
-            shaped((span, width), bf16),
+            shaped((width, 3 * span // LANES * HEAD_SIZE), bf16),
+            shaped(attend_shape, bf16),
             shaped((8, 3 * span), f32),
         ],
         [
@@ -1290,23 +1434,150 @@
     return kept.reshape(shape[:axis] + (heads * HEAD_SIZE,) + shape[axis + 1 :])
 
 
-def pack_flat(arrays, multiple):
-    flat = jnp.concatenate([array.reshape(-1) for array in arrays])
-    return jnp.pad(flat, (0, -flat.size % multiple)).reshape(-1, LANES)
-
-
-def unpack_ranks(packs, arrays, dims):
-    every = packs.reshape(packs.shape[0], -1)
-    out = []
-    start = 0
-    for array, dim in zip(arrays, dims):
-        piece = every[:, start : start + array.size].reshape((-1,) + array.shape)
-        start += array.size
-        piece = jnp.moveaxis(piece, 0, dim)
-        shape = list(array.shape)
-        shape[dim] = -1
-        out.append(piece.reshape(shape))
-    return out
+def join_ranks(pack, dim):
+    moved = jnp.moveaxis(pack, 0, dim)
+    shape = list(pack.shape[1:])
+    shape[dim] = -1
+    return moved.reshape(shape)
+
+
+def turn(block, own, step, last):
+    return jnp.where(block == own, step, jnp.where(block < own, 0, last))
+
+
+def local_call(kernel, name, grid, in_specs, out_specs, outs, moved, args, prefetch=0):
+    return pl.pallas_call(
+        kernel,
+        name=name,
+        grid_spec=pltpu.PrefetchScalarGridSpec(
+            num_scalar_prefetch=prefetch, grid=grid, in_specs=in_specs, out_specs=out_specs
+        ),
+        out_shape=outs,
+        compiler_params=pltpu.CompilerParams(vmem_limit_bytes=56 * 2**20),
+        cost_estimate=pl.CostEstimate(flops=0, bytes_accessed=moved, transcendentals=0),
+    )(*args)
+
+
+def mlp_unpack_kernel(*refs):
+    *everys, expand, shrink = refs
+    for k, every in enumerate(everys):
+
+        @pl.when(pl.program_id(0) == k)
+        def _(every=every):
+            parts = [[every[core, 0, n].astype(f32) for core in range(2)] for n in range(2)]
+            expand[0] = jnp.concatenate(parts[0], axis=1)
+            shrink[0] = jnp.concatenate([part.T for part in parts[1]], axis=0)
+
+
+def mlp_unpack(everys):
+    depth = len(everys)
+    _, _, shard, inner = everys[0].shape
+    everys = [every.reshape(2, 4, 2, shard, inner) for every in everys]
+    block = (2, 1, 2, shard, inner)
+    return local_call(
+        mlp_unpack_kernel,
+        "mlp_unpack",
+        (depth, 4),
+        [pl.BlockSpec(block, lambda b, j, k=k: (0, turn(b, k, j, 3), 0, 0, 0)) for k in range(depth)],
+        [
+            pl.BlockSpec((1, shard, 2 * inner), lambda b, j: (b, 0, j)),
+            pl.BlockSpec((1, 2 * inner, shard), lambda b, j: (b, j, 0)),
+        ],
+        [shaped((depth, shard, 8 * inner), f32), shaped((depth, 8 * inner, shard), f32)],
+        depth * shard * inner * 96,
+        everys,
+    )
+
+
+def project_unpack_kernel(*refs):
+    *everys, project = refs
+    for k, every in enumerate(everys):
+
+        @pl.when(pl.program_id(0) == k)
+        def _(every=every):
+            each = every.shape[-1] // 3
+            parts = [
+                every[d % 2, d // 2, 0].astype(f32)[:, n * each : (n + 1) * each] for n in range(3) for d in range(8)
+            ]
+            project[0, 0] = jnp.concatenate(parts, axis=1)
+
+
+def project_unpack(everys):
+    depth = len(everys)
+    _, _, half, columns = everys[0].shape
+    everys = [every.reshape(2, 4, 2, half, columns) for every in everys]
+    (project,) = local_call(
+        project_unpack_kernel,
+        "project_unpack",
+        (depth, 2),
+        [
+            pl.BlockSpec((2, 4, 1, half, columns), lambda b, j, k=k: (0, 0, turn(b, k, j, 1), 0, 0))
+            for k in range(depth)
+        ],
+        [pl.BlockSpec((1, 1, half, 8 * columns), lambda b, j: (b, j, 0, 0))],
+        [shaped((depth, 2, half, 8 * columns), f32)],
+        depth * half * columns * 96,
+        everys,
+    )
+    return project.reshape(depth, 2 * half, 8 * columns)
+
+
+def attend_unpack_kernel(rank, *refs):
+    *everys, attend = refs
+    for k, every in enumerate(everys):
+
+        @pl.when(pl.program_id(0) == k)
+        def _(every=every):
+            attend[0, 0] = every[0, 0].astype(f32)
+
+
+def attend_unpack(everys, rank, shard, pieces, rows):
+    depth = len(everys)
+    width = everys[0].shape[-1]
+    everys = [every.reshape(8, pieces, rows, width) for every in everys]
+    steps = shard // rows
+
+    def chosen(b, i, ranks, k):
+        g = ranks[0] * steps + i
+        d = g // pieces
+        own = b == k
+        return jnp.where(own, d % 2 * 4 + d // 2, 0), jnp.where(own, g % pieces, 0), 0, 0
+
+    (attend,) = local_call(
+        attend_unpack_kernel,
+        "attend_unpack",
+        (depth, steps),
+        [pl.BlockSpec((1, 1, rows, width), partial(chosen, k=k)) for k in range(depth)],
+        [pl.BlockSpec((1, 1, rows, width), lambda b, i, ranks: (b, i, 0, 0))],
+        [shaped((depth, steps, rows, width), f32)],
+        depth * shard * width * 6,
+        [rank.reshape(1), *everys],
+        1,
+    )
+    return attend.reshape(depth, shard, width)
+
+
+def adaptive_grad_kernel(silu, mods, out):
+    out[0] = dot(silu[...], mods[0], TN)
+
+
+def adaptive_grad(silu, mods):
+    depth, count, columns = mods.shape
+    shard = silu.shape[1]
+    (grad,) = local_call(
+        adaptive_grad_kernel,
+        "adaptive_grad",
+        (depth, 3),
+        [
+            pl.BlockSpec((count, shard), lambda b, j: (0, 0)),
+            pl.BlockSpec((1, count, columns // 3), lambda b, j: (b, 0, j)),
+        ],
+        [pl.BlockSpec((1, shard, columns // 3), lambda b, j: (b, 0, j))],
+        [shaped((depth, shard, columns), f32)],
+        depth * shard * columns * 4,
+        [silu, mods],
+    )
+    return grad
 
 
 def body(
@@ -1355,9 +1626,13 @@
 
     piece_rows = min(shard, head_cols)
     pieces_each = head_cols // piece_rows
-    project_own = lax.dynamic_index_in_dim(
-        project_weight.reshape(depth, shard, 3, team, head_cols), place, axis=3, keepdims=False
-    ).reshape(depth, shard, 3 * head_cols)
+    project_own = jnp.concatenate(
+        [
+            lax.dynamic_slice_in_dim(project_weight, part * width + place * head_cols, head_cols, axis=2)
+            for part in range(3)
+        ],
+        axis=2,
+    )
     attend_own = jnp.stack(
         [
             lax.dynamic_slice_in_dim(
@@ -1372,13 +1647,13 @@
 
     smalls = [
         patch_weight,
-        patch_bias,
+        patch_bias[None],
         adaptive_bias,
         project_bias,
         attend_bias,
         expand_bias,
         shrink_bias,
-        final_offset,
+        final_offset[None],
         final_weight,
         conditioning,
     ]
@@ -1386,7 +1661,7 @@
     grad_tiles = to_tokens(cotangent, PATCH)
     patch_in, patch_out = patch_tiles.shape[2], grad_tiles.shape[2]
     tiles = jnp.concatenate([patch_tiles, grad_tiles], axis=2)
-    packs, every_tile = prologue(pack_flat(smalls, 2048), tiles.reshape(-1, LANES), 8)
+    packs, every_tile = prologue(smalls, tiles.reshape(-1, LANES), 8)
     (
         patch_full,
         patch_bias_full,
@@ -1398,7 +1673,7 @@
         final_offset_full,
         final_full,
         cond_all,
-    ) = unpack_ranks(packs, smalls, [1, 0, 1, 1, 1, 1, 1, 0, 0, 0])
+    ) = [join_ranks(pack, dim) for pack, dim in zip(packs, [1, 1, 1, 1, 1, 1, 1, 1, 0, 0])]
 
     whole = every_tile.reshape((rows, cols, images, rows_tile, cols_tile, -1)).transpose(2, 0, 3, 1, 4, 5)
     whole = whole.reshape(images, sequence, patch_in + patch_out)
@@ -1436,90 +1711,69 @@
 
     silu_all = jax.nn.silu(cond_all.astype(f32)).astype(bf16)
     silu_rows = lax.dynamic_slice_in_dim(silu_all, rank * shard, shard, axis=1)
-    mod_cols, final_cols = adaptive_weight.shape[2] // team, final_adaptive.shape[1] // team
-    parts = [
-        dot(silu_rows, slice_of(adaptive_weight[b], 1, mod_cols), ((1,), (0,))) for b in range(depth)
-    ] + [dot(silu_rows, slice_of(final_adaptive, 1, final_cols), ((1,), (0,)))]
-    parts = jnp.concatenate(parts, axis=1).reshape(ranks, images, -1)
+    pair = 2 * width
+    block_of = jnp.minimum(place // 3, depth - 1)
+    pair_weight = lax.dynamic_slice(adaptive_weight, (block_of, 0, place % 3 * pair), (1, shard, pair))[0]
+    pair_weight = jnp.where(place < 3 * depth, pair_weight, final_adaptive)
+    parts = dot(silu_rows, pair_weight, NN).reshape(ranks, images * 2, width)
     mods, (project_next, attend_next) = conditioning_exchange(
         parts, 9, [Line(project_own[0]), Chain(attend_own[0], shard)]
     )
-    mods = mods.transpose(1, 0, 2)
-
-    def attention_matrices(project_parts, attend_parts):
-        project = pad_heads(project_parts.reshape(width, 3, head_cols), 2).reshape(width, -1)
-        return project, pad_heads(attend_parts.reshape(head_cols, width), 0)
-
-    pieces = []
-    for b in range(depth):
-        block_mod = mods[:, :, b * mod_cols : (b + 1) * mod_cols].reshape(images, -1)
-        block_mod = (block_mod + adaptive_offset[b].astype(f32)).reshape(images, 6, 1, width)
-        pieces.append([block_mod[:, s] for s in range(6)])
-    final_mod = mods[:, :, depth * mod_cols :].reshape(images, -1) + final_offset_full.astype(f32)
-    final_mod = final_mod.reshape(images, 2, 1, width)
-    final_shift, final_scale = final_mod[:, 0], final_mod[:, 1]
+    mods = mods.reshape(team, images, 2, width).transpose(1, 0, 2, 3).reshape(images, 2 * team, width)
+    offsets = [adaptive_offset.reshape(6 * depth, width), final_offset_full.reshape(2, width)]
+    mods = mods[:, : 6 * depth + 2] + jnp.concatenate(offsets, axis=0).astype(f32)
+    added = jnp.stack([attend_offset, shrink_offset], axis=1).reshape(2 * depth, width).astype(f32)
+    vecs = jnp.concatenate([mods, jnp.broadcast_to(added, (images, 2 * depth, width))], axis=1)
+    final_shift, final_scale = mods[:, 6 * depth, None], mods[:, 6 * depth + 1, None]
+    head_biases = jnp.moveaxis(project_offset.astype(f32).reshape(depth, 2, team, head_cols), 2, 0)
+    head_biases = lax.dynamic_index_in_dim(head_biases, place, axis=0, keepdims=False)
+    head_biases = jnp.stack([head_biases[:, 0], jnp.zeros((depth, head_cols), f32), head_biases[:, 1]], axis=1)
+    head_biases = pad_heads(head_biases, 2).reshape(depth, -1)
+    hidden_biases = slice_of(expand_offset.astype(f32), 1, hidden_cols)
 
     records = []
     for b in range(depth):
-        project, attend = attention_matrices(project_next, attend_next)
-        shift1, scale1, gate1, shift2, scale2, gate2 = pieces[b]
-        bias = project_offset[b].astype(f32).reshape(2, team, head_cols)
-        bias = lax.dynamic_index_in_dim(bias, place, axis=1, keepdims=False)
-        bias = pad_heads(jnp.stack([bias[0], jnp.zeros_like(bias[0]), bias[1]]), 1).reshape(-1)
-        attention_weights = (project, bias, attend)
         routed = b > 0
-        base = resid[:, :kept_local] if routed else resid
-        gate_rows = kept_rows if routed else jnp.ones((images, tile_tokens, 1), f32)
-        keys = key_bias if routed else jnp.zeros((images, sequence), f32)
-
-        def rows_with(parts, bias_row):
-            row = jnp.broadcast_to(bias_row.astype(f32), (images, 1, width))
-            return jnp.concatenate(parts + [row], axis=1)
-
+        length = kept_local if routed else tile_tokens
+        base = resid
         tasks = [Line(expand_own[b])]
         if not routed:
             tasks.append(Line(shrink_own[b]))
-        (*attention_saved, attended, mid), gathered = attention_forward(
+        (*attention_saved, attended, mid, project, attend), gathered = attention_forward(
+            b,
+            length,
             base,
-            gate_rows,
-            rows_with([shift1, scale1, gate1], attend_offset[b]),
-            attention_weights,
-            keys[:, None, :],
+            kept_rows,
+            vecs,
+            (project_next.reshape(width, -1), head_biases[b], attend_next.reshape(-1, width)),
+            key_bias[:, None, :],
             4 * b,
             tasks,
         )
         expand = gathered[0].reshape(width, hidden_cols)
         shrink = (shrink_next if routed else gathered[1]).reshape(width, hidden_cols)
-        mlp_weights = (expand, slice_of(expand_offset[b].astype(f32), 0, hidden_cols), shrink)
+        mlp_weights = (expand, hidden_biases[b], shrink)
         tasks = []
         if b + 1 < depth:
             tasks = [Line(project_own[b + 1]), Chain(attend_own[b + 1], shard), Line(shrink_own[b + 1])]
         (*mlp_saved, expanded, after), gathered = mlp_forward(
-            mid,
-            gate_rows,
-            rows_with([shift2, scale2, gate2], shrink_offset[b]),
-            mlp_weights,
-            4 * b + 1,
-            tasks,
+            b, mid, kept_rows, vecs, mlp_weights, 4 * b + 1, tasks
         )
         if tasks:
             project_next, attend_next, shrink_next = gathered
-        records.append(
-            (base, mid, attended, expanded, attention_weights, mlp_weights, keys, gate_rows, attention_saved, mlp_saved)
-        )
+        records.append((base, mid, attended, expanded, (project, attend), mlp_weights, attention_saved, mlp_saved))
         resid = jnp.concatenate([after, resid[:, kept_local:]], axis=1) if routed else after
 
     final_normed = modulate(resid, final_shift, final_scale).astype(bf16)
-    outputs = jnp.einsum("ikd,dc->ikc", final_normed, final_full, preferred_element_type=f32) + final_bias.astype(f32)
+    outputs = jnp.einsum("ikd,dc->cik", final_normed, final_full, preferred_element_type=f32)
+    outputs = outputs + final_bias.astype(f32)[:, None, None]
     final_bias_term = jnp.sum(grad_outputs.astype(f32), axis=(0, 1))
-    final_weight_term = jnp.einsum("ikd,ikc->dc", final_normed, grad_outputs, preferred_element_type=f32)
+    final_weight_term = jnp.einsum("ikd,ikc->cd", final_normed, grad_outputs, preferred_element_type=f32)
     grad_final = jnp.einsum("ikc,dc->ikd", grad_outputs, final_full, preferred_element_type=f32)
     grad_resid, grad_final_shift, grad_final_scale = modulate_back(resid, final_scale, grad_final)
     final_mod_term = jnp.stack([grad_final_shift, grad_final_scale], axis=1)
 
-    mod_terms = [None] * depth
-    bias_terms = [None] * depth
-    token_terms = [None] * depth
+    block_sums, block_biases = [], []
     spread = [[None, None, None] for _ in range(depth)]
 
     def folded(source, inbox):
@@ -1529,114 +1783,99 @@
     def fold_mlp(terms, inboxes):
         return jnp.stack([folded(term, inbox) for term, inbox in zip(terms, inboxes)])
 
-    def fold_attention(terms, inboxes):
-        project_part = folded(terms[0], inboxes[0]).reshape(2, shard // 2, -1)
-        attend_part = terms[1].astype(f32) + jnp.sum(inboxes[1].astype(f32), axis=1)
-        return project_part, attend_part.astype(bf16).reshape(2, head_cols // 2, width)
-
-    attention_terms, waiting = None, []
+    def fold_project(term, inbox):
+        return folded(term, inbox).reshape(2, shard // 2, -1)
+
+    def fold_attend(term, inbox):
+        total = term.astype(f32) + jnp.sum(inbox.astype(f32), axis=1)
+        return total.astype(bf16).reshape(2, head_cols // 2, width)
+
+    attend_shape = (pieces_each, piece_rows, width)
+    project_term, waiting = None, []
     for b in reversed(range(depth)):
-        base, mid, attended, expanded, attention_weights, mlp_weights, keys, gate_rows, attention_saved, mlp_saved = records[b]
-        shift1, scale1, gate1, shift2, scale2, gate2 = pieces[b]
+        base, mid, attended, expanded, attention_weights, mlp_weights, attention_saved, mlp_saved = records[b]
         routed = b > 0
-        grad_after = grad_resid[:, :kept_local] if routed else grad_resid
-        tasks = []
-        if attention_terms is not None:
-            tasks = [Fold(attention_terms[0]), FoldTo(attention_terms[1], shard)]
+        tasks = [] if project_term is None else [Fold(project_term)]
         (grad_mid, mlp_sums, grad_expand, grad_shrink, grad_expand_bias), inboxes = mlp_backward(
-            grad_after,
-            mid,
-            expanded,
-            gate_rows,
-            jnp.concatenate([scale2, gate2], axis=1),
-            mlp_weights,
-            mlp_saved,
-            4 * b + 2,
-            tasks,
+            b, grad_resid, mid, expanded, kept_rows, vecs, mlp_weights, mlp_saved, 4 * b + 2, tasks
         )
         if tasks:
-            waiting += [(b + 1, n, part) for n, part in zip((1, 2), fold_attention(attention_terms, inboxes))]
+            waiting.append((b + 1, 1, fold_project(project_term, inboxes[0])))
         mlp_terms = [term.reshape(ranks, shard, hidden_cols) for term in (grad_expand, grad_shrink)]
-        tasks = [Fold(term) for term in mlp_terms] + [PlaneGather(part, late=1) for _, _, part in waiting]
+        tasks = [Fold(term) for term in mlp_terms] + [FoldTo(attend_shape, shard, 2)]
+        tasks += [PlaneGather(part, late=1) for _, _, part in waiting]
         (grad_base, attention_sums, grad_project, grad_attend, grad_project_bias), inboxes = attention_backward(
+            b,
+            attend_shape,
             grad_mid,
             base,
             attended,
-            gate_rows,
-            jnp.concatenate([scale1, gate1], axis=1),
+            kept_rows,
+            vecs,
             attention_weights,
-            keys[:, :, None],
+            key_bias[:, :, None],
             attention_saved,
             4 * b + 3,
             tasks,
         )
-        for (block, n, _), every in zip(waiting, inboxes[2:]):
+        for (block, n, _), every in zip(waiting, inboxes[3:]):
             spread[block][n] = every
-        waiting = [(b, 0, fold_mlp(mlp_terms, inboxes[:2]))]
-        attention_terms = (
-            unpad_heads(grad_project.reshape(width, 3, -1), 2).reshape(ranks, shard, 3 * head_cols),
-            unpad_heads(grad_attend, 0).reshape(pieces_each, piece_rows, width),
-        )
-        grad_bias = unpad_heads(grad_project_bias[0].reshape(3, -1), 1)
-        bias_terms[b] = jnp.concatenate([grad_bias[0], grad_bias[2], grad_expand_bias[0]])
-        token_terms[b] = jnp.sum(jnp.stack([attention_sums[:, 3], mlp_sums[:, 3]]), axis=1)
+        waiting = [(b, 0, fold_mlp(mlp_terms, inboxes[:2])), (b, 2, fold_attend(grad_attend, inboxes[2]))]
+        project_term = grad_project.reshape(ranks, shard, 3 * head_cols)
+        block_sums = [attention_sums, mlp_sums] + block_sums
+        block_biases = [grad_project_bias, grad_expand_bias] + block_biases
         grad_resid = jnp.concatenate([grad_base, grad_resid[:, kept_local:]], axis=1) if routed else grad_base
-        mod_terms[b] = jnp.concatenate([attention_sums[:, :3], mlp_sums[:, :3]], axis=1)
 
     patch_bias_term = jnp.sum(grad_resid, axis=(0, 1))
     grad_embed = grad_resid.astype(bf16)
     patch_term = jnp.einsum("ikc,ikd->cd", patches, grad_embed, preferred_element_type=f32)
-    grad_patches = jnp.einsum("ikd,cd->ikc", grad_embed, patch_full, preferred_element_type=f32)
-
-    mod_slices = [
-        term.reshape(images, team, -1) for term in mod_terms + [final_mod_term]
-    ]
-    mod_slices = jnp.concatenate(mod_slices, axis=2).transpose(1, 0, 2)
-    bias_row = jnp.tile(jnp.pad(final_bias_term, (0, shard - patch_out)), ranks)
-    token_rows = jnp.concatenate(
-        [patch_term, patch_bias_term[None], final_weight_term.T] + token_terms + [bias_row[None]], axis=0
-    )
-    row_count = token_rows.shape[0]
-    token_rows = jnp.pad(token_rows, ((0, -row_count % team), (0, 0)))
-    token_rows = token_rows.reshape(team, -1, ranks, shard).transpose(0, 2, 1, 3)
-    biases = pack_flat(bias_terms, 1024)
-    tokens_out = jnp.concatenate([outputs, grad_patches], axis=2).reshape(-1, LANES)
-    tasks = [Fold(attention_terms[0]), FoldTo(attention_terms[1], shard)]
-    tasks += [PlaneGather(part) for _, _, part in waiting]
+    grad_patches = jnp.einsum("ikd,cd->cik", grad_embed, patch_full, preferred_element_type=f32)
+
+    edge_rows = jnp.stack([patch_bias_term, jnp.pad(final_bias_term, (0, width - patch_out))])
+    tokens_out = jnp.concatenate([outputs, grad_patches], axis=0).reshape(patch_out + patch_in, -1)
+    tasks = [Fold(project_term)] + [PlaneGather(part) for _, _, part in waiting]
     (all_mods, all_sums, all_biases, all_tokens), inboxes = epilogue(
-        mod_slices, token_rows, biases, tokens_out, 10, tasks
-    )
-    for (block, n, _), every in zip(waiting, inboxes[2:]):
+        block_sums,
+        final_mod_term,
+        block_biases,
+        patch_term,
+        final_weight_term,
+        edge_rows,
+        tokens_out,
+        10,
+        tasks,
+    )
+    for (block, n, _), every in zip(waiting, inboxes[1:]):
         spread[block][n] = every
-    last_parts = fold_attention(attention_terms, inboxes[:2])
-
-    mod_every = all_mods.reshape(team, ranks * images, -1).transpose(1, 0, 2)
-    mod_width = adaptive_weight.shape[2]
-    block_mods = [
-        mod_every[:, :, b * mod_cols : (b + 1) * mod_cols].reshape(ranks * images, mod_width) for b in range(depth)
-    ]
-    final_mods = mod_every[:, :, depth * mod_cols :].reshape(ranks * images, -1)
+    last_part = fold_project(project_term, inboxes[0])
+
+    mod_every = all_mods.reshape(team, ranks * images, pair)
+    mod_width = 3 * pair
+    block_mods = jnp.stack(
+        [mod_every[3 * b : 3 * b + 3].transpose(1, 0, 2).reshape(ranks * images, mod_width) for b in range(depth)]
+    )
+    final_mods = mod_every[3 * depth]
     grad_silu = dot(final_mods, final_adaptive, NT)
     for b in range(depth):
         grad_silu = grad_silu + dot(block_mods[b], adaptive_weight[b], NT)
     grad_silu, last = closing(
-        grad_silu.reshape(ranks, images, shard), 11, [PlaneGather(part) for part in last_parts]
-    )
-    spread[0][1], spread[0][2] = last
+        grad_silu.reshape(ranks, images, shard), 11, [PlaneGather(last_part)]
+    )
+    spread[0][1] = last[0]
     grad_silu = grad_silu.transpose(1, 0, 2).reshape(images, width)
     conditioning_grad = jax.vjp(jax.nn.silu, conditioning.astype(f32))[1](grad_silu)[0]
-    adaptive_weight_grad = jnp.stack([dot(silu_rows, m, TN) for m in block_mods])
+    adaptive_weight_grad = adaptive_grad(silu_rows, block_mods)
     final_adaptive_grad = dot(silu_rows, final_mods, TN)
 
     def rank_part(full):
         part = full.shape[-1] // ranks
         return lax.dynamic_slice_in_dim(full, rank * part, part, axis=full.ndim - 1)
 
-    adaptive_bias_grad = rank_part(jnp.stack([jnp.sum(m.astype(f32), axis=0) for m in block_mods]))
+    adaptive_bias_grad = rank_part(jnp.sum(block_mods.astype(f32), axis=1))
     final_offset_grad = rank_part(jnp.sum(final_mods.astype(f32), axis=0))
 
-    ordered = all_tokens.reshape(team, images, tile_tokens, -1).transpose(1, 2, 0, 3)
-    ordered = ordered.reshape(images, sequence, patch_out + patch_in)
+    ordered = all_tokens.reshape(team, patch_out + patch_in, images, tile_tokens)
+    ordered = ordered.transpose(2, 3, 0, 1).reshape(images, sequence, patch_out + patch_in)
     tile_rows = lax.axis_index("row") * rows_tile + jnp.arange(rows_tile, dtype=jnp.int32)
     tile_cols = lax.axis_index("col") * cols_tile + jnp.arange(cols_tile, dtype=jnp.int32)
     tile_ids = (tile_rows[:, None] * grid_cols + tile_cols).reshape(-1)
@@ -1645,50 +1884,39 @@
     prediction = to_planes(tile_out[..., :patch_out], PATCH, channels_out, rows_tile, cols_tile)
     latent_grad = to_planes(tile_out[..., patch_out:], PATCH, channels_in, rows_tile, cols_tile)
 
-    def in_order(every):
-        split = every.reshape((2, team // 2) + every.shape[1:])
-        return jnp.swapaxes(split, 0, 1).reshape(every.shape)
-
-    project_grads, attend_grads, expand_grads, shrink_grads = [], [], [], []
-    for mlp_every, project_every, attend_every in spread:
-        mlp_every = in_order(mlp_every)
-        expand_grads.append(mlp_every[:, 0].transpose(1, 0, 2).reshape(shard, -1).astype(f32))
-        shrink_grads.append(mlp_every[:, 1].transpose(0, 2, 1).reshape(-1, shard).astype(f32))
-        project_every = in_order(project_every).reshape(team, shard, 3, head_cols)
-        project_grads.append(project_every.transpose(1, 2, 0, 3).reshape(shard, -1).astype(f32))
-        attend_every = in_order(attend_every).reshape(width, width)
-        attend_grads.append(lax.dynamic_slice_in_dim(attend_every, rank * shard, shard, axis=0).astype(f32))
-
-    sums = all_sums.reshape(-1, shard)
-    biases = all_biases.reshape(team, -1)[:, : depth * (2 * head_cols + hidden_cols)]
-    biases = biases.reshape(team, depth, -1).transpose(1, 0, 2)
-    project_bias_grad = jnp.concatenate(
-        [biases[:, :, part * head_cols : (part + 1) * head_cols].reshape(depth, width) for part in range(2)], axis=1
-    )
-    expand_bias_grad = biases[:, :, 2 * head_cols :].reshape(depth, -1)
-    first = patch_in + 1 + patch_out
-    block_sums = sums[first : first + 2 * depth].reshape(depth, 2, shard)
+    expand_weight_grad, shrink_weight_grad = mlp_unpack([parts[0] for parts in spread])
+    project_weight_grad = project_unpack([parts[1] for parts in spread])
+    attend_weight_grad = attend_unpack([parts[2] for parts in spread], rank, shard, pieces_each, piece_rows)
+
+    sums = lax.dynamic_slice_in_dim(all_sums.reshape(-1, width), rank * shard, shard, axis=1)
+    first = patch_in + patch_out
+    token_sums = sums[first + 2 : first + 2 + 2 * depth].reshape(depth, 2, shard)
+    final_bias_grad = all_sums.reshape(-1, width)[first + 1, :patch_out]
+    rows_of = all_biases.transpose(1, 0, 2)[: 2 * depth].reshape(depth, 2, team, -1)
+    expand_bias_grad = rows_of[:, 1, :, :hidden_cols].reshape(depth, -1)
+    head_rows = unpad_heads(rows_of[:, 0].reshape(depth, team, 3, -1), 3)
+    project_bias_grad = jnp.stack([head_rows[:, :, 0], head_rows[:, :, 2]], axis=1).reshape(depth, -1)
 
     return (
         prediction,
         latent_grad,
         conditioning_grad,
         sums[:patch_in],
-        sums[patch_in],
+        sums[first],
         adaptive_weight_grad,
         adaptive_bias_grad,
-        jnp.stack(project_grads),
+        project_weight_grad,
         rank_part(project_bias_grad),
-        jnp.stack(attend_grads),
-        block_sums[:, 0],
-        jnp.stack(expand_grads),
+        attend_weight_grad,
+        token_sums[:, 0],
+        expand_weight_grad,
         rank_part(expand_bias_grad),
-        jnp.stack(shrink_grads),
-        block_sums[:, 1],
+        shrink_weight_grad,
+        token_sums[:, 1],
         final_adaptive_grad,
         final_offset_grad,
-        sums[patch_in + 1 : first].T,
-        sums[first + 2 * depth, :patch_out],
+        sums[patch_in:first].T,
+        final_bias_grad,
     )
 
 

time: 975 us -> 783 us (0.80)
  local copies, waits for them, and re-layouts: 236 us -> 48.7 us
  Pallas kernels: 642 us -> 677 us
  other arithmetic: 58.1 us -> 27.1 us
    convert_element_type x25 -> x4, local copies, waits for them, and re-layouts: 64.7 us -> 0.12 us  [the longest x2 0.09 us: body(): project_offset.astype(f32).reshape(depth, 2, team, head_cols)]
    reshape x52 -> x13, local copies, waits for them, and re-layouts: 47.6 us -> 3.53 us  [the longest x3 1.18 us: body(): mods.reshape(team, images, 2, width).transpose(1, 0, 2, 3)]
    pallas_call x0 -> x4, Pallas kernels: none -> 33 us  [local_call(): pl.pallas_call(kernel, name=name, grid_spec=pltpu.PrefetchScalarGridSpec(...]
    another operation x28 -> x8, local copies, waits for them, and re-layouts: 31 us -> 0.38 us  [the longest x2 0.18 us: body(): jnp.stack([attend_offset, shrink_offset], axis=1).reshape(2 * depth, width)]
    another operation x7 -> x4, other arithmetic: 29 us -> 1.4 us  [the longest x1 0.71 us: body(): jnp.stack([mod_every[3 * b:3 * b + 3].transpose(1, 0, 2).reshape(ranks *...]
    slice x32 -> x14, local copies, waits for them, and re-layouts: 20.5 us -> 2.4 us  [the longest x1 0.67 us: body(): sums[first]]
    unnamed x138 -> x130, local copies, waits for them, and re-layouts: 24.4 us -> 19.7 us
where the time goes in v4:
time: 783 us; the launch traced here: 774 us
  Pallas kernels  677 us (86%)
  local copies, waits for them, and re-layouts  48.7 us (6%)
  other arithmetic  27.1 us (3%)
  matrix products  18.5 us (2%)
    pallas_call x12, Pallas kernels, call(): pl.pallas_call(run, name=name, out_shape=list(outs) + task_outs, in_specs...  644 us
    pallas_call x4, Pallas kernels, local_call(): pl.pallas_call(kernel, name=name, grid_spec=pltpu.PrefetchScalarGridSpec(...  33 us
    unnamed x130, local copies, waits for them, and re-layouts  19.7 us

profile of v4, /device:TPU:0, one launch (start us, length us, event | category | flops | bytes accessed | tf_op | source)
XLA Modules:
  0.0 773.9 jit_solution(12951315722451439248)
XLA Ops:
  0.7 1.7 constant_dynamic-slice_fusion.12
  8.6 19.6 %prologue.1 = (bf16[4,16,288]{2,1,0:T(8,128)(2,1)}, bf16[4,1,288]{2,1,0:T(2,128)(2,1)}, bf16[4,2,1728]{2,1,0:T(2,128)(2,1)}, bf16[4,2,576]{2,1,0:T(2,128)(2,1)},...) custom-call(bf16[16,288]{1,0:T(8,128)(2,1)} %refs_0_.1, ...), custom_call_target="tpu_custom_call" | custom-call | bytes 471744 | tf_op jit(solution)/shard_map/prologue/pallas_call | solution.py:600
  29.1 1.9 fusion.7
  32.6 27.5 %conditioning.1 = (f32[8,4,1152]{2,1,0:T(4,128)}, bf16[4,288,432]{2,1,0:T(8,128)(2,1)}, bf16[1,144,1152]{2,1,0:T(8,128)(2,1)}) custom-call(f32[4,4,1152]{2,1,0:T(4,128)} %reshape.438.refs_0_, bf16[288,432]{1,0:T(8,128)(2,1)} %get-tuple-element.263.refs_1_, bf16[1,144,1152]{2,1,0:T(8,128)(2,1)} %get-tuple-element.259.refs_2_), custom_call_target="tpu_custom_call" | custom-call | bytes 221184 | tf_op jit(solution)/shard_map/conditioning/pallas_call | solution.py:600
  65.7 1.4 fusion.6.refs_0_.refs_1_
  68.1 1.5 dynamic-slice_bitcast_fusion
  69.6 2.6 dynamic-slice_bitcast_fusion.1
  73.9 70.8 %attention_forward.2 = (bf16[2,8,128,1152]{3,2,1,0:T(8,128)(2,1)}, bf16[2,1024,768]{2,1,0:T(8,128)(2,1)}, bf16[2,1024,256]{2,1,0:T(8,128)(2,1)}, f32[2,2,4,256]{...) custom-call(f32[2,128,1152]{2,1,0:T(8,128)} %fusion.6.refs_0_.refs_1, ...), custom_call_target="tpu_custom_call" | custom-call | flops 28991029248 | bytes 16330496 | tf_op jit(solution)/shard_map/attention_forward/pallas_call | solution.py:600
  145.4 60.1 %mlp_forward.2 = (bf16[2,8,128,1152]{3,2,1,0:T(8,128)(2,1)}, f32[2,8,128,576]{3,2,1,0:T(8,128)}, f32[2,128,1152]{2,1,0:T(8,128)}, f32[2,128,1152]{2,1,0:T(8,128)...) custom-call(f32[2,128,1152]{2,1,0:T(8,128)} %get-tuple-element.116.refs_0_.refs_1_, ...), custom_call_target="tpu_custom_call" | custom-call | flops 32614907904 | bytes 15799296 | tf_op jit(solution)/shard_map/mlp_forward/pallas_call | solution.py:600
  205.5 53.4 %attention_forward.3 = (bf16[2,8,96,1152]{3,2,1,0:T(8,128)(2,1)}, bf16[2,768,768]{2,1,0:T(8,128)(2,1)}, bf16[2,768,256]{2,1,0:T(8,128)(2,1)}, f32[2,2,4,192]{3,2...) custom-call(f32[2,128,1152]{2,1,0:T(8,128)} %get-tuple-element.120.r, ...), custom_call_target="tpu_custom_call" | custom-call | flops 21743271936 | bytes 13508352 | tf_op jit(solution)/shard_map/attention_forward/pallas_call | solution.py:600
  258.9 41.5 %mlp_forward.3 = (bf16[2,8,96,1152]{3,2,1,0:T(8,128)(2,1)}, f32[2,8,96,576]{3,2,1,0:T(8,128)}, f32[2,96,1152]{2,1,0:T(8,128)}, f32[2,96,1152]{2,1,0:T(8,128)}) custom-call(f32[2,96,1152]{2,1,0:T(8,128)} %get-tuple-element.123.refs_0_.refs_1_, f32[2,96,1]{2,1,0:T(8,128)} %compare_convert_fusion.refs_1_.refs_3_, ...), custom_call_target="tpu_custom_call" | custom-call | flops 24461180928 | bytes 12555264 | tf_op jit(solution)/shard_map/mlp_forward/pallas_call | solution.py:600
  301.5 1.4 fusion.27
  303.9 1.2 multiply_reduce_fusion
  305.1 1.4 subtract_multiply_fusion.refs_0_
  306.5 43.6 %mlp_backward.2 = (f32[2,96,1152]{2,1,0:T(8,128)}, f32[2,8,1152]{2,1,0:T(8,128)}, bf16[1152,576]{1,0:T(8,128)(2,1)}, bf16[1152,576]{1,0:T(8,128)(2,1)}, f32[8,576]{1,0:T(8,128)}) custom-call(f32[2,128,1152]{2,1,0:T(8,128)} %subtract_multiply_fusion.refs_0_, f32[2,96,1152]{2,1,0:T(8,128)} %get-tuple-element.123.refs_0_.refs_1_, ...), custom_call_target="tpu_custom_call" | custom-call | flops 48922361856 | bytes 16478976 | tf_op jit(solution)/shard_map/mlp_backward/pallas_call | solution.py:600
  351.3 87.9 %attention_backward.2 = (f32[2,96,1152]{2,1,0:T(8,128)}, f32[2,8,1152]{2,1,0:T(8,128)}, bf16[1152,432]{1,0:T(8,128)(2,1)}, bf16[1,144,1152]{2,1,0:T(8,128)(2,1)}...) custom-call(f32[2,96,1152]{2,1,0:T(8,128)} %get-tuple-element.131.re, ...), custom_call_target="tpu_custom_call" | custom-call | flops 43486543872 | bytes 14488320 | tf_op jit(solution)/shard_map/attention_backward/pallas_call | solution.py:600
  439.2 2.3 pad_maximum_fusion.1.refs_0_
  441.5 53.8 %mlp_backward.3 = (f32[2,128,1152]{2,1,0:T(8,128)}, f32[2,8,1152]{2,1,0:T(8,128)}, bf16[1152,576]{1,0:T(8,128)(2,1)}, bf16[1152,576]{1,0:T(8,128)(2,1)}, f32[8,576]{1,0:T(8,128)}, /*index=5*/bf16[3,288,432]{2,1,0:T(8,128)(2,1)}) custom-call(f32[2,128,1152]{2,1,0:T(8,128)} %pad_maximum_fusion.1.refs_0_, f32[2,128,1152]{2,1,0:T(8,128)} %get-tuple-element.116.refs_0_.refs_1_, ...), custom_call_target="tpu_custom_call" | custom-call | flops 65229815808 | bytes 19723008 | tf_op jit(solution)/shard_map/mlp_backward/pallas_call | solution.py:600
  495.3 1.4 convert_reduce_fusion.7
  503.6 108.3 %attention_backward.3 = (f32[2,128,1152]{2,1,0:T(8,128)}, f32[2,8,1152]{2,1,0:T(8,128)}, bf16[1152,432]{1,0:T(8,128)(2,1)}, bf16[1,144,1152]{2,1,0:T(8,128)(2,1)...) custom-call(f32[2,128,1152]{2,1,0:T(8,128)} %get-tuple-element.146.r, ...), custom_call_target="tpu_custom_call" | custom-call | flops 57982058496 | bytes 17605376 | tf_op jit(solution)/shard_map/attention_backward/pallas_call | solution.py:600
  611.9 1.5 convert_reduce_fusion.4
  616.1 1.2 fusion.13
  623.8 58.3 %epilogue.1 = (bf16[8,4,4,1152]{3,2,1,0:T(4,128)(2,1)}, f32[8,7,1152]{2,1,0:T(8,128)}, f32[8,8,768]{2,1,0:T(8,128)}, f32[8,48,256]{2,1,0:T(8,128)}, bf16[3,288,4...) custom-call(f32[2,8,1152]{2,1,0:T(8,128)} %get-tuple-element.161.refs_0_, ...), custom_call_target="tpu_custom_call" | custom-call | bytes 1821696 | tf_op jit(solution)/shard_map/epilogue/pallas_call | solution.py:600
  682.1 14.7 %mlp_unpack.1 = (f32[2,288,4608]{2,1,0:T(8,128)}, f32[2,4608,288]{2,1,0:T(8,128)}) custom-call(bf16[2,4,2,288,576]{4,3,2,1,0:T(8,128)(2,1)} %bitcast.202, bf16[2,4,2,288,576]{4,3,2,1,0:T(8,128)(2,1)} %bitcast.201), custom_call_target="tpu_custom_call" | custom-call | bytes 31850496 | tf_op jit(solution)/shard_map/mlp_unpack/pallas_call | solution.py:1449
  696.8 12.7 %copy.124 = f32[2,4608,288]{1,2,0:T(8,128)} copy(f32[2,4608,288]{2,1,0:T(8,128)} %get-tuple-element.240) | data formatting | bytes 21233664
  709.5 3.9 attend_unpack.1
  716.7 3.2 fusion
  720.1 3.3 fusion.2
  724.6 19.6 %closing.1 = (f32[4,2,288]{2,1,0:T(2,128)}, bf16[8,2,144,432]{3,2,1,0:T(8,128)(2,1)}) custom-call(f32[4,2,288]{2,1,0:T(2,128)} %reshape.466.refs_0_, bf16[2,144,432]{2,1,0:T(8,128)(2,1)} %fusion.19.refs_1_), custom_call_target="tpu_custom_call" | custom-call | bytes 18432 | tf_op jit(solution)/shard_map/closing/pallas_call | solution.py:600
  744.2 6.5 project_unpack.1
  752.3 7.8 %adaptive_grad.1 = f32[2,288,6912]{2,1,0:T(8,128)} custom-call(bf16[8,288]{1,0:T(8,128)(2,1)} %copy-done.22, bf16[2,8,6912]{2,1,0:T(8,128)(2,1)} %pad_maximum_fusion.6.mods), custom_call_target="tpu_custom_call" | custom-call | bytes 15925248 | tf_op jit(solution)/shard_map/adaptive_grad/pallas_call | solution.py:1449
  760.9 2.1 fusion.56
  (284 shorter events, 53.6 us)
Async XLA Ops:
  3.6 3.1 copy-start.37
  3.6 3.9 copy-start.55
  3.6 4.4 copy-start.56
  3.6 25.5 %copy-start.3 = (bf16[288,2304]{1,0:T(8,128)(2,1)S(1)}, bf16[288,2304]{1,0:T(8,128)(2,1)}, u32[]{:S(2)}) copy-start(bf16[288,2304]{1,0:T(8,128)(2,1)} %param.37) | copy-start | bytes 3981316
  29.0 2.5 copy-start.14
  31.6 29.8 %copy-start.36 = (bf16[4,2,1728]{2,1,0:T(2,128)(2,1)S(1)}, bf16[4,2,1728]{2,1,0:T(2,128)(2,1)}, u32[]{:S(2)}) copy-start(bf16[4,2,1728]{2,1,0:T(2,128)(2,1)} %get-tuple-element.109) | copy-start | bytes 82948
  32.6 28.9 %copy-start.41 = (bf16[4,1,576]{2,1,0:T(2,128)(2,1)S(1)}, bf16[4,1,576]{2,1,0:T(2,128)(2,1)}, u32[]{:S(2)}) copy-start(bf16[4,1,576]{2,1,0:T(2,128)(2,1)} %get-tuple-element.110) | copy-start | bytes 13828
  32.6 29.1 %copy-start.50 = (bf16[4,2,288]{2,1,0:T(2,128)(2,1)S(1)}, bf16[4,2,288]{2,1,0:T(2,128)(2,1)}, u32[]{:S(2)}) copy-start(bf16[4,2,288]{2,1,0:T(2,128)(2,1)} %get-tuple-element.111) | copy-start | bytes 13828
  32.6 29.2 %copy-start.49 = (bf16[4,2,288]{2,1,0:T(2,128)(2,1)S(1)}, bf16[4,2,288]{2,1,0:T(2,128)(2,1)}, u32[]{:S(2)}) copy-start(bf16[4,2,288]{2,1,0:T(2,128)(2,1)} %get-tuple-element.112) | copy-start | bytes 13828
  60.1 2.6 copy-start.33
  60.1 3.0 copy-start.21
  64.1 239.7 %copy-start.27 = (bf16[2,128,48]{1,2,0:T(8,128)(2,1)}, bf16[2,128,48]{1,2,0:T(8,128)(2,1)S(1)}, u32[]{:S(2)}) copy-start(bf16[2,128,48]{1,2,0:T(8,128)(2,1)S(1)} %convolution_convert_fusion) | copy-start | bytes 73732
  69.6 2.8 copy-start.51
  73.2 71.5 %copy-start.31 = (s32[768]{0:T(1024)}, s32[768]{0:T(1024)S(1)}, u32[]{:S(2)}) copy-start(s32[768]{0:T(1024)S(1)} %add.319) | copy-start | bytes 9220
  73.9 70.8 %copy-start.38 = (bf16[4,2,1152]{2,1,0:T(2,128)(2,1)S(1)}, bf16[4,2,1152]{2,1,0:T(2,128)(2,1)}, u32[]{:S(2)}) copy-start(bf16[4,2,1152]{2,1,0:T(2,128)(2,1)} %get-tuple-element.118) | copy-start | bytes 55300
  300.4 2.5 copy-start.1
  301.5 3.6 copy-start.5
  301.5 2.4 copy-start.57
  306.5 43.7 %copy-start.32 = (s32[768]{0:T(1024)S(1)}, s32[768]{0:T(1024)}, u32[]{:S(2)}) copy-start(s32[768]{0:T(1024)} %copy-done.31) | copy-start | bytes 9220
  306.5 43.7 %copy-start.52 = (s32[2]{0:T(128)S(1)}, s32[2]{0:T(128)}, u32[]{:S(2)}) copy-start(s32[2]{0:T(128)} %param.24) | copy-start | bytes 28
  351.3 88.0 %slice-start = ((f32[2,128,1152]{2,1,0:T(8,128)}), f32[2,32,1152]{2,1,0:T(8,128)S(1)}, s32[]{:S(2)}) async-start(f32[2,128,1152]{2,1,0:T(8,128)} %subtract_multiply_fusion.refs_0_), calls=%async_computation | async-start | bytes 589824 | tf_op jit(solution)/shard_map/slice | solution.py:1827
  611.9 2.3 copy-start.10
  616.0 2.2 copy-start.59
  616.0 2.2 copy-start.2
  616.0 2.2 copy-start.6
  616.0 2.2 copy-start.30
  709.5 3.9 copy-start.25
  720.1 3.4 copy-start.4
  752.3 7.8 %copy-start.40 = (f32[4,2,288]{2,1,0:T(2,128)S(1)}, f32[4,2,288]{2,1,0:T(2,128)}, u32[]{:S(2)}) copy-start(f32[4,2,288]{2,1,0:T(2,128)} %get-tuple-element.178) | copy-start | bytes 27652
  752.3 7.9 %copy-start.39 = (bf16[2,1152]{1,0:T(2,128)(2,1)S(1)}, bf16[2,1152]{1,0:T(2,128)(2,1)}, u32[]{:S(2)}) copy-start(bf16[2,1152]{1,0:T(2,128)(2,1)} %refs_9_.1) | copy-start | bytes 13828
  752.3 8.5 %copy-start.23 = (bf16[8,288]{1,0:T(8,128)(2,1)S(1)}, bf16[8,288]{1,0:T(8,128)(2,1)}, u32[]{:S(2)}) copy-start(bf16[8,288]{1,0:T(8,128)(2,1)} %copy-done.22) | copy-start | bytes 13828
  765.3 3.6 copy-start.19
  (29 other events, 47.1 us)

commit v5 on v4

--- a/solution.py
+++ b/solution.py
@@ -255,9 +255,10 @@
 class Fold:
     reach = 2
 
-    def __init__(self, source):
+    def __init__(self, source, late=0):
         ranks = lax.axis_size("batch")
         self.ins = [source]
+        self.late = late
         self.outs = [jax.ShapeDtypeStruct((ranks - 1,) + source.shape[1:], source.dtype)]
         self.sems = [(ranks - 1,), (ranks - 1,)]
 
@@ -265,7 +266,6 @@
         (self.source,), (self.inbox,) = ins, outs
         self.send, self.recv = sems
         self.steps = 1
-        self.late = 0
 
     def copies(self):
         for n in range(lax.axis_size("batch") - 1):
@@ -286,18 +286,18 @@
 class FoldTo:
     reach = 2
 
-    def __init__(self, shape, shard, late):
+    def __init__(self, shape, shard, late, source=None):
         pieces, self.rows, width = shape
         others = lax.axis_size("batch") - 1
         self.shard = shard
-        self.ins = []
+        self.ins = [] if source is None else [source]
         self.outs = [jax.ShapeDtypeStruct((pieces, others, self.rows, width), bf16)]
         self.sems = [(pieces, others), (pieces, others)]
         self.late, self.pieces = late, pieces
 
     def bind(self, ins, outs, sems):
         (self.inbox,) = outs
-        self.source = None
+        self.source = ins[0] if ins else None
         self.send, self.recv = sems
         self.steps = 1
         self.rank, self.others = lax.axis_index("batch"), lax.axis_size("batch") - 1
@@ -368,8 +368,9 @@
     def first(self):
         own = self.whole("own")
         source = own if self.source is None else self.source
-        self.go(0, source, own, "x")
-        self.go(1, source, own, "y")
+        parts = [pl.ds(0, self.half), pl.ds(self.half, self.half)]
+        for slot, part, who in ((0, 0, "x"), (1, 1, "y"), (8, 1, "x"), (9, 0, "y")):
+            self.go(slot, source.at[parts[part]], self.part("own", part), who)
         self.go(2, source, own, "core")
 
     def second(self):
@@ -377,7 +378,9 @@
         self.go(3, self.part("x", 0), self.part("x", 0), "y")
         self.arrived(1)
         self.go(4, self.part("y", 1), self.part("y", 1), "x")
+        self.arrived(8)
         self.go(5, self.whole("x"), self.whole("x"), "core")
+        self.arrived(9)
         self.go(6, self.whole("y"), self.whole("y"), "core")
 
     def finish(self):
@@ -389,11 +392,12 @@
 class PlaneGather:
     reach = 0
 
-    def __init__(self, source, late=0):
+    def __init__(self, source, plan=(0, 1, 2)):
         self.ins = [source]
+        self.plan = plan
         self.outs = [jax.ShapeDtypeStruct((8,) + source.shape, source.dtype)]
-        self.sems = [(8,), (8,), (1,)]
-        self.late = late
+        self.sems = [(10,), (10,), (1,)]
+        self.late = 0
 
     def bind(self, ins, outs, sems):
         (self.source,), (self.target,) = ins, outs
@@ -423,21 +427,27 @@
     def __init__(self, tasks):
         self.tasks = tasks
         self.now = 0
+        self.done = [[] for _ in tasks]
 
     def partners(self):
         reach = max([task.reach for task in self.tasks], default=0)
         return [[], [rank_at(1), rank_at(-1)], other_ranks()][reach]
 
     def tick(self):
+        for task, done in zip(self.tasks, self.done):
+            plan = getattr(task, "plan", None) or range(task.late, task.late + task.steps)
+            if len(done) < task.steps and len(done) < len(plan) and plan[len(done)] <= self.now:
+                task.step(len(done))
+                done.append(self.now)
+        self.now += 1
+
+    def finish(self):
+        for most in range(max([task.steps for task in self.tasks], default=0)):
+            for task, done in zip(self.tasks, self.done):
+                if len(done) == most and most < task.steps:
+                    task.step(most)
+                    done.append(self.now)
         for task in self.tasks:
-            if 0 <= self.now - task.late < task.steps:
-                task.step(self.now - task.late)
-        self.now += 1
-
-    def finish(self):
-        for task in self.tasks:
-            for r in range(max(self.now - task.late, 0), task.steps):
-                task.step(r)
             task.finish()
 
 
@@ -498,8 +508,8 @@
         pltpu.VMEM((images, 4, length, width), f32),
         pltpu.VMEM((images, 6, half, width), bf16),
         pltpu.VMEM((images, 6, half, width), bf16),
-        pltpu.SemaphoreType.DMA((images, 8)),
-        pltpu.SemaphoreType.DMA((images, 8)),
+        pltpu.SemaphoreType.DMA((images, 10)),
+        pltpu.SemaphoreType.DMA((images, 10)),
         pltpu.SemaphoreType.DMA((images, 7)),
         pltpu.SemaphoreType.DMA((images, 7)),
     ]
@@ -573,8 +583,36 @@
     return grad_in, column_sum(grad), column_sum(grad * unit)
 
 
+class Far:
+    def __init__(self, what):
+        self.what = what
+
+
+class Copying:
+    def __init__(self, sems):
+        self.sems = sems
+        self.open = {}
+
+    def start(self, name, source, target):
+        copy = pltpu.make_async_copy(source, target, self.sems.at[len(self.open)])
+        copy.start()
+        self.open[name] = copy
+
+    def wait(self, *names):
+        for name in names:
+            self.open[name].wait()
+
+
+def scratch_like(array):
+    return pltpu.VMEM(array.shape, array.dtype)
+
+
 def call(kernel, name, ident, outs, scratch, flops, args, tasks=()):
     vmem, anywhere = pl.BlockSpec(memory_space=pltpu.VMEM), pl.BlockSpec(memory_space=pl.ANY)
+    in_specs = [anywhere if isinstance(a, Far) else vmem for a in args]
+    out_specs = [anywhere if isinstance(o, Far) else vmem for o in outs]
+    args = [a.what if isinstance(a, Far) else a for a in args]
+    outs = [o.what if isinstance(o, Far) else o for o in outs]
     moved = sum(a.size * a.dtype.itemsize for a in args) + sum(o.size * o.dtype.itemsize for o in outs)
     task_ins = [array for task in tasks for array in task.ins]
     task_outs = [shape for task in tasks for shape in task.outs]
@@ -601,8 +639,8 @@
         run,
         name=name,
         out_shape=list(outs) + task_outs,
-        in_specs=[vmem] * len(args) + [anywhere] * len(task_ins),
-        out_specs=[vmem] * len(outs) + [anywhere] * len(task_outs),
+        in_specs=in_specs + [anywhere] * len(task_ins),
+        out_specs=out_specs + [anywhere] * len(task_outs),
         scratch_shapes=list(scratch) + task_sems,
         compiler_params=pltpu.CompilerParams(
             collective_id=ident, has_side_effects=True, vmem_limit_bytes=60 * 2**20
@@ -617,41 +655,56 @@
 
 
 def prologue_kernel(background, *refs):
-    count = (len(refs) - 6) // 2
-    smalls, tiles = refs[:count], refs[count]
-    packs, every_tile = refs[count + 1 : 2 * count + 1], refs[2 * count + 1]
-    zs, zr, ps, pr = refs[2 * count + 2 :]
+    smalls = refs[:-8]
+    tiles, packs, every_tile, pack, zs, zr, ps, pr = refs[-8:]
+    lanes = pack.shape[1]
+    rows = []
+    for small in smalls:
+        value = small[...].astype(f32)
+        rows += [value[:, start : start + lanes] for start in range(0, value.shape[1], lanes)]
+    used = sum(value.shape[0] for value in rows)
+    if used < pack.shape[0]:
+        rows.append(jnp.zeros((pack.shape[0] - used, lanes), f32))
+    pack[...] = jnp.concatenate(rows, axis=0).astype(bf16)
     ranks, peers = other_ranks(), plane_peers()
     greet(ranks + peers)
     rank, place = lax.axis_index("batch"), team_place()
-    copies = [
-        remote(small, pack.at[rank], zs.at[m, n], zr.at[m, n], who)
-        for m, (small, pack) in enumerate(zip(smalls, packs))
-        for n, who in enumerate(ranks)
-    ] + [remote(tiles, every_tile.at[place], ps.at[n], pr.at[n], who) for n, who in enumerate(peers)]
+    copies = [remote(pack, packs.at[rank], zs.at[n], zr.at[n], who) for n, who in enumerate(ranks)]
+    for n, who in enumerate(peers):
+        copies.append(remote(tiles, every_tile.at[place], ps.at[n], pr.at[n], who))
     for copy in copies:
         copy.start()
-    for small, pack in zip(smalls, packs):
-        pack[rank] = small[...]
+    packs[rank] = pack[...]
     every_tile[place] = tiles[...]
     for copy in copies:
         copy.wait()
 
 
-def prologue(smalls, tiles, ident):
+def prologue(smalls, dims, tiles, ident):
     ranks = lax.axis_size("batch")
     dma = pltpu.SemaphoreType.DMA
-    (*packs, every_tile), _ = call(
+    lanes = min(small.shape[1] for small in smalls)
+    rows = sum(small.size // lanes for small in smalls)
+    pack = (rows + -rows % 16, lanes)
+    (packs, every_tile), _ = call(
         prologue_kernel,
         "prologue",
         ident,
-        [shaped((ranks,) + small.shape, small.dtype) for small in smalls]
-        + [shaped((8,) + tiles.shape, tiles.dtype)],
-        [dma((len(smalls), ranks - 1)), dma((len(smalls), ranks - 1)), dma((7,)), dma((7,))],
+        [shaped((ranks,) + pack, bf16), shaped((8,) + tiles.shape, tiles.dtype)],
+        [pltpu.VMEM(pack, bf16), dma((ranks - 1,)), dma((ranks - 1,)), dma((7,)), dma((7,))],
         0,
         (*smalls, tiles),
     )
-    return packs, every_tile
+    parts, start = [], 0
+    for small, dim in zip(smalls, dims):
+        count, each = small.shape[0], small.shape[1] // lanes
+        part = packs[:, start : start + count * each].reshape(ranks, each, count, lanes)
+        start += count * each
+        if dim == 0:
+            parts.append(part.transpose(0, 2, 1, 3).reshape(ranks * count, -1))
+        else:
+            parts.append(part.transpose(2, 0, 1, 3).reshape(count, -1))
+    return parts, every_tile
 
 
 def conditioning_kernel(background, parts, mods, inbox, zs, zr, ps, pr):
@@ -715,11 +768,15 @@
     block_sums, (final_sums,) = take(2 * depth), take(1)
     block_biases = take(2 * depth)
     patch_term, final_term, edge_rows, tokens = take(4)
-    all_mods, all_sums, all_biases, all_tokens = take(4)
+    all_mods, all_rows, all_tokens = take(3)
     mods, sums, biases, mods_in, sums_in, rank_mods, rank_sums, rank_biases_in, ps, pr, zs, zr, qs, qr = refs
     ranks, peers = other_ranks(), plane_peers()
-    rank, place = lax.axis_index("batch"), team_place()
-    cols = lax.axis_size("col")
+    rank = lax.axis_index("batch")
+    around = sides()
+    place = around[0] * 4 + around[1]["own"]
+    gather_tokens, gather_mods, gather_rows = [
+        Gather(full, qs.at[n], qr.at[n], around) for n, full in enumerate((all_tokens, all_mods, all_rows))
+    ]
     images = final_sums.shape[0]
     each = sums.shape[1]
 
@@ -749,21 +806,19 @@
         biases[n, : source.shape[1]] = source[0]
 
     greet(ranks + peers)
-    first, extra = [], []
+    first = []
     for n, who in enumerate(peers):
-        there = who["row"] * cols + who["col"]
+        there = lax.rem(who["col"], 2) * 4 + who["row"] * 2 + who["col"] // 2
         first.append(remote(mods.at[there], mods_in.at[n], ps.at[0, n], pr.at[0, n], who))
         first.append(remote(sums.at[there], sums_in.at[n], ps.at[1, n], pr.at[1, n], who))
-        extra.append(remote(tokens, all_tokens.at[place], ps.at[2, n], pr.at[2, n], who))
     second = [
         remote(biases, rank_biases_in.at[n], zs.at[0, n], zr.at[0, n], who) for n, who in enumerate(ranks)
     ]
     for copy in first + second:
         copy.start()
+    all_tokens[place] = tokens[...]
+    gather_tokens.first()
     background.tick()
-    for copy in extra:
-        copy.start()
-    all_tokens[place] = tokens[...]
     for copy in first:
         copy.wait()
     mod_total, sum_total = mods[place], sums[place]
@@ -789,17 +844,17 @@
     for n in range(1, rank_sums.shape[0]):
         sum_own = sum_own + rank_sums[n]
     all_mods[place] = rank_mods[...]
-    all_sums[place] = sum_own
-    all_biases[place] = bias_total
-    last = []
-    for n, who in enumerate(peers):
-        for m, target in enumerate((all_mods, all_sums, all_biases)):
-            last.append(remote(target.at[place], target.at[place], qs.at[m, n], qr.at[m, n], who))
-    for copy in last:
-        copy.start()
+    all_rows[place, 0, :each] = sum_own
+    all_rows[place, 1, :, : biases.shape[1]] = bias_total
+    gather_mods.first()
+    gather_rows.first()
+    gather_tokens.second()
     background.tick()
-    for copy in last + extra:
-        copy.wait()
+    for gather in (gather_mods, gather_rows):
+        gather.second()
+    for gather in (gather_tokens, gather_mods, gather_rows):
+        gather.finish()
+        gather.drain()
     background.finish()
 
 
@@ -819,8 +874,7 @@
         ident,
         [
             shaped((8, ranks) + mods[1:], bf16),
-            shaped(sums, f32),
-            shaped((8,) + biases, f32),
+            shaped((8, 2, 8, width), f32),
             shaped((8,) + tokens.shape, f32),
         ],
         [
@@ -832,12 +886,12 @@
             pltpu.VMEM((ranks,) + mods[1:], bf16),
             pltpu.VMEM((ranks,) + sums[1:], f32),
             pltpu.VMEM((ranks - 1,) + biases, f32),
-            dma((3, 7)),
-            dma((3, 7)),
+            dma((2, 7)),
+            dma((2, 7)),
             dma((3, ranks - 1)),
             dma((3, ranks - 1)),
-            dma((3, 7)),
-            dma((3, 7)),
+            dma((3, 10)),
+            dma((3, 10)),
         ],
         0,
         (*block_sums, final_sums, *block_biases, patch_term, final_term, edge_rows, tokens),
@@ -879,8 +933,11 @@
 
 
 def mlp_forward_kernel(
-    block, background, mid, gate_rows, vecs, expand, expand_bias, shrink, full, hidden, expanded, after, *comm
+    block, background, mid, gate_rows, vecs, pair_far, expand_bias, full_far, hidden_far, expanded, after,
+    full, hidden, pair, expand, shrink, moves, *comm
 ):
+    moving = Copying(moves)
+    moving.start("pair", pair_far, pair)
     place = sides()
     core, chips, address = place
     images = full.shape[0]
@@ -912,57 +969,78 @@
         expanded[i] = value
         after[i] = mid[i] + gate(i) * row(i, 6 * block + 5) * value
 
+    def keep(i):
+        moving.start(("full", i), full.at[i], full_far.at[i])
+        moving.start(("hidden", i), hidden.at[i], hidden_far.at[i])
+
     begin(0)
     background.tick()
+    moving.wait("pair")
+    expand[...] = pair[:, : expand.shape[1]]
+    shrink[...] = pair[:, expand.shape[1] :]
     gathers[0].second()
     begin(1)
     gathers[0].finish()
     compute(0, (gathers[1].second, scatters[0].first))
+    keep(0)
     background.tick()
     gathers[1].finish()
     compute(1, (scatters[0].second, scatters[1].first))
+    keep(1)
     background.tick()
     end(0)
     scatters[1].second()
     end(1)
     for part in gathers + scatters:
         part.drain()
+    moving.wait(*[(name, i) for name in ("full", "hidden") for i in range(images)])
     background.finish()
 
 
 def mlp_forward(block, mid, gate_rows, vecs, weights, ident, tasks=()):
-    expand, expand_bias, shrink = weights
+    pair, expand_bias = weights
     images, length, width = mid.shape
-    inner = expand.shape[1]
+    inner = pair.shape[1] // 2
     return call(
         partial(mlp_forward_kernel, block),
         "mlp_forward",
         ident,
         [
-            shaped((images, 8, length, width), bf16),
-            shaped((images, 8, length, inner), f32),
+            Far(shaped((images, 8, length, width), bf16)),
+            Far(shaped((images, 8, length, inner), f32)),
             shaped((images, length, width), f32),
             shaped((images, length, width), f32),
         ],
-        comm_scratch(images, length, width),
+        [
+            pltpu.VMEM((images, 8, length, width), bf16),
+            pltpu.VMEM((images, 8, length, inner), f32),
+            scratch_like(pair),
+            pltpu.VMEM((width, inner), bf16),
+            pltpu.VMEM((width, inner), bf16),
+            pltpu.SemaphoreType.DMA((1 + 2 * images,)),
+        ]
+        + comm_scratch(images, length, width),
         4 * images * 8 * length * width * inner * 6,
         (
             mid,
             gate_rows,
             vecs,
-            expand,
+            Far(pair),
             expand_bias.reshape(1, -1),
-            shrink,
         ),
         tasks,
     )
 
 
 def mlp_backward_kernel(
-    block, background, grad_after, mid, expanded, gate_rows, vecs, expand, shrink, normed, hidden,
-    grad_mid, sums, grad_expand, grad_shrink, grad_bias,
-    full, grad_hidden, active, sum_expand, sum_shrink, *comm
+    block, background, grad_after, mid, expanded, gate_rows, vecs, pair_far, normed_far, hidden_far,
+    grad_mid, sums, grad_pair, grad_bias,
+    full, grad_hidden, active, sum_expand, sum_shrink, pair, expand, shrink, normed, hidden, moves, *comm
 ):
+    moving = Copying(moves)
+    moving.start("pair", pair_far, pair)
+    moving.start("hidden", hidden_far, hidden)
+    moving.start("normed", normed_far, normed)
     place = sides()
     core, chips, address = place
     gathers, scatters = exchanges(full, comm, place)
@@ -1000,7 +1078,7 @@
         if i == 0:
             sum_shrink[...] = term
         else:
-            grad_shrink[...] = (sum_shrink[...] + term).astype(bf16)
+            sum_shrink[...] += term
 
     def weigh_expand(i):
         low = flat(grad_hidden[i])
@@ -1009,7 +1087,7 @@
             sum_expand[...] = term
             grad_bias[...] = row_sums(low)
         else:
-            grad_expand[...] = (sum_expand[...] + term).astype(bf16)
+            grad_pair[...] = jnp.concatenate([sum_expand[...] + term, sum_shrink[...]], axis=1).astype(bf16)
             grad_bias[...] += row_sums(low)
 
     def end(i):
@@ -1020,15 +1098,23 @@
 
     begin(0)
     background.tick()
+    moving.wait("pair")
+    expand[...] = pair[:, : expand.shape[1]]
+    shrink[...] = pair[:, expand.shape[1] :]
     gathers[0].second()
     begin(1)
     gathers[0].finish()
+    moving.wait("hidden")
     compute(0, (gathers[1].second, scatters[0].first))
+    background.tick()
     gathers[1].finish()
     compute(1, (scatters[0].second, scatters[1].first))
+    background.tick()
     weigh_shrink(0)
     end(0)
     scatters[1].second()
+    background.tick()
+    moving.wait("normed")
     weigh_expand(0)
     weigh_shrink(1)
     weigh_expand(1)
@@ -1039,10 +1125,10 @@
 
 
 def mlp_backward(block, grad_after, mid, expanded, gate_rows, vecs, weights, saved, ident, tasks=()):
-    expand, _, shrink = weights
+    pair, _ = weights
     normed, hidden = saved
     images, length, width = mid.shape
-    inner = expand.shape[1]
+    inner = pair.shape[1] // 2
     return call(
         partial(mlp_backward_kernel, block),
         "mlp_backward",
@@ -1050,8 +1136,7 @@
         [
             shaped((images, length, width), f32),
             shaped((images, 8, width), f32),
-            shaped((width, inner), bf16),
-            shaped((width, inner), bf16),
+            shaped((width, 2 * inner), bf16),
             shaped((8, inner), f32),
         ],
         [
@@ -1060,6 +1145,12 @@
             pltpu.VMEM((images, 8, length, inner), bf16),
             pltpu.VMEM((width, inner), f32),
             pltpu.VMEM((width, inner), f32),
+            scratch_like(pair),
+            pltpu.VMEM((width, inner), bf16),
+            pltpu.VMEM((width, inner), bf16),
+            scratch_like(normed),
+            scratch_like(hidden),
+            pltpu.SemaphoreType.DMA((3,)),
         ]
         + comm_scratch(images, length, width),
         8 * images * 8 * length * width * inner * 6,
@@ -1069,10 +1160,9 @@
             expanded,
             gate_rows,
             vecs,
-            expand,
-            shrink,
-            normed,
-            hidden,
+            Far(pair),
+            Far(normed),
+            Far(hidden),
         ),
         tasks,
     )
@@ -1116,8 +1206,10 @@
 
 def attention_forward_kernel(
     block, background, base, gate_rows, vecs, project_own, project_bias, attend_own, key_bias,
-    full, packed, mixed, log_total, attended, mid, project, attend, *comm
+    full_far, packed_far, mixed_far, log_total, attended, mid, project, attend,
+    full, packed, mixed, moves, *comm
 ):
+    moving = Copying(moves)
     place = sides()
     core, chips, address = place
     images, _, length, _ = full.shape
@@ -1178,6 +1270,13 @@
         attended[i] = value
         mid[i] = base[i, :length] + gate(i) * row(i, 6 * block + 2) * value
 
+    def nothing():
+        pass
+
+    def keep(i):
+        for name, near, far in (("full", full, full_far), ("packed", packed, packed_far), ("mixed", mixed, mixed_far)):
+            moving.start((name, i), near.at[i], far.at[i])
+
     begin(0)
     background.tick()
     project[...] = pad_lanes(project_own[...])
@@ -1186,13 +1285,17 @@
     begin(1)
     gathers[0].finish()
     compute(0, (gathers[1].second, background.tick, scatters[0].first))
+    keep(0)
     gathers[1].finish()
-    compute(1, (scatters[0].second, background.tick, scatters[1].first))
+    compute(1, (scatters[0].second, nothing, scatters[1].first))
+    keep(1)
+    background.tick()
     end(0)
     scatters[1].second()
     end(1)
     for part in gathers + scatters:
         part.drain()
+    moving.wait(*moving.open)
     background.finish()
 
 
@@ -1205,16 +1308,22 @@
         "attention_forward",
         ident,
         [
-            shaped((images, 8, length, width), bf16),
-            shaped((images, 8 * length, 3 * span), bf16),
-            shaped((images, 8 * length, span), bf16),
+            Far(shaped((images, 8, length, width), bf16)),
+            Far(shaped((images, 8 * length, 3 * span), bf16)),
+            Far(shaped((images, 8 * length, span), bf16)),
             shaped((images, span // LANES, 4, 2 * length), f32),
             shaped((images, length, width), f32),
             shaped((images, length, width), f32),
             shaped((width, 3 * span), bf16),
             shaped((span, width), bf16),
         ],
-        comm_scratch(images, length, width),
+        [
+            pltpu.VMEM((images, 8, length, width), bf16),
+            pltpu.VMEM((images, 8 * length, 3 * span), bf16),
+            pltpu.VMEM((images, 8 * length, span), bf16),
+            pltpu.SemaphoreType.DMA((3 * images,)),
+        ]
+        + comm_scratch(images, length, width),
         8 * images * 8 * length * width * span * 6,
         (
             base,
@@ -1230,10 +1339,17 @@
 
 
 def attention_backward_kernel(
-    block, background, grad_mid, base, attended, gate_rows, vecs, project, attend, key_bias, normed, packed, mixed, log_total,
+    block, background, grad_mid, base, attended, gate_rows, vecs, project_far, attend_far, key_bias, normed_far, packed_far, mixed_far, log_total,
     grad_base, sums, grad_project, grad_attend, grad_bias,
-    full, grad_mixed, grad_packed, grad_keys, grad_values, sum_project, sum_attend, *comm
+    full, grad_mixed, grad_packed, grad_keys, grad_values, sum_project, sum_attend,
+    project, attend, normed, packed, mixed, moves, *comm
 ):
+    moving = Copying(moves)
+    moving.start("attend", attend_far, attend)
+    moving.start("packed", packed_far, packed)
+    moving.start("mixed", mixed_far, mixed)
+    moving.start("project", project_far, project)
+    moving.start("normed", normed_far, normed)
     place = sides()
     core, chips, address = place
     images, _, length, _ = full.shape
@@ -1310,7 +1426,7 @@
         if i == 0:
             sum_attend[...] = term
         else:
-            grad_attend[...] = cut_rows(sum_attend[...] + term).astype(bf16).reshape(grad_attend.shape)
+            grad_attend[...] = cut_rows(sum_attend[...] + term).reshape(grad_attend.shape).astype(bf16)
 
     def weigh_project(i):
         low = grad_packed[i]
@@ -1331,13 +1447,13 @@
     def nothing():
         pass
 
-    def begin_extra():
-        gathers[1].second()
+    def finish_extra():
+        gathers[1].finish()
         background.tick()
 
     def early_attend():
-        weigh_attend(0)
-        weigh_attend(1)
+        for i in range(images):
+            weigh_attend(i)
         for task in background.tasks:
             if task.source is None:
                 task.source = grad_attend
@@ -1352,13 +1468,15 @@
     gathers[0].second()
     begin(1)
     gathers[0].finish()
-    compute(0, (begin_extra, gathers[1].finish, nothing))
+    moving.wait("attend", "packed", "mixed", "project", "normed")
+    compute(0, (gathers[1].second, finish_extra, nothing))
     scatters[0].first()
     compute(1, (early_attend, middle, background.tick))
     scatters[1].first()
     weigh_project(0)
     end(0)
     scatters[1].second()
+    background.tick()
     weigh_project(1)
     end(1)
     for part in gathers + scatters:
@@ -1393,6 +1511,12 @@
             pltpu.VMEM((tokens, LANES), f32),
             pltpu.VMEM((width, 3 * span), f32),
             pltpu.VMEM((span, width), f32),
+            scratch_like(project),
+            scratch_like(attend),
+            scratch_like(normed),
+            scratch_like(packed),
+            scratch_like(mixed),
+            pltpu.SemaphoreType.DMA((5,)),
         ]
         + comm_scratch(images, length, width),
         16 * images * 8 * length * width * span * 6,
@@ -1402,12 +1526,12 @@
             attended,
             gate_rows,
             vecs,
-            project,
-            attend,
+            Far(project),
+            Far(attend),
             key_bias,
-            normed,
-            packed,
-            mixed,
+            Far(normed),
+            Far(packed),
+            Far(mixed),
             log_total,
         ),
         tasks,
@@ -1432,13 +1556,6 @@
     split = array.reshape(shape[:axis] + (heads, LANES) + shape[axis + 1 :])
     kept = lax.slice_in_dim(split, 0, HEAD_SIZE, axis=axis + 1)
     return kept.reshape(shape[:axis] + (heads * HEAD_SIZE,) + shape[axis + 1 :])
-
-
-def join_ranks(pack, dim):
-    moved = jnp.moveaxis(pack, 0, dim)
-    shape = list(pack.shape[1:])
-    shape[dim] = -1
-    return moved.reshape(shape)
 
 
 def turn(block, own, step, last):
@@ -1464,26 +1581,28 @@
 
         @pl.when(pl.program_id(0) == k)
         def _(every=every):
-            parts = [[every[core, 0, n].astype(f32) for core in range(2)] for n in range(2)]
-            expand[0] = jnp.concatenate(parts[0], axis=1)
-            shrink[0] = jnp.concatenate([part.T for part in parts[1]], axis=0)
+            first, second = every[0, 0].astype(f32), every[1, 0].astype(f32)
+            inner = first.shape[1] // 2
+            expand[0] = jnp.concatenate([first[:, :inner], second[:, :inner]], axis=1)
+            shrink[0] = jnp.concatenate([first[:, inner:], second[:, inner:]], axis=1)
 
 
 def mlp_unpack(everys):
     depth = len(everys)
-    _, _, shard, inner = everys[0].shape
-    everys = [every.reshape(2, 4, 2, shard, inner) for every in everys]
-    block = (2, 1, 2, shard, inner)
+    _, _, half, pair = everys[0].shape
+    shard, inner = 2 * half, pair // 2
+    everys = [every.reshape(2, 4, shard, pair) for every in everys]
+    block = (2, 1, shard, pair)
     return local_call(
         mlp_unpack_kernel,
         "mlp_unpack",
         (depth, 4),
-        [pl.BlockSpec(block, lambda b, j, k=k: (0, turn(b, k, j, 3), 0, 0, 0)) for k in range(depth)],
+        [pl.BlockSpec(block, lambda b, j, k=k: (0, turn(b, k, j, 3), 0, 0)) for k in range(depth)],
         [
             pl.BlockSpec((1, shard, 2 * inner), lambda b, j: (b, 0, j)),
-            pl.BlockSpec((1, 2 * inner, shard), lambda b, j: (b, j, 0)),
+            pl.BlockSpec((1, shard, 2 * inner), lambda b, j: (b, 0, j)),
         ],
-        [shaped((depth, shard, 8 * inner), f32), shaped((depth, 8 * inner, shard), f32)],
+        [shaped((depth, shard, 8 * inner), f32), shaped((depth, shard, 8 * inner), f32)],
         depth * shard * inner * 96,
         everys,
     )
@@ -1624,7 +1743,7 @@
     def slice_of(array, axis, count):
         return lax.dynamic_slice_in_dim(array, place * count, count, axis=axis)
 
-    piece_rows = min(shard, head_cols)
+    piece_rows = min(shard, HEAD_SIZE)
     pieces_each = head_cols // piece_rows
     project_own = jnp.concatenate(
         [
@@ -1642,11 +1761,13 @@
         ],
         axis=1,
     )
-    expand_own = slice_of(expand_weight, 2, hidden_cols)
-    shrink_own = slice_of(shrink_weight, 1, hidden_cols).transpose(0, 2, 1)
+    pair_own = jnp.concatenate(
+        [slice_of(expand_weight, 2, hidden_cols), slice_of(shrink_weight, 1, hidden_cols).transpose(0, 2, 1)], axis=2
+    )
 
     smalls = [
         patch_weight,
+        final_weight.T,
         patch_bias[None],
         adaptive_bias,
         project_bias,
@@ -1654,16 +1775,16 @@
         expand_bias,
         shrink_bias,
         final_offset[None],
-        final_weight,
         conditioning,
     ]
     patch_tiles = to_tokens(latents, PATCH)
     grad_tiles = to_tokens(cotangent, PATCH)
     patch_in, patch_out = patch_tiles.shape[2], grad_tiles.shape[2]
     tiles = jnp.concatenate([patch_tiles, grad_tiles], axis=2)
-    packs, every_tile = prologue(smalls, tiles.reshape(-1, LANES), 8)
+    packs, every_tile = prologue(smalls, [1] * 9 + [0], tiles.reshape(-1, LANES), 8)
     (
         patch_full,
+        final_turned,
         patch_bias_full,
         adaptive_offset,
         project_offset,
@@ -1671,9 +1792,10 @@
         expand_offset,
         shrink_offset,
         final_offset_full,
-        final_full,
         cond_all,
-    ) = [join_ranks(pack, dim) for pack, dim in zip(packs, [1, 1, 1, 1, 1, 1, 1, 1, 0, 0])]
+    ) = packs
+    patch_bias_full, final_offset_full = patch_bias_full[0], final_offset_full[0]
+    final_full = final_turned.T
 
     whole = every_tile.reshape((rows, cols, images, rows_tile, cols_tile, -1)).transpose(2, 0, 3, 1, 4, 5)
     whole = whole.reshape(images, sequence, patch_in + patch_out)
@@ -1736,9 +1858,7 @@
         routed = b > 0
         length = kept_local if routed else tile_tokens
         base = resid
-        tasks = [Line(expand_own[b])]
-        if not routed:
-            tasks.append(Line(shrink_own[b]))
+        tasks = [Line(pair_own[b])]
         (*attention_saved, attended, mid, project, attend), gathered = attention_forward(
             b,
             length,
@@ -1750,17 +1870,15 @@
             4 * b,
             tasks,
         )
-        expand = gathered[0].reshape(width, hidden_cols)
-        shrink = (shrink_next if routed else gathered[1]).reshape(width, hidden_cols)
-        mlp_weights = (expand, hidden_biases[b], shrink)
+        mlp_weights = (gathered[0].reshape(width, 2 * hidden_cols), hidden_biases[b])
         tasks = []
         if b + 1 < depth:
-            tasks = [Line(project_own[b + 1]), Chain(attend_own[b + 1], shard), Line(shrink_own[b + 1])]
+            tasks = [Line(project_own[b + 1]), Chain(attend_own[b + 1], shard)]
         (*mlp_saved, expanded, after), gathered = mlp_forward(
             b, mid, kept_rows, vecs, mlp_weights, 4 * b + 1, tasks
         )
         if tasks:
-            project_next, attend_next, shrink_next = gathered
+            project_next, attend_next = gathered
         records.append((base, mid, attended, expanded, (project, attend), mlp_weights, attention_saved, mlp_saved))
         resid = jnp.concatenate([after, resid[:, kept_local:]], axis=1) if routed else after
 
@@ -1780,9 +1898,6 @@
         own = lax.dynamic_index_in_dim(source, rank, axis=0, keepdims=False)
         return (own.astype(f32) + jnp.sum(inbox.astype(f32), axis=0)).astype(bf16)
 
-    def fold_mlp(terms, inboxes):
-        return jnp.stack([folded(term, inbox) for term, inbox in zip(terms, inboxes)])
-
     def fold_project(term, inbox):
         return folded(term, inbox).reshape(2, shard // 2, -1)
 
@@ -1791,19 +1906,28 @@
         return total.astype(bf16).reshape(2, head_cols // 2, width)
 
     attend_shape = (pieces_each, piece_rows, width)
-    project_term, waiting = None, []
+    project_term = None
     for b in reversed(range(depth)):
         base, mid, attended, expanded, attention_weights, mlp_weights, attention_saved, mlp_saved = records[b]
         routed = b > 0
-        tasks = [] if project_term is None else [Fold(project_term)]
-        (grad_mid, mlp_sums, grad_expand, grad_shrink, grad_expand_bias), inboxes = mlp_backward(
+        tasks = []
+        if project_term is not None:
+            tasks = [Fold(project_term), FoldTo(attend_shape, shard, 0, grad_attend)]
+        (grad_mid, mlp_sums, grad_pair, grad_expand_bias), inboxes = mlp_backward(
             b, grad_resid, mid, expanded, kept_rows, vecs, mlp_weights, mlp_saved, 4 * b + 2, tasks
         )
-        if tasks:
-            waiting.append((b + 1, 1, fold_project(project_term, inboxes[0])))
-        mlp_terms = [term.reshape(ranks, shard, hidden_cols) for term in (grad_expand, grad_shrink)]
-        tasks = [Fold(term) for term in mlp_terms] + [FoldTo(attend_shape, shard, 2)]
-        tasks += [PlaneGather(part, late=1) for _, _, part in waiting]
+        mlp_term = grad_pair.reshape(ranks, shard, 2 * hidden_cols)
+        waiting = []
+        early = b == 0
+        tasks = [Fold(mlp_term)] + ([FoldTo(attend_shape, shard, 2)] if early else [])
+        if project_term is not None:
+            waiting = [
+                (b + 1, 0, mlp_part),
+                (b + 1, 1, fold_project(project_term, inboxes[0])),
+                (b + 1, 2, fold_attend(grad_attend, inboxes[1])),
+            ]
+        folds = len(tasks)
+        tasks += [PlaneGather(part, plan) for (_, _, part), plan in zip(waiting, ((1, 3), (3, 5), (5,)))]
         (grad_base, attention_sums, grad_project, grad_attend, grad_project_bias), inboxes = attention_backward(
             b,
             attend_shape,
@@ -1818,9 +1942,11 @@
             4 * b + 3,
             tasks,
         )
-        for (block, n, _), every in zip(waiting, inboxes[3:]):
+        for (block, n, _), every in zip(waiting, inboxes[folds:]):
             spread[block][n] = every
-        waiting = [(b, 0, fold_mlp(mlp_terms, inboxes[:2])), (b, 2, fold_attend(grad_attend, inboxes[2]))]
+        mlp_part = folded(mlp_term, inboxes[0]).reshape(2, shard // 2, -1)
+        if early:
+            waiting = [(b, 0, mlp_part), (b, 2, fold_attend(grad_attend, inboxes[1]))]
         project_term = grad_project.reshape(ranks, shard, 3 * head_cols)
         block_sums = [attention_sums, mlp_sums] + block_sums
         block_biases = [grad_project_bias, grad_expand_bias] + block_biases
@@ -1832,9 +1958,9 @@
     grad_patches = jnp.einsum("ikd,cd->cik", grad_embed, patch_full, preferred_element_type=f32)
 
     edge_rows = jnp.stack([patch_bias_term, jnp.pad(final_bias_term, (0, width - patch_out))])
-    tokens_out = jnp.concatenate([outputs, grad_patches], axis=0).reshape(patch_out + patch_in, -1)
-    tasks = [Fold(project_term)] + [PlaneGather(part) for _, _, part in waiting]
-    (all_mods, all_sums, all_biases, all_tokens), inboxes = epilogue(
+    tokens_out = jnp.concatenate([outputs, grad_patches], axis=0).reshape(2, (patch_out + patch_in) // 2, -1)
+    tasks = [Fold(project_term, late=1)] + [PlaneGather(part, (0, 2)) for _, _, part in waiting]
+    (all_mods, all_rows, all_tokens), inboxes = epilogue(
         block_sums,
         final_mod_term,
         block_biases,
@@ -1874,7 +2000,11 @@
     adaptive_bias_grad = rank_part(jnp.sum(block_mods.astype(f32), axis=1))
     final_offset_grad = rank_part(jnp.sum(final_mods.astype(f32), axis=0))
 
-    ordered = all_tokens.reshape(team, patch_out + patch_in, images, tile_tokens)
+    def in_order(every):
+        split = every.reshape((2, team // 2) + every.shape[1:])
+        return jnp.swapaxes(split, 0, 1).reshape(every.shape)
+
+    ordered = in_order(all_tokens).reshape(team, patch_out + patch_in, images, tile_tokens)
     ordered = ordered.transpose(2, 3, 0, 1).reshape(images, sequence, patch_out + patch_in)
     tile_rows = lax.axis_index("row") * rows_tile + jnp.arange(rows_tile, dtype=jnp.int32)
     tile_cols = lax.axis_index("col") * cols_tile + jnp.arange(cols_tile, dtype=jnp.int32)
@@ -1888,13 +2018,17 @@
     project_weight_grad = project_unpack([parts[1] for parts in spread])
     attend_weight_grad = attend_unpack([parts[2] for parts in spread], rank, shard, pieces_each, piece_rows)
 
-    sums = lax.dynamic_slice_in_dim(all_sums.reshape(-1, width), rank * shard, shard, axis=1)
     first = patch_in + patch_out
+    each = -(-(first + 2 + 2 * depth) // team)
+    all_sums = all_rows[:, 0, :each].reshape(-1, width)
+    all_biases = in_order(all_rows[:, 1])
+    sums = lax.dynamic_slice_in_dim(all_sums, rank * shard, shard, axis=1)
     token_sums = sums[first + 2 : first + 2 + 2 * depth].reshape(depth, 2, shard)
-    final_bias_grad = all_sums.reshape(-1, width)[first + 1, :patch_out]
+    final_bias_grad = all_sums[first + 1, :patch_out]
     rows_of = all_biases.transpose(1, 0, 2)[: 2 * depth].reshape(depth, 2, team, -1)
     expand_bias_grad = rows_of[:, 1, :, :hidden_cols].reshape(depth, -1)
-    head_rows = unpad_heads(rows_of[:, 0].reshape(depth, team, 3, -1), 3)
+    head_rows = rows_of[:, 0, :, : 3 * head_cols // HEAD_SIZE * LANES]
+    head_rows = unpad_heads(head_rows.reshape(depth, team, 3, -1), 3)
     project_bias_grad = jnp.stack([head_rows[:, :, 0], head_rows[:, :, 2]], axis=1).reshape(depth, -1)
 
     return (
@@ -1911,7 +2045,7 @@
         token_sums[:, 0],
         expand_weight_grad,
         rank_part(expand_bias_grad),
-        shrink_weight_grad,
+        shrink_weight_grad.transpose(0, 2, 1),
         token_sums[:, 1],
         final_adaptive_grad,
         final_offset_grad,

time: 783 us -> 692 us (0.88)
  Pallas kernels: 677 us -> 600 us
  local copies, waits for them, and re-layouts: 48.7 us -> 35.7 us
    pallas_call x12, Pallas kernels: 644 us -> 567 us  [call(): pl.pallas_call(run, name=name, out_shape=list(outs) + task_outs, in_specs...]
    unnamed x130 -> x107, local copies, waits for them, and re-layouts: 19.7 us -> 5.63 us
where the time goes in v5:
time: 692 us; the launch traced here: 682 us
  Pallas kernels  600 us (87%)
  local copies, waits for them, and re-layouts  35.7 us (5%)
  other arithmetic  25.3 us (4%)
  matrix products  18.4 us (3%)
    pallas_call x12, Pallas kernels, call(): pl.pallas_call(run, name=name, out_shape=list(outs) + task_outs, in_specs...  567 us
    pallas_call x4, Pallas kernels, local_call(): pl.pallas_call(kernel, name=name, grid_spec=pltpu.PrefetchScalarGridSpec(...  33.5 us

profile of v5, /device:TPU:0, one launch (start us, length us, event | category | flops | bytes accessed | tf_op | source)
XLA Modules:
  0.0 681.8 jit_solution(7652315905278030552)
XLA Ops:
  0.7 1.7 constant_dynamic-slice_fusion.13
  9.0 14.8 %prologue.1 = (bf16[4,96,288]{2,1,0:T(8,128)(2,1)}, bf16[8,96,128]{2,1,0:T(8,128)(2,1)}) custom-call(bf16[16,288]{1,0:T(8,128)(2,1)} %refs_0_.1, bf16[32,288]{1,0:T(8,128)(2,1)} %bitcast.252, bf16[1,288]{1,0:T(2,128)(2,1)} %broadcast_in_dim.18.refs_2_, bf16[2,1728]{1,0:T(2,128)(2,1)} %refs_3_.1, bf16[2,576]{1,0:T(2,128)(2,1)} %refs_4_.1, ...), custom_call_target="tpu_custom_call" | custom-call | bytes 492480 | tf_op jit(solution)/shard_map/prologue/pallas_call | solution.py:638
  25.0 1.7 fusion.9
  27.4 29.6 %conditioning.1 = (f32[8,4,1152]{2,1,0:T(4,128)}, bf16[4,288,432]{2,1,0:T(8,128)(2,1)}, bf16[2,72,1152]{2,1,0:T(8,128)(2,1)}) custom-call(f32[4,4,1152]{2,1,0:T(4,128)} %reshape.435.refs_0_, bf16[288,432]{1,0:T(8,128)(2,1)} %get-tuple-element.231.refs_1_, bf16[2,72,1152]{2,1,0:T(8,128)(2,1)} %get-tuple-element.229.refs_2_), custom_call_target="tpu_custom_call" | custom-call | bytes 221184 | tf_op jit(solution)/shard_map/conditioning/pallas_call | solution.py:638
  62.6 1.4 fusion.6.refs_0_.refs_1_
  65.0 1.5 constant_dynamic-slice_fusion.9
  66.5 1.5 dynamic-slice_bitcast_fusion
  68.0 1.5 fusion.18
  71.2 63.7 %attention_forward.2 = (bf16[2,8,128,1152]{3,2,1,0:T(8,128)(2,1)}, bf16[2,1024,768]{2,1,0:T(8,128)(2,1)}, bf16[2,1024,256]{2,1,0:T(8,128)(2,1)}, f32[2,2,4,256]{...) custom-call(f32[2,128,1152]{2,1,0:T(8,128)} %fusion.6.refs_0_.refs_1, ...), custom_call_target="tpu_custom_call" | custom-call | flops 28991029248 | bytes 16330496 | tf_op jit(solution)/shard_map/attention_forward/pallas_call | solution.py:638
  135.7 46.3 %mlp_forward.2 = (bf16[2,8,128,1152]{3,2,1,0:T(8,128)(2,1)}, f32[2,8,128,576]{3,2,1,0:T(8,128)}, f32[2,128,1152]{2,1,0:T(8,128)}, f32[2,128,1152]{2,1,0:T(8,128)...) custom-call(f32[2,128,1152]{2,1,0:T(8,128)} %get-tuple-element.93.refs_0_.refs_1_, ...), custom_call_target="tpu_custom_call" | custom-call | flops 32614907904 | bytes 15799296 | tf_op jit(solution)/shard_map/mlp_forward/pallas_call | solution.py:638
  182.0 55.3 %attention_forward.3 = (bf16[2,8,96,1152]{3,2,1,0:T(8,128)(2,1)}, bf16[2,768,768]{2,1,0:T(8,128)(2,1)}, bf16[2,768,256]{2,1,0:T(8,128)(2,1)}, f32[2,2,4,192]{3,2...) custom-call(f32[2,128,1152]{2,1,0:T(8,128)} %get-tuple-element.95.re, ...), custom_call_target="tpu_custom_call" | custom-call | flops 21743271936 | bytes 13508352 | tf_op jit(solution)/shard_map/attention_forward/pallas_call | solution.py:638
  237.3 36.1 %mlp_forward.3 = (bf16[2,8,96,1152]{3,2,1,0:T(8,128)(2,1)}, f32[2,8,96,576]{3,2,1,0:T(8,128)}, f32[2,96,1152]{2,1,0:T(8,128)}, f32[2,96,1152]{2,1,0:T(8,128)}) custom-call(f32[2,96,1152]{2,1,0:T(8,128)} %get-tuple-element.98.refs_0_.refs_1_, f32[2,96,1]{2,1,0:T(8,128)} %compare_convert_fusion.refs_1_.refs_3_, ...), custom_call_target="tpu_custom_call" | custom-call | flops 24461180928 | bytes 12555264 | tf_op jit(solution)/shard_map/mlp_forward/pallas_call | solution.py:638
  274.5 1.4 fusion.30
  277.1 1.2 multiply_reduce_fusion
  278.3 1.4 subtract_multiply_fusion.refs_0_
  279.7 39.2 %mlp_backward.2 = (f32[2,96,1152]{2,1,0:T(8,128)}, f32[2,8,1152]{2,1,0:T(8,128)}, bf16[1152,1152]{1,0:T(8,128)(2,1)}, f32[8,576]{1,0:T(8,128)}) custom-call(f32[2,128,1152]{2,1,0:T(8,128)} %subtract_multiply_fusion.refs_0_, f32[2,96,1152]{2,1,0:T(8,128)} %get-tuple-element.98.refs_0_.refs_1_, f32[2,96,1152]{2,1,0:T(8,128)} %get-tuple-element.101.refs_2_, ...), custom_call_target="tpu_custom_call" | custom-call | flops 48922361856 | bytes 16478976 | tf_op jit(solution)/shard_map/mlp_backward/pallas_call | solution.py:638
  320.1 59.6 %attention_backward.2 = (f32[2,96,1152]{2,1,0:T(8,128)}, f32[2,8,1152]{2,1,0:T(8,128)}, bf16[1152,432]{1,0:T(8,128)(2,1)}, bf16[2,72,1152]{2,1,0:T(8,128)(2,1)},...) custom-call(f32[2,96,1152]{2,1,0:T(8,128)} %get-tuple-element.104.refs_0_, ...), custom_call_target="tpu_custom_call" | custom-call | flops 43486543872 | bytes 14488320 | tf_op jit(solution)/shard_map/attention_backward/pallas_call | solution.py:638
  379.7 2.3 pad_maximum_fusion.1.refs_0_
  382.0 53.4 %mlp_backward.3 = (f32[2,128,1152]{2,1,0:T(8,128)}, f32[2,8,1152]{2,1,0:T(8,128)}, bf16[1152,1152]{1,0:T(8,128)(2,1)}, f32[8,576]{1,0:T(8,128)}, bf16[3,288,432]...) custom-call(f32[2,128,1152]{2,1,0:T(8,128)} %pad_maximum_fusion.1.refs_0_, ...), custom_call_target="tpu_custom_call" | custom-call | flops 65229815808 | bytes 19723008 | tf_op jit(solution)/shard_map/mlp_backward/pallas_call | solution.py:638
  435.3 1.5 convert_reduce_fusion.3
  440.0 1.1 constant_dynamic-slice_fusion.8
  442.2 96.2 %attention_backward.3 = (f32[2,128,1152]{2,1,0:T(8,128)}, f32[2,8,1152]{2,1,0:T(8,128)}, bf16[1152,432]{1,0:T(8,128)(2,1)}, bf16[2,72,1152]{2,1,0:T(8,128)(2,1)}...) custom-call(f32[2,128,1152]{2,1,0:T(8,128)} %get-tuple-element.119.r, ...), custom_call_target="tpu_custom_call" | custom-call | flops 57982058496 | bytes 17605376 | tf_op jit(solution)/shard_map/attention_backward/pallas_call | solution.py:638
  538.4 1.6 convert_reduce_fusion.2
  549.0 56.6 %epilogue.1 = (bf16[8,4,4,1152]{3,2,1,0:T(4,128)(2,1)}, f32[8,2,8,1152]{3,2,1,0:T(8,128)}, f32[8,2,24,256]{3,2,1,0:T(8,128)}, bf16[3,288,432]{2,1,0:T(8,128)(2,1...) custom-call(f32[2,8,1152]{2,1,0:T(8,128)} %get-tuple-element.131.refs_0_, ...), custom_call_target="tpu_custom_call" | custom-call | bytes 1956864 | tf_op jit(solution)/shard_map/epilogue/pallas_call | solution.py:638
  605.6 13.1 %mlp_unpack.1 = (f32[2,288,4608]{2,1,0:T(8,128)}, f32[2,288,4608]{2,1,0:T(8,128)}) custom-call(bf16[2,4,288,1152]{3,2,1,0:T(8,128)(2,1)} %bitcast.208, bf16[2,4,288,1152]{3,2,1,0:T(8,128)(2,1)} %bitcast.207), custom_call_target="tpu_custom_call" | custom-call | bytes 31850496 | tf_op jit(solution)/shard_map/mlp_unpack/pallas_call | solution.py:1566
  618.7 6.1 attend_unpack.1
  628.1 3.2 fusion
  631.5 3.3 fusion.2
  636.0 15.9 %closing.1 = (f32[4,2,288]{2,1,0:T(2,128)}, bf16[8,2,144,432]{3,2,1,0:T(8,128)(2,1)}) custom-call(f32[4,2,288]{2,1,0:T(2,128)} %reshape.461.refs_0_, bf16[2,144,432]{2,1,0:T(8,128)(2,1)} %fusion.19.refs_1_), custom_call_target="tpu_custom_call" | custom-call | bytes 18432 | tf_op jit(solution)/shard_map/closing/pallas_call | solution.py:638
  651.9 6.5 project_unpack.1
  660.0 7.8 %adaptive_grad.1 = f32[2,288,6912]{2,1,0:T(8,128)} custom-call(bf16[8,288]{1,0:T(8,128)(2,1)} %copy-done.21, bf16[2,8,6912]{2,1,0:T(8,128)(2,1)} %pad_maximum_fusion.6.mods), custom_call_target="tpu_custom_call" | custom-call | bytes 15925248 | tf_op jit(solution)/shard_map/adaptive_grad/pallas_call | solution.py:1566
  668.6 2.1 fusion.60
  (277 shorter events, 50.9 us)
Async XLA Ops:
  3.8 1.7 copy-start.34
  4.8 3.1 copy-start.46
  4.8 3.7 copy-start.47
  5.0 19.9 %copy-start.3 = (bf16[288,2304]{1,0:T(8,128)(2,1)S(1)}, bf16[288,2304]{1,0:T(8,128)(2,1)}, u32[]{:S(2)}) copy-start(bf16[288,2304]{1,0:T(8,128)(2,1)} %param.37) | copy-start | bytes 3981316
  24.9 1.8 copy-start.21
  26.7 31.5 %copy-start.18 = (bf16[4,96,288]{2,1,0:T(8,128)(2,1)S(1)}, bf16[4,96,288]{2,1,0:T(8,128)(2,1)}, u32[]{:S(2)}) copy-start(bf16[4,96,288]{2,1,0:T(8,128)(2,1)} %get-tuple-element.89) | copy-start | bytes 663556
  57.0 2.6 copy-start.32
  58.1 2.0 copy-start.20
  61.0 216.0 %copy-start.26 = (bf16[2,128,48]{1,2,0:T(8,128)(2,1)}, bf16[2,128,48]{1,2,0:T(8,128)(2,1)S(1)}, u32[]{:S(2)}) copy-start(bf16[2,128,48]{1,2,0:T(8,128)(2,1)S(1)} %convolution_convert_fusion) | copy-start | bytes 73732
  68.0 1.6 copy-start.42
  70.5 64.3 %copy-start.30 = (s32[768]{0:T(1024)}, s32[768]{0:T(1024)S(1)}, u32[]{:S(2)}) copy-start(s32[768]{0:T(1024)S(1)} %add.321) | copy-start | bytes 9220
  273.4 2.5 copy-start.1
  274.5 3.8 copy-start.5
  275.9 2.4 copy-start.37
  276.2 2.1 copy-start.44
  279.7 39.3 %copy-start.31 = (s32[768]{0:T(1024)S(1)}, s32[768]{0:T(1024)}, u32[]{:S(2)}) copy-start(s32[768]{0:T(1024)} %copy-done.30) | copy-start | bytes 9220
  279.7 39.3 %copy-start.43 = (s32[2]{0:T(128)S(1)}, s32[2]{0:T(128)}, u32[]{:S(2)}) copy-start(s32[2]{0:T(128)} %param.24) | copy-start | bytes 28
  320.1 59.6 %slice-start = ((f32[2,128,1152]{2,1,0:T(8,128)}), f32[2,32,1152]{2,1,0:T(8,128)S(1)}, s32[]{:S(2)}) async-start(f32[2,128,1152]{2,1,0:T(8,128)} %subtract_multiply_fusion.refs_0_), calls=%async_computation | async-start | bytes 589824 | tf_op jit(solution)/shard_map/slice | solution.py:1953
  435.3 1.5 copy-start.14
  435.3 2.3 copy-start.10
  437.7 2.1 copy-start.7
  538.3 1.6 copy-start.15
  538.4 2.4 copy-start.8
  546.5 1.9 copy-start.40
  546.5 1.9 copy-start.39
  618.7 6.1 copy-start.11
  626.1 1.8 copy-start.19
  631.5 3.4 copy-start.4
  660.0 7.8 %copy-start.36 = (f32[4,2,288]{2,1,0:T(2,128)S(1)}, f32[4,2,288]{2,1,0:T(2,128)}, u32[]{:S(2)}) copy-start(f32[4,2,288]{2,1,0:T(2,128)} %get-tuple-element.147) | copy-start | bytes 27652
  660.0 7.9 %copy-start.35 = (bf16[2,1152]{1,0:T(2,128)(2,1)S(1)}, bf16[2,1152]{1,0:T(2,128)(2,1)}, u32[]{:S(2)}) copy-start(bf16[2,1152]{1,0:T(2,128)(2,1)} %refs_9_.1) | copy-start | bytes 13828
  660.0 8.5 %copy-start.22 = (bf16[8,288]{1,0:T(8,128)(2,1)S(1)}, bf16[8,288]{1,0:T(8,128)(2,1)}, u32[]{:S(2)}) copy-start(bf16[8,288]{1,0:T(8,128)(2,1)} %copy-done.21) | copy-start | bytes 13828
  668.6 2.1 copy-start.12
  (18 other events, 23.4 us)

commit v6 on v5

--- a/solution.py
+++ b/solution.py
@@ -655,8 +655,11 @@
 
 
 def prologue_kernel(background, *refs):
-    smalls = refs[:-8]
-    tiles, packs, every_tile, pack, zs, zr, ps, pr = refs[-8:]
+    smalls = refs[:-21]
+    (
+        cond, pair_weight, tiles, packs, every_tile, silu_rows, mods,
+        pack, cond_in, parts, parts_in, zs, zr, ps, pr, cs, cr, qs, qr, ms, mr,
+    ) = refs[-21:]
     lanes = pack.shape[1]
     rows = []
     for small in smalls:
@@ -669,31 +672,84 @@
     ranks, peers = other_ranks(), plane_peers()
     greet(ranks + peers)
     rank, place = lax.axis_index("batch"), team_place()
+    first = [remote(cond.at[who["batch"]], cond_in.at[rank], cs.at[n], cr.at[n], who) for n, who in enumerate(ranks)]
     copies = [remote(pack, packs.at[rank], zs.at[n], zr.at[n], who) for n, who in enumerate(ranks)]
     for n, who in enumerate(peers):
         copies.append(remote(tiles, every_tile.at[place], ps.at[n], pr.at[n], who))
-    for copy in copies:
+    for copy in first + copies:
         copy.start()
+    cond_in[rank] = cond[rank]
     packs[rank] = pack[...]
     every_tile[place] = tiles[...]
-    for copy in copies:
+    for copy in first:
         copy.wait()
 
-
-def prologue(smalls, dims, tiles, ident):
-    ranks = lax.axis_size("batch")
+    count, images, width = cond_in.shape[0], cond_in.shape[1], parts.shape[2]
+    value = jnp.concatenate([cond_in[z].astype(f32) for z in range(count)], axis=0)
+    low = (value / (1.0 + jnp.exp(-value))).astype(bf16)
+    silu_rows[...] = low
+    value = dot(low, pair_weight[...], NN)
+    for z in range(count):
+        for i in range(images):
+            n = z * images + i
+            for p in range(2):
+                parts[z, i * 2 + p] = value[n, p * width : (p + 1) * width]
+    second = [
+        remote(parts.at[who["batch"]], parts_in.at[n], qs.at[n], qr.at[n], who) for n, who in enumerate(ranks)
+    ]
+    for copy in second:
+        copy.start()
+    background.tick()
+    total = parts[rank]
+    for n, copy in enumerate(second):
+        copy.wait()
+        total = total + parts_in[n]
+    mods[place] = total
+    third = [
+        remote(mods.at[place], mods.at[place], ms.at[n], mr.at[n], who) for n, who in enumerate(peers)
+    ]
+    for copy in third:
+        copy.start()
+    background.tick()
+    for copy in copies + third:
+        copy.wait()
+    background.finish()
+
+
+def prologue(smalls, dims, cond, pair_weight, tiles, ident, tasks):
+    ranks, images, _ = cond.shape
     dma = pltpu.SemaphoreType.DMA
     lanes = min(small.shape[1] for small in smalls)
     rows = sum(small.size // lanes for small in smalls)
     pack = (rows + -rows % 16, lanes)
-    (packs, every_tile), _ = call(
+    width = pair_weight.shape[1] // 2
+    part = (2 * images, width)
+    others = [dma((ranks - 1,)), dma((ranks - 1,))]
+    seven = [dma((7,)), dma((7,))]
+    (packs, every_tile, silu_rows, mods), gathered = call(
         prologue_kernel,
         "prologue",
         ident,
-        [shaped((ranks,) + pack, bf16), shaped((8,) + tiles.shape, tiles.dtype)],
-        [pltpu.VMEM(pack, bf16), dma((ranks - 1,)), dma((ranks - 1,)), dma((7,)), dma((7,))],
+        [
+            shaped((ranks,) + pack, bf16),
+            shaped((8,) + tiles.shape, tiles.dtype),
+            shaped((ranks * images, cond.shape[2]), bf16),
+            shaped((8,) + part, f32),
+        ],
+        [
+            pltpu.VMEM(pack, bf16),
+            pltpu.VMEM(cond.shape, bf16),
+            pltpu.VMEM((ranks,) + part, f32),
+            pltpu.VMEM((ranks - 1,) + part, f32),
+        ]
+        + others
+        + seven
+        + others
+        + others
+        + seven,
         0,
-        (*smalls, tiles),
+        (*smalls, cond, pair_weight, tiles),
+        tasks,
     )
     parts, start = [], 0
     for small, dim in zip(smalls, dims):
@@ -704,55 +760,7 @@
             parts.append(part.transpose(0, 2, 1, 3).reshape(ranks * count, -1))
         else:
             parts.append(part.transpose(2, 0, 1, 3).reshape(count, -1))
-    return parts, every_tile
-
-
-def conditioning_kernel(background, parts, mods, inbox, zs, zr, ps, pr):
-    ranks, peers = other_ranks(), plane_peers()
-    greet(ranks + peers)
-    rank, place = lax.axis_index("batch"), team_place()
-    first = [
-        remote(parts.at[who["batch"]], inbox.at[n], zs.at[n], zr.at[n], who) for n, who in enumerate(ranks)
-    ]
-    for copy in first:
-        copy.start()
-    background.tick()
-    total = parts[rank]
-    for n, copy in enumerate(first):
-        copy.wait()
-        total = total + inbox[n]
-    mods[place] = total
-    second = [
-        remote(mods.at[place], mods.at[place], ps.at[n], pr.at[n], who) for n, who in enumerate(peers)
-    ]
-    for copy in second:
-        copy.start()
-    background.tick()
-    for copy in second:
-        copy.wait()
-    background.finish()
-
-
-def conditioning_exchange(parts, ident, tasks):
-    ranks = parts.shape[0]
-    dma = pltpu.SemaphoreType.DMA
-    (mods,), gathered = call(
-        conditioning_kernel,
-        "conditioning",
-        ident,
-        [shaped((8,) + parts.shape[1:], f32)],
-        [
-            pltpu.VMEM((ranks - 1,) + parts.shape[1:], f32),
-            dma((ranks - 1,)),
-            dma((ranks - 1,)),
-            dma((7,)),
-            dma((7,)),
-        ],
-        0,
-        (parts,),
-        tasks,
-    )
-    return mods, gathered
+    return parts, every_tile, silu_rows, mods, gathered
 
 
 def epilogue_kernel(
@@ -848,10 +856,9 @@
     all_rows[place, 1, :, : biases.shape[1]] = bias_total
     gather_mods.first()
     gather_rows.first()
-    gather_tokens.second()
+    for gather in (gather_tokens, gather_mods, gather_rows):
+        gather.second()
     background.tick()
-    for gather in (gather_mods, gather_rows):
-        gather.second()
     for gather in (gather_tokens, gather_mods, gather_rows):
         gather.finish()
         gather.drain()
@@ -973,8 +980,8 @@
         moving.start(("full", i), full.at[i], full_far.at[i])
         moving.start(("hidden", i), hidden.at[i], hidden_far.at[i])
 
+    background.tick()
     begin(0)
-    background.tick()
     moving.wait("pair")
     expand[...] = pair[:, : expand.shape[1]]
     shrink[...] = pair[:, expand.shape[1] :]
@@ -1096,8 +1103,8 @@
         sums[i, 0:1] = shift_sum
         sums[i, 1:2] = scale_sum
 
+    background.tick()
     begin(0)
-    background.tick()
     moving.wait("pair")
     expand[...] = pair[:, : expand.shape[1]]
     shrink[...] = pair[:, expand.shape[1] :]
@@ -1277,8 +1284,8 @@
         for name, near, far in (("full", full, full_far), ("packed", packed, packed_far), ("mixed", mixed, mixed_far)):
             moving.start((name, i), near.at[i], far.at[i])
 
+    background.tick()
     begin(0)
-    background.tick()
     project[...] = pad_lanes(project_own[...])
     attend[...] = pad_rows(attend_own[...])
     gathers[0].second()
@@ -1447,8 +1454,8 @@
     def nothing():
         pass
 
-    def finish_extra():
-        gathers[1].finish()
+    def begin_extra():
+        gathers[1].second()
         background.tick()
 
     def early_attend():
@@ -1463,20 +1470,19 @@
         scatters[0].second()
         background.tick()
 
+    background.tick()
     begin(0)
-    background.tick()
     gathers[0].second()
     begin(1)
     gathers[0].finish()
     moving.wait("attend", "packed", "mixed", "project", "normed")
-    compute(0, (gathers[1].second, finish_extra, nothing))
+    compute(0, (begin_extra, gathers[1].finish, nothing))
     scatters[0].first()
     compute(1, (early_attend, middle, background.tick))
     scatters[1].first()
     weigh_project(0)
     end(0)
     scatters[1].second()
-    background.tick()
     weigh_project(1)
     end(1)
     for part in gathers + scatters:
@@ -1647,27 +1653,36 @@
 
         @pl.when(pl.program_id(0) == k)
         def _(every=every):
-            attend[0, 0] = every[0, 0].astype(f32)
+            cores, _, pieces = every.shape[:3]
+            for n in range(attend.shape[1]):
+                attend[0, n] = every[n // pieces, 0, n % pieces].astype(f32)
 
 
 def attend_unpack(everys, rank, shard, pieces, rows):
     depth = len(everys)
     width = everys[0].shape[-1]
-    everys = [every.reshape(8, pieces, rows, width) for every in everys]
+    everys = [every.reshape(2, 4, pieces, rows, width) for every in everys]
     steps = shard // rows
-
-    def chosen(b, i, ranks, k):
-        g = ranks[0] * steps + i
-        d = g // pieces
-        own = b == k
-        return jnp.where(own, d % 2 * 4 + d // 2, 0), jnp.where(own, g % pieces, 0), 0, 0
+    if steps == 2 * pieces:
+        block, count = (2, 1, pieces, rows, width), steps
+
+        def chosen(b, i, ranks):
+            return 0, ranks[0], 0, 0, 0
+
+    else:
+        block, count = (1, 1, 1, rows, width), 1
+
+        def chosen(b, i, ranks):
+            g = ranks[0] * steps + i
+            d = g // pieces
+            return d % 2, d // 2, g % pieces, 0, 0
 
     (attend,) = local_call(
         attend_unpack_kernel,
         "attend_unpack",
-        (depth, steps),
-        [pl.BlockSpec((1, 1, rows, width), partial(chosen, k=k)) for k in range(depth)],
-        [pl.BlockSpec((1, 1, rows, width), lambda b, i, ranks: (b, i, 0, 0))],
+        (depth, steps // count),
+        [pl.BlockSpec(block, chosen) for _ in range(depth)],
+        [pl.BlockSpec((1, count, rows, width), lambda b, i, ranks: (b, i, 0, 0))],
         [shaped((depth, steps, rows, width), f32)],
         depth * shard * width * 6,
         [rank.reshape(1), *everys],
@@ -1775,13 +1790,24 @@
         expand_bias,
         shrink_bias,
         final_offset[None],
-        conditioning,
     ]
     patch_tiles = to_tokens(latents, PATCH)
     grad_tiles = to_tokens(cotangent, PATCH)
     patch_in, patch_out = patch_tiles.shape[2], grad_tiles.shape[2]
     tiles = jnp.concatenate([patch_tiles, grad_tiles], axis=2)
-    packs, every_tile = prologue(smalls, [1] * 9 + [0], tiles.reshape(-1, LANES), 8)
+    pair = 2 * width
+    block_of = jnp.minimum(place // 3, depth - 1)
+    pair_weight = lax.dynamic_slice(adaptive_weight, (block_of, 0, place % 3 * pair), (1, shard, pair))[0]
+    pair_weight = jnp.where(place < 3 * depth, pair_weight, final_adaptive)
+    packs, every_tile, silu_rows, mods, (project_next, attend_next) = prologue(
+        smalls,
+        [1] * 9,
+        conditioning.reshape(images, ranks, shard).transpose(1, 0, 2),
+        pair_weight,
+        tiles.reshape(-1, LANES),
+        8,
+        [Line(project_own[0]), Chain(attend_own[0], shard)],
+    )
     (
         patch_full,
         final_turned,
@@ -1792,7 +1818,6 @@
         expand_offset,
         shrink_offset,
         final_offset_full,
-        cond_all,
     ) = packs
     patch_bias_full, final_offset_full = patch_bias_full[0], final_offset_full[0]
     final_full = final_turned.T
@@ -1831,16 +1856,6 @@
         + position
     )
 
-    silu_all = jax.nn.silu(cond_all.astype(f32)).astype(bf16)
-    silu_rows = lax.dynamic_slice_in_dim(silu_all, rank * shard, shard, axis=1)
-    pair = 2 * width
-    block_of = jnp.minimum(place // 3, depth - 1)
-    pair_weight = lax.dynamic_slice(adaptive_weight, (block_of, 0, place % 3 * pair), (1, shard, pair))[0]
-    pair_weight = jnp.where(place < 3 * depth, pair_weight, final_adaptive)
-    parts = dot(silu_rows, pair_weight, NN).reshape(ranks, images * 2, width)
-    mods, (project_next, attend_next) = conditioning_exchange(
-        parts, 9, [Line(project_own[0]), Chain(attend_own[0], shard)]
-    )
     mods = mods.reshape(team, images, 2, width).transpose(1, 0, 2, 3).reshape(images, 2 * team, width)
     offsets = [adaptive_offset.reshape(6 * depth, width), final_offset_full.reshape(2, width)]
     mods = mods[:, : 6 * depth + 2] + jnp.concatenate(offsets, axis=0).astype(f32)
@@ -1927,7 +1942,7 @@
                 (b + 1, 2, fold_attend(grad_attend, inboxes[1])),
             ]
         folds = len(tasks)
-        tasks += [PlaneGather(part, plan) for (_, _, part), plan in zip(waiting, ((1, 3), (3, 5), (5,)))]
+        tasks += [PlaneGather(part, (1, 3)) for _, _, part in waiting]
         (grad_base, attention_sums, grad_project, grad_attend, grad_project_bias), inboxes = attention_backward(
             b,
             attend_shape,
@@ -1959,7 +1974,7 @@
 
     edge_rows = jnp.stack([patch_bias_term, jnp.pad(final_bias_term, (0, width - patch_out))])
     tokens_out = jnp.concatenate([outputs, grad_patches], axis=0).reshape(2, (patch_out + patch_in) // 2, -1)
-    tasks = [Fold(project_term, late=1)] + [PlaneGather(part, (0, 2)) for _, _, part in waiting]
+    tasks = [Fold(project_term, late=1)] + [PlaneGather(part, plan) for (_, _, part), plan in zip(waiting, ((0, 2), (2,)))]
     (all_mods, all_rows, all_tokens), inboxes = epilogue(
         block_sums,
         final_mod_term,

time: 692 us -> 680 us (0.983)
  Pallas kernels: 600 us -> 586 us
    pallas_call x12 -> x11, Pallas kernels: 567 us -> 555 us  [call(): pl.pallas_call(run, name=name, out_shape=list(outs) + task_outs, in_specs...]
where the time goes in v6:
time: 680 us; the launch traced here: 670 us
  Pallas kernels  586 us (86%)
  local copies, waits for them, and re-layouts  37.8 us (6%)
  other arithmetic  27.8 us (4%)
  matrix products  16.6 us (2%)
    pallas_call x11, Pallas kernels, call(): pl.pallas_call(run, name=name, out_shape=list(outs) + task_outs, in_specs...  555 us
    pallas_call x4, Pallas kernels, local_call(): pl.pallas_call(kernel, name=name, grid_spec=pltpu.PrefetchScalarGridSpec(...  30.6 us

profile of v6, /device:TPU:0, one launch (start us, length us, event | category | flops | bytes accessed | tf_op | source)
XLA Modules:
  0.0 670.3 jit_solution(2438562014463952736)
XLA Ops:
  0.7 1.7 constant_dynamic-slice_fusion.14
  5.2 2.7 bitcast_select_fusion.refs_10_
  12.9 38.0 %prologue.1 = (bf16[4,80,288]{2,1,0:T(8,128)(2,1)}, bf16[8,96,128]{2,1,0:T(8,128)(2,1)}, bf16[8,288]{1,0:T(8,128)(2,1)}, f32[8,4,1152]{2,1,0:T(4,128)}, bf16[4,2...) custom-call(bf16[16,288]{1,0:T(8,128)(2,1)} %refs_0_.1, bf16[32,288]{1,0:T(8,128)(2,1)} %bitcast.253, ...), custom_call_target="tpu_custom_call" | custom-call | bytes 1934784 | tf_op jit(solution)/shard_map/prologue/pallas_call | solution.py:638
  60.0 1.4 fusion.6.refs_0_.refs_1_
  61.3 1.5 constant_dynamic-slice_fusion.9
  62.8 1.5 dynamic-slice_bitcast_fusion
  64.4 1.5 fusion.15
  67.6 63.9 %attention_forward.2 = (bf16[2,8,128,1152]{3,2,1,0:T(8,128)(2,1)}, bf16[2,1024,768]{2,1,0:T(8,128)(2,1)}, bf16[2,1024,256]{2,1,0:T(8,128)(2,1)}, f32[2,2,4,256]{...) custom-call(f32[2,128,1152]{2,1,0:T(8,128)} %fusion.6.refs_0_.refs_1, ...), custom_call_target="tpu_custom_call" | custom-call | flops 28991029248 | bytes 16330496 | tf_op jit(solution)/shard_map/attention_forward/pallas_call | solution.py:638
  132.4 46.3 %mlp_forward.2 = (bf16[2,8,128,1152]{3,2,1,0:T(8,128)(2,1)}, f32[2,8,128,576]{3,2,1,0:T(8,128)}, f32[2,128,1152]{2,1,0:T(8,128)}, f32[2,128,1152]{2,1,0:T(8,128)...) custom-call(f32[2,128,1152]{2,1,0:T(8,128)} %get-tuple-element.94.refs_0_.refs_1_, ...), custom_call_target="tpu_custom_call" | custom-call | flops 32614907904 | bytes 15799296 | tf_op jit(solution)/shard_map/mlp_forward/pallas_call | solution.py:638
  178.7 55.0 %attention_forward.3 = (bf16[2,8,96,1152]{3,2,1,0:T(8,128)(2,1)}, bf16[2,768,768]{2,1,0:T(8,128)(2,1)}, bf16[2,768,256]{2,1,0:T(8,128)(2,1)}, f32[2,2,4,192]{3,2...) custom-call(f32[2,128,1152]{2,1,0:T(8,128)} %get-tuple-element.96.re, ...), custom_call_target="tpu_custom_call" | custom-call | flops 21743271936 | bytes 13508352 | tf_op jit(solution)/shard_map/attention_forward/pallas_call | solution.py:638
  233.8 36.1 %mlp_forward.3 = (bf16[2,8,96,1152]{3,2,1,0:T(8,128)(2,1)}, f32[2,8,96,576]{3,2,1,0:T(8,128)}, f32[2,96,1152]{2,1,0:T(8,128)}, f32[2,96,1152]{2,1,0:T(8,128)}) custom-call(f32[2,96,1152]{2,1,0:T(8,128)} %get-tuple-element.99.refs_0_.refs_1_, f32[2,96,1]{2,1,0:T(8,128)} %compare_convert_fusion.refs_1_.refs_3_, ...), custom_call_target="tpu_custom_call" | custom-call | flops 24461180928 | bytes 12555264 | tf_op jit(solution)/shard_map/mlp_forward/pallas_call | solution.py:638
  270.9 1.4 fusion.27
  273.5 1.2 multiply_reduce_fusion
  274.8 1.4 subtract_multiply_fusion.refs_0_
  276.2 39.0 %mlp_backward.2 = (f32[2,96,1152]{2,1,0:T(8,128)}, f32[2,8,1152]{2,1,0:T(8,128)}, bf16[1152,1152]{1,0:T(8,128)(2,1)}, f32[8,576]{1,0:T(8,128)}) custom-call(f32[2,128,1152]{2,1,0:T(8,128)} %subtract_multiply_fusion.refs_0_, f32[2,96,1152]{2,1,0:T(8,128)} %get-tuple-element.99.refs_0_.refs_1_, f32[2,96,1152]{2,1,0:T(8,128)} %get-tuple-element.102.refs_2_, ...), custom_call_target="tpu_custom_call" | custom-call | flops 48922361856 | bytes 16478976 | tf_op jit(solution)/shard_map/mlp_backward/pallas_call | solution.py:638
  316.3 59.7 %attention_backward.2 = (f32[2,96,1152]{2,1,0:T(8,128)}, f32[2,8,1152]{2,1,0:T(8,128)}, bf16[1152,432]{1,0:T(8,128)(2,1)}, bf16[2,72,1152]{2,1,0:T(8,128)(2,1)},...) custom-call(f32[2,96,1152]{2,1,0:T(8,128)} %get-tuple-element.105.refs_0_, ...), custom_call_target="tpu_custom_call" | custom-call | flops 43486543872 | bytes 14488320 | tf_op jit(solution)/shard_map/attention_backward/pallas_call | solution.py:638
  376.0 2.3 pad_maximum_fusion.1.refs_0_
  378.3 53.0 %mlp_backward.3 = (f32[2,128,1152]{2,1,0:T(8,128)}, f32[2,8,1152]{2,1,0:T(8,128)}, bf16[1152,1152]{1,0:T(8,128)(2,1)}, f32[8,576]{1,0:T(8,128)}, bf16[3,288,432]...) custom-call(f32[2,128,1152]{2,1,0:T(8,128)} %pad_maximum_fusion.1.refs_0_, ...), custom_call_target="tpu_custom_call" | custom-call | flops 65229815808 | bytes 19723008 | tf_op jit(solution)/shard_map/mlp_backward/pallas_call | solution.py:638
  431.3 1.5 convert_reduce_fusion.3
  436.0 1.1 constant_dynamic-slice_fusion.8
  438.2 93.7 %attention_backward.3 = (f32[2,128,1152]{2,1,0:T(8,128)}, f32[2,8,1152]{2,1,0:T(8,128)}, bf16[1152,432]{1,0:T(8,128)(2,1)}, bf16[2,72,1152]{2,1,0:T(8,128)(2,1)}...) custom-call(f32[2,128,1152]{2,1,0:T(8,128)} %get-tuple-element.120.r, ...), custom_call_target="tpu_custom_call" | custom-call | flops 57982058496 | bytes 17605376 | tf_op jit(solution)/shard_map/attention_backward/pallas_call | solution.py:638
  531.9 1.6 convert_reduce_fusion.2
  534.6 1.1 constant_dynamic-slice_fusion.6
  542.5 53.2 %epilogue.1 = (bf16[8,4,4,1152]{3,2,1,0:T(4,128)(2,1)}, f32[8,2,8,1152]{3,2,1,0:T(8,128)}, f32[8,2,24,256]{3,2,1,0:T(8,128)}, bf16[3,288,432]{2,1,0:T(8,128)(2,1...) custom-call(f32[2,8,1152]{2,1,0:T(8,128)} %get-tuple-element.132.refs_0_, ...), custom_call_target="tpu_custom_call" | custom-call | bytes 1956864 | tf_op jit(solution)/shard_map/epilogue/pallas_call | solution.py:638
  595.7 13.1 %mlp_unpack.1 = (f32[2,288,4608]{2,1,0:T(8,128)}, f32[2,288,4608]{2,1,0:T(8,128)}) custom-call(bf16[2,4,288,1152]{3,2,1,0:T(8,128)(2,1)} %bitcast.208, bf16[2,4,288,1152]{3,2,1,0:T(8,128)(2,1)} %bitcast.207), custom_call_target="tpu_custom_call" | custom-call | bytes 31850496 | tf_op jit(solution)/shard_map/mlp_unpack/pallas_call | solution.py:1572
  608.9 3.2 attend_unpack.1
  615.4 3.2 fusion
  618.7 3.3 fusion.2
  623.3 17.2 %closing.1 = (f32[4,2,288]{2,1,0:T(2,128)}, bf16[8,2,144,432]{3,2,1,0:T(8,128)(2,1)}) custom-call(f32[4,2,288]{2,1,0:T(2,128)} %reshape.461.refs_0_, bf16[2,144,432]{2,1,0:T(8,128)(2,1)} %fusion.16.refs_1_), custom_call_target="tpu_custom_call" | custom-call | bytes 18432 | tf_op jit(solution)/shard_map/closing/pallas_call | solution.py:638
  640.5 6.5 project_unpack.1
  648.6 7.8 %adaptive_grad.1 = f32[2,288,6912]{2,1,0:T(8,128)} custom-call(bf16[8,288]{1,0:T(8,128)(2,1)} %get-tuple-element.150.silu, bf16[2,8,6912]{2,1,0:T(8,128)(2,1)} %pad_maximum_fusion.6.mods), custom_call_target="tpu_custom_call" | custom-call | bytes 15925248 | tf_op jit(solution)/shard_map/adaptive_grad/pallas_call | solution.py:1572
  656.4 2.1 fusion.56
  (273 shorter events, 51.7 us)
Async XLA Ops:
  3.7 1.6 copy-start.3
  5.2 2.7 copy-start.23
  5.2 3.5 copy-start.32
  8.0 3.1 copy-start.34
  8.0 3.8 copy-start.46
  8.0 4.4 copy-start.47
  52.7 4.3 copy-start.20
  58.4 215.1 %copy-start.24 = (bf16[2,128,48]{1,2,0:T(8,128)(2,1)}, bf16[2,128,48]{1,2,0:T(8,128)(2,1)S(1)}, u32[]{:S(2)}) copy-start(bf16[2,128,48]{1,2,0:T(8,128)(2,1)S(1)} %convolution_convert_fusion) | copy-start | bytes 73732
  58.6 2.8 copy-start.16
  64.4 1.6 copy-start.42
  66.9 64.6 %copy-start.28 = (s32[768]{0:T(1024)}, s32[768]{0:T(1024)S(1)}, u32[]{:S(2)}) copy-start(s32[768]{0:T(1024)S(1)} %add.314) | copy-start | bytes 9220
  269.8 2.5 copy-start.1
  270.9 3.8 copy-start.5
  272.4 2.4 copy-start.37
  272.6 2.1 copy-start.44
  276.2 39.1 %copy-start.29 = (s32[768]{0:T(1024)S(1)}, s32[768]{0:T(1024)}, u32[]{:S(2)}) copy-start(s32[768]{0:T(1024)} %copy-done.28) | copy-start | bytes 9220
  276.2 39.1 %copy-start.43 = (s32[2]{0:T(128)S(1)}, s32[2]{0:T(128)}, u32[]{:S(2)}) copy-start(s32[2]{0:T(128)} %param.24) | copy-start | bytes 28
  316.3 59.7 %slice-start = ((f32[2,128,1152]{2,1,0:T(8,128)}), f32[2,32,1152]{2,1,0:T(8,128)S(1)}, s32[]{:S(2)}) async-start(f32[2,128,1152]{2,1,0:T(8,128)} %subtract_multiply_fusion.refs_0_), calls=%async_computation | async-start | bytes 589824 | tf_op jit(solution)/shard_map/slice | solution.py:1968
  431.3 1.5 copy-start.14
  431.3 2.3 copy-start.10
  433.7 2.1 copy-start.7
  531.9 1.6 copy-start.15
  531.9 2.4 copy-start.8
  540.0 1.9 copy-start.40
  540.0 1.9 copy-start.39
  608.9 3.2 copy-start.11
  613.4 1.8 copy-start.19
  618.7 3.4 copy-start.4
  648.6 7.8 %copy-start.33 = (bf16[8,288]{1,0:T(8,128)(2,1)S(1)}, bf16[8,288]{1,0:T(8,128)(2,1)}, u32[]{:S(2)}) copy-start(bf16[8,288]{1,0:T(8,128)(2,1)} %get-tuple-element.150.silu) | copy-start | bytes 13828
  656.4 2.1 copy-start.36
  656.4 2.2 copy-start.35
  656.4 2.8 copy-start.12
  (18 other events, 23.3 us)

commit v7 on v6

--- a/solution.py
+++ b/solution.py
@@ -777,7 +777,7 @@
     block_biases = take(2 * depth)
     patch_term, final_term, edge_rows, tokens = take(4)
     all_mods, all_rows, all_tokens = take(3)
-    mods, sums, biases, mods_in, sums_in, rank_mods, rank_sums, rank_biases_in, ps, pr, zs, zr, qs, qr = refs
+    mods, sums, biases, mods_low, sums_low, mods_in, sums_in, rank_mods, rank_sums, rank_biases_in, ps, pr, zs, zr, qs, qr = refs
     ranks, peers = other_ranks(), plane_peers()
     rank = lax.axis_index("batch")
     around = sides()
@@ -813,12 +813,14 @@
     for n, source in enumerate(block_biases):
         biases[n, : source.shape[1]] = source[0]
 
+    mods_low[...] = mods[...].astype(bf16)
+    sums_low[...] = sums[...].astype(bf16)
     greet(ranks + peers)
     first = []
     for n, who in enumerate(peers):
         there = lax.rem(who["col"], 2) * 4 + who["row"] * 2 + who["col"] // 2
-        first.append(remote(mods.at[there], mods_in.at[n], ps.at[0, n], pr.at[0, n], who))
-        first.append(remote(sums.at[there], sums_in.at[n], ps.at[1, n], pr.at[1, n], who))
+        first.append(remote(mods_low.at[there], mods_in.at[n], ps.at[0, n], pr.at[0, n], who))
+        first.append(remote(sums_low.at[there], sums_in.at[n], ps.at[1, n], pr.at[1, n], who))
     second = [
         remote(biases, rank_biases_in.at[n], zs.at[0, n], zr.at[0, n], who) for n, who in enumerate(ranks)
     ]
@@ -831,8 +833,8 @@
         copy.wait()
     mod_total, sum_total = mods[place], sums[place]
     for n in range(len(peers)):
-        mod_total = mod_total + mods_in[n]
-        sum_total = sum_total + sums_in[n]
+        mod_total = mod_total + mods_in[n].astype(f32)
+        sum_total = sum_total + sums_in[n].astype(f32)
     rank_mods[rank] = mod_total.astype(bf16)
     rank_sums[rank] = sum_total
     third = []
@@ -888,8 +890,10 @@
             pltpu.VMEM(mods, f32),
             pltpu.VMEM(sums, f32),
             pltpu.VMEM(biases, f32),
-            pltpu.VMEM((7,) + mods[1:], f32),
-            pltpu.VMEM((7,) + sums[1:], f32),
+            pltpu.VMEM(mods, bf16),
+            pltpu.VMEM(sums, bf16),
+            pltpu.VMEM((7,) + mods[1:], bf16),
+            pltpu.VMEM((7,) + sums[1:], bf16),
             pltpu.VMEM((ranks,) + mods[1:], bf16),
             pltpu.VMEM((ranks,) + sums[1:], f32),
             pltpu.VMEM((ranks - 1,) + biases, f32),
@@ -982,11 +986,11 @@
 
     background.tick()
     begin(0)
+    gathers[0].second()
+    begin(1)
     moving.wait("pair")
     expand[...] = pair[:, : expand.shape[1]]
     shrink[...] = pair[:, expand.shape[1] :]
-    gathers[0].second()
-    begin(1)
     gathers[0].finish()
     compute(0, (gathers[1].second, scatters[0].first))
     keep(0)
@@ -1105,11 +1109,11 @@
 
     background.tick()
     begin(0)
+    gathers[0].second()
+    begin(1)
     moving.wait("pair")
     expand[...] = pair[:, : expand.shape[1]]
     shrink[...] = pair[:, expand.shape[1] :]
-    gathers[0].second()
-    begin(1)
     gathers[0].finish()
     moving.wait("hidden")
     compute(0, (gathers[1].second, scatters[0].first))
@@ -1286,17 +1290,16 @@
 
     background.tick()
     begin(0)
+    gathers[0].second()
+    begin(1)
     project[...] = pad_lanes(project_own[...])
     attend[...] = pad_rows(attend_own[...])
-    gathers[0].second()
-    begin(1)
     gathers[0].finish()
     compute(0, (gathers[1].second, background.tick, scatters[0].first))
     keep(0)
     gathers[1].finish()
-    compute(1, (scatters[0].second, nothing, scatters[1].first))
+    compute(1, (scatters[0].second, background.tick, scatters[1].first))
     keep(1)
-    background.tick()
     end(0)
     scatters[1].second()
     end(1)
@@ -1587,10 +1590,13 @@
 
         @pl.when(pl.program_id(0) == k)
         def _(every=every):
-            first, second = every[0, 0].astype(f32), every[1, 0].astype(f32)
-            inner = first.shape[1] // 2
-            expand[0] = jnp.concatenate([first[:, :inner], second[:, :inner]], axis=1)
-            shrink[0] = jnp.concatenate([first[:, inner:], second[:, inner:]], axis=1)
+            pair = every.shape[3]
+            inner = pair // 2
+            for chip in range(4):
+                first, second = every[0, chip].astype(f32), every[1, chip].astype(f32)
+                lanes = pl.ds(chip * pair, pair)
+                expand[0, :, lanes] = jnp.concatenate([first[:, :inner], second[:, :inner]], axis=1)
+                shrink[0, :, lanes] = jnp.concatenate([first[:, inner:], second[:, inner:]], axis=1)
 
 
 def mlp_unpack(everys):
@@ -1598,15 +1604,17 @@
     _, _, half, pair = everys[0].shape
     shard, inner = 2 * half, pair // 2
     everys = [every.reshape(2, 4, shard, pair) for every in everys]
-    block = (2, 1, shard, pair)
+    steps = 3 if shard % 48 == 0 else 1
+    rows = shard // steps
+    block = (2, 4, rows, pair)
     return local_call(
         mlp_unpack_kernel,
         "mlp_unpack",
-        (depth, 4),
-        [pl.BlockSpec(block, lambda b, j, k=k: (0, turn(b, k, j, 3), 0, 0)) for k in range(depth)],
+        (depth, steps),
+        [pl.BlockSpec(block, lambda b, j, k=k: (0, 0, turn(b, k, j, steps - 1), 0)) for k in range(depth)],
         [
-            pl.BlockSpec((1, shard, 2 * inner), lambda b, j: (b, 0, j)),
-            pl.BlockSpec((1, shard, 2 * inner), lambda b, j: (b, 0, j)),
+            pl.BlockSpec((1, rows, 8 * inner), lambda b, j: (b, j, 0)),
+            pl.BlockSpec((1, rows, 8 * inner), lambda b, j: (b, j, 0)),
         ],
         [shaped((depth, shard, 8 * inner), f32), shaped((depth, shard, 8 * inner), f32)],
         depth * shard * inner * 96,
@@ -1701,12 +1709,12 @@
     (grad,) = local_call(
         adaptive_grad_kernel,
         "adaptive_grad",
-        (depth, 3),
+        (depth, 1),
         [
             pl.BlockSpec((count, shard), lambda b, j: (0, 0)),
-            pl.BlockSpec((1, count, columns // 3), lambda b, j: (b, 0, j)),
+            pl.BlockSpec((1, count, columns), lambda b, j: (b, 0, j)),
         ],
-        [pl.BlockSpec((1, shard, columns // 3), lambda b, j: (b, 0, j))],
+        [pl.BlockSpec((1, shard, columns), lambda b, j: (b, 0, j))],
         [shaped((depth, shard, columns), f32)],
         depth * shard * columns * 4,
         [silu, mods],

time: 680 us -> 677 us (level)
  no operation moved by 1% of the time
where the time goes in v7:
time: 677 us; the launch traced here: 667 us
  Pallas kernels  583 us (86%)
  local copies, waits for them, and re-layouts  37.8 us (6%)
  other arithmetic  27.8 us (4%)
  matrix products  16.6 us (2%)
    pallas_call x11, Pallas kernels, call(): pl.pallas_call(run, name=name, out_shape=list(outs) + task_outs, in_specs...  552 us
    pallas_call x4, Pallas kernels, local_call(): pl.pallas_call(kernel, name=name, grid_spec=pltpu.PrefetchScalarGridSpec(...  30.4 us

profile of v7, /device:TPU:0, one launch (start us, length us, event | category | flops | bytes accessed | tf_op | source)
XLA Modules:
  0.0 667.1 jit_solution(16031311445847016800)
XLA Ops:
  0.7 1.7 constant_dynamic-slice_fusion.14
  5.2 2.7 bitcast_select_fusion.refs_10_
  12.9 38.0 %prologue.1 = (bf16[4,80,288]{2,1,0:T(8,128)(2,1)}, bf16[8,96,128]{2,1,0:T(8,128)(2,1)}, bf16[8,288]{1,0:T(8,128)(2,1)}, f32[8,4,1152]{2,1,0:T(4,128)}, bf16[4,2...) custom-call(bf16[16,288]{1,0:T(8,128)(2,1)} %refs_0_.1, bf16[32,288]{1,0:T(8,128)(2,1)} %bitcast.253, ...), custom_call_target="tpu_custom_call" | custom-call | bytes 1934784 | tf_op jit(solution)/shard_map/prologue/pallas_call | solution.py:638
  60.0 1.4 fusion.6.refs_0_.refs_1_
  61.3 1.5 constant_dynamic-slice_fusion.9
  62.8 1.5 dynamic-slice_bitcast_fusion
  64.4 1.5 fusion.15
  67.6 63.9 %attention_forward.2 = (bf16[2,8,128,1152]{3,2,1,0:T(8,128)(2,1)}, bf16[2,1024,768]{2,1,0:T(8,128)(2,1)}, bf16[2,1024,256]{2,1,0:T(8,128)(2,1)}, f32[2,2,4,256]{...) custom-call(f32[2,128,1152]{2,1,0:T(8,128)} %fusion.6.refs_0_.refs_1, ...), custom_call_target="tpu_custom_call" | custom-call | flops 28991029248 | bytes 16330496 | tf_op jit(solution)/shard_map/attention_forward/pallas_call | solution.py:638
  132.4 46.4 %mlp_forward.2 = (bf16[2,8,128,1152]{3,2,1,0:T(8,128)(2,1)}, f32[2,8,128,576]{3,2,1,0:T(8,128)}, f32[2,128,1152]{2,1,0:T(8,128)}, f32[2,128,1152]{2,1,0:T(8,128)...) custom-call(f32[2,128,1152]{2,1,0:T(8,128)} %get-tuple-element.94.refs_0_.refs_1_, ...), custom_call_target="tpu_custom_call" | custom-call | flops 32614907904 | bytes 15799296 | tf_op jit(solution)/shard_map/mlp_forward/pallas_call | solution.py:638
  178.7 55.7 %attention_forward.3 = (bf16[2,8,96,1152]{3,2,1,0:T(8,128)(2,1)}, bf16[2,768,768]{2,1,0:T(8,128)(2,1)}, bf16[2,768,256]{2,1,0:T(8,128)(2,1)}, f32[2,2,4,192]{3,2...) custom-call(f32[2,128,1152]{2,1,0:T(8,128)} %get-tuple-element.96.re, ...), custom_call_target="tpu_custom_call" | custom-call | flops 21743271936 | bytes 13508352 | tf_op jit(solution)/shard_map/attention_forward/pallas_call | solution.py:638
  234.4 35.9 %mlp_forward.3 = (bf16[2,8,96,1152]{3,2,1,0:T(8,128)(2,1)}, f32[2,8,96,576]{3,2,1,0:T(8,128)}, f32[2,96,1152]{2,1,0:T(8,128)}, f32[2,96,1152]{2,1,0:T(8,128)}) custom-call(f32[2,96,1152]{2,1,0:T(8,128)} %get-tuple-element.99.refs_0_.refs_1_, f32[2,96,1]{2,1,0:T(8,128)} %compare_convert_fusion.refs_1_.refs_3_, ...), custom_call_target="tpu_custom_call" | custom-call | flops 24461180928 | bytes 12555264 | tf_op jit(solution)/shard_map/mlp_forward/pallas_call | solution.py:638
  271.5 1.4 fusion.27
  274.1 1.2 multiply_reduce_fusion
  275.3 1.4 subtract_multiply_fusion.refs_0_
  276.7 39.0 %mlp_backward.2 = (f32[2,96,1152]{2,1,0:T(8,128)}, f32[2,8,1152]{2,1,0:T(8,128)}, bf16[1152,1152]{1,0:T(8,128)(2,1)}, f32[8,576]{1,0:T(8,128)}) custom-call(f32[2,128,1152]{2,1,0:T(8,128)} %subtract_multiply_fusion.refs_0_, f32[2,96,1152]{2,1,0:T(8,128)} %get-tuple-element.99.refs_0_.refs_1_, f32[2,96,1152]{2,1,0:T(8,128)} %get-tuple-element.102.refs_2_, ...), custom_call_target="tpu_custom_call" | custom-call | flops 48922361856 | bytes 16478976 | tf_op jit(solution)/shard_map/mlp_backward/pallas_call | solution.py:638
  316.8 58.7 %attention_backward.2 = (f32[2,96,1152]{2,1,0:T(8,128)}, f32[2,8,1152]{2,1,0:T(8,128)}, bf16[1152,432]{1,0:T(8,128)(2,1)}, bf16[2,72,1152]{2,1,0:T(8,128)(2,1)},...) custom-call(f32[2,96,1152]{2,1,0:T(8,128)} %get-tuple-element.105.refs_0_, ...), custom_call_target="tpu_custom_call" | custom-call | flops 43486543872 | bytes 14488320 | tf_op jit(solution)/shard_map/attention_backward/pallas_call | solution.py:638
  375.5 2.3 pad_maximum_fusion.1.refs_0_
  377.8 53.7 %mlp_backward.3 = (f32[2,128,1152]{2,1,0:T(8,128)}, f32[2,8,1152]{2,1,0:T(8,128)}, bf16[1152,1152]{1,0:T(8,128)(2,1)}, f32[8,576]{1,0:T(8,128)}, bf16[3,288,432]...) custom-call(f32[2,128,1152]{2,1,0:T(8,128)} %pad_maximum_fusion.1.refs_0_, ...), custom_call_target="tpu_custom_call" | custom-call | flops 65229815808 | bytes 19723008 | tf_op jit(solution)/shard_map/mlp_backward/pallas_call | solution.py:638
  431.6 1.5 convert_reduce_fusion.3
  436.2 1.1 constant_dynamic-slice_fusion.8
  438.4 93.4 %attention_backward.3 = (f32[2,128,1152]{2,1,0:T(8,128)}, f32[2,8,1152]{2,1,0:T(8,128)}, bf16[1152,432]{1,0:T(8,128)(2,1)}, bf16[2,72,1152]{2,1,0:T(8,128)(2,1)}...) custom-call(f32[2,128,1152]{2,1,0:T(8,128)} %get-tuple-element.120.r, ...), custom_call_target="tpu_custom_call" | custom-call | flops 57982058496 | bytes 17605376 | tf_op jit(solution)/shard_map/attention_backward/pallas_call | solution.py:638
  531.8 1.6 convert_reduce_fusion.2
  534.5 1.1 constant_dynamic-slice_fusion.6
  542.5 50.7 %epilogue.1 = (bf16[8,4,4,1152]{3,2,1,0:T(4,128)(2,1)}, f32[8,2,8,1152]{3,2,1,0:T(8,128)}, f32[8,2,24,256]{3,2,1,0:T(8,128)}, bf16[3,288,432]{2,1,0:T(8,128)(2,1...) custom-call(f32[2,8,1152]{2,1,0:T(8,128)} %get-tuple-element.132.refs_0_, ...), custom_call_target="tpu_custom_call" | custom-call | bytes 1956864 | tf_op jit(solution)/shard_map/epilogue/pallas_call | solution.py:638
  593.2 12.7 %mlp_unpack.1 = (f32[2,288,4608]{2,1,0:T(8,128)}, f32[2,288,4608]{2,1,0:T(8,128)}) custom-call(bf16[2,4,288,1152]{3,2,1,0:T(8,128)(2,1)} %bitcast.208, bf16[2,4,288,1152]{3,2,1,0:T(8,128)(2,1)} %bitcast.207), custom_call_target="tpu_custom_call" | custom-call | bytes 31850496 | tf_op jit(solution)/shard_map/mlp_unpack/pallas_call | solution.py:1575
  605.9 3.2 attend_unpack.1
  612.3 3.2 fusion
  615.7 3.3 fusion.2
  620.2 16.8 %closing.1 = (f32[4,2,288]{2,1,0:T(2,128)}, bf16[8,2,144,432]{3,2,1,0:T(8,128)(2,1)}) custom-call(f32[4,2,288]{2,1,0:T(2,128)} %reshape.461.refs_0_, bf16[2,144,432]{2,1,0:T(8,128)(2,1)} %fusion.16.refs_1_), custom_call_target="tpu_custom_call" | custom-call | bytes 18432 | tf_op jit(solution)/shard_map/closing/pallas_call | solution.py:638
  637.0 6.5 project_unpack.1
  645.2 8.0 %adaptive_grad.1 = f32[2,288,6912]{2,1,0:T(8,128)} custom-call(bf16[8,288]{1,0:T(8,128)(2,1)} %get-tuple-element.150.silu, bf16[2,8,6912]{2,1,0:T(8,128)(2,1)} %pad_maximum_fusion.6.mods), custom_call_target="tpu_custom_call" | custom-call | bytes 15925248 | tf_op jit(solution)/shard_map/adaptive_grad/pallas_call | solution.py:1575
  653.2 2.1 fusion.56
  (273 shorter events, 51.7 us)
Async XLA Ops:
  3.7 1.6 copy-start.3
  5.2 2.7 copy-start.23
  5.2 3.5 copy-start.32
  8.0 3.1 copy-start.34
  8.0 3.8 copy-start.46
  8.0 4.4 copy-start.47
  52.7 4.3 copy-start.20
  58.4 215.6 %copy-start.24 = (bf16[2,128,48]{1,2,0:T(8,128)(2,1)}, bf16[2,128,48]{1,2,0:T(8,128)(2,1)S(1)}, u32[]{:S(2)}) copy-start(bf16[2,128,48]{1,2,0:T(8,128)(2,1)S(1)} %convolution_convert_fusion) | copy-start | bytes 73732
  58.6 2.8 copy-start.16
  64.4 1.6 copy-start.42
  66.9 64.6 %copy-start.28 = (s32[768]{0:T(1024)}, s32[768]{0:T(1024)S(1)}, u32[]{:S(2)}) copy-start(s32[768]{0:T(1024)S(1)} %add.314) | copy-start | bytes 9220
  270.4 2.5 copy-start.1
  271.5 3.8 copy-start.5
  272.9 2.4 copy-start.37
  273.2 2.1 copy-start.44
  276.7 39.1 %copy-start.29 = (s32[768]{0:T(1024)S(1)}, s32[768]{0:T(1024)}, u32[]{:S(2)}) copy-start(s32[768]{0:T(1024)} %copy-done.28) | copy-start | bytes 9220
  276.7 39.1 %copy-start.43 = (s32[2]{0:T(128)S(1)}, s32[2]{0:T(128)}, u32[]{:S(2)}) copy-start(s32[2]{0:T(128)} %param.24) | copy-start | bytes 28
  316.8 58.7 %slice-start = ((f32[2,128,1152]{2,1,0:T(8,128)}), f32[2,32,1152]{2,1,0:T(8,128)S(1)}, s32[]{:S(2)}) async-start(f32[2,128,1152]{2,1,0:T(8,128)} %subtract_multiply_fusion.refs_0_), calls=%async_computation | async-start | bytes 589824 | tf_op jit(solution)/shard_map/slice | solution.py:1976
  431.6 1.5 copy-start.14
  431.6 2.3 copy-start.10
  433.9 2.1 copy-start.7
  531.8 1.6 copy-start.15
  531.8 2.4 copy-start.8
  539.9 1.9 copy-start.40
  539.9 1.9 copy-start.39
  605.9 3.2 copy-start.11
  610.3 1.8 copy-start.19
  615.7 3.4 copy-start.4
  645.2 8.0 %copy-start.33 = (bf16[8,288]{1,0:T(8,128)(2,1)S(1)}, bf16[8,288]{1,0:T(8,128)(2,1)}, u32[]{:S(2)}) copy-start(bf16[8,288]{1,0:T(8,128)(2,1)} %get-tuple-element.150.silu) | copy-start | bytes 13828
  653.2 2.1 copy-start.36
  653.2 2.2 copy-start.35
  653.2 2.8 copy-start.12
  (18 other events, 23.3 us)
